TPU v7x, 32 devices: a whole 2x2x4 slice. The times are simulated.
32 devices in a mesh: gx: 4 (over y, core), gy: 8 (over z, x).
Axes of the slice: x: 2, y: 2, z: 4, core: 2. Of those that a mesh axis runs over, the one named last changes fastest.
Arguments:
- control: float32 [1, 2, 6, 384, 1536], P(None, None, None, 'gy', 'gx'), may hold values from -6 to 6
- sigma: float32 [2, 6, 384, 1536], P(None, None, 'gy', 'gx'), may hold values from 0.5 to 5
- kappa: float32 [5, 384, 1536], P(None, 'gy', 'gx'), may hold values from 0.05 to 5
- beta: float32 [6, 384, 1536], P(None, 'gy', 'gx'), may hold values from -3 to 3
- sea_mask: int32 [384, 1536], P('gy', 'gx'), may hold values 0 or 1
- x_inverse: float32 [1536, 1536], P('gx'), as said below
- y_inverse: float32 [384, 384], P('gx')
- ssh_coef: float32 [2, 6], replicated, may hold values from -1.5 to 1.5
- obs_owner: int32 [1024, 1], P(('gx', 'gy')), may hold values from 0 to 31; in each aligned block of 32 rows (0 to 31, 32 to 63, ...) at most 2 rows name the same one
- tile_index: int32 [1024], P(('gx', 'gy')), may hold values from 0 to 18046, as said below
- obs_frac: float32 [2, 1024], P(None, ('gx', 'gy')), may hold values from 0 to 1
- obs_count: int32 [32], P(('gx', 'gy')), may hold values from 16 to 32
Outputs:
- increments: float32 [1, 2, 6, 384, 1536], P(None, None, None, 'gy', 'gx')
- sea_height: float32 [1, 384, 1536], P(None, 'gy', 'gx')
- obs_equiv: float32 [2, 13, 1024], P(None, None, ('gx', 'gy'))
Inputs may be any that keep to these rules, and one draw needn't show every extreme that they name: `obs_owner`: among the slots of one device, at most 2 name the same owner. `tile_index`: row * 384 + column of a cell in the device's own tile, with row below 47 and column below 383. `x_inverse`: the zonal inverse is symmetric.
All inputs are finite; a program needn't handle non-finite values. No bound on the sum of `sea_mask` on one device may be relied on, other than what follows from the above.
Results may differ from a plain program's by a relative error of at most 0.00013.
Values sent between devices are 32-bit elements; how exact they have to be, the bound alone decides.
No kernel may reach another device: no remote copies, remote signals or barrier semaphores. Data moves between devices by JAX's collectives and lax.ppermute only.
A program may use at most 128 MiB of HBM per device.

v0:
```python
import functools

import jax
import jax.numpy as jnp
from jax import lax
from jax.experimental import pallas as pl
from jax.experimental.pallas import tpu as pltpu
from jax.sharding import PartitionSpec as P

STEPS = 2
CAP = 2
LANES = 128
SUB = 8
RANK_ROWS = 16
NN = (((1,), (0,)), ((), ()))
NT = (((1,), (1,)), ((), ()))


class Plan:
    def __init__(self, fields, rows, cols, parts):
        self.fields, self.rows, self.cols, self.parts = fields, rows, cols, parts
        self.blocks = cols // LANES
        tiles = fields * self.blocks
        share = fields * cols // parts
        self.full = share // LANES
        self.rest = share % LANES
        self.sides = LANES // self.rest if self.rest else 0
        self.groups = rows // SUB
        self.packs = -(-self.groups // self.sides) if self.rest else 0
        self.width = self.full * rows + self.packs * SUB
        self.columns = (self.full + (1 if self.rest else 0)) * LANES
        self.fits = (
            cols % LANES == 0
            and rows % SUB == 0
            and fields * cols % parts == 0
            and (self.rest == 0 or LANES % self.rest == 0)
            and tiles - self.full * parts == (parts // self.sides if self.rest else 0)
        )

    def home(self, tile):
        if tile < self.full * self.parts:
            return tile // self.full, tile % self.full
        return None, tile - self.full * self.parts

    def pack_rest(self, tile, place):
        lane_side = lax.broadcasted_iota(jnp.int32, (SUB, LANES), 1) // self.rest
        out = []
        for pack in range(self.packs):
            joined = None
            for side in range(self.sides):
                group = pack * self.sides + side
                if group >= self.groups:
                    break
                piece = tile[group * SUB : (group + 1) * SUB, :]
                shift = ((side - place) * self.rest) % LANES
                if shift:
                    piece = pltpu.roll(piece, shift, axis=1)
                joined = piece if joined is None else jnp.where(lane_side == side, piece, joined)
            out.append(joined)
        return out

    def unpack_rest(self, packs, place):
        pieces = []
        for group in range(self.groups):
            pack, side = divmod(group, self.sides)
            shift = ((place - side) * self.rest) % LANES
            piece = packs[pack]
            pieces.append(pltpu.roll(piece, shift, axis=1) if shift else piece)
        return jnp.concatenate(pieces, axis=0)

    def store_tile(self, out_ref, tile_index, tile):
        device, place = self.home(tile_index)
        if device is not None:
            out_ref[device, place * self.rows : (place + 1) * self.rows, :] = tile
            return
        for side in range(self.sides):
            device = place * self.sides + side
            for pack, value in enumerate(self.pack_rest(tile, side)):
                start = self.full * self.rows + pack * SUB
                out_ref[device, start : start + SUB, :] = value

    def load_tile(self, in_ref, tile_index):
        device, place = self.home(tile_index)
        if device is not None:
            return in_ref[device, place * self.rows : (place + 1) * self.rows, :]
        lane_side = lax.broadcasted_iota(jnp.int32, (self.rows, LANES), 1) // self.rest
        joined = None
        for side in range(self.sides):
            packs = self.load_packs(in_ref, place * self.sides + side)
            piece = self.unpack_rest(packs, side)
            joined = piece if joined is None else jnp.where(lane_side == side, piece, joined)
        return joined

    def load_packs(self, in_ref, device):
        base = self.full * self.rows
        return [in_ref[device, base + p * SUB : base + (p + 1) * SUB, :] for p in range(self.packs)]


def split(value):
    high = value.astype(jnp.bfloat16)
    low = (value - high.astype(jnp.float32)).astype(jnp.bfloat16)
    return high, low


def dot(a, b, dims=NN):
    return lax.dot_general(a, b, dims, preferred_element_type=jnp.float32)


def dot_split(a, b):
    return dot(a[0], b[0]) + (dot(a[0], b[1]) + dot(a[1], b[0]))


def call(kernel, out_shape, operands, scalars=(), flops=0):
    outs = out_shape if isinstance(out_shape, (list, tuple)) else [out_shape]
    moved = sum(a.size * a.dtype.itemsize for a in list(operands) + list(outs))
    specs = [
        pl.BlockSpec(memory_space=pltpu.SMEM if i in scalars else pltpu.VMEM)
        for i in range(len(operands))
    ]
    out_spec = pl.BlockSpec(memory_space=pltpu.VMEM)
    many = isinstance(out_shape, (list, tuple))
    return pl.pallas_call(
        kernel,
        out_shape=out_shape,
        in_specs=specs,
        out_specs=[out_spec] * len(outs) if many else out_spec,
        compiler_params=pltpu.CompilerParams(vmem_limit_bytes=min(48, 6 + 3 * moved // 2**20) * 2**20),
        cost_estimate=pl.CostEstimate(flops=flops, bytes_accessed=moved, transcendentals=0),
    )(*operands)


def gather_pieces(block, axis, count):
    held = [(0, block)]
    bit = count // 2
    while bit:
        pairs = [(i, i ^ bit) for i in range(count)]
        held = held + [(mask ^ bit, lax.ppermute(piece, axis, pairs)) for mask, piece in held]
        bit //= 2
    return held


def prepare_x(x_inverse):
    rows, cols = x_inverse.shape

    def kernel(x_ref, high_ref, low_ref):
        for start in range(0, cols, rows):
            high, low = split(jnp.transpose(x_ref[:, start : start + rows]))
            high_ref[start : start + rows, :] = high
            low_ref[start : start + rows, :] = low

    shape = jax.ShapeDtypeStruct((cols, rows), jnp.bfloat16)
    return call(kernel, [shape, shape], [x_inverse])


def prepare_y(masks, pieces, me):
    rows, cols = pieces[0].shape

    def kernel(me_ref, *refs):
        high_ref, low_ref = refs[-2:]
        for mask, ref in zip(masks, refs):
            start = pl.multiple_of((me_ref[0] ^ mask) * rows, rows)
            high, low = split(ref[...])
            high_ref[pl.ds(start, rows), :] = high
            low_ref[pl.ds(start, rows), :] = low

    shape = jax.ShapeDtypeStruct((cols, cols), jnp.bfloat16)
    return call(kernel, [shape, shape], [me] + pieces, scalars=(0,))


def zonal(plan, masks, pieces, me, x_high, x_low, sea_mask):
    fields, rows, cols = plan.fields, plan.rows, plan.cols

    def kernel(me_ref, high_ref, low_ref, sea_ref, *refs):
        out_ref = refs[-1]
        total = None
        for mask, ref in zip(masks, refs):
            start = pl.multiple_of((me_ref[0] ^ mask) * cols, cols)
            values = split(ref[...].reshape(fields * rows, cols))
            weights = (high_ref[pl.ds(start, cols), :], low_ref[pl.ds(start, cols), :])
            part = dot_split(values, weights)
            total = part if total is None else total + part
        total = total.reshape(fields, rows, cols)
        sea = sea_ref[...].astype(jnp.float32)
        for block in range(plan.blocks):
            lanes = slice(block * LANES, (block + 1) * LANES)
            for field in range(fields):
                tile = sea[:, lanes] * total[field, :, lanes]
                plan.store_tile(out_ref, field * plan.blocks + block, tile)

    return call(
        kernel,
        jax.ShapeDtypeStruct((plan.parts, plan.width, LANES), jnp.float32),
        [me, x_high, x_low, sea_mask] + pieces,
        scalars=(0,),
        flops=6 * fields * rows * cols * cols * len(pieces),
    )


def meridional(plan, lines, y_high, y_low):
    rows, parts = plan.rows, plan.parts

    def kernel(in_ref, high_ref, low_ref, out_ref):
        columns = [
            in_ref[:, i * rows : (i + 1) * rows, :].reshape(parts * rows, LANES)
            for i in range(plan.full)
        ]
        if plan.rest:
            columns.append(
                jnp.concatenate(
                    [plan.unpack_rest(plan.load_packs(in_ref, d), 0) for d in range(parts)], axis=0
                )
            )
        values = split(jnp.concatenate(columns, axis=1))
        solved = dot_split((high_ref[...], low_ref[...]), values)
        for i in range(plan.full):
            tile = solved[:, i * LANES : (i + 1) * LANES]
            out_ref[:, i * rows : (i + 1) * rows, :] = tile.reshape(parts, rows, LANES)
        if plan.rest:
            last = solved[:, plan.full * LANES :]
            for d in range(parts):
                packs = plan.pack_rest(last[d * rows : (d + 1) * rows, :], 0)
                for p, value in enumerate(packs):
                    start = plan.full * rows + p * SUB
                    out_ref[d, start : start + SUB, :] = value

    return call(
        kernel,
        jax.ShapeDtypeStruct(lines.shape, jnp.float32),
        [lines, y_high, y_low],
        flops=6 * (parts * rows) ** 2 * plan.columns,
    )


def solve_columns(plan, in_ref, kappa_ref, sea_ref, levels, store):
    kinds = plan.fields // levels
    for block in range(plan.blocks):
        lanes = slice(block * LANES, (block + 1) * LANES)
        sea = sea_ref[:, lanes].astype(jnp.float32)
        inverse, upper = [], []
        kappa = [kappa_ref[level, :, lanes] for level in range(levels - 1)]
        for level in range(levels):
            below = kappa[level - 1] if level > 0 else 0.0
            above = kappa[level] if level < levels - 1 else 0.0
            pivot = 1.0 + below + above
            if level > 0:
                pivot = pivot + below * upper[-1]
            inverse.append(1.0 / pivot)
            upper.append(-above * inverse[-1])
        for kind in range(kinds):
            forward = []
            for level in range(levels):
                tile = plan.load_tile(in_ref, (kind * levels + level) * plan.blocks + block)
                right = sea * tile
                if level > 0:
                    right = right + kappa[level - 1] * forward[-1]
                forward.append(right * inverse[level])
            value = forward[-1]
            store(kind, levels - 1, lanes, value)
            for level in range(levels - 2, -1, -1):
                value = forward[level] - upper[level] * value
                store(kind, level, lanes, value)


def vertical(plan, returned, kappa, sea_mask, levels):
    def kernel(in_ref, kappa_ref, sea_ref, out_ref):
        def store(kind, level, lanes, value):
            out_ref[kind * levels + level, :, lanes] = value

        solve_columns(plan, in_ref, kappa_ref, sea_ref, levels, store)

    return call(
        kernel,
        jax.ShapeDtypeStruct((plan.fields, plan.rows, plan.cols), jnp.float32),
        [returned, kappa, sea_mask],
    )


def finish(plan, returned, temper_field, kappa, sea_mask, sigma, beta, ssh_coef, obs, devices):
    levels = sigma.shape[1]
    rows, cols = plan.rows, plan.cols
    records = 2 * levels + 1
    owner_row, tile_index, obs_frac, obs_count, owner_col = obs
    slots = owner_row.shape[1]
    extra = [] if temper_field is None else [temper_field]

    def kernel(ssh_ref, count_ref, in_ref, kappa_ref, sea_ref, sigma_ref, beta_ref,
               owner_ref, tile_ref, frac_ref, column_ref, *refs):
        inc_ref, height_ref, send_ref, profile_ref = refs[-4:]

        def store(kind, level, lanes, value):
            profile_ref[(kind + len(extra)) * levels + level, :, lanes] = value

        solve_columns(plan, in_ref, kappa_ref, sea_ref, levels, store)
        for block in range(plan.blocks):
            lanes = slice(block * LANES, (block + 1) * LANES)
            height = None
            for level in range(levels):
                source = refs[0] if extra else profile_ref
                temper = sigma_ref[0, level, :, lanes] * source[level, :, lanes]
                saline = (
                    sigma_ref[1, level, :, lanes] * profile_ref[levels + level, :, lanes]
                    + beta_ref[level, :, lanes] * temper
                )
                term = ssh_ref[0, level] * temper + ssh_ref[1, level] * saline
                height = term if height is None else height + term
                profile_ref[level, :, lanes] = temper
                profile_ref[levels + level, :, lanes] = saline
                inc_ref[0, level, :, lanes] = temper
                inc_ref[1, level, :, lanes] = saline
            profile_ref[2 * levels, :, lanes] = height
            height_ref[:, lanes] = height

        cell = tile_ref[...]
        row, col = cell // cols, cell % cols
        frac_x, frac_y = frac_ref[0:1, :], frac_ref[1:2, :]
        along = lax.broadcasted_iota(jnp.int32, (cols, slots), 0)
        weight_x = jnp.where(along == col, 1.0 - frac_x, jnp.where(along == col + 1, frac_x, 0.0))
        across = lax.broadcasted_iota(jnp.int32, (rows, slots), 0)
        weight_y = jnp.where(across == row, 1.0 - frac_y, jnp.where(across == row + 1, frac_y, 0.0))
        partial = lax.dot_general(
            profile_ref[...].reshape(records * rows, cols),
            weight_x,
            NN,
            precision=lax.Precision.HIGHEST,
            preferred_element_type=jnp.float32,
        ).reshape(records, rows, slots)
        interp = jnp.sum(partial * weight_y[None], axis=1)
        slot = lax.broadcasted_iota(jnp.int32, (1, slots), 1)
        interp = interp * (slot < count_ref[0]).astype(jnp.float32)
        earlier = lax.broadcasted_iota(jnp.int32, (slots, slots), 0) < lax.broadcasted_iota(
            jnp.int32, (slots, slots), 1
        )
        owner = owner_ref[...]
        same = jnp.where((column_ref[...] == owner) & earlier, 1.0, 0.0)
        rank = jnp.sum(same, axis=0, keepdims=True).astype(jnp.int32)
        padded = jnp.concatenate(
            [interp, jnp.zeros((RANK_ROWS - records, slots), jnp.float32)], axis=0
        )
        ranked = jnp.concatenate(
            [jnp.where(rank == r, padded, 0.0) for r in range(CAP)], axis=0
        )
        ranked = jnp.concatenate(
            [ranked, jnp.zeros((LANES - CAP * RANK_ROWS, slots), jnp.float32)], axis=0
        )
        to_owner = (owner == lax.broadcasted_iota(jnp.int32, (devices, slots), 0)).astype(
            jnp.float32
        )
        send_ref[...] = lax.dot_general(
            to_owner, ranked, NT, precision=lax.Precision.HIGHEST, preferred_element_type=jnp.float32
        )

    operands = [ssh_coef, obs_count, returned, kappa, sea_mask, sigma, beta,
                owner_row, tile_index, obs_frac, owner_col] + extra
    outs = [
        jax.ShapeDtypeStruct((2, levels, rows, cols), jnp.float32),
        jax.ShapeDtypeStruct((rows, cols), jnp.float32),
        jax.ShapeDtypeStruct((devices, LANES), jnp.float32),
    ]
    moved = sum(a.size * a.dtype.itemsize for a in operands + outs)
    return pl.pallas_call(
        kernel,
        out_shape=outs,
        in_specs=[pl.BlockSpec(memory_space=pltpu.SMEM)] * 2
        + [pl.BlockSpec(memory_space=pltpu.VMEM)] * (len(operands) - 2),
        out_specs=[pl.BlockSpec(memory_space=pltpu.VMEM)] * 3,
        scratch_shapes=[pltpu.VMEM((records, rows, cols), jnp.float32)],
        compiler_params=pltpu.CompilerParams(vmem_limit_bytes=32 * 2**20),
        cost_estimate=pl.CostEstimate(flops=10**7, bytes_accessed=moved, transcendentals=0),
    )(*operands)


def receive(arrived, records):
    devices = arrived.shape[0]

    def kernel(in_ref, out_ref):
        turned = jnp.transpose(in_ref[...])
        for r in range(CAP):
            out_ref[r] = turned[r * RANK_ROWS : r * RANK_ROWS + records, :]

    return call(kernel, jax.ShapeDtypeStruct((CAP, records, devices), jnp.float32), [arrived])


def body(gx_count, gy_count, control, sigma, kappa, beta, sea_mask, x_inverse, y_inverse, ssh_coef,
         obs_owner, tile_index, obs_frac, obs_count):
    _, kinds, levels, rows, cols = control.shape
    devices = gx_count * gy_count
    plan = Plan(levels, rows, cols, gy_count)
    chunks = kinds
    if not plan.fits:
        plan, chunks = Plan(kinds * levels, rows, cols, gy_count), 1
    me = lax.axis_index("gx").astype(jnp.int32).reshape(1)
    x_high, x_low = prepare_x(x_inverse)
    fields = list(control.reshape(chunks, plan.fields, rows, cols))
    y_parts = None
    result = None
    for step in range(STEPS):
        sent = []
        for chunk in range(chunks):
            held = gather_pieces(fields[chunk], "gx", gx_count)
            packed = zonal(
                plan, [m for m, _ in held], [p for _, p in held], me, x_high, x_low, sea_mask
            )
            sent.append(lax.all_to_all(packed, "gy", split_axis=0, concat_axis=0, tiled=True))
        if y_parts is None:
            held = gather_pieces(y_inverse, "gx", gx_count)
            y_parts = prepare_y([m for m, _ in held], [p for _, p in held], me)
        for chunk in range(chunks):
            solved = meridional(plan, sent[chunk], *y_parts)
            returned = lax.all_to_all(solved, "gy", split_axis=0, concat_axis=0, tiled=True)
            if step < STEPS - 1 or chunk < chunks - 1:
                fields[chunk] = vertical(plan, returned, kappa, sea_mask, levels)
            else:
                obs = (
                    obs_owner.reshape(1, -1),
                    tile_index.reshape(1, -1),
                    obs_frac,
                    obs_count,
                    obs_owner,
                )
                result = finish(
                    plan, returned, fields[0] if chunks > 1 else None, kappa, sea_mask, sigma,
                    beta, ssh_coef, obs, devices,
                )
    increments, height, outgoing = result
    arrived = lax.all_to_all(outgoing, ("gx", "gy"), split_axis=0, concat_axis=0, tiled=True)
    return increments[None], height[None], receive(arrived, kinds * levels + 1)


def solution(mesh):
    return jax.shard_map(
        functools.partial(body, mesh.shape["gx"], mesh.shape["gy"]),
        mesh=mesh,
        in_specs=(
            P(None, None, None, "gy", "gx"),
            P(None, None, "gy", "gx"),
            P(None, "gy", "gx"),
            P(None, "gy", "gx"),
            P("gy", "gx"),
            P("gx", None),
            P("gx", None),
            P(),
            P(("gx", "gy"), None),
            P(("gx", "gy")),
            P(None, ("gx", "gy")),
            P(("gx", "gy")),
        ),
        out_specs=(
            P(None, None, None, "gy", "gx"),
            P(None, "gy", "gx"),
            P(None, None, ("gx", "gy")),
        ),
        check_vma=False,
    )
```

profile of v0, /device:TPU:0, one launch (start us, length us, event | category | flops | bytes accessed | tf_op | source)
XLA Modules:
  0.0 184.9 jit_solution(11692876210792390609)
XLA Ops:
  1.8 3.0 %collective-permute-start.9 = (f32[6,48,384]{2,1,0:T(8,128)S(1)}, f32[6,48,384]{2,1,0:T(8,128)}, u32[]{:S(2)}, u32[]{:S(2)}) collective-permute-start(f32[6,48,384]{2,1,0:T(8,128)S(1)} %get-tuple-element.23.refs_0_), channel_id=1, source_target_pairs={{0,16},{8,24},{16,0},{24,8},{1,17},{9,25},{17,1},{25,9},{2,18},{10... | collective-permute-start | bytes 1327112 | tf_op jit(solution)/shard_map/ppermute | solution.py:137
  4.9 10.3 %collective-permute-done.9.refs_1_ = f32[6,48,384]{2,1,0:T(8,128)} collective-permute-done((f32[6,48,384]{2,1,0:T(8,128)S(1)}, f32[6,48,384]{2,1,0:T(8,128)}, u32[]{:S(2)}, u32[]{:S(2)}) %collective-permute-start.9) | collective-permute-done | bytes 442400 | tf_op jit(solution)/shard_map/ppermute | solution.py:137
  15.1 1.7 collective-permute-start
  19.4 4.0 %shard_map.146 = f32[8,112,128]{2,1,0:T(8,128)} custom-call(s32[1]{0:T(128)} %bitcast.me_ref, bf16[1536,384]{1,0:T(8,128)(2,1)S(1)} %get-tuple-element.10.high_ref, bf16[1536,384]{1,0:T(8,128)(2,1)S(1)} %get-tuple-element.11.low_ref, s32[48,384]{1,0:T(8,128)S(1)} %copy-done.1, f32[6,48,384]{2,1,0:T(8,128)S(1)} %get-tuple-element.23.refs_0_, ...), custom_call_target="tpu_custom_call" | custom-call | flops 1019215872 | bytes 4661252 | tf_op jit(solution)/shard_map/pallas_call | solution.py:122
  23.4 5.8 %all-to-all-start.4 = ((f32[8,112,128]{2,1,0:T(8,128)}), f32[8,112,128]{2,1,0:T(8,128)S(1)}, u32[]{:S(2)}, u32[]{:S(2)}) async-start(f32[8,112,128]{2,1,0:T(8,128)} %shard_map.146), calls=%async_computation.4 | async-start | bytes 917504 | tf_op jit(solution)/shard_map/all_to_all | solution.py:403
  31.9 3.7 %shard_map.140 = f32[8,112,128]{2,1,0:T(8,128)} custom-call(s32[1]{0:T(128)} %bitcast.me_ref, bf16[1536,384]{1,0:T(8,128)(2,1)S(1)} %get-tuple-element.10.high_ref, bf16[1536,384]{1,0:T(8,128)(2,1)S(1)} %get-tuple-element.11.low_ref, s32[48,384]{1,0:T(8,128)S(1)} %copy-done.1, f32[6,48,384]{2,1,0:T(8,128)S(1)} %get-tuple-element.24.refs_0_, ...), custom_call_target="tpu_custom_call" | custom-call | flops 1019215872 | bytes 4661252 | tf_op jit(solution)/shard_map/pallas_call | solution.py:122
  35.6 7.1 %all-to-all-done.4.in_ref = f32[8,112,128]{2,1,0:T(8,128)S(1)} async-done(((f32[8,112,128]{2,1,0:T(8,128)}), f32[8,112,128]{2,1,0:T(8,128)S(1)}, u32[]{:S(2)}, u32[]{:S(2)}) %all-to-all-start.4) | async-done | bytes 458784 | tf_op jit(solution)/shard_map/all_to_all | solution.py:403
  42.7 4.1 %all-to-all-start = ((f32[8,112,128]{2,1,0:T(8,128)}), f32[8,112,128]{2,1,0:T(8,128)}, u32[]{:S(2)}, u32[]{:S(2)}) async-start(f32[8,112,128]{2,1,0:T(8,128)} %shard_map.140), calls=%async_computation | async-start | bytes 917504 | tf_op jit(solution)/shard_map/all_to_all | solution.py:403
  47.4 4.6 %collective-permute-done.3.refs_1_ = f32[96,384]{1,0:T(8,128)S(1)} collective-permute-done((f32[96,384]{1,0:T(8,128)S(1)}, f32[96,384]{1,0:T(8,128)S(1)}, u32[]{:S(2)}, u32[]{:S(2)}) %collective-permute-start.3) | collective-permute-done | bytes 147488 | tf_op jit(solution)/shard_map/ppermute | solution.py:137
  56.1 3.6 %all-to-all-done.in_ref = f32[8,112,128]{2,1,0:T(8,128)} async-done(((f32[8,112,128]{2,1,0:T(8,128)}), f32[8,112,128]{2,1,0:T(8,128)}, u32[]{:S(2)}, u32[]{:S(2)}) %all-to-all-start) | async-done | bytes 458784 | tf_op jit(solution)/shard_map/all_to_all | solution.py:403
  59.7 4.1 %all-to-all-start.5 = ((f32[8,112,128]{2,1,0:T(8,128)}), f32[8,112,128]{2,1,0:T(8,128)}, u32[]{:S(2)}, u32[]{:S(2)}) async-start(f32[8,112,128]{2,1,0:T(8,128)} %copy-done.8), calls=%async_computation.5 | async-start | bytes 917504 | tf_op jit(solution)/shard_map/all_to_all | solution.py:409
  63.9 1.8 shard_map.142
  66.5 9.9 %all-to-all-done.5.in_ref = f32[8,112,128]{2,1,0:T(8,128)} async-done(((f32[8,112,128]{2,1,0:T(8,128)}), f32[8,112,128]{2,1,0:T(8,128)}, u32[]{:S(2)}, u32[]{:S(2)}) %all-to-all-start.5) | async-done | bytes 458784 | tf_op jit(solution)/shard_map/all_to_all | solution.py:409
  76.4 4.1 %all-to-all-start.1 = ((f32[8,112,128]{2,1,0:T(8,128)}), f32[8,112,128]{2,1,0:T(8,128)}, u32[]{:S(2)}, u32[]{:S(2)}) async-start(f32[8,112,128]{2,1,0:T(8,128)} %copy-done.7), calls=%async_computation.1 | async-start | bytes 917504 | tf_op jit(solution)/shard_map/all_to_all | solution.py:409
  80.5 2.0 %shard_map.148.refs_0_ = f32[6,48,384]{2,1,0:T(8,128)} custom-call(f32[8,112,128]{2,1,0:T(8,128)} %all-to-all-done.5.in_ref, f32[5,48,384]{2,1,0:T(8,128)S(1)} %copy-done, s32[48,384]{1,0:T(8,128)S(1)} %copy-done.1), custom_call_target="tpu_custom_call" | custom-call | bytes 1343488 | tf_op jit(solution)/shard_map/pallas_call | solution.py:122
  83.0 10.3 %collective-permute-done.12.refs_1_ = f32[6,48,384]{2,1,0:T(8,128)} collective-permute-done((f32[6,48,384]{2,1,0:T(8,128)}, f32[6,48,384]{2,1,0:T(8,128)}, u32[]{:S(2)}, u32[]{:S(2)}) %collective-permute-start.12) | collective-permute-done | bytes 442400 | tf_op jit(solution)/shard_map/ppermute | solution.py:137
  93.3 2.0 %shard_map.143.refs_0_ = f32[6,48,384]{2,1,0:T(8,128)} custom-call(f32[8,112,128]{2,1,0:T(8,128)} %all-to-all-done.1.in_ref, f32[5,48,384]{2,1,0:T(8,128)S(1)} %copy-done, s32[48,384]{1,0:T(8,128)S(1)} %copy-done.1), custom_call_target="tpu_custom_call" | custom-call | bytes 1343488 | tf_op jit(solution)/shard_map/pallas_call | solution.py:122
  95.8 3.3 %shard_map.149 = f32[8,112,128]{2,1,0:T(8,128)S(1)} custom-call(s32[1]{0:T(128)} %bitcast.me_ref, bf16[1536,384]{1,0:T(8,128)(2,1)S(1)} %get-tuple-element.10.high_ref, bf16[1536,384]{1,0:T(8,128)(2,1)S(1)} %get-tuple-element.11.low_ref, s32[48,384]{1,0:T(8,128)S(1)} %copy-done.1, f32[6,48,384]{2,1,0:T(8,128)} %shard_map.148.refs_0_, ...), custom_call_target="tpu_custom_call" | custom-call | flops 1019215872 | bytes 4661252 | tf_op jit(solution)/shard_map/pallas_call | solution.py:122
  99.9 5.7 %all-to-all-start.6 = ((f32[8,112,128]{2,1,0:T(8,128)}), f32[8,112,128]{2,1,0:T(8,128)}, u32[]{:S(2)}, u32[]{:S(2)}) async-start(f32[8,112,128]{2,1,0:T(8,128)} %copy-done.3), calls=%async_computation.6 | async-start | bytes 917504 | tf_op jit(solution)/shard_map/all_to_all | solution.py:403
  105.6 2.6 %collective-permute-done.6.refs_1_ = f32[6,48,384]{2,1,0:T(8,128)} collective-permute-done((f32[6,48,384]{2,1,0:T(8,128)}, f32[6,48,384]{2,1,0:T(8,128)}, u32[]{:S(2)}, u32[]{:S(2)}) %collective-permute-start.6) | collective-permute-done | bytes 442400 | tf_op jit(solution)/shard_map/ppermute | solution.py:137
  108.2 2.0 %collective-permute-done.8.refs_3_ = f32[6,48,384]{2,1,0:T(8,128)S(1)} collective-permute-done((f32[6,48,384]{2,1,0:T(8,128)}, f32[6,48,384]{2,1,0:T(8,128)S(1)}, u32[]{:S(2)}, u32[]{:S(2)}) %collective-permute-start.8) | collective-permute-done | bytes 442400 | tf_op jit(solution)/shard_map/ppermute | solution.py:137
  110.2 3.0 %shard_map.144 = f32[8,112,128]{2,1,0:T(8,128)S(1)} custom-call(s32[1]{0:T(128)} %bitcast.me_ref, bf16[1536,384]{1,0:T(8,128)(2,1)S(1)} %get-tuple-element.10.high_ref, bf16[1536,384]{1,0:T(8,128)(2,1)S(1)} %get-tuple-element.11.low_ref, s32[48,384]{1,0:T(8,128)S(1)} %copy-done.1, f32[6,48,384]{2,1,0:T(8,128)} %shard_map.143.refs_0_, ...), custom_call_target="tpu_custom_call" | custom-call | flops 1019215872 | bytes 4661252 | tf_op jit(solution)/shard_map/pallas_call | solution.py:122
  114.0 5.2 %all-to-all-done.6.in_ref = f32[8,112,128]{2,1,0:T(8,128)} async-done(((f32[8,112,128]{2,1,0:T(8,128)}), f32[8,112,128]{2,1,0:T(8,128)}, u32[]{:S(2)}, u32[]{:S(2)}) %all-to-all-start.6) | async-done | bytes 458784 | tf_op jit(solution)/shard_map/all_to_all | solution.py:403
  119.2 3.6 %all-to-all-start.2 = ((f32[8,112,128]{2,1,0:T(8,128)}), f32[8,112,128]{2,1,0:T(8,128)S(1)}, u32[]{:S(2)}, u32[]{:S(2)}) async-start(f32[8,112,128]{2,1,0:T(8,128)} %copy-done.4), calls=%async_computation.2 | async-start | bytes 917504 | tf_op jit(solution)/shard_map/all_to_all | solution.py:403
  122.8 2.6 %shard_map.150 = f32[8,112,128]{2,1,0:T(8,128)} custom-call(f32[8,112,128]{2,1,0:T(8,128)} %all-to-all-done.6.in_ref, bf16[384,384]{1,0:T(8,128)(2,1)S(1)} %get-tuple-element.12.high_ref, bf16[384,384]{1,0:T(8,128)(2,1)S(1)} %get-tuple-element.13.low_ref), custom_call_target="tpu_custom_call" | custom-call | flops 339738624 | bytes 1507328 | tf_op jit(solution)/shard_map/pallas_call | solution.py:122
  125.4 10.7 %all-to-all-done.2.in_ref = f32[8,112,128]{2,1,0:T(8,128)S(1)} async-done(((f32[8,112,128]{2,1,0:T(8,128)}), f32[8,112,128]{2,1,0:T(8,128)S(1)}, u32[]{:S(2)}, u32[]{:S(2)}) %all-to-all-start.2) | async-done | bytes 458784 | tf_op jit(solution)/shard_map/all_to_all | solution.py:403
  136.1 3.6 %all-to-all-start.7 = ((f32[8,112,128]{2,1,0:T(8,128)}), f32[8,112,128]{2,1,0:T(8,128)S(1)}, u32[]{:S(2)}, u32[]{:S(2)}) async-start(f32[8,112,128]{2,1,0:T(8,128)} %shard_map.150), calls=%async_computation.7 | async-start | bytes 917504 | tf_op jit(solution)/shard_map/all_to_all | solution.py:409
  141.3 11.7 %all-to-all-done.7.in_ref = f32[8,112,128]{2,1,0:T(8,128)S(1)} async-done(((f32[8,112,128]{2,1,0:T(8,128)}), f32[8,112,128]{2,1,0:T(8,128)S(1)}, u32[]{:S(2)}, u32[]{:S(2)}) %all-to-all-start.7) | async-done | bytes 458784 | tf_op jit(solution)/shard_map/all_to_all | solution.py:409
  153.0 3.6 %all-to-all-start.3 = ((f32[8,112,128]{2,1,0:T(8,128)}), f32[8,112,128]{2,1,0:T(8,128)S(1)}, u32[]{:S(2)}, u32[]{:S(2)}) async-start(f32[8,112,128]{2,1,0:T(8,128)} %shard_map.145), calls=%async_computation.3 | async-start | bytes 917504 | tf_op jit(solution)/shard_map/all_to_all | solution.py:409
  157.6 12.3 %all-to-all-done.3.in_ref = f32[8,112,128]{2,1,0:T(8,128)S(1)} async-done(((f32[8,112,128]{2,1,0:T(8,128)}), f32[8,112,128]{2,1,0:T(8,128)S(1)}, u32[]{:S(2)}, u32[]{:S(2)}) %all-to-all-start.3) | async-done | bytes 458784 | tf_op jit(solution)/shard_map/all_to_all | solution.py:409
  170.9 2.7 %shard_map.152 = (f32[2,6,48,384]{3,2,1,0:T(8,128)}, f32[48,384]{1,0:T(8,128)}, f32[32,128]{1,0:T(8,128)S(1)}) custom-call(f32[2,6]{1,0:T(2,128)S(1)} %copy-done.13, s32[1]{0:T(128)S(6)} %copy.20.count_ref, f32[8,112,128]{2,1,0:T(8,128)S(1)} %all-to-all-done.3.in_ref, f32[5,48,384]{2,1,0:T(8,128)S(1)} %copy-done, s32[48,384]{1,0:T(8,128)S(1)} %copy-done.1, ...), custom_call_target="tpu_custom_call" | custom-call | flops 10000000 | bytes 3646132 | tf_op jit(solution)/shard_map/pallas_call | solution.py:360
  173.6 10.6 %all_to_all.51 = f32[32,1,128]{2,1,0:T(1,128)S(1)} all-to-all(f32[32,1,128]{2,1,0:T(1,128)S(1)} %bitcast.14), channel_id=1, replica_groups=mesh['gx'=4,'gy'=8] {'gx','gy'}, dimensions={0} | all-to-all | bytes 32768 | tf_op jit(solution)/shard_map/all_to_all | solution.py:425
  (65 shorter events, 17.9 us)
Async XLA Ops:
  1.8 13.3 %collective-permute-start.9 = (f32[6,48,384]{2,1,0:T(8,128)S(1)}, f32[6,48,384]{2,1,0:T(8,128)}, u32[]{:S(2)}, u32[]{:S(2)}) collective-permute-start(f32[6,48,384]{2,1,0:T(8,128)S(1)} %get-tuple-element.23.refs_0_), channel_id=1, source_target_pairs={{0,16},{8,24},{16,0},{24,8},{1,17},{9,25},{17,1},{25,9},{2,18},{10... | collective-permute-start | bytes 1327112 | tf_op jit(solution)/shard_map/ppermute | solution.py:137
  4.9 14.4 %collective-permute-start.10 = (f32[6,48,384]{2,1,0:T(8,128)S(1)}, f32[6,48,384]{2,1,0:T(8,128)}, u32[]{:S(2)}, u32[]{:S(2)}) collective-permute-start(f32[6,48,384]{2,1,0:T(8,128)S(1)} %get-tuple-element.23.refs_0_), channel_id=1, source_target_pairs={{0,8},{8,0},{16,24},{24,16},{1,9},{9,1},{17,25},{25,17},{2,10},{10... | collective-permute-start | bytes 1327112 | tf_op jit(solution)/shard_map/ppermute | solution.py:137
  15.1 4.1 %collective-permute-start.11 = (f32[6,48,384]{2,1,0:T(8,128)}, f32[6,48,384]{2,1,0:T(8,128)}, u32[]{:S(2)}, u32[]{:S(2)}) collective-permute-start(f32[6,48,384]{2,1,0:T(8,128)} %collective-permute-done.9.refs_1_), channel_id=1, source_target_pairs={{0,8},{8,0},{16,24},{24,16},{1,9},{9,1},{17,25},{25,17},{2,10},{10... | collective-permute-start | bytes 1327112 | tf_op jit(solution)/shard_map/ppermute | solution.py:137
  15.1 14.1 %collective-permute-start = (f32[6,48,384]{2,1,0:T(8,128)S(1)}, f32[6,48,384]{2,1,0:T(8,128)}, u32[]{:S(2)}, u32[]{:S(2)}) collective-permute-start(f32[6,48,384]{2,1,0:T(8,128)S(1)} %get-tuple-element.24.refs_0_), channel_id=1, source_target_pairs={{0,16},{8,24},{16,0},{24,8},{1,17},{9,25},{17,1},{25,9},{2,18},{10... | collective-permute-start | bytes 1327112 | tf_op jit(solution)/shard_map/ppermute | solution.py:137
  16.9 1.7 copy-start.2
  23.4 19.3 %all-to-all-start.4 = ((f32[8,112,128]{2,1,0:T(8,128)}), f32[8,112,128]{2,1,0:T(8,128)S(1)}, u32[]{:S(2)}, u32[]{:S(2)}) async-start(f32[8,112,128]{2,1,0:T(8,128)} %shard_map.146), calls=%async_computation.4 | async-start | bytes 917504 | tf_op jit(solution)/shard_map/all_to_all | solution.py:403
  29.2 17.6 %copy-start.11 = (f32[96,384]{1,0:T(8,128)S(1)}, f32[96,384]{1,0:T(8,128)}, u32[]{:S(2)}) copy-start(f32[96,384]{1,0:T(8,128)} %refs_0_.1) | copy-start | bytes 442372
  29.2 1.9 %collective-permute-start.1 = (f32[6,48,384]{2,1,0:T(8,128)S(1)}, f32[6,48,384]{2,1,0:T(8,128)S(1)}, u32[]{:S(2)}, u32[]{:S(2)}) collective-permute-start(f32[6,48,384]{2,1,0:T(8,128)S(1)} %get-tuple-element.24.refs_0_), channel_id=1, source_target_pairs={{0,8},{8,0},{16,24},{24,16},{1,9},{9,1},{17,25},{25,17},{2,10},{10... | collective-permute-start | bytes 1327112 | tf_op jit(solution)/shard_map/ppermute | solution.py:137
  29.3 2.6 %collective-permute-start.2 = (f32[6,48,384]{2,1,0:T(8,128)}, f32[6,48,384]{2,1,0:T(8,128)S(1)}, u32[]{:S(2)}, u32[]{:S(2)}) collective-permute-start(f32[6,48,384]{2,1,0:T(8,128)} %collective-permute-done.refs_1_), channel_id=1, source_target_pairs={{0,8},{8,0},{16,24},{24,16},{1,9},{9,1},{17,25},{25,17},{2,10},{10... | collective-permute-start | bytes 1327112 | tf_op jit(solution)/shard_map/ppermute | solution.py:137
  42.7 9.4 %copy-start.5 = (f32[8,112,128]{2,1,0:T(8,128)}, f32[8,112,128]{2,1,0:T(8,128)S(1)}, u32[]{:S(2)}) copy-start(f32[8,112,128]{2,1,0:T(8,128)S(1)} %all-to-all-done.4.in_ref) | copy-start | bytes 1376260
  42.7 17.1 %all-to-all-start = ((f32[8,112,128]{2,1,0:T(8,128)}), f32[8,112,128]{2,1,0:T(8,128)}, u32[]{:S(2)}, u32[]{:S(2)}) async-start(f32[8,112,128]{2,1,0:T(8,128)} %shard_map.140), calls=%async_computation | async-start | bytes 917504 | tf_op jit(solution)/shard_map/all_to_all | solution.py:403
  46.8 5.2 %collective-permute-start.3 = (f32[96,384]{1,0:T(8,128)S(1)}, f32[96,384]{1,0:T(8,128)S(1)}, u32[]{:S(2)}, u32[]{:S(2)}) collective-permute-start(f32[96,384]{1,0:T(8,128)S(1)} %copy-done.11), channel_id=1, source_target_pairs={{0,16},{8,24},{16,0},{24,8},{1,17},{9,25},{17,1},{25,9},{2,18},{10... | collective-permute-start | bytes 442376 | tf_op jit(solution)/shard_map/ppermute | solution.py:137
  47.4 4.6 %collective-permute-start.4 = (f32[96,384]{1,0:T(8,128)S(1)}, f32[96,384]{1,0:T(8,128)S(1)}, u32[]{:S(2)}, u32[]{:S(2)}) collective-permute-start(f32[96,384]{1,0:T(8,128)S(1)} %copy-done.11), channel_id=1, source_target_pairs={{0,8},{8,0},{16,24},{24,16},{1,9},{9,1},{17,25},{25,17},{2,10},{10... | collective-permute-start | bytes 442376 | tf_op jit(solution)/shard_map/ppermute | solution.py:137
  52.0 1.4 collective-permute-start.5
  59.7 16.7 %all-to-all-start.5 = ((f32[8,112,128]{2,1,0:T(8,128)}), f32[8,112,128]{2,1,0:T(8,128)}, u32[]{:S(2)}, u32[]{:S(2)}) async-start(f32[8,112,128]{2,1,0:T(8,128)} %copy-done.8), calls=%async_computation.5 | async-start | bytes 917504 | tf_op jit(solution)/shard_map/all_to_all | solution.py:409
  63.9 16.7 %copy-start = (f32[5,48,384]{2,1,0:T(8,128)S(1)}, f32[5,48,384]{2,1,0:T(8,128)}, u32[]{:S(2)}) copy-start(f32[5,48,384]{2,1,0:T(8,128)} %kappa_ref.7) | copy-start | bytes 1105924
  76.4 16.9 %all-to-all-start.1 = ((f32[8,112,128]{2,1,0:T(8,128)}), f32[8,112,128]{2,1,0:T(8,128)}, u32[]{:S(2)}, u32[]{:S(2)}) async-start(f32[8,112,128]{2,1,0:T(8,128)} %copy-done.7), calls=%async_computation.1 | async-start | bytes 917504 | tf_op jit(solution)/shard_map/all_to_all | solution.py:409
  82.5 10.8 %collective-permute-start.12 = (f32[6,48,384]{2,1,0:T(8,128)}, f32[6,48,384]{2,1,0:T(8,128)}, u32[]{:S(2)}, u32[]{:S(2)}) collective-permute-start(f32[6,48,384]{2,1,0:T(8,128)} %shard_map.148.refs_0_), channel_id=1, source_target_pairs={{0,16},{8,24},{16,0},{24,8},{1,17},{9,25},{17,1},{25,9},{2,18},{10... | collective-permute-start | bytes 1327112 | tf_op jit(solution)/shard_map/ppermute | solution.py:137
  83.0 12.8 %collective-permute-start.13 = (f32[6,48,384]{2,1,0:T(8,128)}, f32[6,48,384]{2,1,0:T(8,128)}, u32[]{:S(2)}, u32[]{:S(2)}) collective-permute-start(f32[6,48,384]{2,1,0:T(8,128)} %shard_map.148.refs_0_), channel_id=1, source_target_pairs={{0,8},{8,0},{16,24},{24,16},{1,9},{9,1},{17,25},{25,17},{2,10},{10... | collective-permute-start | bytes 1327112 | tf_op jit(solution)/shard_map/ppermute | solution.py:137
  93.3 2.5 %collective-permute-start.14 = (f32[6,48,384]{2,1,0:T(8,128)}, f32[6,48,384]{2,1,0:T(8,128)}, u32[]{:S(2)}, u32[]{:S(2)}) collective-permute-start(f32[6,48,384]{2,1,0:T(8,128)} %collective-permute-done.12.refs_1_), channel_id=1, source_target_pairs={{0,8},{8,0},{16,24},{24,16},{1,9},{9,1},{17,25},{25,17},{2,10},{10... | collective-permute-start | bytes 1327112 | tf_op jit(solution)/shard_map/ppermute | solution.py:137
  95.3 12.9 %collective-permute-start.6 = (f32[6,48,384]{2,1,0:T(8,128)}, f32[6,48,384]{2,1,0:T(8,128)}, u32[]{:S(2)}, u32[]{:S(2)}) collective-permute-start(f32[6,48,384]{2,1,0:T(8,128)} %shard_map.143.refs_0_), channel_id=1, source_target_pairs={{0,16},{8,24},{16,0},{24,8},{1,17},{9,25},{17,1},{25,9},{2,18},{10... | collective-permute-start | bytes 1327112 | tf_op jit(solution)/shard_map/ppermute | solution.py:137
  99.9 19.3 %all-to-all-start.6 = ((f32[8,112,128]{2,1,0:T(8,128)}), f32[8,112,128]{2,1,0:T(8,128)}, u32[]{:S(2)}, u32[]{:S(2)}) async-start(f32[8,112,128]{2,1,0:T(8,128)} %copy-done.3), calls=%async_computation.6 | async-start | bytes 917504 | tf_op jit(solution)/shard_map/all_to_all | solution.py:403
  105.6 2.6 %collective-permute-start.7 = (f32[6,48,384]{2,1,0:T(8,128)}, f32[6,48,384]{2,1,0:T(8,128)S(1)}, u32[]{:S(2)}, u32[]{:S(2)}) collective-permute-start(f32[6,48,384]{2,1,0:T(8,128)} %shard_map.143.refs_0_), channel_id=1, source_target_pairs={{0,8},{8,0},{16,24},{24,16},{1,9},{9,1},{17,25},{25,17},{2,10},{10... | collective-permute-start | bytes 1327112 | tf_op jit(solution)/shard_map/ppermute | solution.py:137
  108.2 2.0 %collective-permute-start.8 = (f32[6,48,384]{2,1,0:T(8,128)}, f32[6,48,384]{2,1,0:T(8,128)S(1)}, u32[]{:S(2)}, u32[]{:S(2)}) collective-permute-start(f32[6,48,384]{2,1,0:T(8,128)} %collective-permute-done.6.refs_1_), channel_id=1, source_target_pairs={{0,8},{8,0},{16,24},{24,16},{1,9},{9,1},{17,25},{25,17},{2,10},{10... | collective-permute-start | bytes 1327112 | tf_op jit(solution)/shard_map/ppermute | solution.py:137
  119.2 16.9 %all-to-all-start.2 = ((f32[8,112,128]{2,1,0:T(8,128)}), f32[8,112,128]{2,1,0:T(8,128)S(1)}, u32[]{:S(2)}, u32[]{:S(2)}) async-start(f32[8,112,128]{2,1,0:T(8,128)} %copy-done.4), calls=%async_computation.2 | async-start | bytes 917504 | tf_op jit(solution)/shard_map/all_to_all | solution.py:403
  136.1 16.9 %all-to-all-start.7 = ((f32[8,112,128]{2,1,0:T(8,128)}), f32[8,112,128]{2,1,0:T(8,128)S(1)}, u32[]{:S(2)}, u32[]{:S(2)}) async-start(f32[8,112,128]{2,1,0:T(8,128)} %shard_map.150), calls=%async_computation.7 | async-start | bytes 917504 | tf_op jit(solution)/shard_map/all_to_all | solution.py:409
  139.7 16.9 %copy-start.12 = (s32[32,1]{0,1:T(1,128)S(1)}, s32[32,1]{0,1:T(1,128)}, u32[]{:S(2)}) copy-start(s32[32,1]{0,1:T(1,128)} %param.20) | copy-start | bytes 388
  141.3 28.6 %copy-start.9 = (f32[2,6,48,384]{3,2,1,0:T(8,128)S(1)}, f32[2,6,48,384]{3,2,1,0:T(8,128)}, u32[]{:S(2)}) copy-start(f32[2,6,48,384]{3,2,1,0:T(8,128)} %sigma_ref.1) | copy-start | bytes 2654212
  141.3 28.6 %copy-start.13 = (f32[2,6]{1,0:T(2,128)S(1)}, f32[2,6]{1,0:T(2,128)}, u32[]{:S(2)}) copy-start(f32[2,6]{1,0:T(2,128)} %ssh_ref.1) | copy-start | bytes 148
  141.3 28.6 %copy-start.14 = (f32[2,32]{1,0:T(2,128)S(1)}, f32[2,32]{1,0:T(2,128)}, u32[]{:S(2)}) copy-start(f32[2,32]{1,0:T(2,128)} %frac_ref.1) | copy-start | bytes 772
  141.3 28.6 %copy-start.15 = (s32[32]{0:T(128)S(1)}, s32[32]{0:T(128)}, u32[]{:S(2)}) copy-start(s32[32]{0:T(128)} %param.21) | copy-start | bytes 388
  153.0 16.9 %all-to-all-start.3 = ((f32[8,112,128]{2,1,0:T(8,128)}), f32[8,112,128]{2,1,0:T(8,128)S(1)}, u32[]{:S(2)}, u32[]{:S(2)}) async-start(f32[8,112,128]{2,1,0:T(8,128)} %shard_map.145), calls=%async_computation.3 | async-start | bytes 917504 | tf_op jit(solution)/shard_map/all_to_all | solution.py:409
  (7 other events, 6.0 us)
where the time goes:
time: 186 us; the launch traced here: 185 us
  waiting for transfers between devices  93.7 us (50%)
  starting transfers between devices  41.8 us (22%)
  Pallas kernels  28.4 us (15%)
  blocking collectives  10.6 us (6%)
  local copies, waits for them, and re-layouts  8.87 us (5%)
    all_to_all x4, waiting for transfers between devices, body(): lax.all_to_all(solved, 'gy', split_axis=0, concat_axis=0, tiled=True)  33.9 us
    ppermute x15, waiting for transfers between devices, gather_pieces(): lax.ppermute(piece, axis, pairs)  33.3 us
    all_to_all x4, waiting for transfers between devices, body(): lax.all_to_all(packed, 'gy', split_axis=0, concat_axis=0, tiled=True)  26.6 us
    pallas_call x14, Pallas kernels, call(): pl.pallas_call(kernel, out_shape=out_shape, in_specs=specs, out_specs=[ou...  25.7 us
    all_to_all x4, starting transfers between devices, body(): lax.all_to_all(packed, 'gy', split_axis=0, concat_axis=0, tiled=True)  19.3 us
    all_to_all x4, starting transfers between devices, body(): lax.all_to_all(solved, 'gy', split_axis=0, concat_axis=0, tiled=True)  15.5 us
    all_to_all x1, blocking collectives, body(): lax.all_to_all(outgoing, ('gx', 'gy'), split_axis=0, concat_axis=0, tiled...  10.6 us
    unnamed x34, local copies, waits for them, and re-layouts  7.67 us
  transfers between devices with their start and end apart: 23, of which 15 were waited for; matrix products, arithmetic and copies ran while one was open for 0% of the time, Pallas kernels for 14%

commit v1 on v0

--- a/solution.py
+++ b/solution.py
@@ -37,10 +37,8 @@
             and tiles - self.full * parts == (parts // self.sides if self.rest else 0)
         )
 
-    def home(self, tile):
-        if tile < self.full * self.parts:
-            return tile // self.full, tile % self.full
-        return None, tile - self.full * self.parts
+    def moved(self, side, place):
+        return ((side - place) * self.rest) % LANES
 
     def pack_rest(self, tile, place):
         lane_side = lax.broadcasted_iota(jnp.int32, (SUB, LANES), 1) // self.rest
@@ -51,49 +49,60 @@
                 group = pack * self.sides + side
                 if group >= self.groups:
                     break
-                piece = tile[group * SUB : (group + 1) * SUB, :]
-                shift = ((side - place) * self.rest) % LANES
-                if shift:
-                    piece = pltpu.roll(piece, shift, axis=1)
+                piece = turn(tile[group * SUB : (group + 1) * SUB, :], self.moved(side, place))
                 joined = piece if joined is None else jnp.where(lane_side == side, piece, joined)
             out.append(joined)
         return out
 
-    def unpack_rest(self, packs, place):
+    def unpack_rest(self, ref, place):
         pieces = []
         for group in range(self.groups):
             pack, side = divmod(group, self.sides)
-            shift = ((place - side) * self.rest) % LANES
-            piece = packs[pack]
-            pieces.append(pltpu.roll(piece, shift, axis=1) if shift else piece)
+            start = self.full * self.rows + pack * SUB
+            pieces.append(turn(ref[start : start + SUB, :], self.moved(place, side)))
         return jnp.concatenate(pieces, axis=0)
 
-    def store_tile(self, out_ref, tile_index, tile):
-        device, place = self.home(tile_index)
-        if device is not None:
-            out_ref[device, place * self.rows : (place + 1) * self.rows, :] = tile
-            return
-        for side in range(self.sides):
-            device = place * self.sides + side
-            for pack, value in enumerate(self.pack_rest(tile, side)):
-                start = self.full * self.rows + pack * SUB
-                out_ref[device, start : start + SUB, :] = value
-
-    def load_tile(self, in_ref, tile_index):
-        device, place = self.home(tile_index)
-        if device is not None:
-            return in_ref[device, place * self.rows : (place + 1) * self.rows, :]
-        lane_side = lax.broadcasted_iota(jnp.int32, (self.rows, LANES), 1) // self.rest
-        joined = None
-        for side in range(self.sides):
-            packs = self.load_packs(in_ref, place * self.sides + side)
-            piece = self.unpack_rest(packs, side)
-            joined = piece if joined is None else jnp.where(lane_side == side, piece, joined)
-        return joined
-
-    def load_packs(self, in_ref, device):
-        base = self.full * self.rows
-        return [in_ref[device, base + p * SUB : base + (p + 1) * SUB, :] for p in range(self.packs)]
+    def store_rest(self, ref, packs):
+        for pack, value in enumerate(packs):
+            start = self.full * self.rows + pack * SUB
+            ref[start : start + SUB, :] = value
+
+    def send_tiles(self, tiles_ref, device, out_ref):
+        for i in range(self.full):
+            out_ref[i * self.rows : (i + 1) * self.rows, :] = tiles_ref[device * self.full + i]
+        if self.rest:
+            tile = tiles_ref[self.parts * self.full + device // self.sides]
+            self.store_rest(out_ref, self.pack_rest(tile, device % self.sides))
+
+    def take_tiles(self, in_ref, device, tiles_ref):
+        for i in range(self.full):
+            tiles_ref[device * self.full + i] = in_ref[i * self.rows : (i + 1) * self.rows, :]
+        if self.rest:
+            place = device % self.sides
+            index = self.parts * self.full + device // self.sides
+            lane_side = lax.broadcasted_iota(jnp.int32, (self.rows, LANES), 1) // self.rest
+            tiles_ref[index] = jnp.where(
+                lane_side == place, self.unpack_rest(in_ref, place), tiles_ref[index]
+            )
+
+    @property
+    def tiles(self):
+        return pltpu.VMEM((self.fields * self.blocks, self.rows, LANES), jnp.float32)
+
+    @property
+    def lines(self):
+        return pltpu.VMEM((self.parts * self.rows, self.columns), jnp.float32)
+
+    @property
+    def blocks_out(self):
+        shape = jax.ShapeDtypeStruct((self.width, LANES), jnp.float32)
+        return [shape] * self.parts
+
+
+def turn(value, shift):
+    if isinstance(shift, int) and shift == 0:
+        return value
+    return pltpu.roll(value, shift, axis=1)
 
 
 def split(value):
@@ -110,7 +119,7 @@
     return dot(a[0], b[0]) + (dot(a[0], b[1]) + dot(a[1], b[0]))
 
 
-def call(kernel, out_shape, operands, scalars=(), flops=0):
+def call(kernel, out_shape, operands, scalars=(), flops=0, scratch=()):
     outs = out_shape if isinstance(out_shape, (list, tuple)) else [out_shape]
     moved = sum(a.size * a.dtype.itemsize for a in list(operands) + list(outs))
     specs = [
@@ -124,6 +133,7 @@
         out_shape=out_shape,
         in_specs=specs,
         out_specs=[out_spec] * len(outs) if many else out_spec,
+        scratch_shapes=list(scratch),
         compiler_params=pltpu.CompilerParams(vmem_limit_bytes=min(48, 6 + 3 * moved // 2**20) * 2**20),
         cost_estimate=pl.CostEstimate(flops=flops, bytes_accessed=moved, transcendentals=0),
     )(*operands)
@@ -139,6 +149,13 @@
     return held
 
 
+def exchange(blocks, axis, count):
+    out = [blocks[0]] + [None] * (count - 1)
+    for mask in range(count - 1, 0, -1):
+        out[mask] = lax.ppermute(blocks[mask], axis, [(i, i ^ mask) for i in range(count)])
+    return out
+
+
 def prepare_x(x_inverse):
     rows, cols = x_inverse.shape
 
@@ -168,10 +185,10 @@
 
 
 def zonal(plan, masks, pieces, me, x_high, x_low, sea_mask):
-    fields, rows, cols = plan.fields, plan.rows, plan.cols
+    fields, rows, cols, parts = plan.fields, plan.rows, plan.cols, plan.parts
 
     def kernel(me_ref, high_ref, low_ref, sea_ref, *refs):
-        out_ref = refs[-1]
+        out_refs, tiles_ref = refs[-parts - 1 : -1], refs[-1]
         total = None
         for mask, ref in zip(masks, refs):
             start = pl.multiple_of((me_ref[0] ^ mask) * cols, cols)
@@ -184,55 +201,56 @@
         for block in range(plan.blocks):
             lanes = slice(block * LANES, (block + 1) * LANES)
             for field in range(fields):
-                tile = sea[:, lanes] * total[field, :, lanes]
-                plan.store_tile(out_ref, field * plan.blocks + block, tile)
+                tiles_ref[field * plan.blocks + block] = sea[:, lanes] * total[field, :, lanes]
+        for mask in range(parts):
+            plan.send_tiles(tiles_ref, me_ref[1] ^ mask, out_refs[mask])
 
     return call(
         kernel,
-        jax.ShapeDtypeStruct((plan.parts, plan.width, LANES), jnp.float32),
+        plan.blocks_out,
         [me, x_high, x_low, sea_mask] + pieces,
         scalars=(0,),
         flops=6 * fields * rows * cols * cols * len(pieces),
+        scratch=[plan.tiles],
     )
 
 
-def meridional(plan, lines, y_high, y_low):
+def meridional(plan, me, lines, y_high, y_low):
     rows, parts = plan.rows, plan.parts
 
-    def kernel(in_ref, high_ref, low_ref, out_ref):
-        columns = [
-            in_ref[:, i * rows : (i + 1) * rows, :].reshape(parts * rows, LANES)
-            for i in range(plan.full)
-        ]
-        if plan.rest:
-            columns.append(
-                jnp.concatenate(
-                    [plan.unpack_rest(plan.load_packs(in_ref, d), 0) for d in range(parts)], axis=0
-                )
-            )
-        values = split(jnp.concatenate(columns, axis=1))
-        solved = dot_split((high_ref[...], low_ref[...]), values)
-        for i in range(plan.full):
-            tile = solved[:, i * LANES : (i + 1) * LANES]
-            out_ref[:, i * rows : (i + 1) * rows, :] = tile.reshape(parts, rows, LANES)
-        if plan.rest:
-            last = solved[:, plan.full * LANES :]
-            for d in range(parts):
-                packs = plan.pack_rest(last[d * rows : (d + 1) * rows, :], 0)
-                for p, value in enumerate(packs):
-                    start = plan.full * rows + p * SUB
-                    out_ref[d, start : start + SUB, :] = value
+    def kernel(me_ref, high_ref, low_ref, *refs):
+        in_refs, out_refs, lines_ref = refs[:parts], refs[parts : 2 * parts], refs[-1]
+        for mask in range(parts):
+            place = pl.ds(pl.multiple_of((me_ref[1] ^ mask) * rows, rows), rows)
+            for i in range(plan.full):
+                lanes = slice(i * LANES, (i + 1) * LANES)
+                lines_ref[place, lanes] = in_refs[mask][i * rows : (i + 1) * rows, :]
+            if plan.rest:
+                lines_ref[place, plan.full * LANES :] = plan.unpack_rest(in_refs[mask], 0)
+        lines_ref[...] = dot_split((high_ref[...], low_ref[...]), split(lines_ref[...]))
+        for mask in range(parts):
+            place = pl.ds(pl.multiple_of((me_ref[1] ^ mask) * rows, rows), rows)
+            for i in range(plan.full):
+                lanes = slice(i * LANES, (i + 1) * LANES)
+                out_refs[mask][i * rows : (i + 1) * rows, :] = lines_ref[place, lanes]
+            if plan.rest:
+                last = lines_ref[place, plan.full * LANES :]
+                plan.store_rest(out_refs[mask], plan.pack_rest(last, 0))
 
     return call(
         kernel,
-        jax.ShapeDtypeStruct(lines.shape, jnp.float32),
-        [lines, y_high, y_low],
+        plan.blocks_out,
+        [me, y_high, y_low] + lines,
+        scalars=(0,),
         flops=6 * (parts * rows) ** 2 * plan.columns,
+        scratch=[plan.lines],
     )
 
 
-def solve_columns(plan, in_ref, kappa_ref, sea_ref, levels, store):
+def solve_columns(plan, me_ref, in_refs, tiles_ref, kappa_ref, sea_ref, levels, store):
     kinds = plan.fields // levels
+    for mask in range(plan.parts):
+        plan.take_tiles(in_refs[mask], me_ref[1] ^ mask, tiles_ref)
     for block in range(plan.blocks):
         lanes = slice(block * LANES, (block + 1) * LANES)
         sea = sea_ref[:, lanes].astype(jnp.float32)
@@ -249,7 +267,7 @@
         for kind in range(kinds):
             forward = []
             for level in range(levels):
-                tile = plan.load_tile(in_ref, (kind * levels + level) * plan.blocks + block)
+                tile = tiles_ref[(kind * levels + level) * plan.blocks + block]
                 right = sea * tile
                 if level > 0:
                     right = right + kappa[level - 1] * forward[-1]
@@ -261,21 +279,25 @@
                 store(kind, level, lanes, value)
 
 
-def vertical(plan, returned, kappa, sea_mask, levels):
-    def kernel(in_ref, kappa_ref, sea_ref, out_ref):
+def vertical(plan, me, returned, kappa, sea_mask, levels):
+    def kernel(me_ref, kappa_ref, sea_ref, *refs):
+        in_refs, (out_ref, tiles_ref) = refs[: plan.parts], refs[plan.parts :]
+
         def store(kind, level, lanes, value):
             out_ref[kind * levels + level, :, lanes] = value
 
-        solve_columns(plan, in_ref, kappa_ref, sea_ref, levels, store)
+        solve_columns(plan, me_ref, in_refs, tiles_ref, kappa_ref, sea_ref, levels, store)
 
     return call(
         kernel,
         jax.ShapeDtypeStruct((plan.fields, plan.rows, plan.cols), jnp.float32),
-        [returned, kappa, sea_mask],
+        [me, kappa, sea_mask] + returned,
+        scalars=(0,),
+        scratch=[plan.tiles],
     )
 
 
-def finish(plan, returned, temper_field, kappa, sea_mask, sigma, beta, ssh_coef, obs, devices):
+def finish(plan, me, returned, temper_field, kappa, sea_mask, sigma, beta, ssh_coef, obs, devices):
     levels = sigma.shape[1]
     rows, cols = plan.rows, plan.cols
     records = 2 * levels + 1
@@ -283,14 +305,16 @@
     slots = owner_row.shape[1]
     extra = [] if temper_field is None else [temper_field]
 
-    def kernel(ssh_ref, count_ref, in_ref, kappa_ref, sea_ref, sigma_ref, beta_ref,
+    def kernel(me_ref, ssh_ref, count_ref, kappa_ref, sea_ref, sigma_ref, beta_ref,
                owner_ref, tile_ref, frac_ref, column_ref, *refs):
-        inc_ref, height_ref, send_ref, profile_ref = refs[-4:]
+        inc_ref, height_ref, send_ref, profile_ref, tiles_ref = refs[-5:]
 
         def store(kind, level, lanes, value):
             profile_ref[(kind + len(extra)) * levels + level, :, lanes] = value
 
-        solve_columns(plan, in_ref, kappa_ref, sea_ref, levels, store)
+        solve_columns(
+            plan, me_ref, refs[len(extra) :], tiles_ref, kappa_ref, sea_ref, levels, store
+        )
         for block in range(plan.blocks):
             lanes = slice(block * LANES, (block + 1) * LANES)
             height = None
@@ -349,8 +373,8 @@
             to_owner, ranked, NT, precision=lax.Precision.HIGHEST, preferred_element_type=jnp.float32
         )
 
-    operands = [ssh_coef, obs_count, returned, kappa, sea_mask, sigma, beta,
-                owner_row, tile_index, obs_frac, owner_col] + extra
+    operands = [me, ssh_coef, obs_count, kappa, sea_mask, sigma, beta,
+                owner_row, tile_index, obs_frac, owner_col] + extra + returned
     outs = [
         jax.ShapeDtypeStruct((2, levels, rows, cols), jnp.float32),
         jax.ShapeDtypeStruct((rows, cols), jnp.float32),
@@ -360,10 +384,10 @@
     return pl.pallas_call(
         kernel,
         out_shape=outs,
-        in_specs=[pl.BlockSpec(memory_space=pltpu.SMEM)] * 2
-        + [pl.BlockSpec(memory_space=pltpu.VMEM)] * (len(operands) - 2),
+        in_specs=[pl.BlockSpec(memory_space=pltpu.SMEM)] * 3
+        + [pl.BlockSpec(memory_space=pltpu.VMEM)] * (len(operands) - 3),
         out_specs=[pl.BlockSpec(memory_space=pltpu.VMEM)] * 3,
-        scratch_shapes=[pltpu.VMEM((records, rows, cols), jnp.float32)],
+        scratch_shapes=[pltpu.VMEM((records, rows, cols), jnp.float32), plan.tiles],
         compiler_params=pltpu.CompilerParams(vmem_limit_bytes=32 * 2**20),
         cost_estimate=pl.CostEstimate(flops=10**7, bytes_accessed=moved, transcendentals=0),
     )(*operands)
@@ -388,7 +412,7 @@
     chunks = kinds
     if not plan.fits:
         plan, chunks = Plan(kinds * levels, rows, cols, gy_count), 1
-    me = lax.axis_index("gx").astype(jnp.int32).reshape(1)
+    me = jnp.stack([lax.axis_index("gx"), lax.axis_index("gy")]).astype(jnp.int32)
     x_high, x_low = prepare_x(x_inverse)
     fields = list(control.reshape(chunks, plan.fields, rows, cols))
     y_parts = None
@@ -397,18 +421,18 @@
         sent = []
         for chunk in range(chunks):
             held = gather_pieces(fields[chunk], "gx", gx_count)
-            packed = zonal(
-                plan, [m for m, _ in held], [p for _, p in held], me, x_high, x_low, sea_mask
-            )
-            sent.append(lax.all_to_all(packed, "gy", split_axis=0, concat_axis=0, tiled=True))
-        if y_parts is None:
-            held = gather_pieces(y_inverse, "gx", gx_count)
-            y_parts = prepare_y([m for m, _ in held], [p for _, p in held], me)
+            masks, pieces = [m for m, _ in held], [p for _, p in held]
+            if y_parts is None:
+                pieces[1], y_inverse = lax.optimization_barrier((pieces[1], y_inverse))
+                held = gather_pieces(y_inverse, "gx", gx_count)
+                y_parts = prepare_y([m for m, _ in held], [p for _, p in held], me)
+            packed = zonal(plan, masks, pieces, me, x_high, x_low, sea_mask)
+            sent.append(exchange(packed, "gy", gy_count))
         for chunk in range(chunks):
-            solved = meridional(plan, sent[chunk], *y_parts)
-            returned = lax.all_to_all(solved, "gy", split_axis=0, concat_axis=0, tiled=True)
+            solved = meridional(plan, me, sent[chunk], *y_parts)
+            returned = exchange(solved, "gy", gy_count)
             if step < STEPS - 1 or chunk < chunks - 1:
-                fields[chunk] = vertical(plan, returned, kappa, sea_mask, levels)
+                fields[chunk] = vertical(plan, me, returned, kappa, sea_mask, levels)
             else:
                 obs = (
                     obs_owner.reshape(1, -1),
@@ -418,7 +442,7 @@
                     obs_owner,
                 )
                 result = finish(
-                    plan, returned, fields[0] if chunks > 1 else None, kappa, sea_mask, sigma,
+                    plan, me, returned, fields[0] if chunks > 1 else None, kappa, sea_mask, sigma,
                     beta, ssh_coef, obs, devices,
                 )
     increments, height, outgoing = result

time: 186 us -> 174 us (0.935)
  starting transfers between devices: 41.8 us -> 95.4 us
  waiting for transfers between devices: 93.7 us -> 40.2 us
  Pallas kernels: 28.4 us -> 22.8 us
  local copies, waits for them, and re-layouts: 8.87 us -> 3.64 us
    ppermute x0 -> x56, starting transfers between devices: none -> 87.4 us  [exchange(): lax.ppermute(blocks[mask], axis, [(i, i ^ mask) for i in range(count)])]
    all_to_all x8 -> x0, waiting for transfers between devices: 60.5 us -> none  [the longest x4 33.9 us: body(): lax.all_to_all(solved, 'gy', split_axis=0, concat_axis=0, tiled=True)]
    all_to_all x8 -> x0, starting transfers between devices: 34.8 us -> none  [the longest x4 19.3 us: body(): lax.all_to_all(packed, 'gy', split_axis=0, concat_axis=0, tiled=True)]
    ppermute x0 -> x56, waiting for transfers between devices: none -> 12 us  [exchange(): lax.ppermute(blocks[mask], axis, [(i, i ^ mask) for i in range(count)])]
    unnamed x34 -> x22, local copies, waits for them, and re-layouts: 7.67 us -> 2.4 us
    pallas_call x14, Pallas kernels: 25.7 us -> 20.7 us  [call(): pl.pallas_call(kernel, out_shape=out_shape, in_specs=specs, out_specs=[ou...]
    ppermute x15, waiting for transfers between devices: 33.3 us -> 28.2 us  [gather_pieces(): lax.ppermute(piece, axis, pairs)]
  transfers between devices with their start and end apart: 23 -> 71, of which waited for: 15 -> 12; matrix products, arithmetic and copies ran while one was open for 0% -> 0% of each run, Pallas kernels for 14% -> 12%
where the time goes in v1:
time: 174 us
  starting transfers between devices  95.4 us (55%)
  waiting for transfers between devices  40.2 us (23%)
  Pallas kernels  22.8 us (13%)
  blocking collectives  10.1 us (6%)
  local copies, waits for them, and re-layouts  3.64 us (2%)
    ppermute x56, starting transfers between devices, exchange(): lax.ppermute(blocks[mask], axis, [(i, i ^ mask) for i in range(count)])  87.4 us
    ppermute x15, waiting for transfers between devices, gather_pieces(): lax.ppermute(piece, axis, pairs)  28.2 us
    pallas_call x14, Pallas kernels, call(): pl.pallas_call(kernel, out_shape=out_shape, in_specs=specs, out_specs=[ou...  20.7 us
    ppermute x56, waiting for transfers between devices, exchange(): lax.ppermute(blocks[mask], axis, [(i, i ^ mask) for i in range(count)])  12 us
    all_to_all x1, blocking collectives, body(): lax.all_to_all(outgoing, ('gx', 'gy'), split_axis=0, concat_axis=0, tiled...  10.1 us
    ppermute x15, starting transfers between devices, gather_pieces(): lax.ppermute(piece, axis, pairs)  7.96 us
  transfers between devices with their start and end apart: 71, of which 12 were waited for; matrix products, arithmetic and copies ran while one was open for 0% of the time, Pallas kernels for 12%

profile of v1, /device:TPU:0, one launch (start us, length us, event | category | flops | bytes accessed | tf_op | source)
XLA Modules:
  0.0 173.8 jit_solution(1530933337755435319)
XLA Ops:
  1.9 3.0 %collective-permute-start = (f32[6,48,384]{2,1,0:T(8,128)S(1)}, f32[6,48,384]{2,1,0:T(8,128)S(1)}, u32[]{:S(2)}, u32[]{:S(2)}) collective-permute-start(f32[6,48,384]{2,1,0:T(8,128)S(1)} %get-tuple-element.156.refs_0_), channel_id=1, source_target_pairs={{0,16},{8,24},{16,0},{24,8},{1,17},{9,25},{17,1},{25,9},{2,18},{10... | collective-permute-start | bytes 1327112 | tf_op jit(solution)/shard_map/ppermute | solution.py:147
  5.0 10.9 %collective-permute-done.refs_1_ = f32[6,48,384]{2,1,0:T(8,128)S(1)} collective-permute-done((f32[6,48,384]{2,1,0:T(8,128)S(1)}, f32[6,48,384]{2,1,0:T(8,128)S(1)}, u32[]{:S(2)}, u32[]{:S(2)}) %collective-permute-start) | collective-permute-done | bytes 442400 | tf_op jit(solution)/shard_map/ppermute | solution.py:147
  16.4 8.1 %collective-permute-done.37.refs_1_ = f32[6,48,384]{2,1,0:T(8,128)S(1)} collective-permute-done((f32[6,48,384]{2,1,0:T(8,128)S(1)}, f32[6,48,384]{2,1,0:T(8,128)S(1)}, u32[]{:S(2)}, u32[]{:S(2)}) %collective-permute-start.37) | collective-permute-done | bytes 442400 | tf_op jit(solution)/shard_map/ppermute | solution.py:147
  30.8 3.0 %shard_map.141 = (f32[112,128]{1,0:T(8,128)S(1)}, f32[112,128]{1,0:T(8,128)S(1)}, f32[112,128]{1,0:T(8,128)S(1)}, f32[112,128]{1,0:T(8,128)S(1)}, f32[112,128]{1...) custom-call(s32[2]{0:T(128)S(1)} %pad_add_fusion.me_ref, ...), custom_call_target="tpu_custom_call" | custom-call | flops 1019215872 | bytes 4661256 | tf_op jit(solution)/shard_map/pallas_call | solution.py:131
  37.4 2.8 %collective-permute-start.9 = (f32[112,128]{1,0:T(8,128)S(1)}, f32[112,128]{1,0:T(8,128)S(1)}, u32[]{:S(2)}, u32[]{:S(2)}) collective-permute-start(f32[112,128]{1,0:T(8,128)S(1)} %get-tuple-element.86), channel_id=1, source_target_pairs={{0,4},{1,5},{2,6},{3,7},{4,0},{5,1},{6,2},{7,3},{8,12},{9,13},{10,... | collective-permute-start | bytes 172040 | tf_op jit(solution)/shard_map/ppermute | solution.py:155
  41.5 3.6 %collective-permute-start.11 = (f32[112,128]{1,0:T(8,128)S(1)}, f32[112,128]{1,0:T(8,128)S(1)}, u32[]{:S(2)}, u32[]{:S(2)}) collective-permute-start(f32[112,128]{1,0:T(8,128)S(1)} %get-tuple-element.88), channel_id=1, source_target_pairs={{0,6},{1,7},{2,4},{3,5},{4,2},{5,3},{6,0},{7,1},{8,14},{9,15},{10,... | collective-permute-start | bytes 172040 | tf_op jit(solution)/shard_map/ppermute | solution.py:155
  45.1 2.5 %shard_map.147 = (f32[112,128]{1,0:T(8,128)S(1)}, f32[112,128]{1,0:T(8,128)S(1)}, f32[112,128]{1,0:T(8,128)S(1)}, f32[112,128]{1,0:T(8,128)S(1)}, f32[112,128]{1...) custom-call(s32[2]{0:T(128)S(1)} %pad_add_fusion.me_ref, ...), custom_call_target="tpu_custom_call" | custom-call | flops 1019215872 | bytes 4661256 | tf_op jit(solution)/shard_map/pallas_call | solution.py:131
  51.2 2.3 %collective-permute-start.43 = (f32[112,128]{1,0:T(8,128)S(1)}, f32[112,128]{1,0:T(8,128)S(1)}, u32[]{:S(2)}, u32[]{:S(2)}) collective-permute-start(f32[112,128]{1,0:T(8,128)S(1)} %get-tuple-element.118), channel_id=1, source_target_pairs={{0,4},{1,5},{2,6},{3,7},{4,0},{5,1},{6,2},{7,3},{8,12},{9,13},{10,... | collective-permute-start | bytes 172040 | tf_op jit(solution)/shard_map/ppermute | solution.py:155
  55.9 3.6 %collective-permute-start.45 = (f32[112,128]{1,0:T(8,128)S(1)}, f32[112,128]{1,0:T(8,128)S(1)}, u32[]{:S(2)}, u32[]{:S(2)}) collective-permute-start(f32[112,128]{1,0:T(8,128)S(1)} %get-tuple-element.120), channel_id=1, source_target_pairs={{0,6},{1,7},{2,4},{3,5},{4,2},{5,3},{6,0},{7,1},{8,14},{9,15},{10,... | collective-permute-start | bytes 172040 | tf_op jit(solution)/shard_map/ppermute | solution.py:155
  64.7 2.3 %collective-permute-start.16 = (f32[112,128]{1,0:T(8,128)S(1)}, f32[112,128]{1,0:T(8,128)S(1)}, u32[]{:S(2)}, u32[]{:S(2)}) collective-permute-start(f32[112,128]{1,0:T(8,128)S(1)} %get-tuple-element.94), channel_id=1, source_target_pairs={{0,4},{1,5},{2,6},{3,7},{4,0},{5,1},{6,2},{7,3},{8,12},{9,13},{10,... | collective-permute-start | bytes 172040 | tf_op jit(solution)/shard_map/ppermute | solution.py:155
  68.6 3.6 %collective-permute-start.18 = (f32[112,128]{1,0:T(8,128)S(1)}, f32[112,128]{1,0:T(8,128)S(1)}, u32[]{:S(2)}, u32[]{:S(2)}) collective-permute-start(f32[112,128]{1,0:T(8,128)S(1)} %get-tuple-element.96), channel_id=1, source_target_pairs={{0,6},{1,7},{2,4},{3,5},{4,2},{5,3},{6,0},{7,1},{8,14},{9,15},{10,... | collective-permute-start | bytes 172040 | tf_op jit(solution)/shard_map/ppermute | solution.py:155
  77.4 2.1 %collective-permute-done.19.refs_7_ = f32[112,128]{1,0:T(8,128)S(1)} collective-permute-done((f32[112,128]{1,0:T(8,128)S(1)}, f32[112,128]{1,0:T(8,128)S(1)}, u32[]{:S(2)}, u32[]{:S(2)}) %collective-permute-start.19) | collective-permute-done | bytes 57376 | tf_op jit(solution)/shard_map/ppermute | solution.py:155
  82.2 2.9 %collective-permute-start.51 = (f32[112,128]{1,0:T(8,128)S(1)}, f32[112,128]{1,0:T(8,128)S(1)}, u32[]{:S(2)}, u32[]{:S(2)}) collective-permute-start(f32[112,128]{1,0:T(8,128)S(1)} %get-tuple-element.127), channel_id=1, source_target_pairs={{0,5},{1,4},{2,7},{3,6},{4,1},{5,0},{6,3},{7,2},{8,13},{9,12},{10,... | collective-permute-start | bytes 172040 | tf_op jit(solution)/shard_map/ppermute | solution.py:155
  85.1 2.3 %collective-permute-start.52 = (f32[112,128]{1,0:T(8,128)S(1)}, f32[112,128]{1,0:T(8,128)S(1)}, u32[]{:S(2)}, u32[]{:S(2)}) collective-permute-start(f32[112,128]{1,0:T(8,128)S(1)} %get-tuple-element.128), channel_id=1, source_target_pairs={{0,6},{1,7},{2,4},{3,5},{4,2},{5,3},{6,0},{7,1},{8,14},{9,15},{10,... | collective-permute-start | bytes 172040 | tf_op jit(solution)/shard_map/ppermute | solution.py:155
  91.1 3.2 %collective-permute-done.53.refs_7_ = f32[112,128]{1,0:T(8,128)S(1)} collective-permute-done((f32[112,128]{1,0:T(8,128)S(1)}, f32[112,128]{1,0:T(8,128)S(1)}, u32[]{:S(2)}, u32[]{:S(2)}) %collective-permute-start.53) | collective-permute-done | bytes 57376 | tf_op jit(solution)/shard_map/ppermute | solution.py:155
  96.3 7.3 %collective-permute-done.54.refs_1_ = f32[6,48,384]{2,1,0:T(8,128)S(1)} collective-permute-done((f32[6,48,384]{2,1,0:T(8,128)S(1)}, f32[6,48,384]{2,1,0:T(8,128)S(1)}, u32[]{:S(2)}, u32[]{:S(2)}) %collective-permute-start.54) | collective-permute-done | bytes 442400 | tf_op jit(solution)/shard_map/ppermute | solution.py:147
  103.6 2.7 %shard_map.144 = (f32[112,128]{1,0:T(8,128)S(1)}, f32[112,128]{1,0:T(8,128)S(1)}, f32[112,128]{1,0:T(8,128)S(1)}, f32[112,128]{1,0:T(8,128)S(1)}, f32[112,128]{1...) custom-call(s32[2]{0:T(128)S(1)} %pad_add_fusion.me_ref, ...), custom_call_target="tpu_custom_call" | custom-call | flops 1019215872 | bytes 4661256 | tf_op jit(solution)/shard_map/pallas_call | solution.py:131
  106.9 3.0 %collective-permute-start.25 = (f32[112,128]{1,0:T(8,128)S(1)}, f32[112,128]{1,0:T(8,128)S(1)}, u32[]{:S(2)}, u32[]{:S(2)}) collective-permute-start(f32[112,128]{1,0:T(8,128)S(1)} %get-tuple-element.101), channel_id=1, source_target_pairs={{0,3},{1,2},{2,1},{3,0},{4,7},{5,6},{6,5},{7,4},{8,11},{9,10},{10,... | collective-permute-start | bytes 172040 | tf_op jit(solution)/shard_map/ppermute | solution.py:155
  109.9 2.9 %collective-permute-start.27 = (f32[112,128]{1,0:T(8,128)S(1)}, f32[112,128]{1,0:T(8,128)S(1)}, u32[]{:S(2)}, u32[]{:S(2)}) collective-permute-start(f32[112,128]{1,0:T(8,128)S(1)} %get-tuple-element.103), channel_id=1, source_target_pairs={{0,5},{1,4},{2,7},{3,6},{4,1},{5,0},{6,3},{7,2},{8,13},{9,12},{10,... | collective-permute-start | bytes 172040 | tf_op jit(solution)/shard_map/ppermute | solution.py:155
  112.8 2.5 %shard_map.150 = (f32[112,128]{1,0:T(8,128)S(1)}, f32[112,128]{1,0:T(8,128)S(1)}, f32[112,128]{1,0:T(8,128)S(1)}, f32[112,128]{1,0:T(8,128)S(1)}, f32[112,128]{1...) custom-call(s32[2]{0:T(128)S(1)} %pad_add_fusion.me_ref, ...), custom_call_target="tpu_custom_call" | custom-call | flops 1019215872 | bytes 4661256 | tf_op jit(solution)/shard_map/pallas_call | solution.py:131
  117.3 2.8 %collective-permute-start.29 = (f32[112,128]{1,0:T(8,128)S(1)}, f32[112,128]{1,0:T(8,128)S(1)}, u32[]{:S(2)}, u32[]{:S(2)}) collective-permute-start(f32[112,128]{1,0:T(8,128)S(1)} %get-tuple-element.105), channel_id=1, source_target_pairs={{0,7},{1,6},{2,5},{3,4},{4,3},{5,2},{6,1},{7,0},{8,15},{9,14},{10,... | collective-permute-start | bytes 172040 | tf_op jit(solution)/shard_map/ppermute | solution.py:155
  120.7 2.9 %collective-permute-start.59 = (f32[112,128]{1,0:T(8,128)S(1)}, f32[112,128]{1,0:T(8,128)S(1)}, u32[]{:S(2)}, u32[]{:S(2)}) collective-permute-start(f32[112,128]{1,0:T(8,128)S(1)} %get-tuple-element.133), channel_id=1, source_target_pairs={{0,3},{1,2},{2,1},{3,0},{4,7},{5,6},{6,5},{7,4},{8,11},{9,10},{10,... | collective-permute-start | bytes 172040 | tf_op jit(solution)/shard_map/ppermute | solution.py:155
  128.5 2.8 %collective-permute-start.63 = (f32[112,128]{1,0:T(8,128)S(1)}, f32[112,128]{1,0:T(8,128)S(1)}, u32[]{:S(2)}, u32[]{:S(2)}) collective-permute-start(f32[112,128]{1,0:T(8,128)S(1)} %get-tuple-element.137), channel_id=1, source_target_pairs={{0,7},{1,6},{2,5},{3,4},{4,3},{5,2},{6,1},{7,0},{8,15},{9,14},{10,... | collective-permute-start | bytes 172040 | tf_op jit(solution)/shard_map/ppermute | solution.py:155
  133.4 2.9 %collective-permute-start.32 = (f32[112,128]{1,0:T(8,128)S(1)}, f32[112,128]{1,0:T(8,128)S(1)}, u32[]{:S(2)}, u32[]{:S(2)}) collective-permute-start(f32[112,128]{1,0:T(8,128)S(1)} %get-tuple-element.109), channel_id=1, source_target_pairs={{0,3},{1,2},{2,1},{3,0},{4,7},{5,6},{6,5},{7,4},{8,11},{9,10},{10,... | collective-permute-start | bytes 172040 | tf_op jit(solution)/shard_map/ppermute | solution.py:155
  136.5 2.8 %collective-permute-start.34 = (f32[112,128]{1,0:T(8,128)S(1)}, f32[112,128]{1,0:T(8,128)S(1)}, u32[]{:S(2)}, u32[]{:S(2)}) collective-permute-start(f32[112,128]{1,0:T(8,128)S(1)} %get-tuple-element.111), channel_id=1, source_target_pairs={{0,5},{1,4},{2,7},{3,6},{4,1},{5,0},{6,3},{7,2},{8,13},{9,12},{10,... | collective-permute-start | bytes 172040 | tf_op jit(solution)/shard_map/ppermute | solution.py:155
  142.8 2.8 %collective-permute-start.36 = (f32[112,128]{1,0:T(8,128)S(1)}, f32[112,128]{1,0:T(8,128)S(1)}, u32[]{:S(2)}, u32[]{:S(2)}) collective-permute-start(f32[112,128]{1,0:T(8,128)S(1)} %get-tuple-element.113), channel_id=1, source_target_pairs={{0,7},{1,6},{2,5},{3,4},{4,3},{5,2},{6,1},{7,0},{8,15},{9,14},{10,... | collective-permute-start | bytes 172040 | tf_op jit(solution)/shard_map/ppermute | solution.py:155
  146.2 2.9 %collective-permute-start.66 = (f32[112,128]{1,0:T(8,128)S(1)}, f32[112,128]{1,0:T(8,128)S(1)}, u32[]{:S(2)}, u32[]{:S(2)}) collective-permute-start(f32[112,128]{1,0:T(8,128)S(1)} %get-tuple-element.141), channel_id=1, source_target_pairs={{0,3},{1,2},{2,1},{3,0},{4,7},{5,6},{6,5},{7,4},{8,11},{9,10},{10,... | collective-permute-start | bytes 172040 | tf_op jit(solution)/shard_map/ppermute | solution.py:155
  149.9 2.1 %collective-permute-start.68 = (f32[112,128]{1,0:T(8,128)S(1)}, f32[112,128]{1,0:T(8,128)S(1)}, u32[]{:S(2)}, u32[]{:S(2)}) collective-permute-start(f32[112,128]{1,0:T(8,128)S(1)} %get-tuple-element.143), channel_id=1, source_target_pairs={{0,5},{1,4},{2,7},{3,6},{4,1},{5,0},{6,3},{7,2},{8,13},{9,12},{10,... | collective-permute-start | bytes 172040 | tf_op jit(solution)/shard_map/ppermute | solution.py:155
  154.0 2.8 %collective-permute-start.70 = (f32[112,128]{1,0:T(8,128)S(1)}, f32[112,128]{1,0:T(8,128)S(1)}, u32[]{:S(2)}, u32[]{:S(2)}) collective-permute-start(f32[112,128]{1,0:T(8,128)S(1)} %get-tuple-element.145), channel_id=1, source_target_pairs={{0,7},{1,6},{2,5},{3,4},{4,3},{5,2},{6,1},{7,0},{8,15},{9,14},{10,... | collective-permute-start | bytes 172040 | tf_op jit(solution)/shard_map/ppermute | solution.py:155
  158.5 2.4 %collective-permute-done.70.refs_8_ = f32[112,128]{1,0:T(8,128)S(1)} collective-permute-done((f32[112,128]{1,0:T(8,128)S(1)}, f32[112,128]{1,0:T(8,128)S(1)}, u32[]{:S(2)}, u32[]{:S(2)}) %collective-permute-start.70) | collective-permute-done | bytes 57376 | tf_op jit(solution)/shard_map/ppermute | solution.py:155
  160.9 2.2 %shard_map.152 = (f32[2,6,48,384]{3,2,1,0:T(8,128)}, f32[48,384]{1,0:T(8,128)}, f32[32,128]{1,0:T(8,128)S(1)}) custom-call(s32[2]{0:T(128)S(1)} %pad_add_fusion.me_ref, f32[2,6]{1,0:T(2,128)S(1)} %copy-done.7, s32[1]{0:T(128)S(6)} %copy.20.count_ref, f32[5,48,384]{2,1,0:T(8,128)S(1)} %copy-done, s32[48,384]{1,0:T(8,128)S(1)} %copy-done.1, ...), custom_call_target="tpu_custom_call" | custom-call | flops 10000000 | bytes 3646140 | tf_op jit(solution)/shard_map/pallas_call | solution.py:384
  163.1 10.1 %all_to_all.11 = f32[32,1,128]{2,1,0:T(1,128)S(1)} all-to-all(f32[32,1,128]{2,1,0:T(1,128)S(1)} %bitcast.15), channel_id=1, replica_groups=mesh['gx'=4,'gy'=8] {'gx','gy'}, dimensions={0} | all-to-all | bytes 32768 | tf_op jit(solution)/shard_map/all_to_all | solution.py:449
  (150 shorter events, 57.8 us)
Async XLA Ops:
  1.9 14.0 %collective-permute-start = (f32[6,48,384]{2,1,0:T(8,128)S(1)}, f32[6,48,384]{2,1,0:T(8,128)S(1)}, u32[]{:S(2)}, u32[]{:S(2)}) collective-permute-start(f32[6,48,384]{2,1,0:T(8,128)S(1)} %get-tuple-element.156.refs_0_), channel_id=1, source_target_pairs={{0,16},{8,24},{16,0},{24,8},{1,17},{9,25},{17,1},{25,9},{2,18},{10... | collective-permute-start | bytes 1327112 | tf_op jit(solution)/shard_map/ppermute | solution.py:147
  4.9 19.6 %collective-permute-start.37 = (f32[6,48,384]{2,1,0:T(8,128)S(1)}, f32[6,48,384]{2,1,0:T(8,128)S(1)}, u32[]{:S(2)}, u32[]{:S(2)}) collective-permute-start(f32[6,48,384]{2,1,0:T(8,128)S(1)} %get-tuple-element.155.refs_0_), channel_id=1, source_target_pairs={{0,16},{8,24},{16,0},{24,8},{1,17},{9,25},{17,1},{25,9},{2,18},{10... | collective-permute-start | bytes 1327112 | tf_op jit(solution)/shard_map/ppermute | solution.py:147
  5.0 23.7 %collective-permute-start.4 = (f32[6,48,384]{2,1,0:T(8,128)S(1)}, f32[6,48,384]{2,1,0:T(8,128)S(1)}, u32[]{:S(2)}, u32[]{:S(2)}) collective-permute-start(f32[6,48,384]{2,1,0:T(8,128)S(1)} %get-tuple-element.156.refs_0_), channel_id=1, source_target_pairs={{0,8},{8,0},{16,24},{24,16},{1,9},{9,1},{17,25},{25,17},{2,10},{10... | collective-permute-start | bytes 1327112 | tf_op jit(solution)/shard_map/ppermute | solution.py:147
  15.9 14.9 %collective-permute-start.5 = (f32[6,48,384]{2,1,0:T(8,128)S(1)}, f32[6,48,384]{2,1,0:T(8,128)}, u32[]{:S(2)}, u32[]{:S(2)}) collective-permute-start(f32[6,48,384]{2,1,0:T(8,128)S(1)} %collective-permute-done.refs_1_), channel_id=1, source_target_pairs={{0,8},{8,0},{16,24},{24,16},{1,9},{9,1},{17,25},{25,17},{2,10},{10... | collective-permute-start | bytes 1327112 | tf_op jit(solution)/shard_map/ppermute | solution.py:147
  15.9 19.7 %collective-permute-start.38 = (f32[6,48,384]{2,1,0:T(8,128)S(1)}, f32[6,48,384]{2,1,0:T(8,128)S(1)}, u32[]{:S(2)}, u32[]{:S(2)}) collective-permute-start(f32[6,48,384]{2,1,0:T(8,128)S(1)} %get-tuple-element.155.refs_0_), channel_id=1, source_target_pairs={{0,8},{8,0},{16,24},{24,16},{1,9},{9,1},{17,25},{25,17},{2,10},{10... | collective-permute-start | bytes 1327112 | tf_op jit(solution)/shard_map/ppermute | solution.py:147
  24.6 15.6 %collective-permute-start.39 = (f32[6,48,384]{2,1,0:T(8,128)S(1)}, f32[6,48,384]{2,1,0:T(8,128)S(1)}, u32[]{:S(2)}, u32[]{:S(2)}) collective-permute-start(f32[6,48,384]{2,1,0:T(8,128)S(1)} %collective-permute-done.37.refs_1_), channel_id=1, source_target_pairs={{0,8},{8,0},{16,24},{24,16},{1,9},{9,1},{17,25},{25,17},{2,10},{10... | collective-permute-start | bytes 1327112 | tf_op jit(solution)/shard_map/ppermute | solution.py:147
  35.6 12.0 %collective-permute-start.7 = (f32[112,128]{1,0:T(8,128)S(1)}, f32[112,128]{1,0:T(8,128)S(1)}, u32[]{:S(2)}, u32[]{:S(2)}) collective-permute-start(f32[112,128]{1,0:T(8,128)S(1)} %get-tuple-element.84), channel_id=1, source_target_pairs={{0,2},{1,3},{2,0},{3,1},{4,6},{5,7},{6,4},{7,5},{8,10},{9,11},{10,... | collective-permute-start | bytes 172040 | tf_op jit(solution)/shard_map/ppermute | solution.py:155
  37.2 10.5 %collective-permute-start.8 = (f32[112,128]{1,0:T(8,128)S(1)}, f32[112,128]{1,0:T(8,128)S(1)}, u32[]{:S(2)}, u32[]{:S(2)}) collective-permute-start(f32[112,128]{1,0:T(8,128)S(1)} %get-tuple-element.85), channel_id=1, source_target_pairs={{0,3},{1,2},{2,1},{3,0},{4,7},{5,6},{6,5},{7,4},{8,11},{9,10},{10,... | collective-permute-start | bytes 172040 | tf_op jit(solution)/shard_map/ppermute | solution.py:155
  37.4 11.9 %collective-permute-start.9 = (f32[112,128]{1,0:T(8,128)S(1)}, f32[112,128]{1,0:T(8,128)S(1)}, u32[]{:S(2)}, u32[]{:S(2)}) collective-permute-start(f32[112,128]{1,0:T(8,128)S(1)} %get-tuple-element.86), channel_id=1, source_target_pairs={{0,4},{1,5},{2,6},{3,7},{4,0},{5,1},{6,2},{7,3},{8,12},{9,13},{10,... | collective-permute-start | bytes 172040 | tf_op jit(solution)/shard_map/ppermute | solution.py:155
  41.5 9.8 %collective-permute-start.11 = (f32[112,128]{1,0:T(8,128)S(1)}, f32[112,128]{1,0:T(8,128)S(1)}, u32[]{:S(2)}, u32[]{:S(2)}) collective-permute-start(f32[112,128]{1,0:T(8,128)S(1)} %get-tuple-element.88), channel_id=1, source_target_pairs={{0,6},{1,7},{2,4},{3,5},{4,2},{5,3},{6,0},{7,1},{8,14},{9,15},{10,... | collective-permute-start | bytes 172040 | tf_op jit(solution)/shard_map/ppermute | solution.py:155
  49.3 10.2 %collective-permute-start.41 = (f32[112,128]{1,0:T(8,128)S(1)}, f32[112,128]{1,0:T(8,128)S(1)}, u32[]{:S(2)}, u32[]{:S(2)}) collective-permute-start(f32[112,128]{1,0:T(8,128)S(1)} %get-tuple-element.116), channel_id=1, source_target_pairs={{0,2},{1,3},{2,0},{3,1},{4,6},{5,7},{6,4},{7,5},{8,10},{9,11},{10,... | collective-permute-start | bytes 172040 | tf_op jit(solution)/shard_map/ppermute | solution.py:155
  49.3 11.7 %collective-permute-start.42 = (f32[112,128]{1,0:T(8,128)S(1)}, f32[112,128]{1,0:T(8,128)S(1)}, u32[]{:S(2)}, u32[]{:S(2)}) collective-permute-start(f32[112,128]{1,0:T(8,128)S(1)} %get-tuple-element.117), channel_id=1, source_target_pairs={{0,3},{1,2},{2,1},{3,0},{4,7},{5,6},{6,5},{7,4},{8,11},{9,10},{10,... | collective-permute-start | bytes 172040 | tf_op jit(solution)/shard_map/ppermute | solution.py:155
  51.2 11.5 %collective-permute-start.43 = (f32[112,128]{1,0:T(8,128)S(1)}, f32[112,128]{1,0:T(8,128)S(1)}, u32[]{:S(2)}, u32[]{:S(2)}) collective-permute-start(f32[112,128]{1,0:T(8,128)S(1)} %get-tuple-element.118), channel_id=1, source_target_pairs={{0,4},{1,5},{2,6},{3,7},{4,0},{5,1},{6,2},{7,3},{8,12},{9,13},{10,... | collective-permute-start | bytes 172040 | tf_op jit(solution)/shard_map/ppermute | solution.py:155
  62.8 9.5 %collective-permute-start.14 = (f32[112,128]{1,0:T(8,128)S(1)}, f32[112,128]{1,0:T(8,128)S(1)}, u32[]{:S(2)}, u32[]{:S(2)}) collective-permute-start(f32[112,128]{1,0:T(8,128)S(1)} %get-tuple-element.92), channel_id=1, source_target_pairs={{0,2},{1,3},{2,0},{3,1},{4,6},{5,7},{6,4},{7,5},{8,10},{9,11},{10,... | collective-permute-start | bytes 172040 | tf_op jit(solution)/shard_map/ppermute | solution.py:155
  63.2 10.6 %collective-permute-start.15 = (f32[112,128]{1,0:T(8,128)S(1)}, f32[112,128]{1,0:T(8,128)S(1)}, u32[]{:S(2)}, u32[]{:S(2)}) collective-permute-start(f32[112,128]{1,0:T(8,128)S(1)} %get-tuple-element.93), channel_id=1, source_target_pairs={{0,3},{1,2},{2,1},{3,0},{4,7},{5,6},{6,5},{7,4},{8,11},{9,10},{10,... | collective-permute-start | bytes 172040 | tf_op jit(solution)/shard_map/ppermute | solution.py:155
  64.7 10.8 %collective-permute-start.16 = (f32[112,128]{1,0:T(8,128)S(1)}, f32[112,128]{1,0:T(8,128)S(1)}, u32[]{:S(2)}, u32[]{:S(2)}) collective-permute-start(f32[112,128]{1,0:T(8,128)S(1)} %get-tuple-element.94), channel_id=1, source_target_pairs={{0,4},{1,5},{2,6},{3,7},{4,0},{5,1},{6,2},{7,3},{8,12},{9,13},{10,... | collective-permute-start | bytes 172040 | tf_op jit(solution)/shard_map/ppermute | solution.py:155
  75.5 9.6 %collective-permute-start.48 = (f32[112,128]{1,0:T(8,128)S(1)}, f32[112,128]{1,0:T(8,128)S(1)}, u32[]{:S(2)}, u32[]{:S(2)}) collective-permute-start(f32[112,128]{1,0:T(8,128)S(1)} %get-tuple-element.124), channel_id=1, source_target_pairs={{0,2},{1,3},{2,0},{3,1},{4,6},{5,7},{6,4},{7,5},{8,10},{9,11},{10,... | collective-permute-start | bytes 172040 | tf_op jit(solution)/shard_map/ppermute | solution.py:155
  75.5 12.0 %collective-permute-start.49 = (f32[112,128]{1,0:T(8,128)S(1)}, f32[112,128]{1,0:T(8,128)S(1)}, u32[]{:S(2)}, u32[]{:S(2)}) collective-permute-start(f32[112,128]{1,0:T(8,128)S(1)} %get-tuple-element.125), channel_id=1, source_target_pairs={{0,3},{1,2},{2,1},{3,0},{4,7},{5,6},{6,5},{7,4},{8,11},{9,10},{10,... | collective-permute-start | bytes 172040 | tf_op jit(solution)/shard_map/ppermute | solution.py:155
  80.4 15.4 %collective-permute-start.20 = (f32[6,48,384]{2,1,0:T(8,128)S(1)}, f32[6,48,384]{2,1,0:T(8,128)S(1)}, u32[]{:S(2)}, u32[]{:S(2)}) collective-permute-start(f32[6,48,384]{2,1,0:T(8,128)S(1)} %shard_map.143.refs_0_), channel_id=1, source_target_pairs={{0,16},{8,24},{16,0},{24,8},{1,17},{9,25},{17,1},{25,9},{2,18},{10... | collective-permute-start | bytes 1327112 | tf_op jit(solution)/shard_map/ppermute | solution.py:147
  96.3 13.6 %collective-permute-start.55 = (f32[6,48,384]{2,1,0:T(8,128)S(1)}, f32[6,48,384]{2,1,0:T(8,128)S(1)}, u32[]{:S(2)}, u32[]{:S(2)}) collective-permute-start(f32[6,48,384]{2,1,0:T(8,128)S(1)} %shard_map.149.refs_0_), channel_id=1, source_target_pairs={{0,8},{8,0},{16,24},{24,16},{1,9},{9,1},{17,25},{25,17},{2,10},{10... | collective-permute-start | bytes 1327112 | tf_op jit(solution)/shard_map/ppermute | solution.py:147
  106.9 10.4 %collective-permute-start.24 = (f32[112,128]{1,0:T(8,128)S(1)}, f32[112,128]{1,0:T(8,128)S(1)}, u32[]{:S(2)}, u32[]{:S(2)}) collective-permute-start(f32[112,128]{1,0:T(8,128)S(1)} %get-tuple-element.100), channel_id=1, source_target_pairs={{0,2},{1,3},{2,0},{3,1},{4,6},{5,7},{6,4},{7,5},{8,10},{9,11},{10,... | collective-permute-start | bytes 172040 | tf_op jit(solution)/shard_map/ppermute | solution.py:155
  106.9 13.2 %collective-permute-start.25 = (f32[112,128]{1,0:T(8,128)S(1)}, f32[112,128]{1,0:T(8,128)S(1)}, u32[]{:S(2)}, u32[]{:S(2)}) collective-permute-start(f32[112,128]{1,0:T(8,128)S(1)} %get-tuple-element.101), channel_id=1, source_target_pairs={{0,3},{1,2},{2,1},{3,0},{4,7},{5,6},{6,5},{7,4},{8,11},{9,10},{10,... | collective-permute-start | bytes 172040 | tf_op jit(solution)/shard_map/ppermute | solution.py:155
  109.9 10.8 %collective-permute-start.26 = (f32[112,128]{1,0:T(8,128)S(1)}, f32[112,128]{1,0:T(8,128)S(1)}, u32[]{:S(2)}, u32[]{:S(2)}) collective-permute-start(f32[112,128]{1,0:T(8,128)S(1)} %get-tuple-element.102), channel_id=1, source_target_pairs={{0,4},{1,5},{2,6},{3,7},{4,0},{5,1},{6,2},{7,3},{8,12},{9,13},{10,... | collective-permute-start | bytes 172040 | tf_op jit(solution)/shard_map/ppermute | solution.py:155
  109.9 10.7 %collective-permute-start.27 = (f32[112,128]{1,0:T(8,128)S(1)}, f32[112,128]{1,0:T(8,128)S(1)}, u32[]{:S(2)}, u32[]{:S(2)}) collective-permute-start(f32[112,128]{1,0:T(8,128)S(1)} %get-tuple-element.103), channel_id=1, source_target_pairs={{0,5},{1,4},{2,7},{3,6},{4,1},{5,0},{6,3},{7,2},{8,13},{9,12},{10,... | collective-permute-start | bytes 172040 | tf_op jit(solution)/shard_map/ppermute | solution.py:155
  120.7 12.1 %collective-permute-start.59 = (f32[112,128]{1,0:T(8,128)S(1)}, f32[112,128]{1,0:T(8,128)S(1)}, u32[]{:S(2)}, u32[]{:S(2)}) collective-permute-start(f32[112,128]{1,0:T(8,128)S(1)} %get-tuple-element.133), channel_id=1, source_target_pairs={{0,3},{1,2},{2,1},{3,0},{4,7},{5,6},{6,5},{7,4},{8,11},{9,10},{10,... | collective-permute-start | bytes 172040 | tf_op jit(solution)/shard_map/ppermute | solution.py:155
  123.6 9.8 %collective-permute-start.60 = (f32[112,128]{1,0:T(8,128)S(1)}, f32[112,128]{1,0:T(8,128)S(1)}, u32[]{:S(2)}, u32[]{:S(2)}) collective-permute-start(f32[112,128]{1,0:T(8,128)S(1)} %get-tuple-element.134), channel_id=1, source_target_pairs={{0,4},{1,5},{2,6},{3,7},{4,0},{5,1},{6,2},{7,3},{8,12},{9,13},{10,... | collective-permute-start | bytes 172040 | tf_op jit(solution)/shard_map/ppermute | solution.py:155
  126.5 9.8 %collective-permute-start.62 = (f32[112,128]{1,0:T(8,128)S(1)}, f32[112,128]{1,0:T(8,128)S(1)}, u32[]{:S(2)}, u32[]{:S(2)}) collective-permute-start(f32[112,128]{1,0:T(8,128)S(1)} %get-tuple-element.136), channel_id=1, source_target_pairs={{0,6},{1,7},{2,4},{3,5},{4,2},{5,3},{6,0},{7,1},{8,14},{9,15},{10,... | collective-permute-start | bytes 172040 | tf_op jit(solution)/shard_map/ppermute | solution.py:155
  133.4 9.4 %collective-permute-start.31 = (f32[112,128]{1,0:T(8,128)S(1)}, f32[112,128]{1,0:T(8,128)S(1)}, u32[]{:S(2)}, u32[]{:S(2)}) collective-permute-start(f32[112,128]{1,0:T(8,128)S(1)} %get-tuple-element.108), channel_id=1, source_target_pairs={{0,2},{1,3},{2,0},{3,1},{4,6},{5,7},{6,4},{7,5},{8,10},{9,11},{10,... | collective-permute-start | bytes 172040 | tf_op jit(solution)/shard_map/ppermute | solution.py:155
  133.4 12.2 %collective-permute-start.32 = (f32[112,128]{1,0:T(8,128)S(1)}, f32[112,128]{1,0:T(8,128)S(1)}, u32[]{:S(2)}, u32[]{:S(2)}) collective-permute-start(f32[112,128]{1,0:T(8,128)S(1)} %get-tuple-element.109), channel_id=1, source_target_pairs={{0,3},{1,2},{2,1},{3,0},{4,7},{5,6},{6,5},{7,4},{8,11},{9,10},{10,... | collective-permute-start | bytes 172040 | tf_op jit(solution)/shard_map/ppermute | solution.py:155
  136.4 9.8 %collective-permute-start.33 = (f32[112,128]{1,0:T(8,128)S(1)}, f32[112,128]{1,0:T(8,128)S(1)}, u32[]{:S(2)}, u32[]{:S(2)}) collective-permute-start(f32[112,128]{1,0:T(8,128)S(1)} %get-tuple-element.110), channel_id=1, source_target_pairs={{0,4},{1,5},{2,6},{3,7},{4,0},{5,1},{6,2},{7,3},{8,12},{9,13},{10,... | collective-permute-start | bytes 172040 | tf_op jit(solution)/shard_map/ppermute | solution.py:155
  136.5 9.7 %collective-permute-start.34 = (f32[112,128]{1,0:T(8,128)S(1)}, f32[112,128]{1,0:T(8,128)S(1)}, u32[]{:S(2)}, u32[]{:S(2)}) collective-permute-start(f32[112,128]{1,0:T(8,128)S(1)} %get-tuple-element.111), channel_id=1, source_target_pairs={{0,5},{1,4},{2,7},{3,6},{4,1},{5,0},{6,3},{7,2},{8,13},{9,12},{10,... | collective-permute-start | bytes 172040 | tf_op jit(solution)/shard_map/ppermute | solution.py:155
  146.2 12.3 %collective-permute-start.66 = (f32[112,128]{1,0:T(8,128)S(1)}, f32[112,128]{1,0:T(8,128)S(1)}, u32[]{:S(2)}, u32[]{:S(2)}) collective-permute-start(f32[112,128]{1,0:T(8,128)S(1)} %get-tuple-element.141), channel_id=1, source_target_pairs={{0,3},{1,2},{2,1},{3,0},{4,7},{5,6},{6,5},{7,4},{8,11},{9,10},{10,... | collective-permute-start | bytes 172040 | tf_op jit(solution)/shard_map/ppermute | solution.py:155
  (49 other events, 483.6 us)

commit v2 on v1

--- a/solution.py
+++ b/solution.py
@@ -90,13 +90,13 @@
         return pltpu.VMEM((self.fields * self.blocks, self.rows, LANES), jnp.float32)
 
     @property
-    def lines(self):
-        return pltpu.VMEM((self.parts * self.rows, self.columns), jnp.float32)
-
-    @property
     def blocks_out(self):
         shape = jax.ShapeDtypeStruct((self.width, LANES), jnp.float32)
         return [shape] * self.parts
+
+
+def part_of(me_ref, mask):
+    return (me_ref[1] // 2) ^ mask
 
 
 def turn(value, shift):
@@ -139,9 +139,17 @@
     )(*operands)
 
 
-def gather_pieces(block, axis, count):
+def after(value, *others):
+    return lax.optimization_barrier((value,) + others)[0]
+
+
+def gather_pieces(block, axis, count, hold=None):
     held = [(0, block)]
     bit = count // 2
+    if bit > 1 and hold is not None:
+        first = lax.ppermute(block, axis, [(i, i ^ bit) for i in range(count)])
+        held = held + [(bit, after(first, *hold))]
+        bit //= 2
     while bit:
         pairs = [(i, i ^ bit) for i in range(count)]
         held = held + [(mask ^ bit, lax.ppermute(piece, axis, pairs)) for mask, piece in held]
@@ -150,9 +158,10 @@
 
 
 def exchange(blocks, axis, count):
-    out = [blocks[0]] + [None] * (count - 1)
-    for mask in range(count - 1, 0, -1):
-        out[mask] = lax.ppermute(blocks[mask], axis, [(i, i ^ mask) for i in range(count)])
+    out = [blocks[0]] + [None] * (len(blocks) - 1)
+    for mask in range(len(blocks) - 1, 0, -1):
+        pairs = [(i, i ^ (2 * mask)) for i in range(count)]
+        out[mask] = lax.ppermute(blocks[mask], axis, pairs)
     return out
 
 
@@ -169,19 +178,31 @@
     return call(kernel, [shape, shape], [x_inverse])
 
 
-def prepare_y(masks, pieces, me):
-    rows, cols = pieces[0].shape
+def prepare_y(masks, pieces, me, rows):
+    owned, half = pieces[0].shape
 
     def kernel(me_ref, *refs):
-        high_ref, low_ref = refs[-2:]
+        high_ref, low_ref, whole_ref = refs[-3:]
+        side = lax.rem(me_ref[1], 2)
         for mask, ref in zip(masks, refs):
-            start = pl.multiple_of((me_ref[0] ^ mask) * rows, rows)
-            high, low = split(ref[...])
-            high_ref[pl.ds(start, rows), :] = high
-            low_ref[pl.ds(start, rows), :] = low
-
-    shape = jax.ShapeDtypeStruct((cols, cols), jnp.bfloat16)
-    return call(kernel, [shape, shape], [me] + pieces, scalars=(0,))
+            start = pl.multiple_of((me_ref[0] ^ mask) * owned, owned)
+            whole_ref[pl.ds(start, owned), :] = ref[...]
+        for other in range(2):
+            for part in range(half // rows):
+                start = pl.multiple_of((2 * part + (side ^ other)) * rows, rows)
+                high, low = split(whole_ref[pl.ds(start, rows), :])
+                out = other * half + part * rows
+                high_ref[out : out + rows, :] = high
+                low_ref[out : out + rows, :] = low
+
+    shape = jax.ShapeDtypeStruct((2 * half, half), jnp.bfloat16)
+    return call(
+        kernel,
+        [shape, shape],
+        [me] + pieces,
+        scalars=(0,),
+        scratch=[pltpu.VMEM((2 * half, half), jnp.float32)],
+    )
 
 
 def zonal(plan, masks, pieces, me, x_high, x_low, sea_mask):
@@ -203,7 +224,7 @@
             for field in range(fields):
                 tiles_ref[field * plan.blocks + block] = sea[:, lanes] * total[field, :, lanes]
         for mask in range(parts):
-            plan.send_tiles(tiles_ref, me_ref[1] ^ mask, out_refs[mask])
+            plan.send_tiles(tiles_ref, part_of(me_ref, mask), out_refs[mask])
 
     return call(
         kernel,
@@ -219,38 +240,54 @@
     rows, parts = plan.rows, plan.parts
 
     def kernel(me_ref, high_ref, low_ref, *refs):
-        in_refs, out_refs, lines_ref = refs[:parts], refs[parts : 2 * parts], refs[-1]
+        in_refs, out_refs, lines_ref, solved_ref = refs[:parts], refs[parts:-2], refs[-2], refs[-1]
         for mask in range(parts):
-            place = pl.ds(pl.multiple_of((me_ref[1] ^ mask) * rows, rows), rows)
+            place = pl.ds(pl.multiple_of(part_of(me_ref, mask) * rows, rows), rows)
             for i in range(plan.full):
                 lanes = slice(i * LANES, (i + 1) * LANES)
                 lines_ref[place, lanes] = in_refs[mask][i * rows : (i + 1) * rows, :]
             if plan.rest:
                 lines_ref[place, plan.full * LANES :] = plan.unpack_rest(in_refs[mask], 0)
-        lines_ref[...] = dot_split((high_ref[...], low_ref[...]), split(lines_ref[...]))
-        for mask in range(parts):
-            place = pl.ds(pl.multiple_of((me_ref[1] ^ mask) * rows, rows), rows)
-            for i in range(plan.full):
-                lanes = slice(i * LANES, (i + 1) * LANES)
-                out_refs[mask][i * rows : (i + 1) * rows, :] = lines_ref[place, lanes]
-            if plan.rest:
-                last = lines_ref[place, plan.full * LANES :]
-                plan.store_rest(out_refs[mask], plan.pack_rest(last, 0))
-
+        solved_ref[...] = dot_split((high_ref[...], low_ref[...]), split(lines_ref[...]))
+        for other in range(2):
+            for part in range(parts):
+                start = (other * parts + part) * rows
+                for i in range(plan.full):
+                    lanes = slice(i * LANES, (i + 1) * LANES)
+                    out_refs[other][part, i * rows : (i + 1) * rows, :] = solved_ref[
+                        start : start + rows, lanes
+                    ]
+                if plan.rest:
+                    last = solved_ref[start : start + rows, plan.full * LANES :]
+                    plan.store_rest(out_refs[other].at[part], plan.pack_rest(last, 0))
+
+    shape = jax.ShapeDtypeStruct((parts, plan.width, LANES), jnp.float32)
     return call(
         kernel,
-        plan.blocks_out,
+        [shape, shape],
         [me, y_high, y_low] + lines,
         scalars=(0,),
-        flops=6 * (parts * rows) ** 2 * plan.columns,
-        scratch=[plan.lines],
+        flops=12 * (parts * rows) ** 2 * plan.columns,
+        scratch=[
+            pltpu.VMEM((parts * rows, plan.columns), jnp.float32),
+            pltpu.VMEM((2 * parts * rows, plan.columns), jnp.float32),
+        ],
     )
+
+
+def add_sides(plan, me, own, other):
+    def kernel(me_ref, own_ref, other_ref, *out_refs):
+        for mask in range(plan.parts):
+            part = part_of(me_ref, mask)
+            out_refs[mask][...] = own_ref[part] + other_ref[part]
+
+    return call(kernel, plan.blocks_out, [me, own, other], scalars=(0,))
 
 
 def solve_columns(plan, me_ref, in_refs, tiles_ref, kappa_ref, sea_ref, levels, store):
     kinds = plan.fields // levels
     for mask in range(plan.parts):
-        plan.take_tiles(in_refs[mask], me_ref[1] ^ mask, tiles_ref)
+        plan.take_tiles(in_refs[mask], part_of(me_ref, mask), tiles_ref)
     for block in range(plan.blocks):
         lanes = slice(block * LANES, (block + 1) * LANES)
         sea = sea_ref[:, lanes].astype(jnp.float32)
@@ -399,38 +436,46 @@
     def kernel(in_ref, out_ref):
         turned = jnp.transpose(in_ref[...])
         for r in range(CAP):
-            out_ref[r] = turned[r * RANK_ROWS : r * RANK_ROWS + records, :]
-
-    return call(kernel, jax.ShapeDtypeStruct((CAP, records, devices), jnp.float32), [arrived])
+            out_ref[:, r, :] = turned[r * RANK_ROWS : r * RANK_ROWS + records, :]
+
+    out = call(kernel, jax.ShapeDtypeStruct((records, CAP, devices), jnp.float32), [arrived])
+    return jnp.swapaxes(out, 0, 1)
 
 
 def body(gx_count, gy_count, control, sigma, kappa, beta, sea_mask, x_inverse, y_inverse, ssh_coef,
          obs_owner, tile_index, obs_frac, obs_count):
     _, kinds, levels, rows, cols = control.shape
     devices = gx_count * gy_count
-    plan = Plan(levels, rows, cols, gy_count)
+    plan = Plan(levels, rows, cols, gy_count // 2)
     chunks = kinds
     if not plan.fits:
-        plan, chunks = Plan(kinds * levels, rows, cols, gy_count), 1
+        plan, chunks = Plan(kinds * levels, rows, cols, gy_count // 2), 1
     me = jnp.stack([lax.axis_index("gx"), lax.axis_index("gy")]).astype(jnp.int32)
     x_high, x_low = prepare_x(x_inverse)
     fields = list(control.reshape(chunks, plan.fields, rows, cols))
-    y_parts = None
-    result = None
+    y_columns = y_inverse.reshape(y_inverse.shape[0], gy_count // 2, 2, rows)
+    y_columns = jnp.where(me[1] % 2 == 0, y_columns[:, :, 0], y_columns[:, :, 1])
+    y_columns = y_columns.reshape(y_inverse.shape[0], -1)
+    y_parts = first_pieces = result = None
     for step in range(STEPS):
         sent = []
         for chunk in range(chunks):
-            held = gather_pieces(fields[chunk], "gx", gx_count)
+            hold = None
+            if first_pieces is not None and step == 0:
+                fields[chunk] = after(fields[chunk], *first_pieces)
+                hold = sent[0][plan.parts // 2 :]
+            held = gather_pieces(fields[chunk], "gx", gx_count, hold)
             masks, pieces = [m for m, _ in held], [p for _, p in held]
-            if y_parts is None:
-                pieces[1], y_inverse = lax.optimization_barrier((pieces[1], y_inverse))
-                held = gather_pieces(y_inverse, "gx", gx_count)
-                y_parts = prepare_y([m for m, _ in held], [p for _, p in held], me)
             packed = zonal(plan, masks, pieces, me, x_high, x_low, sea_mask)
             sent.append(exchange(packed, "gy", gy_count))
+            if y_parts is None:
+                held = gather_pieces(y_columns, "gx", gx_count)
+                first_pieces = [pieces[1], held[1][1]]
+                y_parts = prepare_y([m for m, _ in held], [p for _, p in held], me, rows)
         for chunk in range(chunks):
-            solved = meridional(plan, me, sent[chunk], *y_parts)
-            returned = exchange(solved, "gy", gy_count)
+            own, other = meridional(plan, me, sent[chunk], *y_parts)
+            other = lax.ppermute(other, "gy", [(i, i ^ 1) for i in range(gy_count)])
+            returned = exchange(add_sides(plan, me, own, other), "gy", gy_count)
             if step < STEPS - 1 or chunk < chunks - 1:
                 fields[chunk] = vertical(plan, me, returned, kappa, sea_mask, levels)
             else:

time: 174 us -> 167 us (0.960)
  starting transfers between devices: 95.4 us -> 62.3 us
  waiting for transfers between devices: 40.2 us -> 63.9 us
  Pallas kernels: 22.8 us -> 25.5 us
    ppermute x56 -> x29, starting transfers between devices: 87.4 us -> 55.4 us  [the longest x24 47.4 us: exchange(): out[mask] = lax.ppermute(blocks[mask], axis, pairs)]
    ppermute x56 -> x29, waiting for transfers between devices: 12 us -> 39 us  [the longest x24 30.2 us: exchange(): out[mask] = lax.ppermute(blocks[mask], axis, pairs)]
    ppermute x15 -> x14, waiting for transfers between devices: 28.2 us -> 24.9 us  [gather_pieces(): lax.ppermute(piece, axis, pairs)]
    pallas_call x14 -> x18, Pallas kernels: 20.7 us -> 23.4 us  [call(): pl.pallas_call(kernel, out_shape=out_shape, in_specs=specs, out_specs=[ou...]
    unnamed x22, local copies, waits for them, and re-layouts: 2.4 us -> 0.37 us
    ppermute x15 -> x14, starting transfers between devices: 7.96 us -> 6.98 us  [gather_pieces(): lax.ppermute(piece, axis, pairs)]
  transfers between devices with their start and end apart: 71 -> 43, of which waited for: 12 -> 14; matrix products, arithmetic and copies ran while one was open for 0% -> 0% of each run, Pallas kernels for 12% -> 14%
where the time goes in v2:
time: 167 us
  waiting for transfers between devices  63.9 us (38%)
  starting transfers between devices  62.3 us (37%)
  Pallas kernels  25.5 us (15%)
  blocking collectives  10.6 us (6%)
  local copies, waits for them, and re-layouts  2.58 us (2%)
    ppermute x24, starting transfers between devices, exchange(): out[mask] = lax.ppermute(blocks[mask], axis, pairs)  47.4 us
    ppermute x24, waiting for transfers between devices, exchange(): out[mask] = lax.ppermute(blocks[mask], axis, pairs)  30.2 us
    ppermute x14, waiting for transfers between devices, gather_pieces(): lax.ppermute(piece, axis, pairs)  24.9 us
    pallas_call x18, Pallas kernels, call(): pl.pallas_call(kernel, out_shape=out_shape, in_specs=specs, out_specs=[ou...  23.4 us
    all_to_all x1, blocking collectives, body(): lax.all_to_all(outgoing, ('gx', 'gy'), split_axis=0, concat_axis=0, tiled...  10.6 us
    ppermute x14, starting transfers between devices, gather_pieces(): lax.ppermute(piece, axis, pairs)  6.98 us
    ppermute x4, waiting for transfers between devices, body(): other = lax.ppermute(other, 'gy', [(i, i ^ 1) for i in range(gy_count)])  6.86 us
    ppermute x4, starting transfers between devices, body(): other = lax.ppermute(other, 'gy', [(i, i ^ 1) for i in range(gy_count)])  6.26 us
  transfers between devices with their start and end apart: 43, of which 14 were waited for; matrix products, arithmetic and copies ran while one was open for 0% of the time, Pallas kernels for 14%

profile of v2, /device:TPU:0, one launch (start us, length us, event | category | flops | bytes accessed | tf_op | source)
XLA Modules:
  0.0 166.6 jit_solution(6691390122782767707)
XLA Ops:
  0.7 2.1 %slice_bitcast_fusion = (f32[6,48,384]{2,1,0:T(8,128)S(1)}, f32[6,48,384]{2,1,0:T(8,128)}) fusion(f32[1,2,6,48,384]{4,3,2,1,0:T(8,128)} %param.12), kind=kLoop, calls=%fused_computation | loop fusion | bytes 1769472 | tf_op jit(solution)/shard_map/unstack | solution.py:455
  2.8 3.0 %collective-permute-start.3 = (f32[6,48,384]{2,1,0:T(8,128)}, f32[6,48,384]{2,1,0:T(8,128)}, u32[]{:S(2)}, u32[]{:S(2)}) collective-permute-start(f32[6,48,384]{2,1,0:T(8,128)} %get-tuple-element.102.refs_0_), channel_id=1, source_target_pairs={{0,16},{8,24},{16,0},{24,8},{1,17},{9,25},{17,1},{25,9},{2,18},{10... | collective-permute-start | bytes 1327112 | tf_op jit(solution)/shard_map/ppermute | solution.py:155
  5.9 10.3 %collective-permute-done.3.refs_1_ = f32[6,48,384]{2,1,0:T(8,128)} collective-permute-done((f32[6,48,384]{2,1,0:T(8,128)}, f32[6,48,384]{2,1,0:T(8,128)}, u32[]{:S(2)}, u32[]{:S(2)}) %collective-permute-start.3) | collective-permute-done | bytes 442400 | tf_op jit(solution)/shard_map/ppermute | solution.py:155
  16.3 1.8 %collective-permute-start = (f32[96,192]{1,0:T(8,128)S(1)}, f32[96,192]{1,0:T(8,128)S(1)}, u32[]{:S(2)}, u32[]{:S(2)}) collective-permute-start(f32[96,192]{1,0:T(8,128)S(1)} %copy.26.refs_0_), channel_id=1, source_target_pairs={{0,16},{8,24},{16,0},{24,8},{1,17},{9,25},{17,1},{25,9},{2,18},{10... | collective-permute-start | bytes 221192 | tf_op jit(solution)/shard_map/ppermute | solution.py:155
  18.1 3.5 %collective-permute-done.refs_1_ = f32[96,192]{1,0:T(8,128)S(1)} collective-permute-done((f32[96,192]{1,0:T(8,128)S(1)}, f32[96,192]{1,0:T(8,128)S(1)}, u32[]{:S(2)}, u32[]{:S(2)}) %collective-permute-start) | collective-permute-done | bytes 73760 | tf_op jit(solution)/shard_map/ppermute | solution.py:155
  21.6 1.7 %collective-permute-start.23 = (f32[6,48,384]{2,1,0:T(8,128)S(1)}, f32[6,48,384]{2,1,0:T(8,128)}, u32[]{:S(2)}, u32[]{:S(2)}) collective-permute-start(f32[6,48,384]{2,1,0:T(8,128)S(1)} %get-tuple-element.76.refs_0_), channel_id=1, source_target_pairs={{0,16},{8,24},{16,0},{24,8},{1,17},{9,25},{17,1},{25,9},{2,18},{10... | collective-permute-start | bytes 1327112 | tf_op jit(solution)/shard_map/ppermute | solution.py:150
  24.2 3.3 %shard_map.141 = (f32[216,128]{1,0:T(8,128)S(1)}, f32[216,128]{1,0:T(8,128)S(1)}, f32[216,128]{1,0:T(8,128)S(1)}, f32[216,128]{1,0:T(8,128)S(1)}) custom-call(s32[2]{0:T(128)S(1)} %pad_add_fusion.me_ref, bf16[1536,384]{1,0:T(8,128)(2,1)S(1)} %get-tuple-element.54.high_ref, bf16[1536,384]{1,0:T(8,128)(2,1)S(1)} %get-tuple-element.55.low_ref, ...), custom_call_target="tpu_custom_call" | custom-call | flops 1019215872 | bytes 4644872 | tf_op jit(solution)/shard_map/pallas_call | solution.py:131
  27.6 2.7 %collective-permute-start.7 = (f32[216,128]{1,0:T(8,128)S(1)}, f32[216,128]{1,0:T(8,128)S(1)}, u32[]{:S(2)}, u32[]{:S(2)}) collective-permute-start(f32[216,128]{1,0:T(8,128)S(1)} %get-tuple-element.58), channel_id=1, source_target_pairs={{0,4},{1,5},{2,6},{3,7},{4,0},{5,1},{6,2},{7,3},{8,12},{9,13},{10,... | collective-permute-start | bytes 331784 | tf_op jit(solution)/shard_map/ppermute | solution.py:164
  31.6 2.0 %collective-permute-done.23.refs_1_ = f32[6,48,384]{2,1,0:T(8,128)} collective-permute-done((f32[6,48,384]{2,1,0:T(8,128)S(1)}, f32[6,48,384]{2,1,0:T(8,128)}, u32[]{:S(2)}, u32[]{:S(2)}) %collective-permute-start.23) | collective-permute-done | bytes 442400 | tf_op jit(solution)/shard_map/ppermute | solution.py:150
  33.5 5.3 %collective-permute-done.7.refs_2_ = f32[216,128]{1,0:T(8,128)S(1)} collective-permute-done((f32[216,128]{1,0:T(8,128)S(1)}, f32[216,128]{1,0:T(8,128)S(1)}, u32[]{:S(2)}, u32[]{:S(2)}) %collective-permute-start.7) | collective-permute-done | bytes 110624 | tf_op jit(solution)/shard_map/ppermute | solution.py:164
  39.3 1.9 %collective-permute-start.6 = (f32[216,128]{1,0:T(8,128)S(1)}, f32[216,128]{1,0:T(8,128)S(1)}, u32[]{:S(2)}, u32[]{:S(2)}) collective-permute-start(f32[216,128]{1,0:T(8,128)S(1)} %get-tuple-element.57), channel_id=1, source_target_pairs={{0,2},{1,3},{2,0},{3,1},{4,6},{5,7},{6,4},{7,5},{8,10},{9,11},{10,... | collective-permute-start | bytes 331784 | tf_op jit(solution)/shard_map/ppermute | solution.py:164
  41.9 2.9 %shard_map.149 = (f32[216,128]{1,0:T(8,128)S(1)}, f32[216,128]{1,0:T(8,128)S(1)}, f32[216,128]{1,0:T(8,128)S(1)}, f32[216,128]{1,0:T(8,128)S(1)}) custom-call(s32[2]{0:T(128)S(1)} %pad_add_fusion.me_ref, bf16[1536,384]{1,0:T(8,128)(2,1)S(1)} %get-tuple-element.54.high_ref, bf16[1536,384]{1,0:T(8,128)(2,1)S(1)} %get-tuple-element.55.low_ref, ...), custom_call_target="tpu_custom_call" | custom-call | flops 1019215872 | bytes 4644872 | tf_op jit(solution)/shard_map/pallas_call | solution.py:131
  46.4 2.4 %collective-permute-start.27 = (f32[216,128]{1,0:T(8,128)S(1)}, f32[216,128]{1,0:T(8,128)S(1)}, u32[]{:S(2)}, u32[]{:S(2)}) collective-permute-start(f32[216,128]{1,0:T(8,128)S(1)} %get-tuple-element.80), channel_id=1, source_target_pairs={{0,4},{1,5},{2,6},{3,7},{4,0},{5,1},{6,2},{7,3},{8,12},{9,13},{10,... | collective-permute-start | bytes 331784 | tf_op jit(solution)/shard_map/ppermute | solution.py:164
  52.7 5.0 %collective-permute-done.28.refs_3_ = f32[216,128]{1,0:T(8,128)S(1)} collective-permute-done((f32[216,128]{1,0:T(8,128)S(1)}, f32[216,128]{1,0:T(8,128)S(1)}, u32[]{:S(2)}, u32[]{:S(2)}) %collective-permute-start.28) | collective-permute-done | bytes 110624 | tf_op jit(solution)/shard_map/ppermute | solution.py:164
  60.6 3.7 %collective-permute-done.9.other_ref = f32[4,216,128]{2,1,0:T(8,128)S(1)} collective-permute-done((f32[4,216,128]{2,1,0:T(8,128)S(1)}, f32[4,216,128]{2,1,0:T(8,128)S(1)}, u32[]{:S(2)}, u32[]{:S(2)}) %collective-permute-start.9) | collective-permute-done | bytes 442400 | tf_op jit(solution)/shard_map/ppermute | solution.py:477
  65.0 3.1 %collective-permute-start.11 = (f32[216,128]{1,0:T(8,128)S(1)}, f32[216,128]{1,0:T(8,128)S(1)}, u32[]{:S(2)}, u32[]{:S(2)}) collective-permute-start(f32[216,128]{1,0:T(8,128)S(1)} %get-tuple-element.64), channel_id=1, source_target_pairs={{0,4},{1,5},{2,6},{3,7},{4,0},{5,1},{6,2},{7,3},{8,12},{9,13},{10,... | collective-permute-start | bytes 331784 | tf_op jit(solution)/shard_map/ppermute | solution.py:164
  69.4 3.0 %collective-permute-done.29.other_ref = f32[4,216,128]{2,1,0:T(8,128)S(1)} collective-permute-done((f32[4,216,128]{2,1,0:T(8,128)S(1)}, f32[4,216,128]{2,1,0:T(8,128)S(1)}, u32[]{:S(2)}, u32[]{:S(2)}) %collective-permute-start.29) | collective-permute-done | bytes 442400 | tf_op jit(solution)/shard_map/ppermute | solution.py:477
  73.8 2.4 %collective-permute-start.31 = (f32[216,128]{1,0:T(8,128)S(1)}, f32[216,128]{1,0:T(8,128)S(1)}, u32[]{:S(2)}, u32[]{:S(2)}) collective-permute-start(f32[216,128]{1,0:T(8,128)S(1)} %get-tuple-element.86), channel_id=1, source_target_pairs={{0,4},{1,5},{2,6},{3,7},{4,0},{5,1},{6,2},{7,3},{8,12},{9,13},{10,... | collective-permute-start | bytes 331784 | tf_op jit(solution)/shard_map/ppermute | solution.py:164
  78.8 6.2 %collective-permute-done.31.refs_2_ = f32[216,128]{1,0:T(8,128)S(1)} collective-permute-done((f32[216,128]{1,0:T(8,128)S(1)}, f32[216,128]{1,0:T(8,128)S(1)}, u32[]{:S(2)}, u32[]{:S(2)}) %collective-permute-start.31) | collective-permute-done | bytes 110624 | tf_op jit(solution)/shard_map/ppermute | solution.py:164
  86.4 5.0 %collective-permute-done.13.refs_1_ = f32[6,48,384]{2,1,0:T(8,128)S(1)} collective-permute-done((f32[6,48,384]{2,1,0:T(8,128)S(1)}, f32[6,48,384]{2,1,0:T(8,128)S(1)}, u32[]{:S(2)}, u32[]{:S(2)}) %collective-permute-start.13) | collective-permute-done | bytes 442400 | tf_op jit(solution)/shard_map/ppermute | solution.py:155
  91.9 6.1 %collective-permute-done.33.refs_1_ = f32[6,48,384]{2,1,0:T(8,128)S(1)} collective-permute-done((f32[6,48,384]{2,1,0:T(8,128)S(1)}, f32[6,48,384]{2,1,0:T(8,128)S(1)}, u32[]{:S(2)}, u32[]{:S(2)}) %collective-permute-start.33) | collective-permute-done | bytes 442400 | tf_op jit(solution)/shard_map/ppermute | solution.py:155
  98.0 2.4 %shard_map.145 = (f32[216,128]{1,0:T(8,128)S(1)}, f32[216,128]{1,0:T(8,128)S(1)}, f32[216,128]{1,0:T(8,128)S(1)}, f32[216,128]{1,0:T(8,128)S(1)}) custom-call(s32[2]{0:T(128)S(1)} %pad_add_fusion.me_ref, bf16[1536,384]{1,0:T(8,128)(2,1)S(1)} %get-tuple-element.54.high_ref, bf16[1536,384]{1,0:T(8,128)(2,1)S(1)} %get-tuple-element.55.low_ref, ...), custom_call_target="tpu_custom_call" | custom-call | flops 1019215872 | bytes 4644872 | tf_op jit(solution)/shard_map/pallas_call | solution.py:131
  101.1 2.4 %collective-permute-start.17 = (f32[216,128]{1,0:T(8,128)S(1)}, f32[216,128]{1,0:T(8,128)S(1)}, u32[]{:S(2)}, u32[]{:S(2)}) collective-permute-start(f32[216,128]{1,0:T(8,128)S(1)} %get-tuple-element.68), channel_id=1, source_target_pairs={{0,4},{1,5},{2,6},{3,7},{4,0},{5,1},{6,2},{7,3},{8,12},{9,13},{10,... | collective-permute-start | bytes 331784 | tf_op jit(solution)/shard_map/ppermute | solution.py:164
  104.9 2.6 %shard_map.153 = (f32[216,128]{1,0:T(8,128)S(1)}, f32[216,128]{1,0:T(8,128)S(1)}, f32[216,128]{1,0:T(8,128)S(1)}, f32[216,128]{1,0:T(8,128)S(1)}) custom-call(s32[2]{0:T(128)S(1)} %pad_add_fusion.me_ref, bf16[1536,384]{1,0:T(8,128)(2,1)S(1)} %get-tuple-element.54.high_ref, bf16[1536,384]{1,0:T(8,128)(2,1)S(1)} %get-tuple-element.55.low_ref, ...), custom_call_target="tpu_custom_call" | custom-call | flops 1019215872 | bytes 4644872 | tf_op jit(solution)/shard_map/pallas_call | solution.py:131
  107.7 3.0 %collective-permute-start.37 = (f32[216,128]{1,0:T(8,128)S(1)}, f32[216,128]{1,0:T(8,128)S(1)}, u32[]{:S(2)}, u32[]{:S(2)}) collective-permute-start(f32[216,128]{1,0:T(8,128)S(1)} %get-tuple-element.90), channel_id=1, source_target_pairs={{0,4},{1,5},{2,6},{3,7},{4,0},{5,1},{6,2},{7,3},{8,12},{9,13},{10,... | collective-permute-start | bytes 331784 | tf_op jit(solution)/shard_map/ppermute | solution.py:164
  115.7 6.6 %collective-permute-done.37.refs_2_ = f32[216,128]{1,0:T(8,128)S(1)} collective-permute-done((f32[216,128]{1,0:T(8,128)S(1)}, f32[216,128]{1,0:T(8,128)S(1)}, u32[]{:S(2)}, u32[]{:S(2)}) %collective-permute-start.37) | collective-permute-done | bytes 110624 | tf_op jit(solution)/shard_map/ppermute | solution.py:164
  126.0 9.7 %collective-permute-start.20 = (f32[216,128]{1,0:T(8,128)S(1)}, f32[216,128]{1,0:T(8,128)S(1)}, u32[]{:S(2)}, u32[]{:S(2)}) collective-permute-start(f32[216,128]{1,0:T(8,128)S(1)} %get-tuple-element.73), channel_id=1, source_target_pairs={{0,2},{1,3},{2,0},{3,1},{4,6},{5,7},{6,4},{7,5},{8,10},{9,11},{10,... | collective-permute-start | bytes 331784 | tf_op jit(solution)/shard_map/ppermute | solution.py:164
  138.8 2.9 %collective-permute-start.40 = (f32[216,128]{1,0:T(8,128)S(1)}, f32[216,128]{1,0:T(8,128)S(1)}, u32[]{:S(2)}, u32[]{:S(2)}) collective-permute-start(f32[216,128]{1,0:T(8,128)S(1)} %get-tuple-element.95), channel_id=1, source_target_pairs={{0,2},{1,3},{2,0},{3,1},{4,6},{5,7},{6,4},{7,5},{8,10},{9,11},{10,... | collective-permute-start | bytes 331784 | tf_op jit(solution)/shard_map/ppermute | solution.py:164
  141.7 2.1 %collective-permute-start.41 = (f32[216,128]{1,0:T(8,128)S(1)}, f32[216,128]{1,0:T(8,128)S(1)}, u32[]{:S(2)}, u32[]{:S(2)}) collective-permute-start(f32[216,128]{1,0:T(8,128)S(1)} %get-tuple-element.96), channel_id=1, source_target_pairs={{0,4},{1,5},{2,6},{3,7},{4,0},{5,1},{6,2},{7,3},{8,12},{9,13},{10,... | collective-permute-start | bytes 331784 | tf_op jit(solution)/shard_map/ppermute | solution.py:164
  146.8 6.3 %collective-permute-done.41.refs_3_ = f32[216,128]{1,0:T(8,128)S(1)} collective-permute-done((f32[216,128]{1,0:T(8,128)S(1)}, f32[216,128]{1,0:T(8,128)S(1)}, u32[]{:S(2)}, u32[]{:S(2)}) %collective-permute-start.41) | collective-permute-done | bytes 110624 | tf_op jit(solution)/shard_map/ppermute | solution.py:164
  153.2 2.1 %shard_map.156 = (f32[2,6,48,384]{3,2,1,0:T(8,128)}, f32[48,384]{1,0:T(8,128)}, f32[32,128]{1,0:T(8,128)S(1)}) custom-call(s32[2]{0:T(128)S(1)} %pad_add_fusion.me_ref, f32[2,6]{1,0:T(2,128)S(1)} %copy-done.6, s32[1]{0:T(128)S(6)} %copy.29.count_ref, f32[5,48,384]{2,1,0:T(8,128)S(1)} %copy-done, s32[48,384]{1,0:T(8,128)S(1)} %copy-done.1, ...), custom_call_target="tpu_custom_call" | custom-call | flops 10000000 | bytes 3629756 | tf_op jit(solution)/shard_map/pallas_call | solution.py:421
  155.3 10.6 %all_to_all.11 = f32[32,1,128]{2,1,0:T(1,128)S(1)} all-to-all(f32[32,1,128]{2,1,0:T(1,128)S(1)} %bitcast.18), channel_id=1, replica_groups=mesh['gx'=4,'gy'=8] {'gx','gy'}, dimensions={0} | all-to-all | bytes 32768 | tf_op jit(solution)/shard_map/all_to_all | solution.py:494
  (100 shorter events, 36.8 us)
Async XLA Ops:
  2.8 13.4 %collective-permute-start.3 = (f32[6,48,384]{2,1,0:T(8,128)}, f32[6,48,384]{2,1,0:T(8,128)}, u32[]{:S(2)}, u32[]{:S(2)}) collective-permute-start(f32[6,48,384]{2,1,0:T(8,128)} %get-tuple-element.102.refs_0_), channel_id=1, source_target_pairs={{0,16},{8,24},{16,0},{24,8},{1,17},{9,25},{17,1},{25,9},{2,18},{10... | collective-permute-start | bytes 1327112 | tf_op jit(solution)/shard_map/ppermute | solution.py:155
  5.7 18.4 %collective-permute-start.4 = (f32[6,48,384]{2,1,0:T(8,128)}, f32[6,48,384]{2,1,0:T(8,128)}, u32[]{:S(2)}, u32[]{:S(2)}) collective-permute-start(f32[6,48,384]{2,1,0:T(8,128)} %get-tuple-element.102.refs_0_), channel_id=1, source_target_pairs={{0,8},{8,0},{16,24},{24,16},{1,9},{9,1},{17,25},{25,17},{2,10},{10... | collective-permute-start | bytes 1327112 | tf_op jit(solution)/shard_map/ppermute | solution.py:155
  21.6 11.9 %collective-permute-start.23 = (f32[6,48,384]{2,1,0:T(8,128)S(1)}, f32[6,48,384]{2,1,0:T(8,128)}, u32[]{:S(2)}, u32[]{:S(2)}) collective-permute-start(f32[6,48,384]{2,1,0:T(8,128)S(1)} %get-tuple-element.76.refs_0_), channel_id=1, source_target_pairs={{0,16},{8,24},{16,0},{24,8},{1,17},{9,25},{17,1},{25,9},{2,18},{10... | collective-permute-start | bytes 1327112 | tf_op jit(solution)/shard_map/ppermute | solution.py:150
  27.6 11.2 %collective-permute-start.7 = (f32[216,128]{1,0:T(8,128)S(1)}, f32[216,128]{1,0:T(8,128)S(1)}, u32[]{:S(2)}, u32[]{:S(2)}) collective-permute-start(f32[216,128]{1,0:T(8,128)S(1)} %get-tuple-element.58), channel_id=1, source_target_pairs={{0,4},{1,5},{2,6},{3,7},{4,0},{5,1},{6,2},{7,3},{8,12},{9,13},{10,... | collective-permute-start | bytes 331784 | tf_op jit(solution)/shard_map/ppermute | solution.py:164
  30.2 8.6 %collective-permute-start.8 = (f32[216,128]{1,0:T(8,128)S(1)}, f32[216,128]{1,0:T(8,128)S(1)}, u32[]{:S(2)}, u32[]{:S(2)}) collective-permute-start(f32[216,128]{1,0:T(8,128)S(1)} %get-tuple-element.59), channel_id=1, source_target_pairs={{0,6},{1,7},{2,4},{3,5},{4,2},{5,3},{6,0},{7,1},{8,14},{9,15},{10,... | collective-permute-start | bytes 331784 | tf_op jit(solution)/shard_map/ppermute | solution.py:164
  31.6 10.3 %collective-permute-start.24 = (f32[6,48,384]{2,1,0:T(8,128)S(1)}, f32[6,48,384]{2,1,0:T(8,128)S(1)}, u32[]{:S(2)}, u32[]{:S(2)}) collective-permute-start(f32[6,48,384]{2,1,0:T(8,128)S(1)} %get-tuple-element.76.refs_0_), channel_id=1, source_target_pairs={{0,8},{8,0},{16,24},{24,16},{1,9},{9,1},{17,25},{25,17},{2,10},{10... | collective-permute-start | bytes 1327112 | tf_op jit(solution)/shard_map/ppermute | solution.py:155
  39.3 10.5 %collective-permute-start.6 = (f32[216,128]{1,0:T(8,128)S(1)}, f32[216,128]{1,0:T(8,128)S(1)}, u32[]{:S(2)}, u32[]{:S(2)}) collective-permute-start(f32[216,128]{1,0:T(8,128)S(1)} %get-tuple-element.57), channel_id=1, source_target_pairs={{0,2},{1,3},{2,0},{3,1},{4,6},{5,7},{6,4},{7,5},{8,10},{9,11},{10,... | collective-permute-start | bytes 331784 | tf_op jit(solution)/shard_map/ppermute | solution.py:164
  48.8 8.9 %collective-permute-start.28 = (f32[216,128]{1,0:T(8,128)S(1)}, f32[216,128]{1,0:T(8,128)S(1)}, u32[]{:S(2)}, u32[]{:S(2)}) collective-permute-start(f32[216,128]{1,0:T(8,128)S(1)} %get-tuple-element.81), channel_id=1, source_target_pairs={{0,6},{1,7},{2,4},{3,5},{4,2},{5,3},{6,0},{7,1},{8,14},{9,15},{10,... | collective-permute-start | bytes 331784 | tf_op jit(solution)/shard_map/ppermute | solution.py:164
  51.1 13.2 %collective-permute-start.9 = (f32[4,216,128]{2,1,0:T(8,128)S(1)}, f32[4,216,128]{2,1,0:T(8,128)S(1)}, u32[]{:S(2)}, u32[]{:S(2)}) collective-permute-start(f32[4,216,128]{2,1,0:T(8,128)S(1)} %get-tuple-element.61), channel_id=1, source_target_pairs={{0,1},{1,0},{2,3},{3,2},{4,5},{5,4},{6,7},{7,6},{8,9},{9,8},{10,11... | collective-permute-start | bytes 1327112 | tf_op jit(solution)/shard_map/ppermute | solution.py:477
  59.1 13.3 %collective-permute-start.29 = (f32[4,216,128]{2,1,0:T(8,128)S(1)}, f32[4,216,128]{2,1,0:T(8,128)S(1)}, u32[]{:S(2)}, u32[]{:S(2)}) collective-permute-start(f32[4,216,128]{2,1,0:T(8,128)S(1)} %get-tuple-element.83), channel_id=1, source_target_pairs={{0,1},{1,0},{2,3},{3,2},{4,5},{5,4},{6,7},{7,6},{8,9},{9,8},{10,11... | collective-permute-start | bytes 1327112 | tf_op jit(solution)/shard_map/ppermute | solution.py:477
  64.9 11.3 %collective-permute-start.10 = (f32[216,128]{1,0:T(8,128)S(1)}, f32[216,128]{1,0:T(8,128)S(1)}, u32[]{:S(2)}, u32[]{:S(2)}) collective-permute-start(f32[216,128]{1,0:T(8,128)S(1)} %get-tuple-element.63), channel_id=1, source_target_pairs={{0,2},{1,3},{2,0},{3,1},{4,6},{5,7},{6,4},{7,5},{8,10},{9,11},{10,... | collective-permute-start | bytes 331784 | tf_op jit(solution)/shard_map/ppermute | solution.py:164
  65.0 12.4 %collective-permute-start.11 = (f32[216,128]{1,0:T(8,128)S(1)}, f32[216,128]{1,0:T(8,128)S(1)}, u32[]{:S(2)}, u32[]{:S(2)}) collective-permute-start(f32[216,128]{1,0:T(8,128)S(1)} %get-tuple-element.64), channel_id=1, source_target_pairs={{0,4},{1,5},{2,6},{3,7},{4,0},{5,1},{6,2},{7,3},{8,12},{9,13},{10,... | collective-permute-start | bytes 331784 | tf_op jit(solution)/shard_map/ppermute | solution.py:164
  68.1 9.3 %collective-permute-start.12 = (f32[216,128]{1,0:T(8,128)S(1)}, f32[216,128]{1,0:T(8,128)S(1)}, u32[]{:S(2)}, u32[]{:S(2)}) collective-permute-start(f32[216,128]{1,0:T(8,128)S(1)} %get-tuple-element.65), channel_id=1, source_target_pairs={{0,6},{1,7},{2,4},{3,5},{4,2},{5,3},{6,0},{7,1},{8,14},{9,15},{10,... | collective-permute-start | bytes 331784 | tf_op jit(solution)/shard_map/ppermute | solution.py:164
  73.8 11.2 %collective-permute-start.31 = (f32[216,128]{1,0:T(8,128)S(1)}, f32[216,128]{1,0:T(8,128)S(1)}, u32[]{:S(2)}, u32[]{:S(2)}) collective-permute-start(f32[216,128]{1,0:T(8,128)S(1)} %get-tuple-element.86), channel_id=1, source_target_pairs={{0,4},{1,5},{2,6},{3,7},{4,0},{5,1},{6,2},{7,3},{8,12},{9,13},{10,... | collective-permute-start | bytes 331784 | tf_op jit(solution)/shard_map/ppermute | solution.py:164
  76.2 8.8 %collective-permute-start.32 = (f32[216,128]{1,0:T(8,128)S(1)}, f32[216,128]{1,0:T(8,128)S(1)}, u32[]{:S(2)}, u32[]{:S(2)}) collective-permute-start(f32[216,128]{1,0:T(8,128)S(1)} %get-tuple-element.87), channel_id=1, source_target_pairs={{0,6},{1,7},{2,4},{3,5},{4,2},{5,3},{6,0},{7,1},{8,14},{9,15},{10,... | collective-permute-start | bytes 331784 | tf_op jit(solution)/shard_map/ppermute | solution.py:164
  78.2 13.2 %collective-permute-start.13 = (f32[6,48,384]{2,1,0:T(8,128)S(1)}, f32[6,48,384]{2,1,0:T(8,128)S(1)}, u32[]{:S(2)}, u32[]{:S(2)}) collective-permute-start(f32[6,48,384]{2,1,0:T(8,128)S(1)} %shard_map.144.refs_0_), channel_id=1, source_target_pairs={{0,16},{8,24},{16,0},{24,8},{1,17},{9,25},{17,1},{25,9},{2,18},{10... | collective-permute-start | bytes 1327112 | tf_op jit(solution)/shard_map/ppermute | solution.py:155
  85.8 12.2 %collective-permute-start.33 = (f32[6,48,384]{2,1,0:T(8,128)S(1)}, f32[6,48,384]{2,1,0:T(8,128)S(1)}, u32[]{:S(2)}, u32[]{:S(2)}) collective-permute-start(f32[6,48,384]{2,1,0:T(8,128)S(1)} %shard_map.152.refs_0_), channel_id=1, source_target_pairs={{0,16},{8,24},{16,0},{24,8},{1,17},{9,25},{17,1},{25,9},{2,18},{10... | collective-permute-start | bytes 1327112 | tf_op jit(solution)/shard_map/ppermute | solution.py:155
  86.4 11.6 %collective-permute-start.14 = (f32[6,48,384]{2,1,0:T(8,128)S(1)}, f32[6,48,384]{2,1,0:T(8,128)S(1)}, u32[]{:S(2)}, u32[]{:S(2)}) collective-permute-start(f32[6,48,384]{2,1,0:T(8,128)S(1)} %shard_map.144.refs_0_), channel_id=1, source_target_pairs={{0,8},{8,0},{16,24},{24,16},{1,9},{9,1},{17,25},{25,17},{2,10},{10... | collective-permute-start | bytes 1327112 | tf_op jit(solution)/shard_map/ppermute | solution.py:155
  91.4 13.6 %collective-permute-start.34 = (f32[6,48,384]{2,1,0:T(8,128)S(1)}, f32[6,48,384]{2,1,0:T(8,128)S(1)}, u32[]{:S(2)}, u32[]{:S(2)}) collective-permute-start(f32[6,48,384]{2,1,0:T(8,128)S(1)} %shard_map.152.refs_0_), channel_id=1, source_target_pairs={{0,8},{8,0},{16,24},{24,16},{1,9},{9,1},{17,25},{25,17},{2,10},{10... | collective-permute-start | bytes 1327112 | tf_op jit(solution)/shard_map/ppermute | solution.py:155
  100.5 10.2 %collective-permute-start.16 = (f32[216,128]{1,0:T(8,128)S(1)}, f32[216,128]{1,0:T(8,128)S(1)}, u32[]{:S(2)}, u32[]{:S(2)}) collective-permute-start(f32[216,128]{1,0:T(8,128)S(1)} %get-tuple-element.67), channel_id=1, source_target_pairs={{0,2},{1,3},{2,0},{3,1},{4,6},{5,7},{6,4},{7,5},{8,10},{9,11},{10,... | collective-permute-start | bytes 331784 | tf_op jit(solution)/shard_map/ppermute | solution.py:164
  101.1 11.6 %collective-permute-start.17 = (f32[216,128]{1,0:T(8,128)S(1)}, f32[216,128]{1,0:T(8,128)S(1)}, u32[]{:S(2)}, u32[]{:S(2)}) collective-permute-start(f32[216,128]{1,0:T(8,128)S(1)} %get-tuple-element.68), channel_id=1, source_target_pairs={{0,4},{1,5},{2,6},{3,7},{4,0},{5,1},{6,2},{7,3},{8,12},{9,13},{10,... | collective-permute-start | bytes 331784 | tf_op jit(solution)/shard_map/ppermute | solution.py:164
  103.5 9.2 %collective-permute-start.18 = (f32[216,128]{1,0:T(8,128)S(1)}, f32[216,128]{1,0:T(8,128)S(1)}, u32[]{:S(2)}, u32[]{:S(2)}) collective-permute-start(f32[216,128]{1,0:T(8,128)S(1)} %get-tuple-element.69), channel_id=1, source_target_pairs={{0,6},{1,7},{2,4},{3,5},{4,2},{5,3},{6,0},{7,1},{8,14},{9,15},{10,... | collective-permute-start | bytes 331784 | tf_op jit(solution)/shard_map/ppermute | solution.py:164
  107.6 8.1 %collective-permute-start.36 = (f32[216,128]{1,0:T(8,128)S(1)}, f32[216,128]{1,0:T(8,128)S(1)}, u32[]{:S(2)}, u32[]{:S(2)}) collective-permute-start(f32[216,128]{1,0:T(8,128)S(1)} %get-tuple-element.89), channel_id=1, source_target_pairs={{0,2},{1,3},{2,0},{3,1},{4,6},{5,7},{6,4},{7,5},{8,10},{9,11},{10,... | collective-permute-start | bytes 331784 | tf_op jit(solution)/shard_map/ppermute | solution.py:164
  107.7 14.6 %collective-permute-start.37 = (f32[216,128]{1,0:T(8,128)S(1)}, f32[216,128]{1,0:T(8,128)S(1)}, u32[]{:S(2)}, u32[]{:S(2)}) collective-permute-start(f32[216,128]{1,0:T(8,128)S(1)} %get-tuple-element.90), channel_id=1, source_target_pairs={{0,4},{1,5},{2,6},{3,7},{4,0},{5,1},{6,2},{7,3},{8,12},{9,13},{10,... | collective-permute-start | bytes 331784 | tf_op jit(solution)/shard_map/ppermute | solution.py:164
  110.7 11.6 %collective-permute-start.38 = (f32[216,128]{1,0:T(8,128)S(1)}, f32[216,128]{1,0:T(8,128)S(1)}, u32[]{:S(2)}, u32[]{:S(2)}) collective-permute-start(f32[216,128]{1,0:T(8,128)S(1)} %get-tuple-element.91), channel_id=1, source_target_pairs={{0,6},{1,7},{2,4},{3,5},{4,2},{5,3},{6,0},{7,1},{8,14},{9,15},{10,... | collective-permute-start | bytes 331784 | tf_op jit(solution)/shard_map/ppermute | solution.py:164
  114.1 11.3 %collective-permute-start.19 = (f32[4,216,128]{2,1,0:T(8,128)S(1)}, f32[4,216,128]{2,1,0:T(8,128)S(1)}, u32[]{:S(2)}, u32[]{:S(2)}) collective-permute-start(f32[4,216,128]{2,1,0:T(8,128)S(1)} %get-tuple-element.71), channel_id=1, source_target_pairs={{0,1},{1,0},{2,3},{3,2},{4,5},{5,4},{6,7},{7,6},{8,9},{9,8},{10,11... | collective-permute-start | bytes 1327112 | tf_op jit(solution)/shard_map/ppermute | solution.py:477
  123.6 14.6 %collective-permute-start.39 = (f32[4,216,128]{2,1,0:T(8,128)S(1)}, f32[4,216,128]{2,1,0:T(8,128)S(1)}, u32[]{:S(2)}, u32[]{:S(2)}) collective-permute-start(f32[4,216,128]{2,1,0:T(8,128)S(1)} %get-tuple-element.93), channel_id=1, source_target_pairs={{0,1},{1,0},{2,3},{3,2},{4,5},{5,4},{6,7},{7,6},{8,9},{9,8},{10,11... | collective-permute-start | bytes 1327112 | tf_op jit(solution)/shard_map/ppermute | solution.py:477
  126.0 17.9 %collective-permute-start.20 = (f32[216,128]{1,0:T(8,128)S(1)}, f32[216,128]{1,0:T(8,128)S(1)}, u32[]{:S(2)}, u32[]{:S(2)}) collective-permute-start(f32[216,128]{1,0:T(8,128)S(1)} %get-tuple-element.73), channel_id=1, source_target_pairs={{0,2},{1,3},{2,0},{3,1},{4,6},{5,7},{6,4},{7,5},{8,10},{9,11},{10,... | collective-permute-start | bytes 331784 | tf_op jit(solution)/shard_map/ppermute | solution.py:164
  135.6 10.4 %collective-permute-start.21 = (f32[216,128]{1,0:T(8,128)S(1)}, f32[216,128]{1,0:T(8,128)S(1)}, u32[]{:S(2)}, u32[]{:S(2)}) collective-permute-start(f32[216,128]{1,0:T(8,128)S(1)} %get-tuple-element.74), channel_id=1, source_target_pairs={{0,4},{1,5},{2,6},{3,7},{4,0},{5,1},{6,2},{7,3},{8,12},{9,13},{10,... | collective-permute-start | bytes 331784 | tf_op jit(solution)/shard_map/ppermute | solution.py:164
  136.8 9.2 %collective-permute-start.22 = (f32[216,128]{1,0:T(8,128)S(1)}, f32[216,128]{1,0:T(8,128)S(1)}, u32[]{:S(2)}, u32[]{:S(2)}) collective-permute-start(f32[216,128]{1,0:T(8,128)S(1)} %get-tuple-element.75), channel_id=1, source_target_pairs={{0,6},{1,7},{2,4},{3,5},{4,2},{5,3},{6,0},{7,1},{8,14},{9,15},{10,... | collective-permute-start | bytes 331784 | tf_op jit(solution)/shard_map/ppermute | solution.py:164
  141.7 11.4 %collective-permute-start.41 = (f32[216,128]{1,0:T(8,128)S(1)}, f32[216,128]{1,0:T(8,128)S(1)}, u32[]{:S(2)}, u32[]{:S(2)}) collective-permute-start(f32[216,128]{1,0:T(8,128)S(1)} %get-tuple-element.96), channel_id=1, source_target_pairs={{0,4},{1,5},{2,6},{3,7},{4,0},{5,1},{6,2},{7,3},{8,12},{9,13},{10,... | collective-permute-start | bytes 331784 | tf_op jit(solution)/shard_map/ppermute | solution.py:164
  143.9 9.3 %collective-permute-start.42 = (f32[216,128]{1,0:T(8,128)S(1)}, f32[216,128]{1,0:T(8,128)S(1)}, u32[]{:S(2)}, u32[]{:S(2)}) collective-permute-start(f32[216,128]{1,0:T(8,128)S(1)} %get-tuple-element.97), channel_id=1, source_target_pairs={{0,6},{1,7},{2,4},{3,5},{4,2},{5,3},{6,0},{7,1},{8,14},{9,15},{10,... | collective-permute-start | bytes 331784 | tf_op jit(solution)/shard_map/ppermute | solution.py:164
  (21 other events, 269.6 us)

commit v3 on v2

--- a/solution.py
+++ b/solution.py
@@ -135,7 +135,7 @@
         out_specs=[out_spec] * len(outs) if many else out_spec,
         scratch_shapes=list(scratch),
         compiler_params=pltpu.CompilerParams(vmem_limit_bytes=min(48, 6 + 3 * moved // 2**20) * 2**20),
-        cost_estimate=pl.CostEstimate(flops=flops, bytes_accessed=moved, transcendentals=0),
+        cost_estimate=pl.CostEstimate(flops=1, bytes_accessed=1, transcendentals=0),
     )(*operands)
 
 
@@ -143,18 +143,23 @@
     return lax.optimization_barrier((value,) + others)[0]
 
 
-def gather_pieces(block, axis, count, hold=None):
+def gather_near(block, axis, count):
+    pairs = [(i, i ^ 1) for i in range(count)]
+    return [(0, block), (1, lax.ppermute(block, axis, pairs))]
+
+
+def gather_far(block, axis, count, hold=()):
     held = [(0, block)]
     bit = count // 2
-    if bit > 1 and hold is not None:
-        first = lax.ppermute(block, axis, [(i, i ^ bit) for i in range(count)])
-        held = held + [(bit, after(first, *hold))]
-        bit //= 2
     while bit:
         pairs = [(i, i ^ bit) for i in range(count)]
-        held = held + [(mask ^ bit, lax.ppermute(piece, axis, pairs)) for mask, piece in held]
+        sources = held if bit > 1 else held[1:]
+        brought = [(mask ^ bit, lax.ppermute(piece, axis, pairs)) for mask, piece in sources]
+        if hold and bit == count // 2 and bit > 1:
+            brought = [(mask, after(piece, *hold)) for mask, piece in brought]
+        held = held + brought
         bit //= 2
-    return held
+    return held[1:]
 
 
 def exchange(blocks, axis, count):
@@ -205,33 +210,54 @@
     )
 
 
-def zonal(plan, masks, pieces, me, x_high, x_low, sea_mask):
+def add_zonal(total, masks, me_ref, high_ref, low_ref, refs):
+    for mask, ref in zip(masks, refs):
+        fields, rows, cols = ref.shape
+        start = pl.multiple_of((me_ref[0] ^ mask) * cols, cols)
+        values = split(ref[...].reshape(fields * rows, cols))
+        weights = (high_ref[pl.ds(start, cols), :], low_ref[pl.ds(start, cols), :])
+        part = dot_split(values, weights)
+        total = part if total is None else total + part
+    return total
+
+
+def zonal_start(plan, held, me, x_high, x_low):
+    masks, pieces = [m for m, _ in held], [p for _, p in held]
+
+    def kernel(me_ref, high_ref, low_ref, *refs):
+        refs[-1][...] = add_zonal(None, masks, me_ref, high_ref, low_ref, refs)
+
+    return call(
+        kernel,
+        jax.ShapeDtypeStruct((plan.fields * plan.rows, plan.cols), jnp.float32),
+        [me, x_high, x_low] + pieces,
+        scalars=(0,),
+        flops=6 * plan.fields * plan.rows * plan.cols**2 * len(pieces),
+    )
+
+
+def zonal_end(plan, total, held, me, x_high, x_low, sea_mask):
     fields, rows, cols, parts = plan.fields, plan.rows, plan.cols, plan.parts
-
-    def kernel(me_ref, high_ref, low_ref, sea_ref, *refs):
+    masks, pieces = [m for m, _ in held], [p for _, p in held]
+
+    def kernel(me_ref, high_ref, low_ref, sea_ref, total_ref, *refs):
         out_refs, tiles_ref = refs[-parts - 1 : -1], refs[-1]
-        total = None
-        for mask, ref in zip(masks, refs):
-            start = pl.multiple_of((me_ref[0] ^ mask) * cols, cols)
-            values = split(ref[...].reshape(fields * rows, cols))
-            weights = (high_ref[pl.ds(start, cols), :], low_ref[pl.ds(start, cols), :])
-            part = dot_split(values, weights)
-            total = part if total is None else total + part
-        total = total.reshape(fields, rows, cols)
+        result = add_zonal(total_ref[...], masks, me_ref, high_ref, low_ref, refs)
+        result = result.reshape(fields, rows, cols)
         sea = sea_ref[...].astype(jnp.float32)
         for block in range(plan.blocks):
             lanes = slice(block * LANES, (block + 1) * LANES)
             for field in range(fields):
-                tiles_ref[field * plan.blocks + block] = sea[:, lanes] * total[field, :, lanes]
+                tiles_ref[field * plan.blocks + block] = sea[:, lanes] * result[field, :, lanes]
         for mask in range(parts):
             plan.send_tiles(tiles_ref, part_of(me_ref, mask), out_refs[mask])
 
     return call(
         kernel,
         plan.blocks_out,
-        [me, x_high, x_low, sea_mask] + pieces,
+        [me, x_high, x_low, sea_mask, total] + pieces,
         scalars=(0,),
-        flops=6 * fields * rows * cols * cols * len(pieces),
+        flops=6 * fields * rows * cols**2 * len(pieces),
         scratch=[plan.tiles],
     )
 
@@ -426,7 +452,7 @@
         out_specs=[pl.BlockSpec(memory_space=pltpu.VMEM)] * 3,
         scratch_shapes=[pltpu.VMEM((records, rows, cols), jnp.float32), plan.tiles],
         compiler_params=pltpu.CompilerParams(vmem_limit_bytes=32 * 2**20),
-        cost_estimate=pl.CostEstimate(flops=10**7, bytes_accessed=moved, transcendentals=0),
+        cost_estimate=pl.CostEstimate(flops=1, bytes_accessed=1, transcendentals=0),
     )(*operands)
 
 
@@ -451,31 +477,49 @@
     if not plan.fits:
         plan, chunks = Plan(kinds * levels, rows, cols, gy_count // 2), 1
     me = jnp.stack([lax.axis_index("gx"), lax.axis_index("gy")]).astype(jnp.int32)
-    x_high, x_low = prepare_x(x_inverse)
-    fields = list(control.reshape(chunks, plan.fields, rows, cols))
+    x_parts = prepare_x(x_inverse)
+    fields = [control[0, 0] if chunks > 1 else control.reshape(plan.fields, rows, cols)]
+    if chunks > 1:
+        control = after(control, fields[0])
+        fields += [control[0, kind] for kind in range(1, kinds)]
     y_columns = y_inverse.reshape(y_inverse.shape[0], gy_count // 2, 2, rows)
     y_columns = jnp.where(me[1] % 2 == 0, y_columns[:, :, 0], y_columns[:, :, 1])
     y_columns = y_columns.reshape(y_inverse.shape[0], -1)
-    y_parts = first_pieces = result = None
+    y_far = gather_far(y_columns, "gx", gx_count)
+    y_held = gather_near(y_columns, "gx", gx_count) + y_far
+    y_parts = prepare_y([m for m, _ in y_held], [p for _, p in y_held], me, rows)
+    side_pairs = [(i, i ^ 1) for i in range(gy_count)]
+    result = None
     for step in range(STEPS):
-        sent = []
+        own, other, sent = [], [], []
         for chunk in range(chunks):
-            hold = None
-            if first_pieces is not None and step == 0:
-                fields[chunk] = after(fields[chunk], *first_pieces)
-                hold = sent[0][plan.parts // 2 :]
-            held = gather_pieces(fields[chunk], "gx", gx_count, hold)
-            masks, pieces = [m for m, _ in held], [p for _, p in held]
-            packed = zonal(plan, masks, pieces, me, x_high, x_low, sea_mask)
+            near = gather_near(fields[chunk], "gx", gx_count)
+            total = zonal_start(plan, near, me, *x_parts)
+            if sent:
+                hold = sent[-1]
+            elif step == 0:
+                hold = [total, y_far[0][1]] + fields[1:]
+            else:
+                hold = [total] + returned
+            far = gather_far(fields[chunk], "gx", gx_count, hold)
+            if own:
+                total = after(total, own[-1])
+            packed = zonal_end(plan, total, far, me, *x_parts, sea_mask)
             sent.append(exchange(packed, "gy", gy_count))
-            if y_parts is None:
-                held = gather_pieces(y_columns, "gx", gx_count)
-                first_pieces = [pieces[1], held[1][1]]
-                y_parts = prepare_y([m for m, _ in held], [p for _, p in held], me, rows)
+            lines = sent[chunk]
+            if other:
+                lines = [after(line, other[-1]) for line in lines]
+            for_own, for_other = meridional(plan, me, lines, *y_parts)
+            own.append(for_own)
+            other.append(lax.ppermute(for_other, "gy", side_pairs))
         for chunk in range(chunks):
-            own, other = meridional(plan, me, sent[chunk], *y_parts)
-            other = lax.ppermute(other, "gy", [(i, i ^ 1) for i in range(gy_count)])
-            returned = exchange(add_sides(plan, me, own, other), "gy", gy_count)
+            if chunk == 0:
+                own[chunk] = after(own[chunk], own[-1])
+            elif step < STEPS - 1:
+                own[chunk] = after(own[chunk], fields[chunk - 1])
+            returned = exchange(add_sides(plan, me, own[chunk], other[chunk]), "gy", gy_count)
+            if chunk < chunks - 1:
+                returned = [after(block, other[-1]) for block in returned]
             if step < STEPS - 1 or chunk < chunks - 1:
                 fields[chunk] = vertical(plan, me, returned, kappa, sea_mask, levels)
             else:

time: 167 us -> 164 us (0.982)
  starting transfers between devices: 62.3 us -> 48.8 us
  waiting for transfers between devices: 63.9 us -> 68.5 us
  local copies, waits for them, and re-layouts: 2.58 us -> 6.79 us
  Pallas kernels: 25.5 us -> 27.4 us
    ppermute x24, starting transfers between devices: 47.4 us -> 36.8 us  [exchange(): out[mask] = lax.ppermute(blocks[mask], axis, pairs)]
    ppermute x24, waiting for transfers between devices: 30.2 us -> 36.8 us  [exchange(): out[mask] = lax.ppermute(blocks[mask], axis, pairs)]
    unnamed x22 -> x24, local copies, waits for them, and re-layouts: 0.37 us -> 4.61 us
    ppermute x19, starting transfers between devices: 15 us -> 12 us  [the longest x10 6.61 us: gather_far(): lax.ppermute(piece, axis, pairs)]
    another operation x1 -> x0, local copies, waits for them, and re-layouts: 2.12 us -> none  [body(): fields = list(control.reshape(chunks, plan.fields, rows, cols))]
    squeeze x0 -> x2, local copies, waits for them, and re-layouts: none -> 2.09 us  [the longest x1 1.05 us: body(): fields += [control[0, kind] for kind in range(1, kinds)]]
    ppermute x19, waiting for transfers between devices: 33.8 us -> 31.7 us  [the longest x10 15.2 us: gather_far(): lax.ppermute(piece, axis, pairs)]
    pallas_call x18 -> x22, Pallas kernels: 23.4 us -> 25.3 us  [call(): pl.pallas_call(kernel, out_shape=out_shape, in_specs=specs, out_specs=[ou...]
  transfers between devices with their start and end apart: 43 -> 43, of which waited for: 14 -> 18; matrix products, arithmetic and copies ran while one was open for 0% -> 1% of each run, Pallas kernels for 14% -> 13%
where the time goes in v3:
time: 164 us
  waiting for transfers between devices  68.5 us (42%)
  starting transfers between devices  48.8 us (30%)
  Pallas kernels  27.4 us (17%)
  blocking collectives  10.8 us (7%)
  local copies, waits for them, and re-layouts  6.79 us (4%)
    ppermute x24, starting transfers between devices, exchange(): out[mask] = lax.ppermute(blocks[mask], axis, pairs)  36.8 us
    ppermute x24, waiting for transfers between devices, exchange(): out[mask] = lax.ppermute(blocks[mask], axis, pairs)  36.8 us
    pallas_call x22, Pallas kernels, call(): pl.pallas_call(kernel, out_shape=out_shape, in_specs=specs, out_specs=[ou...  25.3 us
    ppermute x10, waiting for transfers between devices, gather_far(): lax.ppermute(piece, axis, pairs)  15.2 us
    ppermute x4, waiting for transfers between devices, body(): other.append(lax.ppermute(for_other, 'gy', side_pairs))  15.1 us
    all_to_all x1, blocking collectives, body(): lax.all_to_all(outgoing, ('gx', 'gy'), split_axis=0, concat_axis=0, tiled...  10.8 us
    ppermute x10, starting transfers between devices, gather_far(): lax.ppermute(piece, axis, pairs)  6.61 us
    unnamed x24, local copies, waits for them, and re-layouts  4.61 us
  transfers between devices with their start and end apart: 43, of which 18 were waited for; matrix products, arithmetic and copies ran while one was open for 1% of the time, Pallas kernels for 13%

profile of v3, /device:TPU:0, one launch (start us, length us, event | category | flops | bytes accessed | tf_op | source)
XLA Modules:
  0.0 164.0 jit_solution(16729262714606286483)
XLA Ops:
  2.2 2.6 %collective-permute-start.4 = (f32[6,48,384]{2,1,0:T(8,128)S(1)}, f32[6,48,384]{2,1,0:T(8,128)}, u32[]{:S(2)}, u32[]{:S(2)}) collective-permute-start(f32[6,48,384]{2,1,0:T(8,128)S(1)} %slice_bitcast_fusion.1.refs_0_), channel_id=1, source_target_pairs={{0,16},{8,24},{16,0},{24,8},{1,17},{9,25},{17,1},{25,9},{2,18},{10... | collective-permute-start | bytes 1327112 | tf_op jit(solution)/shard_map/ppermute | solution.py:157
  6.0 1.7 %copy-done.2 = f32[384,1536]{1,0:T(8,128)S(1)} copy-done((f32[384,1536]{1,0:T(8,128)S(1)}, f32[384,1536]{1,0:T(8,128)}, u32[]{:S(2)}) %copy-start.2) | copy-done | bytes 2359320
  12.8 4.8 %collective-permute-done.1.refs_2_ = f32[96,192]{1,0:T(8,128)S(1)} collective-permute-done((f32[96,192]{1,0:T(8,128)S(1)}, f32[96,192]{1,0:T(8,128)S(1)}, u32[]{:S(2)}, u32[]{:S(2)}) %collective-permute-start.1) | collective-permute-done | bytes 73760 | tf_op jit(solution)/shard_map/ppermute | solution.py:157
  17.7 1.8 %collective-permute-start.10 = (f32[6,48,384]{2,1,0:T(8,128)S(1)}, f32[6,48,384]{2,1,0:T(8,128)S(1)}, u32[]{:S(2)}, u32[]{:S(2)}) collective-permute-start(f32[6,48,384]{2,1,0:T(8,128)S(1)} %slice_bitcast_fusion.refs_0_), channel_id=1, source_target_pairs={{0,16},{8,24},{16,0},{24,8},{1,17},{9,25},{17,1},{25,9},{2,18},{10... | collective-permute-start | bytes 1327112 | tf_op jit(solution)/shard_map/ppermute | solution.py:157
  19.7 2.1 %shard_map.142 = (f32[216,128]{1,0:T(8,128)S(1)}, f32[216,128]{1,0:T(8,128)S(1)}, f32[216,128]{1,0:T(8,128)S(1)}, f32[216,128]{1,0:T(8,128)S(1)}) custom-call(s32[2]{0:T(128)S(1)} %pad_add_fusion.me_ref, bf16[1536,384]{1,0:T(8,128)(2,1)S(1)} %get-tuple-element.78.high_ref, bf16[1536,384]{1,0:T(8,128)(2,1)S(1)} %get-tuple-element.79.low_ref, ...), custom_call_target="tpu_custom_call" | custom-call | flops 1 | bytes 1 | tf_op jit(solution)/shard_map/pallas_call | solution.py:131
  21.8 1.9 %collective-permute-start.6 = (f32[216,128]{1,0:T(8,128)S(1)}, f32[216,128]{1,0:T(8,128)S(1)}, u32[]{:S(2)}, u32[]{:S(2)}) collective-permute-start(f32[216,128]{1,0:T(8,128)S(1)} %get-tuple-element.83), channel_id=1, source_target_pairs={{0,2},{1,3},{2,0},{3,1},{4,6},{5,7},{6,4},{7,5},{8,10},{9,11},{10,... | collective-permute-start | bytes 331784 | tf_op jit(solution)/shard_map/ppermute | solution.py:169
  23.7 2.6 %collective-permute-start.7 = (f32[216,128]{1,0:T(8,128)S(1)}, f32[216,128]{1,0:T(8,128)S(1)}, u32[]{:S(2)}, u32[]{:S(2)}) collective-permute-start(f32[216,128]{1,0:T(8,128)S(1)} %get-tuple-element.84), channel_id=1, source_target_pairs={{0,4},{1,5},{2,6},{3,7},{4,0},{5,1},{6,2},{7,3},{8,12},{9,13},{10,... | collective-permute-start | bytes 331784 | tf_op jit(solution)/shard_map/ppermute | solution.py:169
  26.3 4.0 %collective-permute-done.10.refs_0_ = f32[6,48,384]{2,1,0:T(8,128)S(1)} collective-permute-done((f32[6,48,384]{2,1,0:T(8,128)S(1)}, f32[6,48,384]{2,1,0:T(8,128)S(1)}, u32[]{:S(2)}, u32[]{:S(2)}) %collective-permute-start.10) | collective-permute-done | bytes 442400 | tf_op jit(solution)/shard_map/ppermute | solution.py:157
  30.3 4.9 %collective-permute-done.7.refs_2_ = f32[216,128]{1,0:T(8,128)S(1)} collective-permute-done((f32[216,128]{1,0:T(8,128)S(1)}, f32[216,128]{1,0:T(8,128)S(1)}, u32[]{:S(2)}, u32[]{:S(2)}) %collective-permute-start.7) | collective-permute-done | bytes 110624 | tf_op jit(solution)/shard_map/ppermute | solution.py:169
  42.4 1.6 shard_map.145
  44.0 1.9 %collective-permute-start.13 = (f32[216,128]{1,0:T(8,128)S(1)}, f32[216,128]{1,0:T(8,128)S(1)}, u32[]{:S(2)}, u32[]{:S(2)}) collective-permute-start(f32[216,128]{1,0:T(8,128)S(1)} %get-tuple-element.92), channel_id=1, source_target_pairs={{0,2},{1,3},{2,0},{3,1},{4,6},{5,7},{6,4},{7,5},{8,10},{9,11},{10,... | collective-permute-start | bytes 331784 | tf_op jit(solution)/shard_map/ppermute | solution.py:169
  48.5 3.0 %collective-permute-done.12.other_ref = f32[4,216,128]{2,1,0:T(8,128)S(1)} collective-permute-done((f32[4,216,128]{2,1,0:T(8,128)S(1)}, f32[4,216,128]{2,1,0:T(8,128)S(1)}, u32[]{:S(2)}, u32[]{:S(2)}) %collective-permute-start.12) | collective-permute-done | bytes 442400 | tf_op jit(solution)/shard_map/ppermute | solution.py:514
  51.5 5.8 %collective-permute-done.14.refs_2_ = f32[216,128]{1,0:T(8,128)S(1)} collective-permute-done((f32[216,128]{1,0:T(8,128)S(1)}, f32[216,128]{1,0:T(8,128)S(1)}, u32[]{:S(2)}, u32[]{:S(2)}) %collective-permute-start.14) | collective-permute-done | bytes 110624 | tf_op jit(solution)/shard_map/ppermute | solution.py:169
  59.9 1.8 %collective-permute-start.17 = (f32[216,128]{1,0:T(8,128)S(1)}, f32[216,128]{1,0:T(8,128)S(1)}, u32[]{:S(2)}, u32[]{:S(2)}) collective-permute-start(f32[216,128]{1,0:T(8,128)S(1)} %get-tuple-element.103), channel_id=1, source_target_pairs={{0,2},{1,3},{2,0},{3,1},{4,6},{5,7},{6,4},{7,5},{8,10},{9,11},{10,... | collective-permute-start | bytes 331784 | tf_op jit(solution)/shard_map/ppermute | solution.py:169
  64.3 4.1 %collective-permute-done.16.other_ref = f32[4,216,128]{2,1,0:T(8,128)S(1)} collective-permute-done((f32[4,216,128]{2,1,0:T(8,128)S(1)}, f32[4,216,128]{2,1,0:T(8,128)S(1)}, u32[]{:S(2)}, u32[]{:S(2)}) %collective-permute-start.16) | collective-permute-done | bytes 442400 | tf_op jit(solution)/shard_map/ppermute | solution.py:514
  68.4 3.6 %collective-permute-done.18.refs_2_ = f32[216,128]{1,0:T(8,128)S(1)} collective-permute-done((f32[216,128]{1,0:T(8,128)S(1)}, f32[216,128]{1,0:T(8,128)S(1)}, u32[]{:S(2)}, u32[]{:S(2)}) %collective-permute-start.18) | collective-permute-done | bytes 110624 | tf_op jit(solution)/shard_map/ppermute | solution.py:169
  75.1 1.8 %collective-permute-start.22 = (f32[216,128]{1,0:T(8,128)S(1)}, f32[216,128]{1,0:T(8,128)S(1)}, u32[]{:S(2)}, u32[]{:S(2)}) collective-permute-start(f32[216,128]{1,0:T(8,128)S(1)} %get-tuple-element.111), channel_id=1, source_target_pairs={{0,2},{1,3},{2,0},{3,1},{4,6},{5,7},{6,4},{7,5},{8,10},{9,11},{10,... | collective-permute-start | bytes 331784 | tf_op jit(solution)/shard_map/ppermute | solution.py:169
  81.1 7.4 %collective-permute-done.23.refs_2_ = f32[216,128]{1,0:T(8,128)S(1)} collective-permute-done((f32[216,128]{1,0:T(8,128)S(1)}, f32[216,128]{1,0:T(8,128)S(1)}, u32[]{:S(2)}, u32[]{:S(2)}) %collective-permute-start.23) | collective-permute-done | bytes 110624 | tf_op jit(solution)/shard_map/ppermute | solution.py:169
  92.0 1.9 %collective-permute-start.26 = (f32[216,128]{1,0:T(8,128)S(1)}, f32[216,128]{1,0:T(8,128)S(1)}, u32[]{:S(2)}, u32[]{:S(2)}) collective-permute-start(f32[216,128]{1,0:T(8,128)S(1)} %get-tuple-element.116), channel_id=1, source_target_pairs={{0,2},{1,3},{2,0},{3,1},{4,6},{5,7},{6,4},{7,5},{8,10},{9,11},{10,... | collective-permute-start | bytes 331784 | tf_op jit(solution)/shard_map/ppermute | solution.py:169
  96.4 5.5 %collective-permute-done.30.refs_0_ = f32[6,48,384]{2,1,0:T(8,128)S(1)} collective-permute-done((f32[6,48,384]{2,1,0:T(8,128)S(1)}, f32[6,48,384]{2,1,0:T(8,128)S(1)}, u32[]{:S(2)}, u32[]{:S(2)}) %collective-permute-start.30) | collective-permute-done | bytes 442400 | tf_op jit(solution)/shard_map/ppermute | solution.py:157
  102.0 3.5 %collective-permute-done.27.refs_2_ = f32[216,128]{1,0:T(8,128)S(1)} collective-permute-done((f32[216,128]{1,0:T(8,128)S(1)}, f32[216,128]{1,0:T(8,128)S(1)}, u32[]{:S(2)}, u32[]{:S(2)}) %collective-permute-start.27) | collective-permute-done | bytes 110624 | tf_op jit(solution)/shard_map/ppermute | solution.py:169
  108.3 1.7 %shard_map.154.total_ref = f32[288,384]{1,0:T(8,128)S(1)} custom-call(s32[2]{0:T(128)S(1)} %pad_add_fusion.me_ref, bf16[1536,384]{1,0:T(8,128)(2,1)S(1)} %get-tuple-element.78.high_ref, bf16[1536,384]{1,0:T(8,128)(2,1)S(1)} %get-tuple-element.79.low_ref, f32[6,48,384]{2,1,0:T(8,128)S(1)} %shard_map.153.refs_0_, f32[6,48,384]{2,1,0:T(8,128)S(1)} %collective-permute-done.29.refs_1_), custom_call_target="tpu_custom_call" | custom-call | flops 1 | bytes 1 | tf_op jit(solution)/shard_map/pallas_call | solution.py:131
  110.0 1.6 shard_map.155
  111.7 1.9 %collective-permute-start.33 = (f32[216,128]{1,0:T(8,128)S(1)}, f32[216,128]{1,0:T(8,128)S(1)}, u32[]{:S(2)}, u32[]{:S(2)}) collective-permute-start(f32[216,128]{1,0:T(8,128)S(1)} %get-tuple-element.125), channel_id=1, source_target_pairs={{0,2},{1,3},{2,0},{3,1},{4,6},{5,7},{6,4},{7,5},{8,10},{9,11},{10,... | collective-permute-start | bytes 331784 | tf_op jit(solution)/shard_map/ppermute | solution.py:169
  116.1 3.3 %collective-permute-done.32.other_ref = f32[4,216,128]{2,1,0:T(8,128)S(1)} collective-permute-done((f32[4,216,128]{2,1,0:T(8,128)S(1)}, f32[4,216,128]{2,1,0:T(8,128)S(1)}, u32[]{:S(2)}, u32[]{:S(2)}) %collective-permute-start.32) | collective-permute-done | bytes 442400 | tf_op jit(solution)/shard_map/ppermute | solution.py:514
  119.4 5.7 %collective-permute-done.34.refs_2_ = f32[216,128]{1,0:T(8,128)S(1)} collective-permute-done((f32[216,128]{1,0:T(8,128)S(1)}, f32[216,128]{1,0:T(8,128)S(1)}, u32[]{:S(2)}, u32[]{:S(2)}) %collective-permute-start.34) | collective-permute-done | bytes 110624 | tf_op jit(solution)/shard_map/ppermute | solution.py:169
  127.7 2.0 %collective-permute-start.37 = (f32[216,128]{1,0:T(8,128)S(1)}, f32[216,128]{1,0:T(8,128)S(1)}, u32[]{:S(2)}, u32[]{:S(2)}) collective-permute-start(f32[216,128]{1,0:T(8,128)S(1)} %get-tuple-element.136), channel_id=1, source_target_pairs={{0,2},{1,3},{2,0},{3,1},{4,6},{5,7},{6,4},{7,5},{8,10},{9,11},{10,... | collective-permute-start | bytes 331784 | tf_op jit(solution)/shard_map/ppermute | solution.py:169
  132.2 4.7 %collective-permute-done.36.other_ref = f32[4,216,128]{2,1,0:T(8,128)S(1)} collective-permute-done((f32[4,216,128]{2,1,0:T(8,128)S(1)}, f32[4,216,128]{2,1,0:T(8,128)S(1)}, u32[]{:S(2)}, u32[]{:S(2)}) %collective-permute-start.36) | collective-permute-done | bytes 442400 | tf_op jit(solution)/shard_map/ppermute | solution.py:514
  137.4 2.8 %collective-permute-start.40 = (f32[216,128]{1,0:T(8,128)S(1)}, f32[216,128]{1,0:T(8,128)S(1)}, u32[]{:S(2)}, u32[]{:S(2)}) collective-permute-start(f32[216,128]{1,0:T(8,128)S(1)} %get-tuple-element.143), channel_id=1, source_target_pairs={{0,2},{1,3},{2,0},{3,1},{4,6},{5,7},{6,4},{7,5},{8,10},{9,11},{10,... | collective-permute-start | bytes 331784 | tf_op jit(solution)/shard_map/ppermute | solution.py:169
  144.6 5.8 %collective-permute-done.41.refs_3_ = f32[216,128]{1,0:T(8,128)S(1)} collective-permute-done((f32[216,128]{1,0:T(8,128)S(1)}, f32[216,128]{1,0:T(8,128)S(1)}, u32[]{:S(2)}, u32[]{:S(2)}) %collective-permute-start.41) | collective-permute-done | bytes 110624 | tf_op jit(solution)/shard_map/ppermute | solution.py:169
  150.4 2.1 %shard_map.160 = (f32[2,6,48,384]{3,2,1,0:T(8,128)}, f32[48,384]{1,0:T(8,128)}, f32[32,128]{1,0:T(8,128)S(1)}) custom-call(s32[2]{0:T(128)S(1)} %pad_add_fusion.me_ref, f32[2,6]{1,0:T(2,128)S(1)} %copy-done.8, s32[1]{0:T(128)S(6)} %copy.29.count_ref, f32[5,48,384]{2,1,0:T(8,128)S(1)} %copy-done, s32[48,384]{1,0:T(8,128)S(1)} %copy-done.1, ...), custom_call_target="tpu_custom_call" | custom-call | flops 1 | bytes 1 | tf_op jit(solution)/shard_map/pallas_call | solution.py:447
  152.5 10.8 %all_to_all.11 = f32[32,1,128]{2,1,0:T(1,128)S(1)} all-to-all(f32[32,1,128]{2,1,0:T(1,128)S(1)} %bitcast.18), channel_id=1, replica_groups=mesh['gx'=4,'gy'=8] {'gx','gy'}, dimensions={0} | all-to-all | bytes 32768 | tf_op jit(solution)/shard_map/all_to_all | solution.py:538
  (107 shorter events, 51.6 us)
Async XLA Ops:
  1.7 7.8 %collective-permute-start.3 = (f32[6,48,384]{2,1,0:T(8,128)S(1)}, f32[6,48,384]{2,1,0:T(8,128)S(1)}, u32[]{:S(2)}, u32[]{:S(2)}) collective-permute-start(f32[6,48,384]{2,1,0:T(8,128)S(1)} %slice_bitcast_fusion.1.refs_0_), channel_id=1, source_target_pairs={{0,8},{8,0},{16,24},{24,16},{1,9},{9,1},{17,25},{25,17},{2,10},{10... | collective-permute-start | bytes 1327112 | tf_op jit(solution)/shard_map/ppermute | solution.py:148
  2.2 15.5 %collective-permute-start.4 = (f32[6,48,384]{2,1,0:T(8,128)S(1)}, f32[6,48,384]{2,1,0:T(8,128)}, u32[]{:S(2)}, u32[]{:S(2)}) collective-permute-start(f32[6,48,384]{2,1,0:T(8,128)S(1)} %slice_bitcast_fusion.1.refs_0_), channel_id=1, source_target_pairs={{0,16},{8,24},{16,0},{24,8},{1,17},{9,25},{17,1},{25,9},{2,18},{10... | collective-permute-start | bytes 1327112 | tf_op jit(solution)/shard_map/ppermute | solution.py:157
  6.0 11.7 %collective-permute-start.1 = (f32[96,192]{1,0:T(8,128)S(1)}, f32[96,192]{1,0:T(8,128)S(1)}, u32[]{:S(2)}, u32[]{:S(2)}) collective-permute-start(f32[96,192]{1,0:T(8,128)S(1)} %copy.26.refs_0_), channel_id=1, source_target_pairs={{0,16},{8,24},{16,0},{24,8},{1,17},{9,25},{17,1},{25,9},{2,18},{10... | collective-permute-start | bytes 221192 | tf_op jit(solution)/shard_map/ppermute | solution.py:157
  17.7 12.6 %collective-permute-start.10 = (f32[6,48,384]{2,1,0:T(8,128)S(1)}, f32[6,48,384]{2,1,0:T(8,128)S(1)}, u32[]{:S(2)}, u32[]{:S(2)}) collective-permute-start(f32[6,48,384]{2,1,0:T(8,128)S(1)} %slice_bitcast_fusion.refs_0_), channel_id=1, source_target_pairs={{0,16},{8,24},{16,0},{24,8},{1,17},{9,25},{17,1},{25,9},{2,18},{10... | collective-permute-start | bytes 1327112 | tf_op jit(solution)/shard_map/ppermute | solution.py:157
  21.8 8.5 %collective-permute-start.6 = (f32[216,128]{1,0:T(8,128)S(1)}, f32[216,128]{1,0:T(8,128)S(1)}, u32[]{:S(2)}, u32[]{:S(2)}) collective-permute-start(f32[216,128]{1,0:T(8,128)S(1)} %get-tuple-element.83), channel_id=1, source_target_pairs={{0,2},{1,3},{2,0},{3,1},{4,6},{5,7},{6,4},{7,5},{8,10},{9,11},{10,... | collective-permute-start | bytes 331784 | tf_op jit(solution)/shard_map/ppermute | solution.py:169
  23.7 11.5 %collective-permute-start.7 = (f32[216,128]{1,0:T(8,128)S(1)}, f32[216,128]{1,0:T(8,128)S(1)}, u32[]{:S(2)}, u32[]{:S(2)}) collective-permute-start(f32[216,128]{1,0:T(8,128)S(1)} %get-tuple-element.84), channel_id=1, source_target_pairs={{0,4},{1,5},{2,6},{3,7},{4,0},{5,1},{6,2},{7,3},{8,12},{9,13},{10,... | collective-permute-start | bytes 331784 | tf_op jit(solution)/shard_map/ppermute | solution.py:169
  26.3 8.9 %collective-permute-start.8 = (f32[216,128]{1,0:T(8,128)S(1)}, f32[216,128]{1,0:T(8,128)S(1)}, u32[]{:S(2)}, u32[]{:S(2)}) collective-permute-start(f32[216,128]{1,0:T(8,128)S(1)} %get-tuple-element.85), channel_id=1, source_target_pairs={{0,6},{1,7},{2,4},{3,5},{4,2},{5,3},{6,0},{7,1},{8,14},{9,15},{10,... | collective-permute-start | bytes 331784 | tf_op jit(solution)/shard_map/ppermute | solution.py:169
  26.3 14.6 %collective-permute-start.9 = (f32[6,48,384]{2,1,0:T(8,128)S(1)}, f32[6,48,384]{2,1,0:T(8,128)S(1)}, u32[]{:S(2)}, u32[]{:S(2)}) collective-permute-start(f32[6,48,384]{2,1,0:T(8,128)S(1)} %slice_bitcast_fusion.refs_0_), channel_id=1, source_target_pairs={{0,8},{8,0},{16,24},{24,16},{1,9},{9,1},{17,25},{25,17},{2,10},{10... | collective-permute-start | bytes 1327112 | tf_op jit(solution)/shard_map/ppermute | solution.py:148
  39.2 12.3 %collective-permute-start.12 = (f32[4,216,128]{2,1,0:T(8,128)S(1)}, f32[4,216,128]{2,1,0:T(8,128)S(1)}, u32[]{:S(2)}, u32[]{:S(2)}) collective-permute-start(f32[4,216,128]{2,1,0:T(8,128)S(1)} %get-tuple-element.90), channel_id=1, source_target_pairs={{0,1},{1,0},{2,3},{3,2},{4,5},{5,4},{6,7},{7,6},{8,9},{9,8},{10,11... | collective-permute-start | bytes 1327112 | tf_op jit(solution)/shard_map/ppermute | solution.py:514
  46.0 11.4 %collective-permute-start.14 = (f32[216,128]{1,0:T(8,128)S(1)}, f32[216,128]{1,0:T(8,128)S(1)}, u32[]{:S(2)}, u32[]{:S(2)}) collective-permute-start(f32[216,128]{1,0:T(8,128)S(1)} %get-tuple-element.94), channel_id=1, source_target_pairs={{0,4},{1,5},{2,6},{3,7},{4,0},{5,1},{6,2},{7,3},{8,12},{9,13},{10,... | collective-permute-start | bytes 331784 | tf_op jit(solution)/shard_map/ppermute | solution.py:169
  47.1 10.2 %collective-permute-start.15 = (f32[216,128]{1,0:T(8,128)S(1)}, f32[216,128]{1,0:T(8,128)S(1)}, u32[]{:S(2)}, u32[]{:S(2)}) collective-permute-start(f32[216,128]{1,0:T(8,128)S(1)} %get-tuple-element.96), channel_id=1, source_target_pairs={{0,6},{1,7},{2,4},{3,5},{4,2},{5,3},{6,0},{7,1},{8,14},{9,15},{10,... | collective-permute-start | bytes 331784 | tf_op jit(solution)/shard_map/ppermute | solution.py:169
  58.7 9.8 %collective-permute-start.16 = (f32[4,216,128]{2,1,0:T(8,128)S(1)}, f32[4,216,128]{2,1,0:T(8,128)S(1)}, u32[]{:S(2)}, u32[]{:S(2)}) collective-permute-start(f32[4,216,128]{2,1,0:T(8,128)S(1)} %get-tuple-element.101), channel_id=1, source_target_pairs={{0,1},{1,0},{2,3},{3,2},{4,5},{5,4},{6,7},{7,6},{8,9},{9,8},{10,11... | collective-permute-start | bytes 1327112 | tf_op jit(solution)/shard_map/ppermute | solution.py:514
  59.9 8.6 %collective-permute-start.17 = (f32[216,128]{1,0:T(8,128)S(1)}, f32[216,128]{1,0:T(8,128)S(1)}, u32[]{:S(2)}, u32[]{:S(2)}) collective-permute-start(f32[216,128]{1,0:T(8,128)S(1)} %get-tuple-element.103), channel_id=1, source_target_pairs={{0,2},{1,3},{2,0},{3,1},{4,6},{5,7},{6,4},{7,5},{8,10},{9,11},{10,... | collective-permute-start | bytes 331784 | tf_op jit(solution)/shard_map/ppermute | solution.py:169
  61.7 10.4 %collective-permute-start.18 = (f32[216,128]{1,0:T(8,128)S(1)}, f32[216,128]{1,0:T(8,128)S(1)}, u32[]{:S(2)}, u32[]{:S(2)}) collective-permute-start(f32[216,128]{1,0:T(8,128)S(1)} %get-tuple-element.105), channel_id=1, source_target_pairs={{0,4},{1,5},{2,6},{3,7},{4,0},{5,1},{6,2},{7,3},{8,12},{9,13},{10,... | collective-permute-start | bytes 331784 | tf_op jit(solution)/shard_map/ppermute | solution.py:169
  62.7 9.3 %collective-permute-start.19 = (f32[216,128]{1,0:T(8,128)S(1)}, f32[216,128]{1,0:T(8,128)S(1)}, u32[]{:S(2)}, u32[]{:S(2)}) collective-permute-start(f32[216,128]{1,0:T(8,128)S(1)} %get-tuple-element.107), channel_id=1, source_target_pairs={{0,6},{1,7},{2,4},{3,5},{4,2},{5,3},{6,0},{7,1},{8,14},{9,15},{10,... | collective-permute-start | bytes 331784 | tf_op jit(solution)/shard_map/ppermute | solution.py:169
  72.9 15.6 %collective-permute-start.21 = (f32[6,48,384]{2,1,0:T(8,128)S(1)}, f32[6,48,384]{2,1,0:T(8,128)S(1)}, u32[]{:S(2)}, u32[]{:S(2)}) collective-permute-start(f32[6,48,384]{2,1,0:T(8,128)S(1)} %shard_map.148.refs_0_), channel_id=1, source_target_pairs={{0,16},{8,24},{16,0},{24,8},{1,17},{9,25},{17,1},{25,9},{2,18},{10... | collective-permute-start | bytes 1327112 | tf_op jit(solution)/shard_map/ppermute | solution.py:157
  76.9 11.6 %collective-permute-start.23 = (f32[216,128]{1,0:T(8,128)S(1)}, f32[216,128]{1,0:T(8,128)S(1)}, u32[]{:S(2)}, u32[]{:S(2)}) collective-permute-start(f32[216,128]{1,0:T(8,128)S(1)} %get-tuple-element.112), channel_id=1, source_target_pairs={{0,4},{1,5},{2,6},{3,7},{4,0},{5,1},{6,2},{7,3},{8,12},{9,13},{10,... | collective-permute-start | bytes 331784 | tf_op jit(solution)/shard_map/ppermute | solution.py:169
  78.0 10.5 %collective-permute-start.24 = (f32[216,128]{1,0:T(8,128)S(1)}, f32[216,128]{1,0:T(8,128)S(1)}, u32[]{:S(2)}, u32[]{:S(2)}) collective-permute-start(f32[216,128]{1,0:T(8,128)S(1)} %get-tuple-element.113), channel_id=1, source_target_pairs={{0,6},{1,7},{2,4},{3,5},{4,2},{5,3},{6,0},{7,1},{8,14},{9,15},{10,... | collective-permute-start | bytes 331784 | tf_op jit(solution)/shard_map/ppermute | solution.py:169
  89.3 12.6 %collective-permute-start.30 = (f32[6,48,384]{2,1,0:T(8,128)S(1)}, f32[6,48,384]{2,1,0:T(8,128)S(1)}, u32[]{:S(2)}, u32[]{:S(2)}) collective-permute-start(f32[6,48,384]{2,1,0:T(8,128)S(1)} %shard_map.153.refs_0_), channel_id=1, source_target_pairs={{0,16},{8,24},{16,0},{24,8},{1,17},{9,25},{17,1},{25,9},{2,18},{10... | collective-permute-start | bytes 1327112 | tf_op jit(solution)/shard_map/ppermute | solution.py:157
  92.0 10.0 %collective-permute-start.26 = (f32[216,128]{1,0:T(8,128)S(1)}, f32[216,128]{1,0:T(8,128)S(1)}, u32[]{:S(2)}, u32[]{:S(2)}) collective-permute-start(f32[216,128]{1,0:T(8,128)S(1)} %get-tuple-element.116), channel_id=1, source_target_pairs={{0,2},{1,3},{2,0},{3,1},{4,6},{5,7},{6,4},{7,5},{8,10},{9,11},{10,... | collective-permute-start | bytes 331784 | tf_op jit(solution)/shard_map/ppermute | solution.py:169
  93.9 11.6 %collective-permute-start.27 = (f32[216,128]{1,0:T(8,128)S(1)}, f32[216,128]{1,0:T(8,128)S(1)}, u32[]{:S(2)}, u32[]{:S(2)}) collective-permute-start(f32[216,128]{1,0:T(8,128)S(1)} %get-tuple-element.117), channel_id=1, source_target_pairs={{0,4},{1,5},{2,6},{3,7},{4,0},{5,1},{6,2},{7,3},{8,12},{9,13},{10,... | collective-permute-start | bytes 331784 | tf_op jit(solution)/shard_map/ppermute | solution.py:169
  94.9 10.5 %collective-permute-start.28 = (f32[216,128]{1,0:T(8,128)S(1)}, f32[216,128]{1,0:T(8,128)S(1)}, u32[]{:S(2)}, u32[]{:S(2)}) collective-permute-start(f32[216,128]{1,0:T(8,128)S(1)} %get-tuple-element.118), channel_id=1, source_target_pairs={{0,6},{1,7},{2,4},{3,5},{4,2},{5,3},{6,0},{7,1},{8,14},{9,15},{10,... | collective-permute-start | bytes 331784 | tf_op jit(solution)/shard_map/ppermute | solution.py:169
  96.4 11.9 %collective-permute-start.29 = (f32[6,48,384]{2,1,0:T(8,128)S(1)}, f32[6,48,384]{2,1,0:T(8,128)S(1)}, u32[]{:S(2)}, u32[]{:S(2)}) collective-permute-start(f32[6,48,384]{2,1,0:T(8,128)S(1)} %shard_map.153.refs_0_), channel_id=1, source_target_pairs={{0,8},{8,0},{16,24},{24,16},{1,9},{9,1},{17,25},{25,17},{2,10},{10... | collective-permute-start | bytes 1327112 | tf_op jit(solution)/shard_map/ppermute | solution.py:148
  106.8 12.6 %collective-permute-start.32 = (f32[4,216,128]{2,1,0:T(8,128)S(1)}, f32[4,216,128]{2,1,0:T(8,128)S(1)}, u32[]{:S(2)}, u32[]{:S(2)}) collective-permute-start(f32[4,216,128]{2,1,0:T(8,128)S(1)} %get-tuple-element.123), channel_id=1, source_target_pairs={{0,1},{1,0},{2,3},{3,2},{4,5},{5,4},{6,7},{7,6},{8,9},{9,8},{10,11... | collective-permute-start | bytes 1327112 | tf_op jit(solution)/shard_map/ppermute | solution.py:514
  113.6 11.6 %collective-permute-start.34 = (f32[216,128]{1,0:T(8,128)S(1)}, f32[216,128]{1,0:T(8,128)S(1)}, u32[]{:S(2)}, u32[]{:S(2)}) collective-permute-start(f32[216,128]{1,0:T(8,128)S(1)} %get-tuple-element.127), channel_id=1, source_target_pairs={{0,4},{1,5},{2,6},{3,7},{4,0},{5,1},{6,2},{7,3},{8,12},{9,13},{10,... | collective-permute-start | bytes 331784 | tf_op jit(solution)/shard_map/ppermute | solution.py:169
  114.6 10.5 %collective-permute-start.35 = (f32[216,128]{1,0:T(8,128)S(1)}, f32[216,128]{1,0:T(8,128)S(1)}, u32[]{:S(2)}, u32[]{:S(2)}) collective-permute-start(f32[216,128]{1,0:T(8,128)S(1)} %get-tuple-element.129), channel_id=1, source_target_pairs={{0,6},{1,7},{2,4},{3,5},{4,2},{5,3},{6,0},{7,1},{8,14},{9,15},{10,... | collective-permute-start | bytes 331784 | tf_op jit(solution)/shard_map/ppermute | solution.py:169
  126.5 10.4 %collective-permute-start.36 = (f32[4,216,128]{2,1,0:T(8,128)S(1)}, f32[4,216,128]{2,1,0:T(8,128)S(1)}, u32[]{:S(2)}, u32[]{:S(2)}) collective-permute-start(f32[4,216,128]{2,1,0:T(8,128)S(1)} %get-tuple-element.134), channel_id=1, source_target_pairs={{0,1},{1,0},{2,3},{3,2},{4,5},{5,4},{6,7},{7,6},{8,9},{9,8},{10,11... | collective-permute-start | bytes 1327112 | tf_op jit(solution)/shard_map/ppermute | solution.py:514
  127.7 13.9 %collective-permute-start.37 = (f32[216,128]{1,0:T(8,128)S(1)}, f32[216,128]{1,0:T(8,128)S(1)}, u32[]{:S(2)}, u32[]{:S(2)}) collective-permute-start(f32[216,128]{1,0:T(8,128)S(1)} %get-tuple-element.136), channel_id=1, source_target_pairs={{0,2},{1,3},{2,0},{3,1},{4,6},{5,7},{6,4},{7,5},{8,10},{9,11},{10,... | collective-permute-start | bytes 331784 | tf_op jit(solution)/shard_map/ppermute | solution.py:169
  129.7 14.1 %collective-permute-start.38 = (f32[216,128]{1,0:T(8,128)S(1)}, f32[216,128]{1,0:T(8,128)S(1)}, u32[]{:S(2)}, u32[]{:S(2)}) collective-permute-start(f32[216,128]{1,0:T(8,128)S(1)} %get-tuple-element.138), channel_id=1, source_target_pairs={{0,4},{1,5},{2,6},{3,7},{4,0},{5,1},{6,2},{7,3},{8,12},{9,13},{10,... | collective-permute-start | bytes 331784 | tf_op jit(solution)/shard_map/ppermute | solution.py:169
  130.8 13.0 %collective-permute-start.39 = (f32[216,128]{1,0:T(8,128)S(1)}, f32[216,128]{1,0:T(8,128)S(1)}, u32[]{:S(2)}, u32[]{:S(2)}) collective-permute-start(f32[216,128]{1,0:T(8,128)S(1)} %get-tuple-element.140), channel_id=1, source_target_pairs={{0,6},{1,7},{2,4},{3,5},{4,2},{5,3},{6,0},{7,1},{8,14},{9,15},{10,... | collective-permute-start | bytes 331784 | tf_op jit(solution)/shard_map/ppermute | solution.py:169
  140.3 10.1 %collective-permute-start.41 = (f32[216,128]{1,0:T(8,128)S(1)}, f32[216,128]{1,0:T(8,128)S(1)}, u32[]{:S(2)}, u32[]{:S(2)}) collective-permute-start(f32[216,128]{1,0:T(8,128)S(1)} %get-tuple-element.144), channel_id=1, source_target_pairs={{0,4},{1,5},{2,6},{3,7},{4,0},{5,1},{6,2},{7,3},{8,12},{9,13},{10,... | collective-permute-start | bytes 331784 | tf_op jit(solution)/shard_map/ppermute | solution.py:169
  141.7 8.7 %collective-permute-start.42 = (f32[216,128]{1,0:T(8,128)S(1)}, f32[216,128]{1,0:T(8,128)S(1)}, u32[]{:S(2)}, u32[]{:S(2)}) collective-permute-start(f32[216,128]{1,0:T(8,128)S(1)} %get-tuple-element.145), channel_id=1, source_target_pairs={{0,6},{1,7},{2,4},{3,5},{4,2},{5,3},{6,0},{7,1},{8,14},{9,15},{10,... | collective-permute-start | bytes 331784 | tf_op jit(solution)/shard_map/ppermute | solution.py:169
  (22 other events, 231.8 us)

commit v4 on v3

--- a/solution.py
+++ b/solution.py
@@ -164,7 +164,7 @@
 
 def exchange(blocks, axis, count):
     out = [blocks[0]] + [None] * (len(blocks) - 1)
-    for mask in range(len(blocks) - 1, 0, -1):
+    for mask in range(1, len(blocks)):
         pairs = [(i, i ^ (2 * mask)) for i in range(count)]
         out[mask] = lax.ppermute(blocks[mask], axis, pairs)
     return out
@@ -496,19 +496,18 @@
             near = gather_near(fields[chunk], "gx", gx_count)
             total = zonal_start(plan, near, me, *x_parts)
             if sent:
-                hold = sent[-1]
+                hold = [total, y_parts[0]] + lines
             elif step == 0:
                 hold = [total, y_far[0][1]] + fields[1:]
             else:
-                hold = [total] + returned
+                hold = [total] + returned[::-1]
             far = gather_far(fields[chunk], "gx", gx_count, hold)
             if own:
                 total = after(total, own[-1])
             packed = zonal_end(plan, total, far, me, *x_parts, sea_mask)
             sent.append(exchange(packed, "gy", gy_count))
-            lines = sent[chunk]
-            if other:
-                lines = [after(line, other[-1]) for line in lines]
+            ready = other[-1] if other else y_parts[0]
+            lines = [after(line, ready) for line in sent[chunk]]
             for_own, for_other = meridional(plan, me, lines, *y_parts)
             own.append(for_own)
             other.append(lax.ppermute(for_other, "gy", side_pairs))
@@ -523,6 +522,7 @@
             if step < STEPS - 1 or chunk < chunks - 1:
                 fields[chunk] = vertical(plan, me, returned, kappa, sea_mask, levels)
             else:
+                returned = [after(block, *fields[:chunk]) for block in returned]
                 obs = (
                     obs_owner.reshape(1, -1),
                     tile_index.reshape(1, -1),

time: 164 us -> 151 us (0.921)
  waiting for transfers between devices: 68.5 us -> 56.6 us
    ppermute x10, waiting for transfers between devices: 15.2 us -> 4.86 us  [gather_far(): lax.ppermute(piece, axis, pairs)]
    ppermute x24, waiting for transfers between devices: 36.8 us -> 32.2 us  [exchange(): out[mask] = lax.ppermute(blocks[mask], axis, pairs)]
    ppermute x4, waiting for transfers between devices: 15.1 us -> 19.5 us  [body(): other.append(lax.ppermute(for_other, 'gy', side_pairs))]
  transfers between devices with their start and end apart: 43 -> 43, of which waited for: 18 -> 17; matrix products, arithmetic and copies ran while one was open for 1% -> 2% of each run, Pallas kernels for 13% -> 14%
where the time goes in v4:
time: 151 us
  waiting for transfers between devices  56.6 us (37%)
  starting transfers between devices  48.7 us (32%)
  Pallas kernels  27.4 us (18%)
  blocking collectives  9.73 us (6%)
  local copies, waits for them, and re-layouts  6.78 us (4%)
  between operations  1.6 us (1%)
    ppermute x24, starting transfers between devices, exchange(): out[mask] = lax.ppermute(blocks[mask], axis, pairs)  35.6 us
    ppermute x24, waiting for transfers between devices, exchange(): out[mask] = lax.ppermute(blocks[mask], axis, pairs)  32.2 us
    pallas_call x22, Pallas kernels, call(): pl.pallas_call(kernel, out_shape=out_shape, in_specs=specs, out_specs=[ou...  25.3 us
    ppermute x4, waiting for transfers between devices, body(): other.append(lax.ppermute(for_other, 'gy', side_pairs))  19.5 us
    all_to_all x1, blocking collectives, body(): lax.all_to_all(outgoing, ('gx', 'gy'), split_axis=0, concat_axis=0, tiled...  9.73 us
    ppermute x10, starting transfers between devices, gather_far(): lax.ppermute(piece, axis, pairs)  7.09 us
    ppermute x10, waiting for transfers between devices, gather_far(): lax.ppermute(piece, axis, pairs)  4.86 us
    unnamed x24, local copies, waits for them, and re-layouts  4.61 us
  transfers between devices with their start and end apart: 43, of which 17 were waited for; matrix products, arithmetic and copies ran while one was open for 2% of the time, Pallas kernels for 14%

profile of v4, /device:TPU:0, one launch (start us, length us, event | category | flops | bytes accessed | tf_op | source)
XLA Modules:
  0.0 150.8 jit_solution(1818991547005490488)
XLA Ops:
  2.2 2.6 %collective-permute-start.4 = (f32[6,48,384]{2,1,0:T(8,128)S(1)}, f32[6,48,384]{2,1,0:T(8,128)}, u32[]{:S(2)}, u32[]{:S(2)}) collective-permute-start(f32[6,48,384]{2,1,0:T(8,128)S(1)} %slice_bitcast_fusion.1.refs_0_), channel_id=1, source_target_pairs={{0,16},{8,24},{16,0},{24,8},{1,17},{9,25},{17,1},{25,9},{2,18},{10... | collective-permute-start | bytes 1327112 | tf_op jit(solution)/shard_map/ppermute | solution.py:157
  12.8 4.8 %collective-permute-done.1.refs_2_ = f32[96,192]{1,0:T(8,128)S(1)} collective-permute-done((f32[96,192]{1,0:T(8,128)S(1)}, f32[96,192]{1,0:T(8,128)S(1)}, u32[]{:S(2)}, u32[]{:S(2)}) %collective-permute-start.1) | collective-permute-done | bytes 73760 | tf_op jit(solution)/shard_map/ppermute | solution.py:157
  20.4 2.1 %shard_map.142 = (f32[216,128]{1,0:T(8,128)S(1)}, f32[216,128]{1,0:T(8,128)S(1)}, f32[216,128]{1,0:T(8,128)S(1)}, f32[216,128]{1,0:T(8,128)S(1)}) custom-call(s32[2]{0:T(128)S(1)} %pad_add_fusion.me_ref, bf16[1536,384]{1,0:T(8,128)(2,1)S(1)} %get-tuple-element.90.high_ref, bf16[1536,384]{1,0:T(8,128)(2,1)S(1)} %get-tuple-element.91.low_ref, ...), custom_call_target="tpu_custom_call" | custom-call | flops 1 | bytes 1 | tf_op jit(solution)/shard_map/pallas_call | solution.py:131
  22.6 3.7 %collective-permute-start.8 = (f32[216,128]{1,0:T(8,128)S(1)}, f32[216,128]{1,0:T(8,128)S(1)}, u32[]{:S(2)}, u32[]{:S(2)}) collective-permute-start(f32[216,128]{1,0:T(8,128)S(1)} %get-tuple-element.100), channel_id=1, source_target_pairs={{0,6},{1,7},{2,4},{3,5},{4,2},{5,3},{6,0},{7,1},{8,14},{9,15},{10,... | collective-permute-start | bytes 331784 | tf_op jit(solution)/shard_map/ppermute | solution.py:169
  30.4 5.5 %collective-permute-done.7.refs_2_ = f32[216,128]{1,0:T(8,128)S(1)} collective-permute-done((f32[216,128]{1,0:T(8,128)S(1)}, f32[216,128]{1,0:T(8,128)S(1)}, u32[]{:S(2)}, u32[]{:S(2)}) %collective-permute-start.7) | collective-permute-done | bytes 110624 | tf_op jit(solution)/shard_map/ppermute | solution.py:169
  40.5 2.5 %collective-permute-start.15 = (f32[216,128]{1,0:T(8,128)S(1)}, f32[216,128]{1,0:T(8,128)S(1)}, u32[]{:S(2)}, u32[]{:S(2)}) collective-permute-start(f32[216,128]{1,0:T(8,128)S(1)} %get-tuple-element.112), channel_id=1, source_target_pairs={{0,6},{1,7},{2,4},{3,5},{4,2},{5,3},{6,0},{7,1},{8,14},{9,15},{10,... | collective-permute-start | bytes 331784 | tf_op jit(solution)/shard_map/ppermute | solution.py:169
  43.0 1.9 %collective-permute-start.13 = (f32[216,128]{1,0:T(8,128)S(1)}, f32[216,128]{1,0:T(8,128)S(1)}, u32[]{:S(2)}, u32[]{:S(2)}) collective-permute-start(f32[216,128]{1,0:T(8,128)S(1)} %get-tuple-element.108), channel_id=1, source_target_pairs={{0,2},{1,3},{2,0},{3,1},{4,6},{5,7},{6,4},{7,5},{8,10},{9,11},{10,... | collective-permute-start | bytes 331784 | tf_op jit(solution)/shard_map/ppermute | solution.py:169
  44.9 5.0 %collective-permute-done.12.other_ref = f32[4,216,128]{2,1,0:T(8,128)S(1)} collective-permute-done((f32[4,216,128]{2,1,0:T(8,128)S(1)}, f32[4,216,128]{2,1,0:T(8,128)S(1)}, u32[]{:S(2)}, u32[]{:S(2)}) %collective-permute-start.12) | collective-permute-done | bytes 442400 | tf_op jit(solution)/shard_map/ppermute | solution.py:513
  49.9 2.6 %collective-permute-done.14.refs_2_ = f32[216,128]{1,0:T(8,128)S(1)} collective-permute-done((f32[216,128]{1,0:T(8,128)S(1)}, f32[216,128]{1,0:T(8,128)S(1)}, u32[]{:S(2)}, u32[]{:S(2)}) %collective-permute-start.14) | collective-permute-done | bytes 110624 | tf_op jit(solution)/shard_map/ppermute | solution.py:169
  55.1 2.3 %collective-permute-start.19 = (f32[216,128]{1,0:T(8,128)S(1)}, f32[216,128]{1,0:T(8,128)S(1)}, u32[]{:S(2)}, u32[]{:S(2)}) collective-permute-start(f32[216,128]{1,0:T(8,128)S(1)} %get-tuple-element.123), channel_id=1, source_target_pairs={{0,6},{1,7},{2,4},{3,5},{4,2},{5,3},{6,0},{7,1},{8,14},{9,15},{10,... | collective-permute-start | bytes 331784 | tf_op jit(solution)/shard_map/ppermute | solution.py:169
  57.3 2.2 %collective-permute-start.17 = (f32[216,128]{1,0:T(8,128)S(1)}, f32[216,128]{1,0:T(8,128)S(1)}, u32[]{:S(2)}, u32[]{:S(2)}) collective-permute-start(f32[216,128]{1,0:T(8,128)S(1)} %get-tuple-element.119), channel_id=1, source_target_pairs={{0,2},{1,3},{2,0},{3,1},{4,6},{5,7},{6,4},{7,5},{8,10},{9,11},{10,... | collective-permute-start | bytes 331784 | tf_op jit(solution)/shard_map/ppermute | solution.py:169
  59.5 3.4 %collective-permute-done.19.refs_3_ = f32[216,128]{1,0:T(8,128)S(1)} collective-permute-done((f32[216,128]{1,0:T(8,128)S(1)}, f32[216,128]{1,0:T(8,128)S(1)}, u32[]{:S(2)}, u32[]{:S(2)}) %collective-permute-start.19) | collective-permute-done | bytes 110624 | tf_op jit(solution)/shard_map/ppermute | solution.py:169
  62.9 3.1 %collective-permute-done.16.other_ref = f32[4,216,128]{2,1,0:T(8,128)S(1)} collective-permute-done((f32[4,216,128]{2,1,0:T(8,128)S(1)}, f32[4,216,128]{2,1,0:T(8,128)S(1)}, u32[]{:S(2)}, u32[]{:S(2)}) %collective-permute-start.16) | collective-permute-done | bytes 442400 | tf_op jit(solution)/shard_map/ppermute | solution.py:513
  69.9 1.8 %collective-permute-start.22 = (f32[216,128]{1,0:T(8,128)S(1)}, f32[216,128]{1,0:T(8,128)S(1)}, u32[]{:S(2)}, u32[]{:S(2)}) collective-permute-start(f32[216,128]{1,0:T(8,128)S(1)} %get-tuple-element.126), channel_id=1, source_target_pairs={{0,6},{1,7},{2,4},{3,5},{4,2},{5,3},{6,0},{7,1},{8,14},{9,15},{10,... | collective-permute-start | bytes 331784 | tf_op jit(solution)/shard_map/ppermute | solution.py:169
  71.7 2.7 %collective-permute-start.24 = (f32[216,128]{1,0:T(8,128)S(1)}, f32[216,128]{1,0:T(8,128)S(1)}, u32[]{:S(2)}, u32[]{:S(2)}) collective-permute-start(f32[216,128]{1,0:T(8,128)S(1)} %get-tuple-element.128), channel_id=1, source_target_pairs={{0,2},{1,3},{2,0},{3,1},{4,6},{5,7},{6,4},{7,5},{8,10},{9,11},{10,... | collective-permute-start | bytes 331784 | tf_op jit(solution)/shard_map/ppermute | solution.py:169
  75.9 1.9 %collective-permute-done.22.refs_3_ = f32[216,128]{1,0:T(8,128)S(1)} collective-permute-done((f32[216,128]{1,0:T(8,128)S(1)}, f32[216,128]{1,0:T(8,128)S(1)}, u32[]{:S(2)}, u32[]{:S(2)}) %collective-permute-start.22) | collective-permute-done | bytes 110624 | tf_op jit(solution)/shard_map/ppermute | solution.py:169
  77.8 3.9 %collective-permute-done.23.refs_2_ = f32[216,128]{1,0:T(8,128)S(1)} collective-permute-done((f32[216,128]{1,0:T(8,128)S(1)}, f32[216,128]{1,0:T(8,128)S(1)}, u32[]{:S(2)}, u32[]{:S(2)}) %collective-permute-start.23) | collective-permute-done | bytes 110624 | tf_op jit(solution)/shard_map/ppermute | solution.py:169
  87.0 2.7 %collective-permute-start.26 = (f32[216,128]{1,0:T(8,128)S(1)}, f32[216,128]{1,0:T(8,128)S(1)}, u32[]{:S(2)}, u32[]{:S(2)}) collective-permute-start(f32[216,128]{1,0:T(8,128)S(1)} %get-tuple-element.133), channel_id=1, source_target_pairs={{0,2},{1,3},{2,0},{3,1},{4,6},{5,7},{6,4},{7,5},{8,10},{9,11},{10,... | collective-permute-start | bytes 331784 | tf_op jit(solution)/shard_map/ppermute | solution.py:169
  93.1 3.7 %collective-permute-done.27.refs_2_ = f32[216,128]{1,0:T(8,128)S(1)} collective-permute-done((f32[216,128]{1,0:T(8,128)S(1)}, f32[216,128]{1,0:T(8,128)S(1)}, u32[]{:S(2)}, u32[]{:S(2)}) %collective-permute-start.27) | collective-permute-done | bytes 110624 | tf_op jit(solution)/shard_map/ppermute | solution.py:169
  101.4 2.1 %collective-permute-start.35 = (f32[216,128]{1,0:T(8,128)S(1)}, f32[216,128]{1,0:T(8,128)S(1)}, u32[]{:S(2)}, u32[]{:S(2)}) collective-permute-start(f32[216,128]{1,0:T(8,128)S(1)} %get-tuple-element.149), channel_id=1, source_target_pairs={{0,6},{1,7},{2,4},{3,5},{4,2},{5,3},{6,0},{7,1},{8,14},{9,15},{10,... | collective-permute-start | bytes 331784 | tf_op jit(solution)/shard_map/ppermute | solution.py:169
  103.5 2.3 %collective-permute-start.33 = (f32[216,128]{1,0:T(8,128)S(1)}, f32[216,128]{1,0:T(8,128)S(1)}, u32[]{:S(2)}, u32[]{:S(2)}) collective-permute-start(f32[216,128]{1,0:T(8,128)S(1)} %get-tuple-element.145), channel_id=1, source_target_pairs={{0,2},{1,3},{2,0},{3,1},{4,6},{5,7},{6,4},{7,5},{8,10},{9,11},{10,... | collective-permute-start | bytes 331784 | tf_op jit(solution)/shard_map/ppermute | solution.py:169
  105.8 5.0 %collective-permute-done.32.other_ref = f32[4,216,128]{2,1,0:T(8,128)S(1)} collective-permute-done((f32[4,216,128]{2,1,0:T(8,128)S(1)}, f32[4,216,128]{2,1,0:T(8,128)S(1)}, u32[]{:S(2)}, u32[]{:S(2)}) %collective-permute-start.32) | collective-permute-done | bytes 442400 | tf_op jit(solution)/shard_map/ppermute | solution.py:513
  110.8 2.3 %collective-permute-done.34.refs_2_ = f32[216,128]{1,0:T(8,128)S(1)} collective-permute-done((f32[216,128]{1,0:T(8,128)S(1)}, f32[216,128]{1,0:T(8,128)S(1)}, u32[]{:S(2)}, u32[]{:S(2)}) %collective-permute-start.34) | collective-permute-done | bytes 110624 | tf_op jit(solution)/shard_map/ppermute | solution.py:169
  115.7 2.1 %collective-permute-start.39 = (f32[216,128]{1,0:T(8,128)S(1)}, f32[216,128]{1,0:T(8,128)S(1)}, u32[]{:S(2)}, u32[]{:S(2)}) collective-permute-start(f32[216,128]{1,0:T(8,128)S(1)} %get-tuple-element.160), channel_id=1, source_target_pairs={{0,6},{1,7},{2,4},{3,5},{4,2},{5,3},{6,0},{7,1},{8,14},{9,15},{10,... | collective-permute-start | bytes 331784 | tf_op jit(solution)/shard_map/ppermute | solution.py:169
  117.9 2.3 %collective-permute-start.37 = (f32[216,128]{1,0:T(8,128)S(1)}, f32[216,128]{1,0:T(8,128)S(1)}, u32[]{:S(2)}, u32[]{:S(2)}) collective-permute-start(f32[216,128]{1,0:T(8,128)S(1)} %get-tuple-element.156), channel_id=1, source_target_pairs={{0,2},{1,3},{2,0},{3,1},{4,6},{5,7},{6,4},{7,5},{8,10},{9,11},{10,... | collective-permute-start | bytes 331784 | tf_op jit(solution)/shard_map/ppermute | solution.py:169
  120.2 6.4 %collective-permute-done.36.other_ref = f32[4,216,128]{2,1,0:T(8,128)S(1)} collective-permute-done((f32[4,216,128]{2,1,0:T(8,128)S(1)}, f32[4,216,128]{2,1,0:T(8,128)S(1)}, u32[]{:S(2)}, u32[]{:S(2)}) %collective-permute-start.36) | collective-permute-done | bytes 442400 | tf_op jit(solution)/shard_map/ppermute | solution.py:513
  127.2 2.2 %collective-permute-start.42 = (f32[216,128]{1,0:T(8,128)S(1)}, f32[216,128]{1,0:T(8,128)S(1)}, u32[]{:S(2)}, u32[]{:S(2)}) collective-permute-start(f32[216,128]{1,0:T(8,128)S(1)} %get-tuple-element.168), channel_id=1, source_target_pairs={{0,6},{1,7},{2,4},{3,5},{4,2},{5,3},{6,0},{7,1},{8,14},{9,15},{10,... | collective-permute-start | bytes 331784 | tf_op jit(solution)/shard_map/ppermute | solution.py:169
  129.4 2.3 %collective-permute-start.40 = (f32[216,128]{1,0:T(8,128)S(1)}, f32[216,128]{1,0:T(8,128)S(1)}, u32[]{:S(2)}, u32[]{:S(2)}) collective-permute-start(f32[216,128]{1,0:T(8,128)S(1)} %get-tuple-element.164), channel_id=1, source_target_pairs={{0,2},{1,3},{2,0},{3,1},{4,6},{5,7},{6,4},{7,5},{8,10},{9,11},{10,... | collective-permute-start | bytes 331784 | tf_op jit(solution)/shard_map/ppermute | solution.py:169
  133.2 1.9 %collective-permute-done.42.refs_4_ = f32[216,128]{1,0:T(8,128)S(1)} collective-permute-done((f32[216,128]{1,0:T(8,128)S(1)}, f32[216,128]{1,0:T(8,128)S(1)}, u32[]{:S(2)}, u32[]{:S(2)}) %collective-permute-start.42) | collective-permute-done | bytes 110624 | tf_op jit(solution)/shard_map/ppermute | solution.py:169
  135.1 3.2 %collective-permute-done.41.refs_3_ = f32[216,128]{1,0:T(8,128)S(1)} collective-permute-done((f32[216,128]{1,0:T(8,128)S(1)}, f32[216,128]{1,0:T(8,128)S(1)}, u32[]{:S(2)}, u32[]{:S(2)}) %collective-permute-start.41) | collective-permute-done | bytes 110624 | tf_op jit(solution)/shard_map/ppermute | solution.py:169
  138.3 2.1 %shard_map.160 = (f32[2,6,48,384]{3,2,1,0:T(8,128)}, f32[48,384]{1,0:T(8,128)}, f32[32,128]{1,0:T(8,128)S(1)}) custom-call(s32[2]{0:T(128)S(1)} %pad_add_fusion.me_ref, f32[2,6]{1,0:T(2,128)S(1)} %copy-done.8, s32[1]{0:T(128)S(6)} %copy.29.count_ref, f32[5,48,384]{2,1,0:T(8,128)S(1)} %copy-done, s32[48,384]{1,0:T(8,128)S(1)} %copy-done.1, ...), custom_call_target="tpu_custom_call" | custom-call | flops 1 | bytes 1 | tf_op jit(solution)/shard_map/pallas_call | solution.py:447
  140.4 9.7 %all_to_all.11 = f32[32,1,128]{2,1,0:T(1,128)S(1)} all-to-all(f32[32,1,128]{2,1,0:T(1,128)S(1)} %bitcast.18), channel_id=1, replica_groups=mesh['gx'=4,'gy'=8] {'gx','gy'}, dimensions={0} | all-to-all | bytes 32768 | tf_op jit(solution)/shard_map/all_to_all | solution.py:538
  (107 shorter events, 46.9 us)
Async XLA Ops:
  2.2 15.5 %collective-permute-start.4 = (f32[6,48,384]{2,1,0:T(8,128)S(1)}, f32[6,48,384]{2,1,0:T(8,128)}, u32[]{:S(2)}, u32[]{:S(2)}) collective-permute-start(f32[6,48,384]{2,1,0:T(8,128)S(1)} %slice_bitcast_fusion.1.refs_0_), channel_id=1, source_target_pairs={{0,16},{8,24},{16,0},{24,8},{1,17},{9,25},{17,1},{25,9},{2,18},{10... | collective-permute-start | bytes 1327112 | tf_op jit(solution)/shard_map/ppermute | solution.py:157
  5.9 11.7 %collective-permute-start.1 = (f32[96,192]{1,0:T(8,128)S(1)}, f32[96,192]{1,0:T(8,128)S(1)}, u32[]{:S(2)}, u32[]{:S(2)}) collective-permute-start(f32[96,192]{1,0:T(8,128)S(1)} %copy.26.refs_0_), channel_id=1, source_target_pairs={{0,16},{8,24},{16,0},{24,8},{1,17},{9,25},{17,1},{25,9},{2,18},{10... | collective-permute-start | bytes 221192 | tf_op jit(solution)/shard_map/ppermute | solution.py:157
  17.7 10.0 %collective-permute-start.9 = (f32[6,48,384]{2,1,0:T(8,128)S(1)}, f32[6,48,384]{2,1,0:T(8,128)S(1)}, u32[]{:S(2)}, u32[]{:S(2)}) collective-permute-start(f32[6,48,384]{2,1,0:T(8,128)S(1)} %slice_bitcast_fusion.refs_0_), channel_id=1, source_target_pairs={{0,8},{8,0},{16,24},{24,16},{1,9},{9,1},{17,25},{25,17},{2,10},{10... | collective-permute-start | bytes 1327112 | tf_op jit(solution)/shard_map/ppermute | solution.py:148
  18.2 17.8 %collective-permute-start.10 = (f32[6,48,384]{2,1,0:T(8,128)S(1)}, f32[6,48,384]{2,1,0:T(8,128)S(1)}, u32[]{:S(2)}, u32[]{:S(2)}) collective-permute-start(f32[6,48,384]{2,1,0:T(8,128)S(1)} %slice_bitcast_fusion.refs_0_), channel_id=1, source_target_pairs={{0,16},{8,24},{16,0},{24,8},{1,17},{9,25},{17,1},{25,9},{2,18},{10... | collective-permute-start | bytes 1327112 | tf_op jit(solution)/shard_map/ppermute | solution.py:157
  26.3 9.6 %collective-permute-start.7 = (f32[216,128]{1,0:T(8,128)S(1)}, f32[216,128]{1,0:T(8,128)S(1)}, u32[]{:S(2)}, u32[]{:S(2)}) collective-permute-start(f32[216,128]{1,0:T(8,128)S(1)} %get-tuple-element.98), channel_id=1, source_target_pairs={{0,4},{1,5},{2,6},{3,7},{4,0},{5,1},{6,2},{7,3},{8,12},{9,13},{10,... | collective-permute-start | bytes 331784 | tf_op jit(solution)/shard_map/ppermute | solution.py:169
  26.3 9.6 %collective-permute-start.6 = (f32[216,128]{1,0:T(8,128)S(1)}, f32[216,128]{1,0:T(8,128)S(1)}, u32[]{:S(2)}, u32[]{:S(2)}) collective-permute-start(f32[216,128]{1,0:T(8,128)S(1)} %get-tuple-element.96), channel_id=1, source_target_pairs={{0,2},{1,3},{2,0},{3,1},{4,6},{5,7},{6,4},{7,5},{8,10},{9,11},{10,... | collective-permute-start | bytes 331784 | tf_op jit(solution)/shard_map/ppermute | solution.py:169
  37.3 12.6 %collective-permute-start.12 = (f32[4,216,128]{2,1,0:T(8,128)S(1)}, f32[4,216,128]{2,1,0:T(8,128)S(1)}, u32[]{:S(2)}, u32[]{:S(2)}) collective-permute-start(f32[4,216,128]{2,1,0:T(8,128)S(1)} %get-tuple-element.106), channel_id=1, source_target_pairs={{0,1},{1,0},{2,3},{3,2},{4,5},{5,4},{6,7},{7,6},{8,9},{9,8},{10,11... | collective-permute-start | bytes 1327112 | tf_op jit(solution)/shard_map/ppermute | solution.py:513
  40.5 9.4 %collective-permute-start.15 = (f32[216,128]{1,0:T(8,128)S(1)}, f32[216,128]{1,0:T(8,128)S(1)}, u32[]{:S(2)}, u32[]{:S(2)}) collective-permute-start(f32[216,128]{1,0:T(8,128)S(1)} %get-tuple-element.112), channel_id=1, source_target_pairs={{0,6},{1,7},{2,4},{3,5},{4,2},{5,3},{6,0},{7,1},{8,14},{9,15},{10,... | collective-permute-start | bytes 331784 | tf_op jit(solution)/shard_map/ppermute | solution.py:169
  43.0 9.5 %collective-permute-start.14 = (f32[216,128]{1,0:T(8,128)S(1)}, f32[216,128]{1,0:T(8,128)S(1)}, u32[]{:S(2)}, u32[]{:S(2)}) collective-permute-start(f32[216,128]{1,0:T(8,128)S(1)} %get-tuple-element.110), channel_id=1, source_target_pairs={{0,4},{1,5},{2,6},{3,7},{4,0},{5,1},{6,2},{7,3},{8,12},{9,13},{10,... | collective-permute-start | bytes 331784 | tf_op jit(solution)/shard_map/ppermute | solution.py:169
  43.0 9.5 %collective-permute-start.13 = (f32[216,128]{1,0:T(8,128)S(1)}, f32[216,128]{1,0:T(8,128)S(1)}, u32[]{:S(2)}, u32[]{:S(2)}) collective-permute-start(f32[216,128]{1,0:T(8,128)S(1)} %get-tuple-element.108), channel_id=1, source_target_pairs={{0,2},{1,3},{2,0},{3,1},{4,6},{5,7},{6,4},{7,5},{8,10},{9,11},{10,... | collective-permute-start | bytes 331784 | tf_op jit(solution)/shard_map/ppermute | solution.py:169
  53.9 12.1 %collective-permute-start.16 = (f32[4,216,128]{2,1,0:T(8,128)S(1)}, f32[4,216,128]{2,1,0:T(8,128)S(1)}, u32[]{:S(2)}, u32[]{:S(2)}) collective-permute-start(f32[4,216,128]{2,1,0:T(8,128)S(1)} %get-tuple-element.117), channel_id=1, source_target_pairs={{0,1},{1,0},{2,3},{3,2},{4,5},{5,4},{6,7},{7,6},{8,9},{9,8},{10,11... | collective-permute-start | bytes 1327112 | tf_op jit(solution)/shard_map/ppermute | solution.py:513
  57.3 9.5 %collective-permute-start.18 = (f32[216,128]{1,0:T(8,128)S(1)}, f32[216,128]{1,0:T(8,128)S(1)}, u32[]{:S(2)}, u32[]{:S(2)}) collective-permute-start(f32[216,128]{1,0:T(8,128)S(1)} %get-tuple-element.121), channel_id=1, source_target_pairs={{0,4},{1,5},{2,6},{3,7},{4,0},{5,1},{6,2},{7,3},{8,12},{9,13},{10,... | collective-permute-start | bytes 331784 | tf_op jit(solution)/shard_map/ppermute | solution.py:169
  57.3 9.5 %collective-permute-start.17 = (f32[216,128]{1,0:T(8,128)S(1)}, f32[216,128]{1,0:T(8,128)S(1)}, u32[]{:S(2)}, u32[]{:S(2)}) collective-permute-start(f32[216,128]{1,0:T(8,128)S(1)} %get-tuple-element.119), channel_id=1, source_target_pairs={{0,2},{1,3},{2,0},{3,1},{4,6},{5,7},{6,4},{7,5},{8,10},{9,11},{10,... | collective-permute-start | bytes 331784 | tf_op jit(solution)/shard_map/ppermute | solution.py:169
  67.7 13.9 %collective-permute-start.21 = (f32[6,48,384]{2,1,0:T(8,128)S(1)}, f32[6,48,384]{2,1,0:T(8,128)S(1)}, u32[]{:S(2)}, u32[]{:S(2)}) collective-permute-start(f32[6,48,384]{2,1,0:T(8,128)S(1)} %shard_map.148.refs_0_), channel_id=1, source_target_pairs={{0,16},{8,24},{16,0},{24,8},{1,17},{9,25},{17,1},{25,9},{2,18},{10... | collective-permute-start | bytes 1327112 | tf_op jit(solution)/shard_map/ppermute | solution.py:157
  69.9 7.9 %collective-permute-start.22 = (f32[216,128]{1,0:T(8,128)S(1)}, f32[216,128]{1,0:T(8,128)S(1)}, u32[]{:S(2)}, u32[]{:S(2)}) collective-permute-start(f32[216,128]{1,0:T(8,128)S(1)} %get-tuple-element.126), channel_id=1, source_target_pairs={{0,6},{1,7},{2,4},{3,5},{4,2},{5,3},{6,0},{7,1},{8,14},{9,15},{10,... | collective-permute-start | bytes 331784 | tf_op jit(solution)/shard_map/ppermute | solution.py:169
  71.7 10.0 %collective-permute-start.23 = (f32[216,128]{1,0:T(8,128)S(1)}, f32[216,128]{1,0:T(8,128)S(1)}, u32[]{:S(2)}, u32[]{:S(2)}) collective-permute-start(f32[216,128]{1,0:T(8,128)S(1)} %get-tuple-element.127), channel_id=1, source_target_pairs={{0,4},{1,5},{2,6},{3,7},{4,0},{5,1},{6,2},{7,3},{8,12},{9,13},{10,... | collective-permute-start | bytes 331784 | tf_op jit(solution)/shard_map/ppermute | solution.py:169
  71.7 10.0 %collective-permute-start.24 = (f32[216,128]{1,0:T(8,128)S(1)}, f32[216,128]{1,0:T(8,128)S(1)}, u32[]{:S(2)}, u32[]{:S(2)}) collective-permute-start(f32[216,128]{1,0:T(8,128)S(1)} %get-tuple-element.128), channel_id=1, source_target_pairs={{0,2},{1,3},{2,0},{3,1},{4,6},{5,7},{6,4},{7,5},{8,10},{9,11},{10,... | collective-permute-start | bytes 331784 | tf_op jit(solution)/shard_map/ppermute | solution.py:169
  83.0 13.8 %collective-permute-start.30 = (f32[6,48,384]{2,1,0:T(8,128)S(1)}, f32[6,48,384]{2,1,0:T(8,128)S(1)}, u32[]{:S(2)}, u32[]{:S(2)}) collective-permute-start(f32[6,48,384]{2,1,0:T(8,128)S(1)} %shard_map.153.refs_0_), channel_id=1, source_target_pairs={{0,16},{8,24},{16,0},{24,8},{1,17},{9,25},{17,1},{25,9},{2,18},{10... | collective-permute-start | bytes 1327112 | tf_op jit(solution)/shard_map/ppermute | solution.py:157
  85.2 7.9 %collective-permute-start.28 = (f32[216,128]{1,0:T(8,128)S(1)}, f32[216,128]{1,0:T(8,128)S(1)}, u32[]{:S(2)}, u32[]{:S(2)}) collective-permute-start(f32[216,128]{1,0:T(8,128)S(1)} %get-tuple-element.137), channel_id=1, source_target_pairs={{0,6},{1,7},{2,4},{3,5},{4,2},{5,3},{6,0},{7,1},{8,14},{9,15},{10,... | collective-permute-start | bytes 331784 | tf_op jit(solution)/shard_map/ppermute | solution.py:169
  87.0 9.8 %collective-permute-start.27 = (f32[216,128]{1,0:T(8,128)S(1)}, f32[216,128]{1,0:T(8,128)S(1)}, u32[]{:S(2)}, u32[]{:S(2)}) collective-permute-start(f32[216,128]{1,0:T(8,128)S(1)} %get-tuple-element.135), channel_id=1, source_target_pairs={{0,4},{1,5},{2,6},{3,7},{4,0},{5,1},{6,2},{7,3},{8,12},{9,13},{10,... | collective-permute-start | bytes 331784 | tf_op jit(solution)/shard_map/ppermute | solution.py:169
  87.0 9.8 %collective-permute-start.26 = (f32[216,128]{1,0:T(8,128)S(1)}, f32[216,128]{1,0:T(8,128)S(1)}, u32[]{:S(2)}, u32[]{:S(2)}) collective-permute-start(f32[216,128]{1,0:T(8,128)S(1)} %get-tuple-element.133), channel_id=1, source_target_pairs={{0,2},{1,3},{2,0},{3,1},{4,6},{5,7},{6,4},{7,5},{8,10},{9,11},{10,... | collective-permute-start | bytes 331784 | tf_op jit(solution)/shard_map/ppermute | solution.py:169
  98.2 12.6 %collective-permute-start.32 = (f32[4,216,128]{2,1,0:T(8,128)S(1)}, f32[4,216,128]{2,1,0:T(8,128)S(1)}, u32[]{:S(2)}, u32[]{:S(2)}) collective-permute-start(f32[4,216,128]{2,1,0:T(8,128)S(1)} %get-tuple-element.143), channel_id=1, source_target_pairs={{0,1},{1,0},{2,3},{3,2},{4,5},{5,4},{6,7},{7,6},{8,9},{9,8},{10,11... | collective-permute-start | bytes 1327112 | tf_op jit(solution)/shard_map/ppermute | solution.py:513
  101.4 9.4 %collective-permute-start.35 = (f32[216,128]{1,0:T(8,128)S(1)}, f32[216,128]{1,0:T(8,128)S(1)}, u32[]{:S(2)}, u32[]{:S(2)}) collective-permute-start(f32[216,128]{1,0:T(8,128)S(1)} %get-tuple-element.149), channel_id=1, source_target_pairs={{0,6},{1,7},{2,4},{3,5},{4,2},{5,3},{6,0},{7,1},{8,14},{9,15},{10,... | collective-permute-start | bytes 331784 | tf_op jit(solution)/shard_map/ppermute | solution.py:169
  103.5 9.6 %collective-permute-start.34 = (f32[216,128]{1,0:T(8,128)S(1)}, f32[216,128]{1,0:T(8,128)S(1)}, u32[]{:S(2)}, u32[]{:S(2)}) collective-permute-start(f32[216,128]{1,0:T(8,128)S(1)} %get-tuple-element.147), channel_id=1, source_target_pairs={{0,4},{1,5},{2,6},{3,7},{4,0},{5,1},{6,2},{7,3},{8,12},{9,13},{10,... | collective-permute-start | bytes 331784 | tf_op jit(solution)/shard_map/ppermute | solution.py:169
  103.5 9.6 %collective-permute-start.33 = (f32[216,128]{1,0:T(8,128)S(1)}, f32[216,128]{1,0:T(8,128)S(1)}, u32[]{:S(2)}, u32[]{:S(2)}) collective-permute-start(f32[216,128]{1,0:T(8,128)S(1)} %get-tuple-element.145), channel_id=1, source_target_pairs={{0,2},{1,3},{2,0},{3,1},{4,6},{5,7},{6,4},{7,5},{8,10},{9,11},{10,... | collective-permute-start | bytes 331784 | tf_op jit(solution)/shard_map/ppermute | solution.py:169
  114.5 12.1 %collective-permute-start.36 = (f32[4,216,128]{2,1,0:T(8,128)S(1)}, f32[4,216,128]{2,1,0:T(8,128)S(1)}, u32[]{:S(2)}, u32[]{:S(2)}) collective-permute-start(f32[4,216,128]{2,1,0:T(8,128)S(1)} %get-tuple-element.154), channel_id=1, source_target_pairs={{0,1},{1,0},{2,3},{3,2},{4,5},{5,4},{6,7},{7,6},{8,9},{9,8},{10,11... | collective-permute-start | bytes 1327112 | tf_op jit(solution)/shard_map/ppermute | solution.py:513
  115.7 13.7 %collective-permute-start.39 = (f32[216,128]{1,0:T(8,128)S(1)}, f32[216,128]{1,0:T(8,128)S(1)}, u32[]{:S(2)}, u32[]{:S(2)}) collective-permute-start(f32[216,128]{1,0:T(8,128)S(1)} %get-tuple-element.160), channel_id=1, source_target_pairs={{0,6},{1,7},{2,4},{3,5},{4,2},{5,3},{6,0},{7,1},{8,14},{9,15},{10,... | collective-permute-start | bytes 331784 | tf_op jit(solution)/shard_map/ppermute | solution.py:169
  117.9 14.6 %collective-permute-start.38 = (f32[216,128]{1,0:T(8,128)S(1)}, f32[216,128]{1,0:T(8,128)S(1)}, u32[]{:S(2)}, u32[]{:S(2)}) collective-permute-start(f32[216,128]{1,0:T(8,128)S(1)} %get-tuple-element.158), channel_id=1, source_target_pairs={{0,4},{1,5},{2,6},{3,7},{4,0},{5,1},{6,2},{7,3},{8,12},{9,13},{10,... | collective-permute-start | bytes 331784 | tf_op jit(solution)/shard_map/ppermute | solution.py:169
  117.9 14.6 %collective-permute-start.37 = (f32[216,128]{1,0:T(8,128)S(1)}, f32[216,128]{1,0:T(8,128)S(1)}, u32[]{:S(2)}, u32[]{:S(2)}) collective-permute-start(f32[216,128]{1,0:T(8,128)S(1)} %get-tuple-element.156), channel_id=1, source_target_pairs={{0,2},{1,3},{2,0},{3,1},{4,6},{5,7},{6,4},{7,5},{8,10},{9,11},{10,... | collective-permute-start | bytes 331784 | tf_op jit(solution)/shard_map/ppermute | solution.py:169
  127.2 7.9 %collective-permute-start.42 = (f32[216,128]{1,0:T(8,128)S(1)}, f32[216,128]{1,0:T(8,128)S(1)}, u32[]{:S(2)}, u32[]{:S(2)}) collective-permute-start(f32[216,128]{1,0:T(8,128)S(1)} %get-tuple-element.168), channel_id=1, source_target_pairs={{0,6},{1,7},{2,4},{3,5},{4,2},{5,3},{6,0},{7,1},{8,14},{9,15},{10,... | collective-permute-start | bytes 331784 | tf_op jit(solution)/shard_map/ppermute | solution.py:169
  129.4 8.9 %collective-permute-start.41 = (f32[216,128]{1,0:T(8,128)S(1)}, f32[216,128]{1,0:T(8,128)S(1)}, u32[]{:S(2)}, u32[]{:S(2)}) collective-permute-start(f32[216,128]{1,0:T(8,128)S(1)} %get-tuple-element.166), channel_id=1, source_target_pairs={{0,4},{1,5},{2,6},{3,7},{4,0},{5,1},{6,2},{7,3},{8,12},{9,13},{10,... | collective-permute-start | bytes 331784 | tf_op jit(solution)/shard_map/ppermute | solution.py:169
  129.4 8.9 %collective-permute-start.40 = (f32[216,128]{1,0:T(8,128)S(1)}, f32[216,128]{1,0:T(8,128)S(1)}, u32[]{:S(2)}, u32[]{:S(2)}) collective-permute-start(f32[216,128]{1,0:T(8,128)S(1)} %get-tuple-element.164), channel_id=1, source_target_pairs={{0,2},{1,3},{2,0},{3,1},{4,6},{5,7},{6,4},{7,5},{8,10},{9,11},{10,... | collective-permute-start | bytes 331784 | tf_op jit(solution)/shard_map/ppermute | solution.py:169
  (22 other events, 233.7 us)

commit v5 on v4

--- a/solution.py
+++ b/solution.py
@@ -54,17 +54,17 @@
             out.append(joined)
         return out
 
-    def unpack_rest(self, ref, place):
+    def unpack_rest(self, ref, place, base=0):
         pieces = []
         for group in range(self.groups):
             pack, side = divmod(group, self.sides)
-            start = self.full * self.rows + pack * SUB
+            start = base + self.full * self.rows + pack * SUB
             pieces.append(turn(ref[start : start + SUB, :], self.moved(place, side)))
         return jnp.concatenate(pieces, axis=0)
 
-    def store_rest(self, ref, packs):
+    def store_rest(self, ref, packs, base=0):
         for pack, value in enumerate(packs):
-            start = self.full * self.rows + pack * SUB
+            start = base + self.full * self.rows + pack * SUB
             ref[start : start + SUB, :] = value
 
     def send_tiles(self, tiles_ref, device, out_ref):
@@ -74,15 +74,16 @@
             tile = tiles_ref[self.parts * self.full + device // self.sides]
             self.store_rest(out_ref, self.pack_rest(tile, device % self.sides))
 
-    def take_tiles(self, in_ref, device, tiles_ref):
+    def take_tiles(self, in_ref, device, tiles_ref, base, tile_base):
         for i in range(self.full):
-            tiles_ref[device * self.full + i] = in_ref[i * self.rows : (i + 1) * self.rows, :]
+            start = base + i * self.rows
+            tiles_ref[tile_base + device * self.full + i] = in_ref[start : start + self.rows, :]
         if self.rest:
             place = device % self.sides
-            index = self.parts * self.full + device // self.sides
+            index = tile_base + self.parts * self.full + device // self.sides
             lane_side = lax.broadcasted_iota(jnp.int32, (self.rows, LANES), 1) // self.rest
             tiles_ref[index] = jnp.where(
-                lane_side == place, self.unpack_rest(in_ref, place), tiles_ref[index]
+                lane_side == place, self.unpack_rest(in_ref, place, base), tiles_ref[index]
             )
 
     @property
@@ -93,6 +94,26 @@
     def blocks_out(self):
         shape = jax.ShapeDtypeStruct((self.width, LANES), jnp.float32)
         return [shape] * self.parts
+
+
+class Stack:
+    def __init__(self, plans):
+        self.rows, self.cols, self.parts = plans[0].rows, plans[0].cols, plans[0].parts
+        self.blocks = plans[0].blocks
+        self.members = []
+        self.fields = self.width = self.columns = 0
+        for plan in plans:
+            self.members.append((plan, self.width, self.fields * self.blocks, self.columns))
+            self.fields += plan.fields
+            self.width += plan.width
+            self.columns += plan.columns
+
+    def take_tiles(self, in_ref, device, tiles_ref):
+        for plan, base, tile_base, _ in self.members:
+            plan.take_tiles(in_ref, device, tiles_ref, base, tile_base)
+
+    tiles = Plan.tiles
+    blocks_out = Plan.blocks_out
 
 
 def part_of(me_ref, mask):
@@ -262,41 +283,49 @@
     )
 
 
-def meridional(plan, me, lines, y_high, y_low):
-    rows, parts = plan.rows, plan.parts
+def meridional(stack, me, lines, y_high, y_low):
+    rows, parts = stack.rows, stack.parts
 
     def kernel(me_ref, high_ref, low_ref, *refs):
-        in_refs, out_refs, lines_ref, solved_ref = refs[:parts], refs[parts:-2], refs[-2], refs[-1]
-        for mask in range(parts):
-            place = pl.ds(pl.multiple_of(part_of(me_ref, mask) * rows, rows), rows)
-            for i in range(plan.full):
-                lanes = slice(i * LANES, (i + 1) * LANES)
-                lines_ref[place, lanes] = in_refs[mask][i * rows : (i + 1) * rows, :]
-            if plan.rest:
-                lines_ref[place, plan.full * LANES :] = plan.unpack_rest(in_refs[mask], 0)
+        in_refs, out_refs = refs[: len(lines)], refs[len(lines) : -2]
+        lines_ref, solved_ref = refs[-2:]
+        for number, (plan, _, _, first) in enumerate(stack.members):
+            for mask in range(parts):
+                ref = in_refs[number * parts + mask]
+                place = pl.ds(pl.multiple_of(part_of(me_ref, mask) * rows, rows), rows)
+                for i in range(plan.full):
+                    lanes = slice(first + i * LANES, first + (i + 1) * LANES)
+                    lines_ref[place, lanes] = ref[i * rows : (i + 1) * rows, :]
+                if plan.rest:
+                    lanes = slice(first + plan.full * LANES, first + plan.columns)
+                    lines_ref[place, lanes] = plan.unpack_rest(ref, 0)
         solved_ref[...] = dot_split((high_ref[...], low_ref[...]), split(lines_ref[...]))
-        for other in range(2):
-            for part in range(parts):
-                start = (other * parts + part) * rows
-                for i in range(plan.full):
-                    lanes = slice(i * LANES, (i + 1) * LANES)
-                    out_refs[other][part, i * rows : (i + 1) * rows, :] = solved_ref[
-                        start : start + rows, lanes
-                    ]
-                if plan.rest:
-                    last = solved_ref[start : start + rows, plan.full * LANES :]
-                    plan.store_rest(out_refs[other].at[part], plan.pack_rest(last, 0))
-
-    shape = jax.ShapeDtypeStruct((parts, plan.width, LANES), jnp.float32)
+        for plan, base, _, first in stack.members:
+            for other in range(2):
+                for part in range(parts):
+                    start = (other * parts + part) * rows
+                    for i in range(plan.full):
+                        out = base + i * rows
+                        out_refs[other][part, out : out + rows, :] = solved_ref[
+                            start : start + rows, first + i * LANES : first + (i + 1) * LANES
+                        ]
+                    if plan.rest:
+                        last = solved_ref[
+                            start : start + rows, first + plan.full * LANES : first + plan.columns
+                        ]
+                        packs = plan.pack_rest(last, 0)
+                        plan.store_rest(out_refs[other].at[part], packs, base)
+
+    shape = jax.ShapeDtypeStruct((parts, stack.width, LANES), jnp.float32)
     return call(
         kernel,
         [shape, shape],
         [me, y_high, y_low] + lines,
         scalars=(0,),
-        flops=12 * (parts * rows) ** 2 * plan.columns,
+        flops=12 * (parts * rows) ** 2 * stack.columns,
         scratch=[
-            pltpu.VMEM((parts * rows, plan.columns), jnp.float32),
-            pltpu.VMEM((2 * parts * rows, plan.columns), jnp.float32),
+            pltpu.VMEM((parts * rows, stack.columns), jnp.float32),
+            pltpu.VMEM((2 * parts * rows, stack.columns), jnp.float32),
         ],
     )
 
@@ -476,53 +505,72 @@
     chunks = kinds
     if not plan.fits:
         plan, chunks = Plan(kinds * levels, rows, cols, gy_count // 2), 1
+    plans = [[plan] for _ in range(chunks)]
+    half = Plan(plan.fields // 2, rows, cols, gy_count // 2)
+    if plan.fields % 2 == 0 and half.fits and half.full:
+        plans[0] = [half, half]
     me = jnp.stack([lax.axis_index("gx"), lax.axis_index("gy")]).astype(jnp.int32)
     x_parts = prepare_x(x_inverse)
-    fields = [control[0, 0] if chunks > 1 else control.reshape(plan.fields, rows, cols)]
-    if chunks > 1:
-        control = after(control, fields[0])
-        fields += [control[0, kind] for kind in range(1, kinds)]
     y_columns = y_inverse.reshape(y_inverse.shape[0], gy_count // 2, 2, rows)
     y_columns = jnp.where(me[1] % 2 == 0, y_columns[:, :, 0], y_columns[:, :, 1])
     y_columns = y_columns.reshape(y_inverse.shape[0], -1)
     y_far = gather_far(y_columns, "gx", gx_count)
+    whole = control.reshape(kinds * levels, rows, cols)
+    fields = [[]]
+    for part in plans[0]:
+        fields[0].append(whole[len(fields[0]) * part.fields : (len(fields[0]) + 1) * part.fields])
+        whole = after(whole, fields[0][-1])
     y_held = gather_near(y_columns, "gx", gx_count) + y_far
     y_parts = prepare_y([m for m, _ in y_held], [p for _, p in y_held], me, rows)
     side_pairs = [(i, i ^ 1) for i in range(gy_count)]
     result = None
     for step in range(STEPS):
-        own, other, sent = [], [], []
+        own, other, lines = [], [], []
         for chunk in range(chunks):
-            near = gather_near(fields[chunk], "gx", gx_count)
-            total = zonal_start(plan, near, me, *x_parts)
-            if sent:
-                hold = [total, y_parts[0]] + lines
-            elif step == 0:
-                hold = [total, y_far[0][1]] + fields[1:]
-            else:
-                hold = [total] + returned[::-1]
-            far = gather_far(fields[chunk], "gx", gx_count, hold)
-            if own:
-                total = after(total, own[-1])
-            packed = zonal_end(plan, total, far, me, *x_parts, sea_mask)
-            sent.append(exchange(packed, "gy", gy_count))
-            ready = other[-1] if other else y_parts[0]
-            lines = [after(line, ready) for line in sent[chunk]]
-            for_own, for_other = meridional(plan, me, lines, *y_parts)
+            held_back, lines, totals = lines, [], []
+            for part, piece in zip(plans[chunk], fields[chunk]):
+                near = gather_near(piece, "gx", gx_count)
+                totals.append(zonal_start(part, near, me, *x_parts))
+            for number, (part, piece) in enumerate(zip(plans[chunk], fields[chunk])):
+                total = totals[number]
+                hold = [total]
+                if chunk > 0:
+                    hold += [y_parts[0]] + held_back
+                elif step > 0:
+                    hold += returned[::-1]
+                else:
+                    hold += lines
+                    if number > 0:
+                        hold += [y_far[0][1]] + [pieces[0] for pieces in fields[1:]]
+                far = gather_far(piece, "gx", gx_count, hold)
+                if own:
+                    total = after(total, own[-1])
+                packed = zonal_end(part, total, far, me, *x_parts, sea_mask)
+                if step == 0 and len(fields) < chunks:
+                    whole = after(whole, packed[0], y_far[0][1])
+                    for later in range(1, chunks):
+                        start = later * plan.fields
+                        fields.append([whole[start : start + plan.fields]])
+                ready = other[-1] if other else y_parts[0] if number else totals[-1]
+                lines += [after(line, ready) for line in exchange(packed, "gy", gy_count)]
+            stack = Stack(plans[chunk])
+            for_own, for_other = meridional(stack, me, lines, *y_parts)
             own.append(for_own)
             other.append(lax.ppermute(for_other, "gy", side_pairs))
         for chunk in range(chunks):
+            stack = Stack(plans[chunk])
             if chunk == 0:
                 own[chunk] = after(own[chunk], own[-1])
             elif step < STEPS - 1:
-                own[chunk] = after(own[chunk], fields[chunk - 1])
-            returned = exchange(add_sides(plan, me, own[chunk], other[chunk]), "gy", gy_count)
+                own[chunk] = after(own[chunk], *fields[chunk - 1])
+            returned = exchange(add_sides(stack, me, own[chunk], other[chunk]), "gy", gy_count)
             if chunk < chunks - 1:
                 returned = [after(block, other[-1]) for block in returned]
             if step < STEPS - 1 or chunk < chunks - 1:
-                fields[chunk] = vertical(plan, me, returned, kappa, sea_mask, levels)
+                fields[chunk] = [vertical(stack, me, returned, kappa, sea_mask, levels)]
             else:
-                returned = [after(block, *fields[:chunk]) for block in returned]
+                tempers = [pieces[0] for pieces in fields[:chunk]]
+                returned = [after(block, *tempers) for block in returned]
                 obs = (
                     obs_owner.reshape(1, -1),
                     tile_index.reshape(1, -1),
@@ -531,9 +579,10 @@
                     obs_owner,
                 )
                 result = finish(
-                    plan, me, returned, fields[0] if chunks > 1 else None, kappa, sea_mask, sigma,
-                    beta, ssh_coef, obs, devices,
+                    stack, me, returned, tempers[0] if chunks > 1 else None, kappa, sea_mask,
+                    sigma, beta, ssh_coef, obs, devices,
                 )
+        plans = [[plan] for _ in range(chunks)]
     increments, height, outgoing = result
     arrived = lax.all_to_all(outgoing, ("gx", "gy"), split_axis=0, concat_axis=0, tiled=True)
     return increments[None], height[None], receive(arrived, kinds * levels + 1)

time: 151 us -> 160 us (1.060)
  starting transfers between devices: 48.7 us -> 55.5 us
  Pallas kernels: 27.4 us -> 29 us
    ppermute x24 -> x27, starting transfers between devices: 35.6 us -> 41.8 us  [exchange(): out[mask] = lax.ppermute(blocks[mask], axis, pairs)]
    squeeze x2 -> x0, local copies, waits for them, and re-layouts: 2.09 us -> none  [the longest x1 1.05 us: body(): fields += [control[0, kind] for kind in range(1, kinds)]]
    slice x0 -> x3, local copies, waits for them, and re-layouts: none -> 1.93 us  [the longest x2 1.9 us: body(): whole[len(fields[0]) * part.fields:(len(fields[0]) + 1) * part.fields]]
    ppermute x10 -> x12, waiting for transfers between devices: 4.86 us -> 2.94 us  [gather_far(): lax.ppermute(piece, axis, pairs)]
    ppermute x24 -> x27, waiting for transfers between devices: 32.2 us -> 33.9 us  [exchange(): out[mask] = lax.ppermute(blocks[mask], axis, pairs)]
    pallas_call x22 -> x24, Pallas kernels: 25.3 us -> 26.9 us  [call(): pl.pallas_call(kernel, out_shape=out_shape, in_specs=specs, out_specs=[ou...]
    unnamed x24 -> x28, local copies, waits for them, and re-layouts: 4.61 us -> 5.14 us
    ppermute x10 -> x12, starting transfers between devices: 7.09 us -> 7.36 us  [gather_far(): lax.ppermute(piece, axis, pairs)]
  transfers between devices with their start and end apart: 43 -> 49, of which waited for: 17 -> 22; matrix products, arithmetic and copies ran while one was open for 2% -> 2% of each run, Pallas kernels for 14% -> 14%
where the time goes in v5:
time: 160 us; the launch traced here: 159 us
  waiting for transfers between devices  55.9 us (35%)
  starting transfers between devices  55.5 us (35%)
  Pallas kernels  29 us (18%)
  blocking collectives  10.1 us (6%)
  local copies, waits for them, and re-layouts  7.15 us (4%)
  between operations  1.66 us (1%)
    ppermute x27, starting transfers between devices, exchange(): out[mask] = lax.ppermute(blocks[mask], axis, pairs)  41.8 us
    ppermute x27, waiting for transfers between devices, exchange(): out[mask] = lax.ppermute(blocks[mask], axis, pairs)  33.9 us
    pallas_call x24, Pallas kernels, call(): pl.pallas_call(kernel, out_shape=out_shape, in_specs=specs, out_specs=[ou...  26.9 us
    ppermute x4, waiting for transfers between devices, body(): other.append(lax.ppermute(for_other, 'gy', side_pairs))  19 us
    all_to_all x1, blocking collectives, body(): lax.all_to_all(outgoing, ('gx', 'gy'), split_axis=0, concat_axis=0, tiled...  10.1 us
    ppermute x12, starting transfers between devices, gather_far(): lax.ppermute(piece, axis, pairs)  7.36 us
    unnamed x28, local copies, waits for them, and re-layouts  5.14 us
    ppermute x4, starting transfers between devices, body(): other.append(lax.ppermute(for_other, 'gy', side_pairs))  4.29 us
  transfers between devices with their start and end apart: 49, of which 22 were waited for; matrix products, arithmetic and copies ran while one was open for 2% of the time, Pallas kernels for 14%

profile of v5, /device:TPU:0, one launch (start us, length us, event | category | flops | bytes accessed | tf_op | source)
XLA Modules:
  0.0 159.4 jit_solution(17560601197859602888)
XLA Ops:
  2.1 2.6 %collective-permute-start.4 = (f32[3,48,384]{2,1,0:T(8,128)S(1)}, f32[3,48,384]{2,1,0:T(8,128)S(1)}, u32[]{:S(2)}, u32[]{:S(2)}) collective-permute-start(f32[3,48,384]{2,1,0:T(8,128)S(1)} %slice.22.refs_0_), channel_id=1, source_target_pairs={{0,16},{8,24},{16,0},{24,8},{1,17},{9,25},{17,1},{25,9},{2,18},{10... | collective-permute-start | bytes 663560 | tf_op jit(solution)/shard_map/ppermute | solution.py:178
  13.5 2.0 %collective-permute-start.10 = (f32[3,48,384]{2,1,0:T(8,128)S(1)}, f32[3,48,384]{2,1,0:T(8,128)S(1)}, u32[]{:S(2)}, u32[]{:S(2)}) collective-permute-start(f32[3,48,384]{2,1,0:T(8,128)S(1)} %slice.18.refs_0_), channel_id=1, source_target_pairs={{0,16},{8,24},{16,0},{24,8},{1,17},{9,25},{17,1},{25,9},{2,18},{10... | collective-permute-start | bytes 663560 | tf_op jit(solution)/shard_map/ppermute | solution.py:178
  17.2 1.9 %collective-permute-done.1.refs_2_ = f32[96,192]{1,0:T(8,128)S(1)} collective-permute-done((f32[96,192]{1,0:T(8,128)S(1)}, f32[96,192]{1,0:T(8,128)S(1)}, u32[]{:S(2)}, u32[]{:S(2)}) %collective-permute-start.1) | collective-permute-done | bytes 73760 | tf_op jit(solution)/shard_map/ppermute | solution.py:178
  19.3 4.1 %collective-permute-start.9 = (f32[112,128]{1,0:T(8,128)S(1)}, f32[112,128]{1,0:T(8,128)S(1)}, u32[]{:S(2)}, u32[]{:S(2)}) collective-permute-start(f32[112,128]{1,0:T(8,128)S(1)} %get-tuple-element.111), channel_id=1, source_target_pairs={{0,6},{1,7},{2,4},{3,5},{4,2},{5,3},{6,0},{7,1},{8,14},{9,15},{10,... | collective-permute-start | bytes 172040 | tf_op jit(solution)/shard_map/ppermute | solution.py:190
  23.4 2.3 %collective-permute-done.9.refs_3_ = f32[112,128]{1,0:T(8,128)S(1)} collective-permute-done((f32[112,128]{1,0:T(8,128)S(1)}, f32[112,128]{1,0:T(8,128)S(1)}, u32[]{:S(2)}, u32[]{:S(2)}) %collective-permute-start.9) | collective-permute-done | bytes 57376 | tf_op jit(solution)/shard_map/ppermute | solution.py:190
  32.7 4.2 %collective-permute-start.14 = (f32[112,128]{1,0:T(8,128)S(1)}, f32[112,128]{1,0:T(8,128)S(1)}, u32[]{:S(2)}, u32[]{:S(2)}) collective-permute-start(f32[112,128]{1,0:T(8,128)S(1)} %get-tuple-element.122), channel_id=1, source_target_pairs={{0,6},{1,7},{2,4},{3,5},{4,2},{5,3},{6,0},{7,1},{8,14},{9,15},{10,... | collective-permute-start | bytes 172040 | tf_op jit(solution)/shard_map/ppermute | solution.py:190
  39.5 2.5 %collective-permute-done.13.refs_6_ = f32[112,128]{1,0:T(8,128)S(1)} collective-permute-done((f32[112,128]{1,0:T(8,128)S(1)}, f32[112,128]{1,0:T(8,128)S(1)}, u32[]{:S(2)}, u32[]{:S(2)}) %collective-permute-start.13) | collective-permute-done | bytes 57376 | tf_op jit(solution)/shard_map/ppermute | solution.py:190
  48.6 2.2 %collective-permute-start.21 = (f32[216,128]{1,0:T(8,128)S(1)}, f32[216,128]{1,0:T(8,128)S(1)}, u32[]{:S(2)}, u32[]{:S(2)}) collective-permute-start(f32[216,128]{1,0:T(8,128)S(1)} %get-tuple-element.134), channel_id=1, source_target_pairs={{0,6},{1,7},{2,4},{3,5},{4,2},{5,3},{6,0},{7,1},{8,14},{9,15},{10,... | collective-permute-start | bytes 331784 | tf_op jit(solution)/shard_map/ppermute | solution.py:190
  51.1 2.0 %collective-permute-start.19 = (f32[216,128]{1,0:T(8,128)S(1)}, f32[216,128]{1,0:T(8,128)S(1)}, u32[]{:S(2)}, u32[]{:S(2)}) collective-permute-start(f32[216,128]{1,0:T(8,128)S(1)} %get-tuple-element.130), channel_id=1, source_target_pairs={{0,2},{1,3},{2,0},{3,1},{4,6},{5,7},{6,4},{7,5},{8,10},{9,11},{10,... | collective-permute-start | bytes 331784 | tf_op jit(solution)/shard_map/ppermute | solution.py:190
  53.1 5.2 %collective-permute-done.18.other_ref = f32[4,224,128]{2,1,0:T(8,128)S(1)} collective-permute-done((f32[4,224,128]{2,1,0:T(8,128)S(1)}, f32[4,224,128]{2,1,0:T(8,128)S(1)}, u32[]{:S(2)}, u32[]{:S(2)}) %collective-permute-start.18) | collective-permute-done | bytes 458784 | tf_op jit(solution)/shard_map/ppermute | solution.py:559
  58.3 3.1 %collective-permute-done.20.refs_2_ = f32[216,128]{1,0:T(8,128)S(1)} collective-permute-done((f32[216,128]{1,0:T(8,128)S(1)}, f32[216,128]{1,0:T(8,128)S(1)}, u32[]{:S(2)}, u32[]{:S(2)}) %collective-permute-start.20) | collective-permute-done | bytes 110624 | tf_op jit(solution)/shard_map/ppermute | solution.py:190
  63.8 2.2 %collective-permute-start.25 = (f32[224,128]{1,0:T(8,128)S(1)}, f32[224,128]{1,0:T(8,128)S(1)}, u32[]{:S(2)}, u32[]{:S(2)}) collective-permute-start(f32[224,128]{1,0:T(8,128)S(1)} %get-tuple-element.145), channel_id=1, source_target_pairs={{0,6},{1,7},{2,4},{3,5},{4,2},{5,3},{6,0},{7,1},{8,14},{9,15},{10,... | collective-permute-start | bytes 344072 | tf_op jit(solution)/shard_map/ppermute | solution.py:190
  66.0 2.2 %collective-permute-start.23 = (f32[224,128]{1,0:T(8,128)S(1)}, f32[224,128]{1,0:T(8,128)S(1)}, u32[]{:S(2)}, u32[]{:S(2)}) collective-permute-start(f32[224,128]{1,0:T(8,128)S(1)} %get-tuple-element.141), channel_id=1, source_target_pairs={{0,2},{1,3},{2,0},{3,1},{4,6},{5,7},{6,4},{7,5},{8,10},{9,11},{10,... | collective-permute-start | bytes 344072 | tf_op jit(solution)/shard_map/ppermute | solution.py:190
  68.3 3.5 %collective-permute-done.25.refs_3_ = f32[224,128]{1,0:T(8,128)S(1)} collective-permute-done((f32[224,128]{1,0:T(8,128)S(1)}, f32[224,128]{1,0:T(8,128)S(1)}, u32[]{:S(2)}, u32[]{:S(2)}) %collective-permute-start.25) | collective-permute-done | bytes 114720 | tf_op jit(solution)/shard_map/ppermute | solution.py:190
  71.8 2.4 %collective-permute-done.22.other_ref = f32[4,216,128]{2,1,0:T(8,128)S(1)} collective-permute-done((f32[4,216,128]{2,1,0:T(8,128)S(1)}, f32[4,216,128]{2,1,0:T(8,128)S(1)}, u32[]{:S(2)}, u32[]{:S(2)}) %collective-permute-start.22) | collective-permute-done | bytes 442400 | tf_op jit(solution)/shard_map/ppermute | solution.py:559
  78.2 2.1 %collective-permute-start.28 = (f32[216,128]{1,0:T(8,128)S(1)}, f32[216,128]{1,0:T(8,128)S(1)}, u32[]{:S(2)}, u32[]{:S(2)}) collective-permute-start(f32[216,128]{1,0:T(8,128)S(1)} %get-tuple-element.148), channel_id=1, source_target_pairs={{0,6},{1,7},{2,4},{3,5},{4,2},{5,3},{6,0},{7,1},{8,14},{9,15},{10,... | collective-permute-start | bytes 331784 | tf_op jit(solution)/shard_map/ppermute | solution.py:190
  80.3 2.4 %collective-permute-start.30 = (f32[216,128]{1,0:T(8,128)S(1)}, f32[216,128]{1,0:T(8,128)S(1)}, u32[]{:S(2)}, u32[]{:S(2)}) collective-permute-start(f32[216,128]{1,0:T(8,128)S(1)} %get-tuple-element.150), channel_id=1, source_target_pairs={{0,2},{1,3},{2,0},{3,1},{4,6},{5,7},{6,4},{7,5},{8,10},{9,11},{10,... | collective-permute-start | bytes 331784 | tf_op jit(solution)/shard_map/ppermute | solution.py:190
  86.1 4.1 %collective-permute-done.29.refs_2_ = f32[216,128]{1,0:T(8,128)S(1)} collective-permute-done((f32[216,128]{1,0:T(8,128)S(1)}, f32[216,128]{1,0:T(8,128)S(1)}, u32[]{:S(2)}, u32[]{:S(2)}) %collective-permute-start.29) | collective-permute-done | bytes 110624 | tf_op jit(solution)/shard_map/ppermute | solution.py:190
  95.4 2.6 %collective-permute-start.32 = (f32[216,128]{1,0:T(8,128)S(1)}, f32[216,128]{1,0:T(8,128)S(1)}, u32[]{:S(2)}, u32[]{:S(2)}) collective-permute-start(f32[216,128]{1,0:T(8,128)S(1)} %get-tuple-element.155), channel_id=1, source_target_pairs={{0,2},{1,3},{2,0},{3,1},{4,6},{5,7},{6,4},{7,5},{8,10},{9,11},{10,... | collective-permute-start | bytes 331784 | tf_op jit(solution)/shard_map/ppermute | solution.py:190
  101.4 3.9 %collective-permute-done.33.refs_2_ = f32[216,128]{1,0:T(8,128)S(1)} collective-permute-done((f32[216,128]{1,0:T(8,128)S(1)}, f32[216,128]{1,0:T(8,128)S(1)}, u32[]{:S(2)}, u32[]{:S(2)}) %collective-permute-start.33) | collective-permute-done | bytes 110624 | tf_op jit(solution)/shard_map/ppermute | solution.py:190
  111.7 2.7 %collective-permute-start.39 = (f32[216,128]{1,0:T(8,128)S(1)}, f32[216,128]{1,0:T(8,128)S(1)}, u32[]{:S(2)}, u32[]{:S(2)}) collective-permute-start(f32[216,128]{1,0:T(8,128)S(1)} %get-tuple-element.167), channel_id=1, source_target_pairs={{0,2},{1,3},{2,0},{3,1},{4,6},{5,7},{6,4},{7,5},{8,10},{9,11},{10,... | collective-permute-start | bytes 331784 | tf_op jit(solution)/shard_map/ppermute | solution.py:190
  114.3 5.0 %collective-permute-done.38.other_ref = f32[4,216,128]{2,1,0:T(8,128)S(1)} collective-permute-done((f32[4,216,128]{2,1,0:T(8,128)S(1)}, f32[4,216,128]{2,1,0:T(8,128)S(1)}, u32[]{:S(2)}, u32[]{:S(2)}) %collective-permute-start.38) | collective-permute-done | bytes 442400 | tf_op jit(solution)/shard_map/ppermute | solution.py:559
  119.3 2.3 %collective-permute-done.40.refs_2_ = f32[216,128]{1,0:T(8,128)S(1)} collective-permute-done((f32[216,128]{1,0:T(8,128)S(1)}, f32[216,128]{1,0:T(8,128)S(1)}, u32[]{:S(2)}, u32[]{:S(2)}) %collective-permute-start.40) | collective-permute-done | bytes 110624 | tf_op jit(solution)/shard_map/ppermute | solution.py:190
  124.2 2.1 %collective-permute-start.45 = (f32[216,128]{1,0:T(8,128)S(1)}, f32[216,128]{1,0:T(8,128)S(1)}, u32[]{:S(2)}, u32[]{:S(2)}) collective-permute-start(f32[216,128]{1,0:T(8,128)S(1)} %get-tuple-element.182), channel_id=1, source_target_pairs={{0,6},{1,7},{2,4},{3,5},{4,2},{5,3},{6,0},{7,1},{8,14},{9,15},{10,... | collective-permute-start | bytes 331784 | tf_op jit(solution)/shard_map/ppermute | solution.py:190
  126.3 2.4 %collective-permute-start.43 = (f32[216,128]{1,0:T(8,128)S(1)}, f32[216,128]{1,0:T(8,128)S(1)}, u32[]{:S(2)}, u32[]{:S(2)}) collective-permute-start(f32[216,128]{1,0:T(8,128)S(1)} %get-tuple-element.178), channel_id=1, source_target_pairs={{0,2},{1,3},{2,0},{3,1},{4,6},{5,7},{6,4},{7,5},{8,10},{9,11},{10,... | collective-permute-start | bytes 331784 | tf_op jit(solution)/shard_map/ppermute | solution.py:190
  128.7 6.4 %collective-permute-done.42.other_ref = f32[4,216,128]{2,1,0:T(8,128)S(1)} collective-permute-done((f32[4,216,128]{2,1,0:T(8,128)S(1)}, f32[4,216,128]{2,1,0:T(8,128)S(1)}, u32[]{:S(2)}, u32[]{:S(2)}) %collective-permute-start.42) | collective-permute-done | bytes 442400 | tf_op jit(solution)/shard_map/ppermute | solution.py:559
  135.7 2.1 %collective-permute-start.48 = (f32[216,128]{1,0:T(8,128)S(1)}, f32[216,128]{1,0:T(8,128)S(1)}, u32[]{:S(2)}, u32[]{:S(2)}) collective-permute-start(f32[216,128]{1,0:T(8,128)S(1)} %get-tuple-element.190), channel_id=1, source_target_pairs={{0,6},{1,7},{2,4},{3,5},{4,2},{5,3},{6,0},{7,1},{8,14},{9,15},{10,... | collective-permute-start | bytes 331784 | tf_op jit(solution)/shard_map/ppermute | solution.py:190
  137.8 2.4 %collective-permute-start.46 = (f32[216,128]{1,0:T(8,128)S(1)}, f32[216,128]{1,0:T(8,128)S(1)}, u32[]{:S(2)}, u32[]{:S(2)}) collective-permute-start(f32[216,128]{1,0:T(8,128)S(1)} %get-tuple-element.186), channel_id=1, source_target_pairs={{0,2},{1,3},{2,0},{3,1},{4,6},{5,7},{6,4},{7,5},{8,10},{9,11},{10,... | collective-permute-start | bytes 331784 | tf_op jit(solution)/shard_map/ppermute | solution.py:190
  141.8 1.9 %collective-permute-done.48.refs_4_ = f32[216,128]{1,0:T(8,128)S(1)} collective-permute-done((f32[216,128]{1,0:T(8,128)S(1)}, f32[216,128]{1,0:T(8,128)S(1)}, u32[]{:S(2)}, u32[]{:S(2)}) %collective-permute-start.48) | collective-permute-done | bytes 110624 | tf_op jit(solution)/shard_map/ppermute | solution.py:190
  143.7 2.8 %collective-permute-done.47.refs_3_ = f32[216,128]{1,0:T(8,128)S(1)} collective-permute-done((f32[216,128]{1,0:T(8,128)S(1)}, f32[216,128]{1,0:T(8,128)S(1)}, u32[]{:S(2)}, u32[]{:S(2)}) %collective-permute-start.47) | collective-permute-done | bytes 110624 | tf_op jit(solution)/shard_map/ppermute | solution.py:190
  146.5 2.1 %shard_map.162 = (f32[2,6,48,384]{3,2,1,0:T(8,128)}, f32[48,384]{1,0:T(8,128)}, f32[32,128]{1,0:T(8,128)S(1)}) custom-call(s32[2]{0:T(128)S(1)} %pad_add_fusion.me_ref, f32[2,6]{1,0:T(2,128)S(1)} %copy-done.8, s32[1]{0:T(128)S(6)} %copy.29.count_ref, f32[5,48,384]{2,1,0:T(8,128)S(1)} %copy-done.1, s32[48,384]{1,0:T(8,128)S(1)} %copy-done, ...), custom_call_target="tpu_custom_call" | custom-call | flops 1 | bytes 1 | tf_op jit(solution)/shard_map/pallas_call | solution.py:476
  148.6 10.1 %all_to_all.11 = f32[32,1,128]{2,1,0:T(1,128)S(1)} all-to-all(f32[32,1,128]{2,1,0:T(1,128)S(1)} %bitcast.15), channel_id=1, replica_groups=mesh['gx'=4,'gy'=8] {'gx','gy'}, dimensions={0} | all-to-all | bytes 32768 | tf_op jit(solution)/shard_map/all_to_all | solution.py:587
  (126 shorter events, 58.0 us)
Async XLA Ops:
  1.6 8.4 %collective-permute-start.3 = (f32[3,48,384]{2,1,0:T(8,128)S(1)}, f32[3,48,384]{2,1,0:T(8,128)S(1)}, u32[]{:S(2)}, u32[]{:S(2)}) collective-permute-start(f32[3,48,384]{2,1,0:T(8,128)S(1)} %slice.22.refs_0_), channel_id=1, source_target_pairs={{0,8},{8,0},{16,24},{24,16},{1,9},{9,1},{17,25},{25,17},{2,10},{10... | collective-permute-start | bytes 663560 | tf_op jit(solution)/shard_map/ppermute | solution.py:169
  2.1 10.7 %collective-permute-start.4 = (f32[3,48,384]{2,1,0:T(8,128)S(1)}, f32[3,48,384]{2,1,0:T(8,128)S(1)}, u32[]{:S(2)}, u32[]{:S(2)}) collective-permute-start(f32[3,48,384]{2,1,0:T(8,128)S(1)} %slice.22.refs_0_), channel_id=1, source_target_pairs={{0,16},{8,24},{16,0},{24,8},{1,17},{9,25},{17,1},{25,9},{2,18},{10... | collective-permute-start | bytes 663560 | tf_op jit(solution)/shard_map/ppermute | solution.py:178
  5.7 17.7 %collective-permute-start.6 = (f32[3,48,384]{2,1,0:T(8,128)S(1)}, f32[3,48,384]{2,1,0:T(8,128)S(1)}, u32[]{:S(2)}, u32[]{:S(2)}) collective-permute-start(f32[3,48,384]{2,1,0:T(8,128)S(1)} %slice.18.refs_0_), channel_id=1, source_target_pairs={{0,8},{8,0},{16,24},{24,16},{1,9},{9,1},{17,25},{25,17},{2,10},{10... | collective-permute-start | bytes 663560 | tf_op jit(solution)/shard_map/ppermute | solution.py:169
  13.5 16.4 %collective-permute-start.10 = (f32[3,48,384]{2,1,0:T(8,128)S(1)}, f32[3,48,384]{2,1,0:T(8,128)S(1)}, u32[]{:S(2)}, u32[]{:S(2)}) collective-permute-start(f32[3,48,384]{2,1,0:T(8,128)S(1)} %slice.18.refs_0_), channel_id=1, source_target_pairs={{0,16},{8,24},{16,0},{24,8},{1,17},{9,25},{17,1},{25,9},{2,18},{10... | collective-permute-start | bytes 663560 | tf_op jit(solution)/shard_map/ppermute | solution.py:178
  19.1 23.2 %collective-permute-start.15 = (f32[6,48,384]{2,1,0:T(8,128)S(1)}, f32[6,48,384]{2,1,0:T(8,128)S(1)}, u32[]{:S(2)}, u32[]{:S(2)}) collective-permute-start(f32[6,48,384]{2,1,0:T(8,128)S(1)} %slice.19.refs_0_), channel_id=1, source_target_pairs={{0,8},{8,0},{16,24},{24,16},{1,9},{9,1},{17,25},{25,17},{2,10},{10... | collective-permute-start | bytes 1327112 | tf_op jit(solution)/shard_map/ppermute | solution.py:169
  19.2 24.7 %collective-permute-start.16 = (f32[6,48,384]{2,1,0:T(8,128)S(1)}, f32[6,48,384]{2,1,0:T(8,128)S(1)}, u32[]{:S(2)}, u32[]{:S(2)}) collective-permute-start(f32[6,48,384]{2,1,0:T(8,128)S(1)} %slice.19.refs_0_), channel_id=1, source_target_pairs={{0,16},{8,24},{16,0},{24,8},{1,17},{9,25},{17,1},{25,9},{2,18},{10... | collective-permute-start | bytes 1327112 | tf_op jit(solution)/shard_map/ppermute | solution.py:178
  45.3 13.0 %collective-permute-start.18 = (f32[4,224,128]{2,1,0:T(8,128)S(1)}, f32[4,224,128]{2,1,0:T(8,128)S(1)}, u32[]{:S(2)}, u32[]{:S(2)}) collective-permute-start(f32[4,224,128]{2,1,0:T(8,128)S(1)} %get-tuple-element.128), channel_id=1, source_target_pairs={{0,1},{1,0},{2,3},{3,2},{4,5},{5,4},{6,7},{7,6},{8,9},{9,8},{10,11... | collective-permute-start | bytes 1376264 | tf_op jit(solution)/shard_map/ppermute | solution.py:559
  48.6 9.7 %collective-permute-start.21 = (f32[216,128]{1,0:T(8,128)S(1)}, f32[216,128]{1,0:T(8,128)S(1)}, u32[]{:S(2)}, u32[]{:S(2)}) collective-permute-start(f32[216,128]{1,0:T(8,128)S(1)} %get-tuple-element.134), channel_id=1, source_target_pairs={{0,6},{1,7},{2,4},{3,5},{4,2},{5,3},{6,0},{7,1},{8,14},{9,15},{10,... | collective-permute-start | bytes 331784 | tf_op jit(solution)/shard_map/ppermute | solution.py:190
  50.8 10.6 %collective-permute-start.20 = (f32[216,128]{1,0:T(8,128)S(1)}, f32[216,128]{1,0:T(8,128)S(1)}, u32[]{:S(2)}, u32[]{:S(2)}) collective-permute-start(f32[216,128]{1,0:T(8,128)S(1)} %get-tuple-element.132), channel_id=1, source_target_pairs={{0,4},{1,5},{2,6},{3,7},{4,0},{5,1},{6,2},{7,3},{8,12},{9,13},{10,... | collective-permute-start | bytes 331784 | tf_op jit(solution)/shard_map/ppermute | solution.py:190
  51.1 10.3 %collective-permute-start.19 = (f32[216,128]{1,0:T(8,128)S(1)}, f32[216,128]{1,0:T(8,128)S(1)}, u32[]{:S(2)}, u32[]{:S(2)}) collective-permute-start(f32[216,128]{1,0:T(8,128)S(1)} %get-tuple-element.130), channel_id=1, source_target_pairs={{0,2},{1,3},{2,0},{3,1},{4,6},{5,7},{6,4},{7,5},{8,10},{9,11},{10,... | collective-permute-start | bytes 331784 | tf_op jit(solution)/shard_map/ppermute | solution.py:190
  62.7 11.5 %collective-permute-start.22 = (f32[4,216,128]{2,1,0:T(8,128)S(1)}, f32[4,216,128]{2,1,0:T(8,128)S(1)}, u32[]{:S(2)}, u32[]{:S(2)}) collective-permute-start(f32[4,216,128]{2,1,0:T(8,128)S(1)} %get-tuple-element.139), channel_id=1, source_target_pairs={{0,1},{1,0},{2,3},{3,2},{4,5},{5,4},{6,7},{7,6},{8,9},{9,8},{10,11... | collective-permute-start | bytes 1327112 | tf_op jit(solution)/shard_map/ppermute | solution.py:559
  63.8 8.0 %collective-permute-start.25 = (f32[224,128]{1,0:T(8,128)S(1)}, f32[224,128]{1,0:T(8,128)S(1)}, u32[]{:S(2)}, u32[]{:S(2)}) collective-permute-start(f32[224,128]{1,0:T(8,128)S(1)} %get-tuple-element.145), channel_id=1, source_target_pairs={{0,6},{1,7},{2,4},{3,5},{4,2},{5,3},{6,0},{7,1},{8,14},{9,15},{10,... | collective-permute-start | bytes 344072 | tf_op jit(solution)/shard_map/ppermute | solution.py:190
  66.0 8.8 %collective-permute-start.24 = (f32[224,128]{1,0:T(8,128)S(1)}, f32[224,128]{1,0:T(8,128)S(1)}, u32[]{:S(2)}, u32[]{:S(2)}) collective-permute-start(f32[224,128]{1,0:T(8,128)S(1)} %get-tuple-element.143), channel_id=1, source_target_pairs={{0,4},{1,5},{2,6},{3,7},{4,0},{5,1},{6,2},{7,3},{8,12},{9,13},{10,... | collective-permute-start | bytes 344072 | tf_op jit(solution)/shard_map/ppermute | solution.py:190
  66.0 8.8 %collective-permute-start.23 = (f32[224,128]{1,0:T(8,128)S(1)}, f32[224,128]{1,0:T(8,128)S(1)}, u32[]{:S(2)}, u32[]{:S(2)}) collective-permute-start(f32[224,128]{1,0:T(8,128)S(1)} %get-tuple-element.141), channel_id=1, source_target_pairs={{0,2},{1,3},{2,0},{3,1},{4,6},{5,7},{6,4},{7,5},{8,10},{9,11},{10,... | collective-permute-start | bytes 344072 | tf_op jit(solution)/shard_map/ppermute | solution.py:190
  75.9 14.2 %collective-permute-start.27 = (f32[6,48,384]{2,1,0:T(8,128)S(1)}, f32[6,48,384]{2,1,0:T(8,128)S(1)}, u32[]{:S(2)}, u32[]{:S(2)}) collective-permute-start(f32[6,48,384]{2,1,0:T(8,128)S(1)} %shard_map.150.refs_0_), channel_id=1, source_target_pairs={{0,16},{8,24},{16,0},{24,8},{1,17},{9,25},{17,1},{25,9},{2,18},{10... | collective-permute-start | bytes 1327112 | tf_op jit(solution)/shard_map/ppermute | solution.py:178
  78.2 7.9 %collective-permute-start.28 = (f32[216,128]{1,0:T(8,128)S(1)}, f32[216,128]{1,0:T(8,128)S(1)}, u32[]{:S(2)}, u32[]{:S(2)}) collective-permute-start(f32[216,128]{1,0:T(8,128)S(1)} %get-tuple-element.148), channel_id=1, source_target_pairs={{0,6},{1,7},{2,4},{3,5},{4,2},{5,3},{6,0},{7,1},{8,14},{9,15},{10,... | collective-permute-start | bytes 331784 | tf_op jit(solution)/shard_map/ppermute | solution.py:190
  80.3 9.9 %collective-permute-start.29 = (f32[216,128]{1,0:T(8,128)S(1)}, f32[216,128]{1,0:T(8,128)S(1)}, u32[]{:S(2)}, u32[]{:S(2)}) collective-permute-start(f32[216,128]{1,0:T(8,128)S(1)} %get-tuple-element.149), channel_id=1, source_target_pairs={{0,4},{1,5},{2,6},{3,7},{4,0},{5,1},{6,2},{7,3},{8,12},{9,13},{10,... | collective-permute-start | bytes 331784 | tf_op jit(solution)/shard_map/ppermute | solution.py:190
  80.3 9.9 %collective-permute-start.30 = (f32[216,128]{1,0:T(8,128)S(1)}, f32[216,128]{1,0:T(8,128)S(1)}, u32[]{:S(2)}, u32[]{:S(2)}) collective-permute-start(f32[216,128]{1,0:T(8,128)S(1)} %get-tuple-element.150), channel_id=1, source_target_pairs={{0,2},{1,3},{2,0},{3,1},{4,6},{5,7},{6,4},{7,5},{8,10},{9,11},{10,... | collective-permute-start | bytes 331784 | tf_op jit(solution)/shard_map/ppermute | solution.py:190
  91.5 13.8 %collective-permute-start.36 = (f32[6,48,384]{2,1,0:T(8,128)S(1)}, f32[6,48,384]{2,1,0:T(8,128)S(1)}, u32[]{:S(2)}, u32[]{:S(2)}) collective-permute-start(f32[6,48,384]{2,1,0:T(8,128)S(1)} %shard_map.155.refs_0_), channel_id=1, source_target_pairs={{0,16},{8,24},{16,0},{24,8},{1,17},{9,25},{17,1},{25,9},{2,18},{10... | collective-permute-start | bytes 1327112 | tf_op jit(solution)/shard_map/ppermute | solution.py:178
  95.4 9.9 %collective-permute-start.33 = (f32[216,128]{1,0:T(8,128)S(1)}, f32[216,128]{1,0:T(8,128)S(1)}, u32[]{:S(2)}, u32[]{:S(2)}) collective-permute-start(f32[216,128]{1,0:T(8,128)S(1)} %get-tuple-element.157), channel_id=1, source_target_pairs={{0,4},{1,5},{2,6},{3,7},{4,0},{5,1},{6,2},{7,3},{8,12},{9,13},{10,... | collective-permute-start | bytes 331784 | tf_op jit(solution)/shard_map/ppermute | solution.py:190
  95.4 9.9 %collective-permute-start.32 = (f32[216,128]{1,0:T(8,128)S(1)}, f32[216,128]{1,0:T(8,128)S(1)}, u32[]{:S(2)}, u32[]{:S(2)}) collective-permute-start(f32[216,128]{1,0:T(8,128)S(1)} %get-tuple-element.155), channel_id=1, source_target_pairs={{0,2},{1,3},{2,0},{3,1},{4,6},{5,7},{6,4},{7,5},{8,10},{9,11},{10,... | collective-permute-start | bytes 331784 | tf_op jit(solution)/shard_map/ppermute | solution.py:190
  106.7 12.6 %collective-permute-start.38 = (f32[4,216,128]{2,1,0:T(8,128)S(1)}, f32[4,216,128]{2,1,0:T(8,128)S(1)}, u32[]{:S(2)}, u32[]{:S(2)}) collective-permute-start(f32[4,216,128]{2,1,0:T(8,128)S(1)} %get-tuple-element.165), channel_id=1, source_target_pairs={{0,1},{1,0},{2,3},{3,2},{4,5},{5,4},{6,7},{7,6},{8,9},{9,8},{10,11... | collective-permute-start | bytes 1327112 | tf_op jit(solution)/shard_map/ppermute | solution.py:559
  109.9 9.4 %collective-permute-start.41 = (f32[216,128]{1,0:T(8,128)S(1)}, f32[216,128]{1,0:T(8,128)S(1)}, u32[]{:S(2)}, u32[]{:S(2)}) collective-permute-start(f32[216,128]{1,0:T(8,128)S(1)} %get-tuple-element.171), channel_id=1, source_target_pairs={{0,6},{1,7},{2,4},{3,5},{4,2},{5,3},{6,0},{7,1},{8,14},{9,15},{10,... | collective-permute-start | bytes 331784 | tf_op jit(solution)/shard_map/ppermute | solution.py:190
  111.7 10.0 %collective-permute-start.40 = (f32[216,128]{1,0:T(8,128)S(1)}, f32[216,128]{1,0:T(8,128)S(1)}, u32[]{:S(2)}, u32[]{:S(2)}) collective-permute-start(f32[216,128]{1,0:T(8,128)S(1)} %get-tuple-element.169), channel_id=1, source_target_pairs={{0,4},{1,5},{2,6},{3,7},{4,0},{5,1},{6,2},{7,3},{8,12},{9,13},{10,... | collective-permute-start | bytes 331784 | tf_op jit(solution)/shard_map/ppermute | solution.py:190
  111.7 10.0 %collective-permute-start.39 = (f32[216,128]{1,0:T(8,128)S(1)}, f32[216,128]{1,0:T(8,128)S(1)}, u32[]{:S(2)}, u32[]{:S(2)}) collective-permute-start(f32[216,128]{1,0:T(8,128)S(1)} %get-tuple-element.167), channel_id=1, source_target_pairs={{0,2},{1,3},{2,0},{3,1},{4,6},{5,7},{6,4},{7,5},{8,10},{9,11},{10,... | collective-permute-start | bytes 331784 | tf_op jit(solution)/shard_map/ppermute | solution.py:190
  123.0 12.2 %collective-permute-start.42 = (f32[4,216,128]{2,1,0:T(8,128)S(1)}, f32[4,216,128]{2,1,0:T(8,128)S(1)}, u32[]{:S(2)}, u32[]{:S(2)}) collective-permute-start(f32[4,216,128]{2,1,0:T(8,128)S(1)} %get-tuple-element.176), channel_id=1, source_target_pairs={{0,1},{1,0},{2,3},{3,2},{4,5},{5,4},{6,7},{7,6},{8,9},{9,8},{10,11... | collective-permute-start | bytes 1327112 | tf_op jit(solution)/shard_map/ppermute | solution.py:559
  124.2 13.6 %collective-permute-start.45 = (f32[216,128]{1,0:T(8,128)S(1)}, f32[216,128]{1,0:T(8,128)S(1)}, u32[]{:S(2)}, u32[]{:S(2)}) collective-permute-start(f32[216,128]{1,0:T(8,128)S(1)} %get-tuple-element.182), channel_id=1, source_target_pairs={{0,6},{1,7},{2,4},{3,5},{4,2},{5,3},{6,0},{7,1},{8,14},{9,15},{10,... | collective-permute-start | bytes 331784 | tf_op jit(solution)/shard_map/ppermute | solution.py:190
  126.3 14.6 %collective-permute-start.44 = (f32[216,128]{1,0:T(8,128)S(1)}, f32[216,128]{1,0:T(8,128)S(1)}, u32[]{:S(2)}, u32[]{:S(2)}) collective-permute-start(f32[216,128]{1,0:T(8,128)S(1)} %get-tuple-element.180), channel_id=1, source_target_pairs={{0,4},{1,5},{2,6},{3,7},{4,0},{5,1},{6,2},{7,3},{8,12},{9,13},{10,... | collective-permute-start | bytes 331784 | tf_op jit(solution)/shard_map/ppermute | solution.py:190
  126.3 14.6 %collective-permute-start.43 = (f32[216,128]{1,0:T(8,128)S(1)}, f32[216,128]{1,0:T(8,128)S(1)}, u32[]{:S(2)}, u32[]{:S(2)}) collective-permute-start(f32[216,128]{1,0:T(8,128)S(1)} %get-tuple-element.178), channel_id=1, source_target_pairs={{0,2},{1,3},{2,0},{3,1},{4,6},{5,7},{6,4},{7,5},{8,10},{9,11},{10,... | collective-permute-start | bytes 331784 | tf_op jit(solution)/shard_map/ppermute | solution.py:190
  135.7 8.0 %collective-permute-start.48 = (f32[216,128]{1,0:T(8,128)S(1)}, f32[216,128]{1,0:T(8,128)S(1)}, u32[]{:S(2)}, u32[]{:S(2)}) collective-permute-start(f32[216,128]{1,0:T(8,128)S(1)} %get-tuple-element.190), channel_id=1, source_target_pairs={{0,6},{1,7},{2,4},{3,5},{4,2},{5,3},{6,0},{7,1},{8,14},{9,15},{10,... | collective-permute-start | bytes 331784 | tf_op jit(solution)/shard_map/ppermute | solution.py:190
  137.8 8.7 %collective-permute-start.47 = (f32[216,128]{1,0:T(8,128)S(1)}, f32[216,128]{1,0:T(8,128)S(1)}, u32[]{:S(2)}, u32[]{:S(2)}) collective-permute-start(f32[216,128]{1,0:T(8,128)S(1)} %get-tuple-element.188), channel_id=1, source_target_pairs={{0,4},{1,5},{2,6},{3,7},{4,0},{5,1},{6,2},{7,3},{8,12},{9,13},{10,... | collective-permute-start | bytes 331784 | tf_op jit(solution)/shard_map/ppermute | solution.py:190
  137.8 8.7 %collective-permute-start.46 = (f32[216,128]{1,0:T(8,128)S(1)}, f32[216,128]{1,0:T(8,128)S(1)}, u32[]{:S(2)}, u32[]{:S(2)}) collective-permute-start(f32[216,128]{1,0:T(8,128)S(1)} %get-tuple-element.186), channel_id=1, source_target_pairs={{0,2},{1,3},{2,0},{3,1},{4,6},{5,7},{6,4},{7,5},{8,10},{9,11},{10,... | collective-permute-start | bytes 331784 | tf_op jit(solution)/shard_map/ppermute | solution.py:190
  (30 other events, 259.3 us)

commit v6 on v4

--- a/solution.py
+++ b/solution.py
@@ -115,8 +115,14 @@
     return lax.dot_general(a, b, dims, preferred_element_type=jnp.float32)
 
 
-def dot_split(a, b):
-    return dot(a[0], b[0]) + (dot(a[0], b[1]) + dot(a[1], b[0]))
+def wide_left(value):
+    high, low = split(value)
+    return jnp.concatenate([high, high, low], axis=1)
+
+
+def wide_right(value):
+    high, low = split(value)
+    return jnp.concatenate([high, low, high], axis=0)
 
 
 def call(kernel, out_shape, operands, scalars=(), flops=0, scratch=()):
@@ -173,21 +179,19 @@
 def prepare_x(x_inverse):
     rows, cols = x_inverse.shape
 
-    def kernel(x_ref, high_ref, low_ref):
-        for start in range(0, cols, rows):
-            high, low = split(jnp.transpose(x_ref[:, start : start + rows]))
-            high_ref[start : start + rows, :] = high
-            low_ref[start : start + rows, :] = low
-
-    shape = jax.ShapeDtypeStruct((cols, rows), jnp.bfloat16)
-    return call(kernel, [shape, shape], [x_inverse])
+    def kernel(x_ref, out_ref):
+        for owner in range(cols // rows):
+            block = jnp.transpose(x_ref[:, owner * rows : (owner + 1) * rows])
+            out_ref[3 * owner * rows : 3 * (owner + 1) * rows, :] = wide_right(block)
+
+    return call(kernel, jax.ShapeDtypeStruct((3 * cols, rows), jnp.bfloat16), [x_inverse])
 
 
 def prepare_y(masks, pieces, me, rows):
     owned, half = pieces[0].shape
 
     def kernel(me_ref, *refs):
-        high_ref, low_ref, whole_ref = refs[-3:]
+        out_ref, whole_ref = refs[-2:]
         side = lax.rem(me_ref[1], 2)
         for mask, ref in zip(masks, refs):
             start = pl.multiple_of((me_ref[0] ^ mask) * owned, owned)
@@ -195,54 +199,50 @@
         for other in range(2):
             for part in range(half // rows):
                 start = pl.multiple_of((2 * part + (side ^ other)) * rows, rows)
-                high, low = split(whole_ref[pl.ds(start, rows), :])
                 out = other * half + part * rows
-                high_ref[out : out + rows, :] = high
-                low_ref[out : out + rows, :] = low
-
-    shape = jax.ShapeDtypeStruct((2 * half, half), jnp.bfloat16)
+                out_ref[out : out + rows, :] = wide_left(whole_ref[pl.ds(start, rows), :])
+
     return call(
         kernel,
-        [shape, shape],
+        jax.ShapeDtypeStruct((2 * half, 3 * half), jnp.bfloat16),
         [me] + pieces,
         scalars=(0,),
         scratch=[pltpu.VMEM((2 * half, half), jnp.float32)],
     )
 
 
-def add_zonal(total, masks, me_ref, high_ref, low_ref, refs):
+def add_zonal(total, masks, me_ref, x_ref, refs):
     for mask, ref in zip(masks, refs):
         fields, rows, cols = ref.shape
-        start = pl.multiple_of((me_ref[0] ^ mask) * cols, cols)
-        values = split(ref[...].reshape(fields * rows, cols))
-        weights = (high_ref[pl.ds(start, cols), :], low_ref[pl.ds(start, cols), :])
-        part = dot_split(values, weights)
+        start = pl.multiple_of((me_ref[0] ^ mask) * (3 * cols), 3 * cols)
+        values = wide_left(ref[...].reshape(fields * rows, cols))
+        part = dot(values, x_ref[pl.ds(start, 3 * cols), :])
         total = part if total is None else total + part
     return total
 
 
-def zonal_start(plan, held, me, x_high, x_low):
+def zonal_start(plan, held, me, x_wide):
     masks, pieces = [m for m, _ in held], [p for _, p in held]
 
-    def kernel(me_ref, high_ref, low_ref, *refs):
-        refs[-1][...] = add_zonal(None, masks, me_ref, high_ref, low_ref, refs)
+    def kernel(me_ref, x_ref, *refs):
+        refs[-1][...] = add_zonal(None, masks, me_ref, x_ref, refs)
 
     return call(
         kernel,
         jax.ShapeDtypeStruct((plan.fields * plan.rows, plan.cols), jnp.float32),
-        [me, x_high, x_low] + pieces,
+        [me, x_wide] + pieces,
         scalars=(0,),
         flops=6 * plan.fields * plan.rows * plan.cols**2 * len(pieces),
     )
 
 
-def zonal_end(plan, total, held, me, x_high, x_low, sea_mask):
+def zonal_end(plan, total, held, me, x_wide, sea_mask):
     fields, rows, cols, parts = plan.fields, plan.rows, plan.cols, plan.parts
     masks, pieces = [m for m, _ in held], [p for _, p in held]
 
-    def kernel(me_ref, high_ref, low_ref, sea_ref, total_ref, *refs):
+    def kernel(me_ref, x_ref, sea_ref, total_ref, *refs):
         out_refs, tiles_ref = refs[-parts - 1 : -1], refs[-1]
-        result = add_zonal(total_ref[...], masks, me_ref, high_ref, low_ref, refs)
+        result = add_zonal(total_ref[...], masks, me_ref, x_ref, refs)
         result = result.reshape(fields, rows, cols)
         sea = sea_ref[...].astype(jnp.float32)
         for block in range(plan.blocks):
@@ -255,18 +255,18 @@
     return call(
         kernel,
         plan.blocks_out,
-        [me, x_high, x_low, sea_mask, total] + pieces,
+        [me, x_wide, sea_mask, total] + pieces,
         scalars=(0,),
         flops=6 * fields * rows * cols**2 * len(pieces),
         scratch=[plan.tiles],
     )
 
 
-def meridional(plan, me, lines, y_high, y_low):
+def meridional(plan, me, lines, y_wide):
     rows, parts = plan.rows, plan.parts
 
-    def kernel(me_ref, high_ref, low_ref, *refs):
-        in_refs, out_refs, lines_ref, solved_ref = refs[:parts], refs[parts:-2], refs[-2], refs[-1]
+    def kernel(me_ref, y_ref, *refs):
+        in_refs, out_refs, lines_ref = refs[:parts], refs[parts:-1], refs[-1]
         for mask in range(parts):
             place = pl.ds(pl.multiple_of(part_of(me_ref, mask) * rows, rows), rows)
             for i in range(plan.full):
@@ -274,30 +274,27 @@
                 lines_ref[place, lanes] = in_refs[mask][i * rows : (i + 1) * rows, :]
             if plan.rest:
                 lines_ref[place, plan.full * LANES :] = plan.unpack_rest(in_refs[mask], 0)
-        solved_ref[...] = dot_split((high_ref[...], low_ref[...]), split(lines_ref[...]))
+        solved = dot(y_ref[...], wide_right(lines_ref[...]))
         for other in range(2):
             for part in range(parts):
                 start = (other * parts + part) * rows
                 for i in range(plan.full):
                     lanes = slice(i * LANES, (i + 1) * LANES)
-                    out_refs[other][part, i * rows : (i + 1) * rows, :] = solved_ref[
+                    out_refs[other][part, i * rows : (i + 1) * rows, :] = solved[
                         start : start + rows, lanes
                     ]
                 if plan.rest:
-                    last = solved_ref[start : start + rows, plan.full * LANES :]
+                    last = solved[start : start + rows, plan.full * LANES :]
                     plan.store_rest(out_refs[other].at[part], plan.pack_rest(last, 0))
 
     shape = jax.ShapeDtypeStruct((parts, plan.width, LANES), jnp.float32)
     return call(
         kernel,
         [shape, shape],
-        [me, y_high, y_low] + lines,
+        [me, y_wide] + lines,
         scalars=(0,),
         flops=12 * (parts * rows) ** 2 * plan.columns,
-        scratch=[
-            pltpu.VMEM((parts * rows, plan.columns), jnp.float32),
-            pltpu.VMEM((2 * parts * rows, plan.columns), jnp.float32),
-        ],
+        scratch=[pltpu.VMEM((parts * rows, plan.columns), jnp.float32)],
     )
 
 
@@ -477,7 +474,7 @@
     if not plan.fits:
         plan, chunks = Plan(kinds * levels, rows, cols, gy_count // 2), 1
     me = jnp.stack([lax.axis_index("gx"), lax.axis_index("gy")]).astype(jnp.int32)
-    x_parts = prepare_x(x_inverse)
+    x_wide = prepare_x(x_inverse)
     fields = [control[0, 0] if chunks > 1 else control.reshape(plan.fields, rows, cols)]
     if chunks > 1:
         control = after(control, fields[0])
@@ -487,16 +484,16 @@
     y_columns = y_columns.reshape(y_inverse.shape[0], -1)
     y_far = gather_far(y_columns, "gx", gx_count)
     y_held = gather_near(y_columns, "gx", gx_count) + y_far
-    y_parts = prepare_y([m for m, _ in y_held], [p for _, p in y_held], me, rows)
+    y_wide = prepare_y([m for m, _ in y_held], [p for _, p in y_held], me, rows)
     side_pairs = [(i, i ^ 1) for i in range(gy_count)]
     result = None
     for step in range(STEPS):
         own, other, sent = [], [], []
         for chunk in range(chunks):
             near = gather_near(fields[chunk], "gx", gx_count)
-            total = zonal_start(plan, near, me, *x_parts)
+            total = zonal_start(plan, near, me, x_wide)
             if sent:
-                hold = [total, y_parts[0]] + lines
+                hold = [total, y_wide] + lines
             elif step == 0:
                 hold = [total, y_far[0][1]] + fields[1:]
             else:
@@ -504,19 +501,23 @@
             far = gather_far(fields[chunk], "gx", gx_count, hold)
             if own:
                 total = after(total, own[-1])
-            packed = zonal_end(plan, total, far, me, *x_parts, sea_mask)
+            packed = zonal_end(plan, total, far, me, x_wide, sea_mask)
             sent.append(exchange(packed, "gy", gy_count))
-            ready = other[-1] if other else y_parts[0]
+            if other:
+                sums = add_sides(plan, me, own[-1], other[-1])
+            ready = sums[0] if other else y_wide
             lines = [after(line, ready) for line in sent[chunk]]
-            for_own, for_other = meridional(plan, me, lines, *y_parts)
+            for_own, for_other = meridional(plan, me, lines, y_wide)
             own.append(for_own)
             other.append(lax.ppermute(for_other, "gy", side_pairs))
         for chunk in range(chunks):
-            if chunk == 0:
-                own[chunk] = after(own[chunk], own[-1])
-            elif step < STEPS - 1:
-                own[chunk] = after(own[chunk], fields[chunk - 1])
-            returned = exchange(add_sides(plan, me, own[chunk], other[chunk]), "gy", gy_count)
+            if chunk == 0 and chunks > 1:
+                blocks = [after(block, own[-1]) for block in sums]
+            else:
+                if chunk > 0 and step < STEPS - 1:
+                    own[chunk] = after(own[chunk], fields[chunk - 1])
+                blocks = add_sides(plan, me, own[chunk], other[chunk])
+            returned = exchange(blocks, "gy", gy_count)
             if chunk < chunks - 1:
                 returned = [after(block, other[-1]) for block in returned]
             if step < STEPS - 1 or chunk < chunks - 1:

time: 151 us -> 157 us (1.040)
  local copies, waits for them, and re-layouts: 6.78 us -> 13 us
    unnamed x24 -> x28, local copies, waits for them, and re-layouts: 4.61 us -> 9.38 us
    ppermute x24, waiting for transfers between devices: 32.2 us -> 28.4 us  [exchange(): out[mask] = lax.ppermute(blocks[mask], axis, pairs)]
  transfers between devices with their start and end apart: 43 -> 43, of which waited for: 17 -> 16; matrix products, arithmetic and copies ran while one was open for 2% -> 2% of each run, Pallas kernels for 14% -> 14%
where the time goes in v6:
time: 157 us; the launch traced here: 156 us
  waiting for transfers between devices  55.1 us (35%)
  starting transfers between devices  48.3 us (31%)
  Pallas kernels  27.9 us (18%)
  local copies, waits for them, and re-layouts  13 us (8%)
  blocking collectives  10 us (6%)
  between operations  1.57 us (1%)
    ppermute x24, starting transfers between devices, exchange(): out[mask] = lax.ppermute(blocks[mask], axis, pairs)  35.5 us
    ppermute x24, waiting for transfers between devices, exchange(): out[mask] = lax.ppermute(blocks[mask], axis, pairs)  28.4 us
    pallas_call x22, Pallas kernels, call(): pl.pallas_call(kernel, out_shape=out_shape, in_specs=specs, out_specs=[ou...  25.8 us
    ppermute x4, waiting for transfers between devices, body(): other.append(lax.ppermute(for_other, 'gy', side_pairs))  20.8 us
    all_to_all x1, blocking collectives, body(): lax.all_to_all(outgoing, ('gx', 'gy'), split_axis=0, concat_axis=0, tiled...  10 us
    unnamed x28, local copies, waits for them, and re-layouts  9.38 us
    ppermute x10, starting transfers between devices, gather_far(): lax.ppermute(piece, axis, pairs)  6.89 us
    ppermute x10, waiting for transfers between devices, gather_far(): lax.ppermute(piece, axis, pairs)  5.91 us
  transfers between devices with their start and end apart: 43, of which 16 were waited for; matrix products, arithmetic and copies ran while one was open for 2% of the time, Pallas kernels for 14%

profile of v6, /device:TPU:0, one launch (start us, length us, event | category | flops | bytes accessed | tf_op | source)
XLA Modules:
  0.0 156.0 jit_solution(7266980624844970840)
XLA Ops:
  2.9 2.5 %collective-permute-start.4 = (f32[6,48,384]{2,1,0:T(8,128)}, f32[6,48,384]{2,1,0:T(8,128)}, u32[]{:S(2)}, u32[]{:S(2)}) collective-permute-start(f32[6,48,384]{2,1,0:T(8,128)} %slice_bitcast_fusion.1.refs_0_), channel_id=1, source_target_pairs={{0,16},{8,24},{16,0},{24,8},{1,17},{9,25},{17,1},{25,9},{2,18},{10... | collective-permute-start | bytes 1327112 | tf_op jit(solution)/shard_map/ppermute | solution.py:163
  10.7 2.1 %shard_map.141.total_ref = f32[288,384]{1,0:T(8,128)S(1)} custom-call(s32[2]{0:T(128)S(1)} %pad_add_fusion.me_ref, bf16[4608,384]{1,0:T(8,128)(2,1)S(1)} %shard_map.140.x_ref, f32[6,48,384]{2,1,0:T(8,128)} %slice_bitcast_fusion.1.refs_0_, f32[6,48,384]{2,1,0:T(8,128)} %collective-permute-done.3.refs_1_), custom_call_target="tpu_custom_call" | custom-call | flops 1 | bytes 1 | tf_op jit(solution)/shard_map/pallas_call | solution.py:137
  12.8 5.9 %collective-permute-done.1.refs_2_ = f32[96,192]{1,0:T(8,128)} collective-permute-done((f32[96,192]{1,0:T(8,128)}, f32[96,192]{1,0:T(8,128)}, u32[]{:S(2)}, u32[]{:S(2)}) %collective-permute-start.1) | collective-permute-done | bytes 73760 | tf_op jit(solution)/shard_map/ppermute | solution.py:163
  21.4 2.0 %shard_map.142 = (f32[216,128]{1,0:T(8,128)S(1)}, f32[216,128]{1,0:T(8,128)S(1)}, f32[216,128]{1,0:T(8,128)S(1)}, f32[216,128]{1,0:T(8,128)S(1)}) custom-call(s32[2]{0:T(128)S(1)} %pad_add_fusion.me_ref, bf16[4608,384]{1,0:T(8,128)(2,1)S(1)} %shard_map.140.x_ref, s32[48,384]{1,0:T(8,128)S(1)} %copy-done.3, f32[288,384]{1,0:T(8,128)S(1)} %shard_map.141.total_ref, ...), custom_call_target="tpu_custom_call" | custom-call | flops 1 | bytes 1 | tf_op jit(solution)/shard_map/pallas_call | solution.py:137
  23.5 3.7 %collective-permute-start.8 = (f32[216,128]{1,0:T(8,128)S(1)}, f32[216,128]{1,0:T(8,128)S(1)}, u32[]{:S(2)}, u32[]{:S(2)}) collective-permute-start(f32[216,128]{1,0:T(8,128)S(1)} %get-tuple-element.98), channel_id=1, source_target_pairs={{0,6},{1,7},{2,4},{3,5},{4,2},{5,3},{6,0},{7,1},{8,14},{9,15},{10,... | collective-permute-start | bytes 331784 | tf_op jit(solution)/shard_map/ppermute | solution.py:175
  31.3 5.5 %collective-permute-done.7.refs_2_ = f32[216,128]{1,0:T(8,128)S(1)} collective-permute-done((f32[216,128]{1,0:T(8,128)S(1)}, f32[216,128]{1,0:T(8,128)S(1)}, u32[]{:S(2)}, u32[]{:S(2)}) %collective-permute-start.7) | collective-permute-done | bytes 110624 | tf_op jit(solution)/shard_map/ppermute | solution.py:175
  41.3 2.5 %collective-permute-start.15 = (f32[216,128]{1,0:T(8,128)S(1)}, f32[216,128]{1,0:T(8,128)S(1)}, u32[]{:S(2)}, u32[]{:S(2)}) collective-permute-start(f32[216,128]{1,0:T(8,128)S(1)} %get-tuple-element.111), channel_id=1, source_target_pairs={{0,6},{1,7},{2,4},{3,5},{4,2},{5,3},{6,0},{7,1},{8,14},{9,15},{10,... | collective-permute-start | bytes 331784 | tf_op jit(solution)/shard_map/ppermute | solution.py:175
  43.8 1.9 %collective-permute-start.13 = (f32[216,128]{1,0:T(8,128)S(1)}, f32[216,128]{1,0:T(8,128)S(1)}, u32[]{:S(2)}, u32[]{:S(2)}) collective-permute-start(f32[216,128]{1,0:T(8,128)S(1)} %get-tuple-element.107), channel_id=1, source_target_pairs={{0,2},{1,3},{2,0},{3,1},{4,6},{5,7},{6,4},{7,5},{8,10},{9,11},{10,... | collective-permute-start | bytes 331784 | tf_op jit(solution)/shard_map/ppermute | solution.py:175
  45.7 5.1 %collective-permute-done.9.other_ref = f32[4,216,128]{2,1,0:T(8,128)S(1)} collective-permute-done((f32[4,216,128]{2,1,0:T(8,128)S(1)}, f32[4,216,128]{2,1,0:T(8,128)S(1)}, u32[]{:S(2)}, u32[]{:S(2)}) %collective-permute-start.9) | collective-permute-done | bytes 442400 | tf_op jit(solution)/shard_map/ppermute | solution.py:512
  51.4 1.9 %collective-permute-done.14.refs_2_ = f32[216,128]{1,0:T(8,128)S(1)} collective-permute-done((f32[216,128]{1,0:T(8,128)S(1)}, f32[216,128]{1,0:T(8,128)S(1)}, u32[]{:S(2)}, u32[]{:S(2)}) %collective-permute-start.14) | collective-permute-done | bytes 110624 | tf_op jit(solution)/shard_map/ppermute | solution.py:175
  55.3 2.2 %collective-permute-start.19 = (f32[216,128]{1,0:T(8,128)S(1)}, f32[216,128]{1,0:T(8,128)S(1)}, u32[]{:S(2)}, u32[]{:S(2)}) collective-permute-start(f32[216,128]{1,0:T(8,128)S(1)} %get-tuple-element.124), channel_id=1, source_target_pairs={{0,6},{1,7},{2,4},{3,5},{4,2},{5,3},{6,0},{7,1},{8,14},{9,15},{10,... | collective-permute-start | bytes 331784 | tf_op jit(solution)/shard_map/ppermute | solution.py:175
  57.5 2.2 %collective-permute-start.17 = (f32[216,128]{1,0:T(8,128)S(1)}, f32[216,128]{1,0:T(8,128)S(1)}, u32[]{:S(2)}, u32[]{:S(2)}) collective-permute-start(f32[216,128]{1,0:T(8,128)S(1)} %get-tuple-element.118), channel_id=1, source_target_pairs={{0,2},{1,3},{2,0},{3,1},{4,6},{5,7},{6,4},{7,5},{8,10},{9,11},{10,... | collective-permute-start | bytes 331784 | tf_op jit(solution)/shard_map/ppermute | solution.py:175
  59.7 3.4 %collective-permute-done.19.refs_3_ = f32[216,128]{1,0:T(8,128)S(1)} collective-permute-done((f32[216,128]{1,0:T(8,128)S(1)}, f32[216,128]{1,0:T(8,128)S(1)}, u32[]{:S(2)}, u32[]{:S(2)}) %collective-permute-start.19) | collective-permute-done | bytes 110624 | tf_op jit(solution)/shard_map/ppermute | solution.py:175
  63.0 3.8 %collective-permute-done.16.other_ref = f32[4,216,128]{2,1,0:T(8,128)S(1)} collective-permute-done((f32[4,216,128]{2,1,0:T(8,128)S(1)}, f32[4,216,128]{2,1,0:T(8,128)S(1)}, u32[]{:S(2)}, u32[]{:S(2)}) %collective-permute-start.16) | collective-permute-done | bytes 442400 | tf_op jit(solution)/shard_map/ppermute | solution.py:512
  70.1 2.1 %collective-permute-start.22 = (f32[216,128]{1,0:T(8,128)S(1)}, f32[216,128]{1,0:T(8,128)S(1)}, u32[]{:S(2)}, u32[]{:S(2)}) collective-permute-start(f32[216,128]{1,0:T(8,128)S(1)} %get-tuple-element.127), channel_id=1, source_target_pairs={{0,6},{1,7},{2,4},{3,5},{4,2},{5,3},{6,0},{7,1},{8,14},{9,15},{10,... | collective-permute-start | bytes 331784 | tf_op jit(solution)/shard_map/ppermute | solution.py:175
  72.2 2.4 %collective-permute-start.24 = (f32[216,128]{1,0:T(8,128)S(1)}, f32[216,128]{1,0:T(8,128)S(1)}, u32[]{:S(2)}, u32[]{:S(2)}) collective-permute-start(f32[216,128]{1,0:T(8,128)S(1)} %get-tuple-element.129), channel_id=1, source_target_pairs={{0,2},{1,3},{2,0},{3,1},{4,6},{5,7},{6,4},{7,5},{8,10},{9,11},{10,... | collective-permute-start | bytes 331784 | tf_op jit(solution)/shard_map/ppermute | solution.py:175
  76.0 2.0 %collective-permute-done.22.refs_3_ = f32[216,128]{1,0:T(8,128)S(1)} collective-permute-done((f32[216,128]{1,0:T(8,128)S(1)}, f32[216,128]{1,0:T(8,128)S(1)}, u32[]{:S(2)}, u32[]{:S(2)}) %collective-permute-start.22) | collective-permute-done | bytes 110624 | tf_op jit(solution)/shard_map/ppermute | solution.py:175
  78.0 3.9 %collective-permute-done.23.refs_2_ = f32[216,128]{1,0:T(8,128)S(1)} collective-permute-done((f32[216,128]{1,0:T(8,128)S(1)}, f32[216,128]{1,0:T(8,128)S(1)}, u32[]{:S(2)}, u32[]{:S(2)}) %collective-permute-start.23) | collective-permute-done | bytes 110624 | tf_op jit(solution)/shard_map/ppermute | solution.py:175
  85.3 2.1 %collective-permute-start.28 = (f32[216,128]{1,0:T(8,128)S(1)}, f32[216,128]{1,0:T(8,128)S(1)}, u32[]{:S(2)}, u32[]{:S(2)}) collective-permute-start(f32[216,128]{1,0:T(8,128)S(1)} %get-tuple-element.138), channel_id=1, source_target_pairs={{0,6},{1,7},{2,4},{3,5},{4,2},{5,3},{6,0},{7,1},{8,14},{9,15},{10,... | collective-permute-start | bytes 331784 | tf_op jit(solution)/shard_map/ppermute | solution.py:175
  87.4 2.4 %collective-permute-start.26 = (f32[216,128]{1,0:T(8,128)S(1)}, f32[216,128]{1,0:T(8,128)S(1)}, u32[]{:S(2)}, u32[]{:S(2)}) collective-permute-start(f32[216,128]{1,0:T(8,128)S(1)} %get-tuple-element.134), channel_id=1, source_target_pairs={{0,2},{1,3},{2,0},{3,1},{4,6},{5,7},{6,4},{7,5},{8,10},{9,11},{10,... | collective-permute-start | bytes 331784 | tf_op jit(solution)/shard_map/ppermute | solution.py:175
  91.2 2.0 %collective-permute-done.28.refs_3_ = f32[216,128]{1,0:T(8,128)S(1)} collective-permute-done((f32[216,128]{1,0:T(8,128)S(1)}, f32[216,128]{1,0:T(8,128)S(1)}, u32[]{:S(2)}, u32[]{:S(2)}) %collective-permute-start.28) | collective-permute-done | bytes 110624 | tf_op jit(solution)/shard_map/ppermute | solution.py:175
  93.2 4.0 %collective-permute-done.27.refs_2_ = f32[216,128]{1,0:T(8,128)S(1)} collective-permute-done((f32[216,128]{1,0:T(8,128)S(1)}, f32[216,128]{1,0:T(8,128)S(1)}, u32[]{:S(2)}, u32[]{:S(2)}) %collective-permute-start.27) | collective-permute-done | bytes 110624 | tf_op jit(solution)/shard_map/ppermute | solution.py:175
  101.6 2.1 %collective-permute-start.35 = (f32[216,128]{1,0:T(8,128)S(1)}, f32[216,128]{1,0:T(8,128)S(1)}, u32[]{:S(2)}, u32[]{:S(2)}) collective-permute-start(f32[216,128]{1,0:T(8,128)S(1)} %get-tuple-element.151), channel_id=1, source_target_pairs={{0,6},{1,7},{2,4},{3,5},{4,2},{5,3},{6,0},{7,1},{8,14},{9,15},{10,... | collective-permute-start | bytes 331784 | tf_op jit(solution)/shard_map/ppermute | solution.py:175
  103.7 2.3 %collective-permute-start.33 = (f32[216,128]{1,0:T(8,128)S(1)}, f32[216,128]{1,0:T(8,128)S(1)}, u32[]{:S(2)}, u32[]{:S(2)}) collective-permute-start(f32[216,128]{1,0:T(8,128)S(1)} %get-tuple-element.147), channel_id=1, source_target_pairs={{0,2},{1,3},{2,0},{3,1},{4,6},{5,7},{6,4},{7,5},{8,10},{9,11},{10,... | collective-permute-start | bytes 331784 | tf_op jit(solution)/shard_map/ppermute | solution.py:175
  106.0 5.1 %collective-permute-done.29.other_ref = f32[4,216,128]{2,1,0:T(8,128)S(1)} collective-permute-done((f32[4,216,128]{2,1,0:T(8,128)S(1)}, f32[4,216,128]{2,1,0:T(8,128)S(1)}, u32[]{:S(2)}, u32[]{:S(2)}) %collective-permute-start.29) | collective-permute-done | bytes 442400 | tf_op jit(solution)/shard_map/ppermute | solution.py:512
  117.4 2.6 %collective-permute-start.37 = (f32[216,128]{1,0:T(8,128)S(1)}, f32[216,128]{1,0:T(8,128)S(1)}, u32[]{:S(2)}, u32[]{:S(2)}) collective-permute-start(f32[216,128]{1,0:T(8,128)S(1)} %get-tuple-element.158), channel_id=1, source_target_pairs={{0,2},{1,3},{2,0},{3,1},{4,6},{5,7},{6,4},{7,5},{8,10},{9,11},{10,... | collective-permute-start | bytes 331784 | tf_op jit(solution)/shard_map/ppermute | solution.py:175
  119.9 6.9 %collective-permute-done.36.other_ref = f32[4,216,128]{2,1,0:T(8,128)S(1)} collective-permute-done((f32[4,216,128]{2,1,0:T(8,128)S(1)}, f32[4,216,128]{2,1,0:T(8,128)S(1)}, u32[]{:S(2)}, u32[]{:S(2)}) %collective-permute-start.36) | collective-permute-done | bytes 442400 | tf_op jit(solution)/shard_map/ppermute | solution.py:512
  127.4 2.1 %collective-permute-start.42 = (f32[216,128]{1,0:T(8,128)S(1)}, f32[216,128]{1,0:T(8,128)S(1)}, u32[]{:S(2)}, u32[]{:S(2)}) collective-permute-start(f32[216,128]{1,0:T(8,128)S(1)} %get-tuple-element.172), channel_id=1, source_target_pairs={{0,6},{1,7},{2,4},{3,5},{4,2},{5,3},{6,0},{7,1},{8,14},{9,15},{10,... | collective-permute-start | bytes 331784 | tf_op jit(solution)/shard_map/ppermute | solution.py:175
  129.6 2.3 %collective-permute-start.40 = (f32[216,128]{1,0:T(8,128)S(1)}, f32[216,128]{1,0:T(8,128)S(1)}, u32[]{:S(2)}, u32[]{:S(2)}) collective-permute-start(f32[216,128]{1,0:T(8,128)S(1)} %get-tuple-element.168), channel_id=1, source_target_pairs={{0,2},{1,3},{2,0},{3,1},{4,6},{5,7},{6,4},{7,5},{8,10},{9,11},{10,... | collective-permute-start | bytes 331784 | tf_op jit(solution)/shard_map/ppermute | solution.py:175
  135.3 3.1 %collective-permute-done.41.refs_3_ = f32[216,128]{1,0:T(8,128)S(1)} collective-permute-done((f32[216,128]{1,0:T(8,128)S(1)}, f32[216,128]{1,0:T(8,128)S(1)}, u32[]{:S(2)}, u32[]{:S(2)}) %collective-permute-start.41) | collective-permute-done | bytes 110624 | tf_op jit(solution)/shard_map/ppermute | solution.py:175
  143.2 2.1 %shard_map.160 = (f32[2,6,48,384]{3,2,1,0:T(8,128)}, f32[48,384]{1,0:T(8,128)}, f32[32,128]{1,0:T(8,128)S(1)}) custom-call(s32[2]{0:T(128)S(1)} %pad_add_fusion.me_ref, f32[2,6]{1,0:T(2,128)S(1)} %copy-done.10, s32[1]{0:T(128)S(6)} %copy.29.count_ref, f32[5,48,384]{2,1,0:T(8,128)S(1)} %copy-done.2, s32[48,384]{1,0:T(8,128)S(1)} %copy-done.5, ...), custom_call_target="tpu_custom_call" | custom-call | flops 1 | bytes 1 | tf_op jit(solution)/shard_map/pallas_call | solution.py:444
  145.3 10.0 %all_to_all.11 = f32[32,1,128]{2,1,0:T(1,128)S(1)} all-to-all(f32[32,1,128]{2,1,0:T(1,128)S(1)} %bitcast.18), channel_id=1, replica_groups=mesh['gx'=4,'gy'=8] {'gx','gy'}, dimensions={0} | all-to-all | bytes 32768 | tf_op jit(solution)/shard_map/all_to_all | solution.py:539
  (111 shorter events, 50.3 us)
Async XLA Ops:
  2.4 8.3 %collective-permute-start.3 = (f32[6,48,384]{2,1,0:T(8,128)}, f32[6,48,384]{2,1,0:T(8,128)}, u32[]{:S(2)}, u32[]{:S(2)}) collective-permute-start(f32[6,48,384]{2,1,0:T(8,128)} %slice_bitcast_fusion.1.refs_0_), channel_id=1, source_target_pairs={{0,8},{8,0},{16,24},{24,16},{1,9},{9,1},{17,25},{25,17},{2,10},{10... | collective-permute-start | bytes 1327112 | tf_op jit(solution)/shard_map/ppermute | solution.py:154
  2.9 15.8 %collective-permute-start.4 = (f32[6,48,384]{2,1,0:T(8,128)}, f32[6,48,384]{2,1,0:T(8,128)}, u32[]{:S(2)}, u32[]{:S(2)}) collective-permute-start(f32[6,48,384]{2,1,0:T(8,128)} %slice_bitcast_fusion.1.refs_0_), channel_id=1, source_target_pairs={{0,16},{8,24},{16,0},{24,8},{1,17},{9,25},{17,1},{25,9},{2,18},{10... | collective-permute-start | bytes 1327112 | tf_op jit(solution)/shard_map/ppermute | solution.py:163
  7.2 11.5 %collective-permute-start.1 = (f32[96,192]{1,0:T(8,128)}, f32[96,192]{1,0:T(8,128)}, u32[]{:S(2)}, u32[]{:S(2)}) collective-permute-start(f32[96,192]{1,0:T(8,128)} %copy.26.refs_0_), channel_id=1, source_target_pairs={{0,16},{8,24},{16,0},{24,8},{1,17},{9,25},{17,1},{25,9},{2,18},{10... | collective-permute-start | bytes 221192 | tf_op jit(solution)/shard_map/ppermute | solution.py:163
  18.7 10.4 %collective-permute-start.10 = (f32[6,48,384]{2,1,0:T(8,128)S(1)}, f32[6,48,384]{2,1,0:T(8,128)S(1)}, u32[]{:S(2)}, u32[]{:S(2)}) collective-permute-start(f32[6,48,384]{2,1,0:T(8,128)S(1)} %slice_bitcast_fusion.refs_0_), channel_id=1, source_target_pairs={{0,8},{8,0},{16,24},{24,16},{1,9},{9,1},{17,25},{25,17},{2,10},{10... | collective-permute-start | bytes 1327112 | tf_op jit(solution)/shard_map/ppermute | solution.py:154
  19.2 17.6 %collective-permute-start.11 = (f32[6,48,384]{2,1,0:T(8,128)S(1)}, f32[6,48,384]{2,1,0:T(8,128)S(1)}, u32[]{:S(2)}, u32[]{:S(2)}) collective-permute-start(f32[6,48,384]{2,1,0:T(8,128)S(1)} %slice_bitcast_fusion.refs_0_), channel_id=1, source_target_pairs={{0,16},{8,24},{16,0},{24,8},{1,17},{9,25},{17,1},{25,9},{2,18},{10... | collective-permute-start | bytes 1327112 | tf_op jit(solution)/shard_map/ppermute | solution.py:163
  27.2 9.6 %collective-permute-start.7 = (f32[216,128]{1,0:T(8,128)S(1)}, f32[216,128]{1,0:T(8,128)S(1)}, u32[]{:S(2)}, u32[]{:S(2)}) collective-permute-start(f32[216,128]{1,0:T(8,128)S(1)} %get-tuple-element.96), channel_id=1, source_target_pairs={{0,4},{1,5},{2,6},{3,7},{4,0},{5,1},{6,2},{7,3},{8,12},{9,13},{10,... | collective-permute-start | bytes 331784 | tf_op jit(solution)/shard_map/ppermute | solution.py:175
  27.2 9.6 %collective-permute-start.6 = (f32[216,128]{1,0:T(8,128)S(1)}, f32[216,128]{1,0:T(8,128)S(1)}, u32[]{:S(2)}, u32[]{:S(2)}) collective-permute-start(f32[216,128]{1,0:T(8,128)S(1)} %get-tuple-element.94), channel_id=1, source_target_pairs={{0,2},{1,3},{2,0},{3,1},{4,6},{5,7},{6,4},{7,5},{8,10},{9,11},{10,... | collective-permute-start | bytes 331784 | tf_op jit(solution)/shard_map/ppermute | solution.py:175
  38.2 12.6 %collective-permute-start.9 = (f32[4,216,128]{2,1,0:T(8,128)S(1)}, f32[4,216,128]{2,1,0:T(8,128)S(1)}, u32[]{:S(2)}, u32[]{:S(2)}) collective-permute-start(f32[4,216,128]{2,1,0:T(8,128)S(1)} %get-tuple-element.101), channel_id=1, source_target_pairs={{0,1},{1,0},{2,3},{3,2},{4,5},{5,4},{6,7},{7,6},{8,9},{9,8},{10,11... | collective-permute-start | bytes 1327112 | tf_op jit(solution)/shard_map/ppermute | solution.py:512
  41.3 10.1 %collective-permute-start.15 = (f32[216,128]{1,0:T(8,128)S(1)}, f32[216,128]{1,0:T(8,128)S(1)}, u32[]{:S(2)}, u32[]{:S(2)}) collective-permute-start(f32[216,128]{1,0:T(8,128)S(1)} %get-tuple-element.111), channel_id=1, source_target_pairs={{0,6},{1,7},{2,4},{3,5},{4,2},{5,3},{6,0},{7,1},{8,14},{9,15},{10,... | collective-permute-start | bytes 331784 | tf_op jit(solution)/shard_map/ppermute | solution.py:175
  43.8 9.5 %collective-permute-start.14 = (f32[216,128]{1,0:T(8,128)S(1)}, f32[216,128]{1,0:T(8,128)S(1)}, u32[]{:S(2)}, u32[]{:S(2)}) collective-permute-start(f32[216,128]{1,0:T(8,128)S(1)} %get-tuple-element.109), channel_id=1, source_target_pairs={{0,4},{1,5},{2,6},{3,7},{4,0},{5,1},{6,2},{7,3},{8,12},{9,13},{10,... | collective-permute-start | bytes 331784 | tf_op jit(solution)/shard_map/ppermute | solution.py:175
  43.8 9.5 %collective-permute-start.13 = (f32[216,128]{1,0:T(8,128)S(1)}, f32[216,128]{1,0:T(8,128)S(1)}, u32[]{:S(2)}, u32[]{:S(2)}) collective-permute-start(f32[216,128]{1,0:T(8,128)S(1)} %get-tuple-element.107), channel_id=1, source_target_pairs={{0,2},{1,3},{2,0},{3,1},{4,6},{5,7},{6,4},{7,5},{8,10},{9,11},{10,... | collective-permute-start | bytes 331784 | tf_op jit(solution)/shard_map/ppermute | solution.py:175
  54.7 12.1 %collective-permute-start.16 = (f32[4,216,128]{2,1,0:T(8,128)S(1)}, f32[4,216,128]{2,1,0:T(8,128)S(1)}, u32[]{:S(2)}, u32[]{:S(2)}) collective-permute-start(f32[4,216,128]{2,1,0:T(8,128)S(1)} %get-tuple-element.115), channel_id=1, source_target_pairs={{0,1},{1,0},{2,3},{3,2},{4,5},{5,4},{6,7},{7,6},{8,9},{9,8},{10,11... | collective-permute-start | bytes 1327112 | tf_op jit(solution)/shard_map/ppermute | solution.py:512
  57.5 9.5 %collective-permute-start.18 = (f32[216,128]{1,0:T(8,128)S(1)}, f32[216,128]{1,0:T(8,128)S(1)}, u32[]{:S(2)}, u32[]{:S(2)}) collective-permute-start(f32[216,128]{1,0:T(8,128)S(1)} %get-tuple-element.121), channel_id=1, source_target_pairs={{0,4},{1,5},{2,6},{3,7},{4,0},{5,1},{6,2},{7,3},{8,12},{9,13},{10,... | collective-permute-start | bytes 331784 | tf_op jit(solution)/shard_map/ppermute | solution.py:175
  57.5 9.5 %collective-permute-start.17 = (f32[216,128]{1,0:T(8,128)S(1)}, f32[216,128]{1,0:T(8,128)S(1)}, u32[]{:S(2)}, u32[]{:S(2)}) collective-permute-start(f32[216,128]{1,0:T(8,128)S(1)} %get-tuple-element.118), channel_id=1, source_target_pairs={{0,2},{1,3},{2,0},{3,1},{4,6},{5,7},{6,4},{7,5},{8,10},{9,11},{10,... | collective-permute-start | bytes 331784 | tf_op jit(solution)/shard_map/ppermute | solution.py:175
  67.9 13.9 %collective-permute-start.21 = (f32[6,48,384]{2,1,0:T(8,128)S(1)}, f32[6,48,384]{2,1,0:T(8,128)S(1)}, u32[]{:S(2)}, u32[]{:S(2)}) collective-permute-start(f32[6,48,384]{2,1,0:T(8,128)S(1)} %shard_map.148.refs_0_), channel_id=1, source_target_pairs={{0,16},{8,24},{16,0},{24,8},{1,17},{9,25},{17,1},{25,9},{2,18},{10... | collective-permute-start | bytes 1327112 | tf_op jit(solution)/shard_map/ppermute | solution.py:163
  72.2 9.6 %collective-permute-start.23 = (f32[216,128]{1,0:T(8,128)S(1)}, f32[216,128]{1,0:T(8,128)S(1)}, u32[]{:S(2)}, u32[]{:S(2)}) collective-permute-start(f32[216,128]{1,0:T(8,128)S(1)} %get-tuple-element.128), channel_id=1, source_target_pairs={{0,4},{1,5},{2,6},{3,7},{4,0},{5,1},{6,2},{7,3},{8,12},{9,13},{10,... | collective-permute-start | bytes 331784 | tf_op jit(solution)/shard_map/ppermute | solution.py:175
  72.2 9.6 %collective-permute-start.24 = (f32[216,128]{1,0:T(8,128)S(1)}, f32[216,128]{1,0:T(8,128)S(1)}, u32[]{:S(2)}, u32[]{:S(2)}) collective-permute-start(f32[216,128]{1,0:T(8,128)S(1)} %get-tuple-element.129), channel_id=1, source_target_pairs={{0,2},{1,3},{2,0},{3,1},{4,6},{5,7},{6,4},{7,5},{8,10},{9,11},{10,... | collective-permute-start | bytes 331784 | tf_op jit(solution)/shard_map/ppermute | solution.py:175
  83.2 14.0 %collective-permute-start.31 = (f32[6,48,384]{2,1,0:T(8,128)S(1)}, f32[6,48,384]{2,1,0:T(8,128)S(1)}, u32[]{:S(2)}, u32[]{:S(2)}) collective-permute-start(f32[6,48,384]{2,1,0:T(8,128)S(1)} %shard_map.154.refs_0_), channel_id=1, source_target_pairs={{0,16},{8,24},{16,0},{24,8},{1,17},{9,25},{17,1},{25,9},{2,18},{10... | collective-permute-start | bytes 1327112 | tf_op jit(solution)/shard_map/ppermute | solution.py:163
  85.3 7.9 %collective-permute-start.28 = (f32[216,128]{1,0:T(8,128)S(1)}, f32[216,128]{1,0:T(8,128)S(1)}, u32[]{:S(2)}, u32[]{:S(2)}) collective-permute-start(f32[216,128]{1,0:T(8,128)S(1)} %get-tuple-element.138), channel_id=1, source_target_pairs={{0,6},{1,7},{2,4},{3,5},{4,2},{5,3},{6,0},{7,1},{8,14},{9,15},{10,... | collective-permute-start | bytes 331784 | tf_op jit(solution)/shard_map/ppermute | solution.py:175
  87.4 9.8 %collective-permute-start.27 = (f32[216,128]{1,0:T(8,128)S(1)}, f32[216,128]{1,0:T(8,128)S(1)}, u32[]{:S(2)}, u32[]{:S(2)}) collective-permute-start(f32[216,128]{1,0:T(8,128)S(1)} %get-tuple-element.136), channel_id=1, source_target_pairs={{0,4},{1,5},{2,6},{3,7},{4,0},{5,1},{6,2},{7,3},{8,12},{9,13},{10,... | collective-permute-start | bytes 331784 | tf_op jit(solution)/shard_map/ppermute | solution.py:175
  87.4 9.8 %collective-permute-start.26 = (f32[216,128]{1,0:T(8,128)S(1)}, f32[216,128]{1,0:T(8,128)S(1)}, u32[]{:S(2)}, u32[]{:S(2)}) collective-permute-start(f32[216,128]{1,0:T(8,128)S(1)} %get-tuple-element.134), channel_id=1, source_target_pairs={{0,2},{1,3},{2,0},{3,1},{4,6},{5,7},{6,4},{7,5},{8,10},{9,11},{10,... | collective-permute-start | bytes 331784 | tf_op jit(solution)/shard_map/ppermute | solution.py:175
  98.5 12.6 %collective-permute-start.29 = (f32[4,216,128]{2,1,0:T(8,128)S(1)}, f32[4,216,128]{2,1,0:T(8,128)S(1)}, u32[]{:S(2)}, u32[]{:S(2)}) collective-permute-start(f32[4,216,128]{2,1,0:T(8,128)S(1)} %get-tuple-element.141), channel_id=1, source_target_pairs={{0,1},{1,0},{2,3},{3,2},{4,5},{5,4},{6,7},{7,6},{8,9},{9,8},{10,11... | collective-permute-start | bytes 1327112 | tf_op jit(solution)/shard_map/ppermute | solution.py:512
  101.6 10.2 %collective-permute-start.35 = (f32[216,128]{1,0:T(8,128)S(1)}, f32[216,128]{1,0:T(8,128)S(1)}, u32[]{:S(2)}, u32[]{:S(2)}) collective-permute-start(f32[216,128]{1,0:T(8,128)S(1)} %get-tuple-element.151), channel_id=1, source_target_pairs={{0,6},{1,7},{2,4},{3,5},{4,2},{5,3},{6,0},{7,1},{8,14},{9,15},{10,... | collective-permute-start | bytes 331784 | tf_op jit(solution)/shard_map/ppermute | solution.py:175
  103.7 9.6 %collective-permute-start.34 = (f32[216,128]{1,0:T(8,128)S(1)}, f32[216,128]{1,0:T(8,128)S(1)}, u32[]{:S(2)}, u32[]{:S(2)}) collective-permute-start(f32[216,128]{1,0:T(8,128)S(1)} %get-tuple-element.149), channel_id=1, source_target_pairs={{0,4},{1,5},{2,6},{3,7},{4,0},{5,1},{6,2},{7,3},{8,12},{9,13},{10,... | collective-permute-start | bytes 331784 | tf_op jit(solution)/shard_map/ppermute | solution.py:175
  103.7 9.6 %collective-permute-start.33 = (f32[216,128]{1,0:T(8,128)S(1)}, f32[216,128]{1,0:T(8,128)S(1)}, u32[]{:S(2)}, u32[]{:S(2)}) collective-permute-start(f32[216,128]{1,0:T(8,128)S(1)} %get-tuple-element.147), channel_id=1, source_target_pairs={{0,2},{1,3},{2,0},{3,1},{4,6},{5,7},{6,4},{7,5},{8,10},{9,11},{10,... | collective-permute-start | bytes 331784 | tf_op jit(solution)/shard_map/ppermute | solution.py:175
  114.7 12.2 %collective-permute-start.36 = (f32[4,216,128]{2,1,0:T(8,128)S(1)}, f32[4,216,128]{2,1,0:T(8,128)S(1)}, u32[]{:S(2)}, u32[]{:S(2)}) collective-permute-start(f32[4,216,128]{2,1,0:T(8,128)S(1)} %get-tuple-element.155), channel_id=1, source_target_pairs={{0,1},{1,0},{2,3},{3,2},{4,5},{5,4},{6,7},{7,6},{8,9},{9,8},{10,11... | collective-permute-start | bytes 1327112 | tf_op jit(solution)/shard_map/ppermute | solution.py:512
  115.6 14.0 %collective-permute-start.39 = (f32[216,128]{1,0:T(8,128)S(1)}, f32[216,128]{1,0:T(8,128)S(1)}, u32[]{:S(2)}, u32[]{:S(2)}) collective-permute-start(f32[216,128]{1,0:T(8,128)S(1)} %get-tuple-element.164), channel_id=1, source_target_pairs={{0,6},{1,7},{2,4},{3,5},{4,2},{5,3},{6,0},{7,1},{8,14},{9,15},{10,... | collective-permute-start | bytes 331784 | tf_op jit(solution)/shard_map/ppermute | solution.py:175
  117.4 15.3 %collective-permute-start.38 = (f32[216,128]{1,0:T(8,128)S(1)}, f32[216,128]{1,0:T(8,128)S(1)}, u32[]{:S(2)}, u32[]{:S(2)}) collective-permute-start(f32[216,128]{1,0:T(8,128)S(1)} %get-tuple-element.161), channel_id=1, source_target_pairs={{0,4},{1,5},{2,6},{3,7},{4,0},{5,1},{6,2},{7,3},{8,12},{9,13},{10,... | collective-permute-start | bytes 331784 | tf_op jit(solution)/shard_map/ppermute | solution.py:175
  117.4 15.3 %collective-permute-start.37 = (f32[216,128]{1,0:T(8,128)S(1)}, f32[216,128]{1,0:T(8,128)S(1)}, u32[]{:S(2)}, u32[]{:S(2)}) collective-permute-start(f32[216,128]{1,0:T(8,128)S(1)} %get-tuple-element.158), channel_id=1, source_target_pairs={{0,2},{1,3},{2,0},{3,1},{4,6},{5,7},{6,4},{7,5},{8,10},{9,11},{10,... | collective-permute-start | bytes 331784 | tf_op jit(solution)/shard_map/ppermute | solution.py:175
  127.4 7.9 %collective-permute-start.42 = (f32[216,128]{1,0:T(8,128)S(1)}, f32[216,128]{1,0:T(8,128)S(1)}, u32[]{:S(2)}, u32[]{:S(2)}) collective-permute-start(f32[216,128]{1,0:T(8,128)S(1)} %get-tuple-element.172), channel_id=1, source_target_pairs={{0,6},{1,7},{2,4},{3,5},{4,2},{5,3},{6,0},{7,1},{8,14},{9,15},{10,... | collective-permute-start | bytes 331784 | tf_op jit(solution)/shard_map/ppermute | solution.py:175
  129.6 8.9 %collective-permute-start.41 = (f32[216,128]{1,0:T(8,128)S(1)}, f32[216,128]{1,0:T(8,128)S(1)}, u32[]{:S(2)}, u32[]{:S(2)}) collective-permute-start(f32[216,128]{1,0:T(8,128)S(1)} %get-tuple-element.170), channel_id=1, source_target_pairs={{0,4},{1,5},{2,6},{3,7},{4,0},{5,1},{6,2},{7,3},{8,12},{9,13},{10,... | collective-permute-start | bytes 331784 | tf_op jit(solution)/shard_map/ppermute | solution.py:175
  129.6 8.9 %collective-permute-start.40 = (f32[216,128]{1,0:T(8,128)S(1)}, f32[216,128]{1,0:T(8,128)S(1)}, u32[]{:S(2)}, u32[]{:S(2)}) collective-permute-start(f32[216,128]{1,0:T(8,128)S(1)} %get-tuple-element.168), channel_id=1, source_target_pairs={{0,2},{1,3},{2,0},{3,1},{4,6},{5,7},{6,4},{7,5},{8,10},{9,11},{10,... | collective-permute-start | bytes 331784 | tf_op jit(solution)/shard_map/ppermute | solution.py:175
  (24 other events, 218.6 us)

commit v7 on v4

--- a/solution.py
+++ b/solution.py
@@ -506,17 +506,21 @@
                 total = after(total, own[-1])
             packed = zonal_end(plan, total, far, me, *x_parts, sea_mask)
             sent.append(exchange(packed, "gy", gy_count))
-            ready = other[-1] if other else y_parts[0]
+            if other:
+                sums = add_sides(plan, me, own[-1], other[-1])
+            ready = sums[0] if other else y_parts[0]
             lines = [after(line, ready) for line in sent[chunk]]
             for_own, for_other = meridional(plan, me, lines, *y_parts)
             own.append(for_own)
             other.append(lax.ppermute(for_other, "gy", side_pairs))
         for chunk in range(chunks):
-            if chunk == 0:
-                own[chunk] = after(own[chunk], own[-1])
-            elif step < STEPS - 1:
-                own[chunk] = after(own[chunk], fields[chunk - 1])
-            returned = exchange(add_sides(plan, me, own[chunk], other[chunk]), "gy", gy_count)
+            if chunk == 0 and chunks > 1:
+                blocks = [after(block, own[-1]) for block in sums]
+            else:
+                if chunk > 0 and step < STEPS - 1:
+                    own[chunk] = after(own[chunk], fields[chunk - 1])
+                blocks = add_sides(plan, me, own[chunk], other[chunk])
+            returned = exchange(blocks, "gy", gy_count)
             if chunk < chunks - 1:
                 returned = [after(block, other[-1]) for block in returned]
             if step < STEPS - 1 or chunk < chunks - 1:

time: 151 us -> 151 us (level)
    ppermute x24, waiting for transfers between devices: 32.2 us -> 30.3 us  [exchange(): out[mask] = lax.ppermute(blocks[mask], axis, pairs)]
where the time goes in v7:
time: 151 us; the launch traced here: 150 us
  waiting for transfers between devices  56.1 us (37%)
  starting transfers between devices  48.5 us (32%)
  Pallas kernels  27.4 us (18%)
  blocking collectives  9.99 us (7%)
  local copies, waits for them, and re-layouts  6.78 us (4%)
  between operations  1.62 us (1%)
    ppermute x24, starting transfers between devices, exchange(): out[mask] = lax.ppermute(blocks[mask], axis, pairs)  35.5 us
    ppermute x24, waiting for transfers between devices, exchange(): out[mask] = lax.ppermute(blocks[mask], axis, pairs)  30.3 us
    pallas_call x22, Pallas kernels, call(): pl.pallas_call(kernel, out_shape=out_shape, in_specs=specs, out_specs=[ou...  25.3 us
    ppermute x4, waiting for transfers between devices, body(): other.append(lax.ppermute(for_other, 'gy', side_pairs))  20.9 us
    all_to_all x1, blocking collectives, body(): lax.all_to_all(outgoing, ('gx', 'gy'), split_axis=0, concat_axis=0, tiled...  9.99 us
    ppermute x10, starting transfers between devices, gather_far(): lax.ppermute(piece, axis, pairs)  7.07 us
    ppermute x10, waiting for transfers between devices, gather_far(): lax.ppermute(piece, axis, pairs)  4.86 us
    unnamed x24, local copies, waits for them, and re-layouts  4.6 us
  transfers between devices with their start and end apart: 43, of which 17 were waited for; matrix products, arithmetic and copies ran while one was open for 2% of the time, Pallas kernels for 14%

profile of v7, /device:TPU:0, one launch (start us, length us, event | category | flops | bytes accessed | tf_op | source)
XLA Modules:
  0.0 150.5 jit_solution(13647303586571255635)
XLA Ops:
  2.2 2.6 %collective-permute-start.4 = (f32[6,48,384]{2,1,0:T(8,128)S(1)}, f32[6,48,384]{2,1,0:T(8,128)}, u32[]{:S(2)}, u32[]{:S(2)}) collective-permute-start(f32[6,48,384]{2,1,0:T(8,128)S(1)} %slice_bitcast_fusion.1.refs_0_), channel_id=1, source_target_pairs={{0,16},{8,24},{16,0},{24,8},{1,17},{9,25},{17,1},{25,9},{2,18},{10... | collective-permute-start | bytes 1327112 | tf_op jit(solution)/shard_map/ppermute | solution.py:157
  12.8 4.8 %collective-permute-done.1.refs_2_ = f32[96,192]{1,0:T(8,128)S(1)} collective-permute-done((f32[96,192]{1,0:T(8,128)S(1)}, f32[96,192]{1,0:T(8,128)S(1)}, u32[]{:S(2)}, u32[]{:S(2)}) %collective-permute-start.1) | collective-permute-done | bytes 73760 | tf_op jit(solution)/shard_map/ppermute | solution.py:157
  20.4 2.1 %shard_map.142 = (f32[216,128]{1,0:T(8,128)S(1)}, f32[216,128]{1,0:T(8,128)S(1)}, f32[216,128]{1,0:T(8,128)S(1)}, f32[216,128]{1,0:T(8,128)S(1)}) custom-call(s32[2]{0:T(128)S(1)} %pad_add_fusion.me_ref, bf16[1536,384]{1,0:T(8,128)(2,1)S(1)} %get-tuple-element.96.high_ref, bf16[1536,384]{1,0:T(8,128)(2,1)S(1)} %get-tuple-element.97.low_ref, ...), custom_call_target="tpu_custom_call" | custom-call | flops 1 | bytes 1 | tf_op jit(solution)/shard_map/pallas_call | solution.py:131
  22.6 3.7 %collective-permute-start.8 = (f32[216,128]{1,0:T(8,128)S(1)}, f32[216,128]{1,0:T(8,128)S(1)}, u32[]{:S(2)}, u32[]{:S(2)}) collective-permute-start(f32[216,128]{1,0:T(8,128)S(1)} %get-tuple-element.106), channel_id=1, source_target_pairs={{0,6},{1,7},{2,4},{3,5},{4,2},{5,3},{6,0},{7,1},{8,14},{9,15},{10,... | collective-permute-start | bytes 331784 | tf_op jit(solution)/shard_map/ppermute | solution.py:169
  30.4 5.5 %collective-permute-done.7.refs_2_ = f32[216,128]{1,0:T(8,128)S(1)} collective-permute-done((f32[216,128]{1,0:T(8,128)S(1)}, f32[216,128]{1,0:T(8,128)S(1)}, u32[]{:S(2)}, u32[]{:S(2)}) %collective-permute-start.7) | collective-permute-done | bytes 110624 | tf_op jit(solution)/shard_map/ppermute | solution.py:169
  40.5 2.5 %collective-permute-start.15 = (f32[216,128]{1,0:T(8,128)S(1)}, f32[216,128]{1,0:T(8,128)S(1)}, u32[]{:S(2)}, u32[]{:S(2)}) collective-permute-start(f32[216,128]{1,0:T(8,128)S(1)} %get-tuple-element.119), channel_id=1, source_target_pairs={{0,6},{1,7},{2,4},{3,5},{4,2},{5,3},{6,0},{7,1},{8,14},{9,15},{10,... | collective-permute-start | bytes 331784 | tf_op jit(solution)/shard_map/ppermute | solution.py:169
  43.0 1.9 %collective-permute-start.13 = (f32[216,128]{1,0:T(8,128)S(1)}, f32[216,128]{1,0:T(8,128)S(1)}, u32[]{:S(2)}, u32[]{:S(2)}) collective-permute-start(f32[216,128]{1,0:T(8,128)S(1)} %get-tuple-element.115), channel_id=1, source_target_pairs={{0,2},{1,3},{2,0},{3,1},{4,6},{5,7},{6,4},{7,5},{8,10},{9,11},{10,... | collective-permute-start | bytes 331784 | tf_op jit(solution)/shard_map/ppermute | solution.py:169
  44.9 5.0 %collective-permute-done.9.other_ref = f32[4,216,128]{2,1,0:T(8,128)S(1)} collective-permute-done((f32[4,216,128]{2,1,0:T(8,128)S(1)}, f32[4,216,128]{2,1,0:T(8,128)S(1)}, u32[]{:S(2)}, u32[]{:S(2)}) %collective-permute-start.9) | collective-permute-done | bytes 442400 | tf_op jit(solution)/shard_map/ppermute | solution.py:515
  50.5 2.0 %collective-permute-done.14.refs_2_ = f32[216,128]{1,0:T(8,128)S(1)} collective-permute-done((f32[216,128]{1,0:T(8,128)S(1)}, f32[216,128]{1,0:T(8,128)S(1)}, u32[]{:S(2)}, u32[]{:S(2)}) %collective-permute-start.14) | collective-permute-done | bytes 110624 | tf_op jit(solution)/shard_map/ppermute | solution.py:169
  54.4 2.2 %collective-permute-start.19 = (f32[216,128]{1,0:T(8,128)S(1)}, f32[216,128]{1,0:T(8,128)S(1)}, u32[]{:S(2)}, u32[]{:S(2)}) collective-permute-start(f32[216,128]{1,0:T(8,128)S(1)} %get-tuple-element.132), channel_id=1, source_target_pairs={{0,6},{1,7},{2,4},{3,5},{4,2},{5,3},{6,0},{7,1},{8,14},{9,15},{10,... | collective-permute-start | bytes 331784 | tf_op jit(solution)/shard_map/ppermute | solution.py:169
  56.7 2.2 %collective-permute-start.17 = (f32[216,128]{1,0:T(8,128)S(1)}, f32[216,128]{1,0:T(8,128)S(1)}, u32[]{:S(2)}, u32[]{:S(2)}) collective-permute-start(f32[216,128]{1,0:T(8,128)S(1)} %get-tuple-element.126), channel_id=1, source_target_pairs={{0,2},{1,3},{2,0},{3,1},{4,6},{5,7},{6,4},{7,5},{8,10},{9,11},{10,... | collective-permute-start | bytes 331784 | tf_op jit(solution)/shard_map/ppermute | solution.py:169
  58.8 3.4 %collective-permute-done.19.refs_3_ = f32[216,128]{1,0:T(8,128)S(1)} collective-permute-done((f32[216,128]{1,0:T(8,128)S(1)}, f32[216,128]{1,0:T(8,128)S(1)}, u32[]{:S(2)}, u32[]{:S(2)}) %collective-permute-start.19) | collective-permute-done | bytes 110624 | tf_op jit(solution)/shard_map/ppermute | solution.py:169
  62.2 3.8 %collective-permute-done.16.other_ref = f32[4,216,128]{2,1,0:T(8,128)S(1)} collective-permute-done((f32[4,216,128]{2,1,0:T(8,128)S(1)}, f32[4,216,128]{2,1,0:T(8,128)S(1)}, u32[]{:S(2)}, u32[]{:S(2)}) %collective-permute-start.16) | collective-permute-done | bytes 442400 | tf_op jit(solution)/shard_map/ppermute | solution.py:515
  69.3 2.1 %collective-permute-start.22 = (f32[216,128]{1,0:T(8,128)S(1)}, f32[216,128]{1,0:T(8,128)S(1)}, u32[]{:S(2)}, u32[]{:S(2)}) collective-permute-start(f32[216,128]{1,0:T(8,128)S(1)} %get-tuple-element.135), channel_id=1, source_target_pairs={{0,6},{1,7},{2,4},{3,5},{4,2},{5,3},{6,0},{7,1},{8,14},{9,15},{10,... | collective-permute-start | bytes 331784 | tf_op jit(solution)/shard_map/ppermute | solution.py:169
  71.4 2.4 %collective-permute-start.24 = (f32[216,128]{1,0:T(8,128)S(1)}, f32[216,128]{1,0:T(8,128)S(1)}, u32[]{:S(2)}, u32[]{:S(2)}) collective-permute-start(f32[216,128]{1,0:T(8,128)S(1)} %get-tuple-element.137), channel_id=1, source_target_pairs={{0,2},{1,3},{2,0},{3,1},{4,6},{5,7},{6,4},{7,5},{8,10},{9,11},{10,... | collective-permute-start | bytes 331784 | tf_op jit(solution)/shard_map/ppermute | solution.py:169
  75.2 1.9 %collective-permute-done.22.refs_3_ = f32[216,128]{1,0:T(8,128)S(1)} collective-permute-done((f32[216,128]{1,0:T(8,128)S(1)}, f32[216,128]{1,0:T(8,128)S(1)}, u32[]{:S(2)}, u32[]{:S(2)}) %collective-permute-start.22) | collective-permute-done | bytes 110624 | tf_op jit(solution)/shard_map/ppermute | solution.py:169
  77.1 3.9 %collective-permute-done.23.refs_2_ = f32[216,128]{1,0:T(8,128)S(1)} collective-permute-done((f32[216,128]{1,0:T(8,128)S(1)}, f32[216,128]{1,0:T(8,128)S(1)}, u32[]{:S(2)}, u32[]{:S(2)}) %collective-permute-start.23) | collective-permute-done | bytes 110624 | tf_op jit(solution)/shard_map/ppermute | solution.py:169
  84.5 2.1 %collective-permute-start.28 = (f32[216,128]{1,0:T(8,128)S(1)}, f32[216,128]{1,0:T(8,128)S(1)}, u32[]{:S(2)}, u32[]{:S(2)}) collective-permute-start(f32[216,128]{1,0:T(8,128)S(1)} %get-tuple-element.146), channel_id=1, source_target_pairs={{0,6},{1,7},{2,4},{3,5},{4,2},{5,3},{6,0},{7,1},{8,14},{9,15},{10,... | collective-permute-start | bytes 331784 | tf_op jit(solution)/shard_map/ppermute | solution.py:169
  86.6 2.4 %collective-permute-start.26 = (f32[216,128]{1,0:T(8,128)S(1)}, f32[216,128]{1,0:T(8,128)S(1)}, u32[]{:S(2)}, u32[]{:S(2)}) collective-permute-start(f32[216,128]{1,0:T(8,128)S(1)} %get-tuple-element.142), channel_id=1, source_target_pairs={{0,2},{1,3},{2,0},{3,1},{4,6},{5,7},{6,4},{7,5},{8,10},{9,11},{10,... | collective-permute-start | bytes 331784 | tf_op jit(solution)/shard_map/ppermute | solution.py:169
  92.4 4.0 %collective-permute-done.27.refs_2_ = f32[216,128]{1,0:T(8,128)S(1)} collective-permute-done((f32[216,128]{1,0:T(8,128)S(1)}, f32[216,128]{1,0:T(8,128)S(1)}, u32[]{:S(2)}, u32[]{:S(2)}) %collective-permute-start.27) | collective-permute-done | bytes 110624 | tf_op jit(solution)/shard_map/ppermute | solution.py:169
  100.7 2.1 %collective-permute-start.35 = (f32[216,128]{1,0:T(8,128)S(1)}, f32[216,128]{1,0:T(8,128)S(1)}, u32[]{:S(2)}, u32[]{:S(2)}) collective-permute-start(f32[216,128]{1,0:T(8,128)S(1)} %get-tuple-element.159), channel_id=1, source_target_pairs={{0,6},{1,7},{2,4},{3,5},{4,2},{5,3},{6,0},{7,1},{8,14},{9,15},{10,... | collective-permute-start | bytes 331784 | tf_op jit(solution)/shard_map/ppermute | solution.py:169
  102.8 2.3 %collective-permute-start.33 = (f32[216,128]{1,0:T(8,128)S(1)}, f32[216,128]{1,0:T(8,128)S(1)}, u32[]{:S(2)}, u32[]{:S(2)}) collective-permute-start(f32[216,128]{1,0:T(8,128)S(1)} %get-tuple-element.155), channel_id=1, source_target_pairs={{0,2},{1,3},{2,0},{3,1},{4,6},{5,7},{6,4},{7,5},{8,10},{9,11},{10,... | collective-permute-start | bytes 331784 | tf_op jit(solution)/shard_map/ppermute | solution.py:169
  105.1 5.3 %collective-permute-done.29.other_ref = f32[4,216,128]{2,1,0:T(8,128)S(1)} collective-permute-done((f32[4,216,128]{2,1,0:T(8,128)S(1)}, f32[4,216,128]{2,1,0:T(8,128)S(1)}, u32[]{:S(2)}, u32[]{:S(2)}) %collective-permute-start.29) | collective-permute-done | bytes 442400 | tf_op jit(solution)/shard_map/ppermute | solution.py:515
  114.7 1.8 %collective-permute-start.39 = (f32[216,128]{1,0:T(8,128)S(1)}, f32[216,128]{1,0:T(8,128)S(1)}, u32[]{:S(2)}, u32[]{:S(2)}) collective-permute-start(f32[216,128]{1,0:T(8,128)S(1)} %get-tuple-element.172), channel_id=1, source_target_pairs={{0,6},{1,7},{2,4},{3,5},{4,2},{5,3},{6,0},{7,1},{8,14},{9,15},{10,... | collective-permute-start | bytes 331784 | tf_op jit(solution)/shard_map/ppermute | solution.py:169
  116.5 2.6 %collective-permute-start.37 = (f32[216,128]{1,0:T(8,128)S(1)}, f32[216,128]{1,0:T(8,128)S(1)}, u32[]{:S(2)}, u32[]{:S(2)}) collective-permute-start(f32[216,128]{1,0:T(8,128)S(1)} %get-tuple-element.166), channel_id=1, source_target_pairs={{0,2},{1,3},{2,0},{3,1},{4,6},{5,7},{6,4},{7,5},{8,10},{9,11},{10,... | collective-permute-start | bytes 331784 | tf_op jit(solution)/shard_map/ppermute | solution.py:169
  119.1 6.9 %collective-permute-done.36.other_ref = f32[4,216,128]{2,1,0:T(8,128)S(1)} collective-permute-done((f32[4,216,128]{2,1,0:T(8,128)S(1)}, f32[4,216,128]{2,1,0:T(8,128)S(1)}, u32[]{:S(2)}, u32[]{:S(2)}) %collective-permute-start.36) | collective-permute-done | bytes 442400 | tf_op jit(solution)/shard_map/ppermute | solution.py:515
  126.6 2.1 %collective-permute-start.42 = (f32[216,128]{1,0:T(8,128)S(1)}, f32[216,128]{1,0:T(8,128)S(1)}, u32[]{:S(2)}, u32[]{:S(2)}) collective-permute-start(f32[216,128]{1,0:T(8,128)S(1)} %get-tuple-element.180), channel_id=1, source_target_pairs={{0,6},{1,7},{2,4},{3,5},{4,2},{5,3},{6,0},{7,1},{8,14},{9,15},{10,... | collective-permute-start | bytes 331784 | tf_op jit(solution)/shard_map/ppermute | solution.py:169
  128.8 2.3 %collective-permute-start.40 = (f32[216,128]{1,0:T(8,128)S(1)}, f32[216,128]{1,0:T(8,128)S(1)}, u32[]{:S(2)}, u32[]{:S(2)}) collective-permute-start(f32[216,128]{1,0:T(8,128)S(1)} %get-tuple-element.176), channel_id=1, source_target_pairs={{0,2},{1,3},{2,0},{3,1},{4,6},{5,7},{6,4},{7,5},{8,10},{9,11},{10,... | collective-permute-start | bytes 331784 | tf_op jit(solution)/shard_map/ppermute | solution.py:169
  132.6 1.9 %collective-permute-done.42.refs_4_ = f32[216,128]{1,0:T(8,128)S(1)} collective-permute-done((f32[216,128]{1,0:T(8,128)S(1)}, f32[216,128]{1,0:T(8,128)S(1)}, u32[]{:S(2)}, u32[]{:S(2)}) %collective-permute-start.42) | collective-permute-done | bytes 110624 | tf_op jit(solution)/shard_map/ppermute | solution.py:169
  134.5 3.2 %collective-permute-done.41.refs_3_ = f32[216,128]{1,0:T(8,128)S(1)} collective-permute-done((f32[216,128]{1,0:T(8,128)S(1)}, f32[216,128]{1,0:T(8,128)S(1)}, u32[]{:S(2)}, u32[]{:S(2)}) %collective-permute-start.41) | collective-permute-done | bytes 110624 | tf_op jit(solution)/shard_map/ppermute | solution.py:169
  137.7 2.1 %shard_map.160 = (f32[2,6,48,384]{3,2,1,0:T(8,128)}, f32[48,384]{1,0:T(8,128)}, f32[32,128]{1,0:T(8,128)S(1)}) custom-call(s32[2]{0:T(128)S(1)} %pad_add_fusion.me_ref, f32[2,6]{1,0:T(2,128)S(1)} %copy-done.8, s32[1]{0:T(128)S(6)} %copy.29.count_ref, f32[5,48,384]{2,1,0:T(8,128)S(1)} %copy-done, s32[48,384]{1,0:T(8,128)S(1)} %copy-done.1, ...), custom_call_target="tpu_custom_call" | custom-call | flops 1 | bytes 1 | tf_op jit(solution)/shard_map/pallas_call | solution.py:447
  139.8 10.0 %all_to_all.11 = f32[32,1,128]{2,1,0:T(1,128)S(1)} all-to-all(f32[32,1,128]{2,1,0:T(1,128)S(1)} %bitcast.18), channel_id=1, replica_groups=mesh['gx'=4,'gy'=8] {'gx','gy'}, dimensions={0} | all-to-all | bytes 32768 | tf_op jit(solution)/shard_map/all_to_all | solution.py:542
  (107 shorter events, 45.9 us)
Async XLA Ops:
  2.2 15.5 %collective-permute-start.4 = (f32[6,48,384]{2,1,0:T(8,128)S(1)}, f32[6,48,384]{2,1,0:T(8,128)}, u32[]{:S(2)}, u32[]{:S(2)}) collective-permute-start(f32[6,48,384]{2,1,0:T(8,128)S(1)} %slice_bitcast_fusion.1.refs_0_), channel_id=1, source_target_pairs={{0,16},{8,24},{16,0},{24,8},{1,17},{9,25},{17,1},{25,9},{2,18},{10... | collective-permute-start | bytes 1327112 | tf_op jit(solution)/shard_map/ppermute | solution.py:157
  5.9 11.7 %collective-permute-start.1 = (f32[96,192]{1,0:T(8,128)S(1)}, f32[96,192]{1,0:T(8,128)S(1)}, u32[]{:S(2)}, u32[]{:S(2)}) collective-permute-start(f32[96,192]{1,0:T(8,128)S(1)} %copy.26.refs_0_), channel_id=1, source_target_pairs={{0,16},{8,24},{16,0},{24,8},{1,17},{9,25},{17,1},{25,9},{2,18},{10... | collective-permute-start | bytes 221192 | tf_op jit(solution)/shard_map/ppermute | solution.py:157
  17.7 10.0 %collective-permute-start.10 = (f32[6,48,384]{2,1,0:T(8,128)S(1)}, f32[6,48,384]{2,1,0:T(8,128)S(1)}, u32[]{:S(2)}, u32[]{:S(2)}) collective-permute-start(f32[6,48,384]{2,1,0:T(8,128)S(1)} %slice_bitcast_fusion.refs_0_), channel_id=1, source_target_pairs={{0,8},{8,0},{16,24},{24,16},{1,9},{9,1},{17,25},{25,17},{2,10},{10... | collective-permute-start | bytes 1327112 | tf_op jit(solution)/shard_map/ppermute | solution.py:148
  18.2 17.7 %collective-permute-start.11 = (f32[6,48,384]{2,1,0:T(8,128)S(1)}, f32[6,48,384]{2,1,0:T(8,128)S(1)}, u32[]{:S(2)}, u32[]{:S(2)}) collective-permute-start(f32[6,48,384]{2,1,0:T(8,128)S(1)} %slice_bitcast_fusion.refs_0_), channel_id=1, source_target_pairs={{0,16},{8,24},{16,0},{24,8},{1,17},{9,25},{17,1},{25,9},{2,18},{10... | collective-permute-start | bytes 1327112 | tf_op jit(solution)/shard_map/ppermute | solution.py:157
  26.3 9.6 %collective-permute-start.7 = (f32[216,128]{1,0:T(8,128)S(1)}, f32[216,128]{1,0:T(8,128)S(1)}, u32[]{:S(2)}, u32[]{:S(2)}) collective-permute-start(f32[216,128]{1,0:T(8,128)S(1)} %get-tuple-element.104), channel_id=1, source_target_pairs={{0,4},{1,5},{2,6},{3,7},{4,0},{5,1},{6,2},{7,3},{8,12},{9,13},{10,... | collective-permute-start | bytes 331784 | tf_op jit(solution)/shard_map/ppermute | solution.py:169
  26.3 9.6 %collective-permute-start.6 = (f32[216,128]{1,0:T(8,128)S(1)}, f32[216,128]{1,0:T(8,128)S(1)}, u32[]{:S(2)}, u32[]{:S(2)}) collective-permute-start(f32[216,128]{1,0:T(8,128)S(1)} %get-tuple-element.102), channel_id=1, source_target_pairs={{0,2},{1,3},{2,0},{3,1},{4,6},{5,7},{6,4},{7,5},{8,10},{9,11},{10,... | collective-permute-start | bytes 331784 | tf_op jit(solution)/shard_map/ppermute | solution.py:169
  37.2 12.6 %collective-permute-start.9 = (f32[4,216,128]{2,1,0:T(8,128)S(1)}, f32[4,216,128]{2,1,0:T(8,128)S(1)}, u32[]{:S(2)}, u32[]{:S(2)}) collective-permute-start(f32[4,216,128]{2,1,0:T(8,128)S(1)} %get-tuple-element.109), channel_id=1, source_target_pairs={{0,1},{1,0},{2,3},{3,2},{4,5},{5,4},{6,7},{7,6},{8,9},{9,8},{10,11... | collective-permute-start | bytes 1327112 | tf_op jit(solution)/shard_map/ppermute | solution.py:515
  40.5 10.0 %collective-permute-start.15 = (f32[216,128]{1,0:T(8,128)S(1)}, f32[216,128]{1,0:T(8,128)S(1)}, u32[]{:S(2)}, u32[]{:S(2)}) collective-permute-start(f32[216,128]{1,0:T(8,128)S(1)} %get-tuple-element.119), channel_id=1, source_target_pairs={{0,6},{1,7},{2,4},{3,5},{4,2},{5,3},{6,0},{7,1},{8,14},{9,15},{10,... | collective-permute-start | bytes 331784 | tf_op jit(solution)/shard_map/ppermute | solution.py:169
  43.0 9.5 %collective-permute-start.14 = (f32[216,128]{1,0:T(8,128)S(1)}, f32[216,128]{1,0:T(8,128)S(1)}, u32[]{:S(2)}, u32[]{:S(2)}) collective-permute-start(f32[216,128]{1,0:T(8,128)S(1)} %get-tuple-element.117), channel_id=1, source_target_pairs={{0,4},{1,5},{2,6},{3,7},{4,0},{5,1},{6,2},{7,3},{8,12},{9,13},{10,... | collective-permute-start | bytes 331784 | tf_op jit(solution)/shard_map/ppermute | solution.py:169
  43.0 9.5 %collective-permute-start.13 = (f32[216,128]{1,0:T(8,128)S(1)}, f32[216,128]{1,0:T(8,128)S(1)}, u32[]{:S(2)}, u32[]{:S(2)}) collective-permute-start(f32[216,128]{1,0:T(8,128)S(1)} %get-tuple-element.115), channel_id=1, source_target_pairs={{0,2},{1,3},{2,0},{3,1},{4,6},{5,7},{6,4},{7,5},{8,10},{9,11},{10,... | collective-permute-start | bytes 331784 | tf_op jit(solution)/shard_map/ppermute | solution.py:169
  53.8 12.2 %collective-permute-start.16 = (f32[4,216,128]{2,1,0:T(8,128)S(1)}, f32[4,216,128]{2,1,0:T(8,128)S(1)}, u32[]{:S(2)}, u32[]{:S(2)}) collective-permute-start(f32[4,216,128]{2,1,0:T(8,128)S(1)} %get-tuple-element.123), channel_id=1, source_target_pairs={{0,1},{1,0},{2,3},{3,2},{4,5},{5,4},{6,7},{7,6},{8,9},{9,8},{10,11... | collective-permute-start | bytes 1327112 | tf_op jit(solution)/shard_map/ppermute | solution.py:515
  56.7 9.5 %collective-permute-start.18 = (f32[216,128]{1,0:T(8,128)S(1)}, f32[216,128]{1,0:T(8,128)S(1)}, u32[]{:S(2)}, u32[]{:S(2)}) collective-permute-start(f32[216,128]{1,0:T(8,128)S(1)} %get-tuple-element.129), channel_id=1, source_target_pairs={{0,4},{1,5},{2,6},{3,7},{4,0},{5,1},{6,2},{7,3},{8,12},{9,13},{10,... | collective-permute-start | bytes 331784 | tf_op jit(solution)/shard_map/ppermute | solution.py:169
  56.7 9.5 %collective-permute-start.17 = (f32[216,128]{1,0:T(8,128)S(1)}, f32[216,128]{1,0:T(8,128)S(1)}, u32[]{:S(2)}, u32[]{:S(2)}) collective-permute-start(f32[216,128]{1,0:T(8,128)S(1)} %get-tuple-element.126), channel_id=1, source_target_pairs={{0,2},{1,3},{2,0},{3,1},{4,6},{5,7},{6,4},{7,5},{8,10},{9,11},{10,... | collective-permute-start | bytes 331784 | tf_op jit(solution)/shard_map/ppermute | solution.py:169
  67.1 13.9 %collective-permute-start.21 = (f32[6,48,384]{2,1,0:T(8,128)S(1)}, f32[6,48,384]{2,1,0:T(8,128)S(1)}, u32[]{:S(2)}, u32[]{:S(2)}) collective-permute-start(f32[6,48,384]{2,1,0:T(8,128)S(1)} %shard_map.148.refs_0_), channel_id=1, source_target_pairs={{0,16},{8,24},{16,0},{24,8},{1,17},{9,25},{17,1},{25,9},{2,18},{10... | collective-permute-start | bytes 1327112 | tf_op jit(solution)/shard_map/ppermute | solution.py:157
  69.3 7.9 %collective-permute-start.22 = (f32[216,128]{1,0:T(8,128)S(1)}, f32[216,128]{1,0:T(8,128)S(1)}, u32[]{:S(2)}, u32[]{:S(2)}) collective-permute-start(f32[216,128]{1,0:T(8,128)S(1)} %get-tuple-element.135), channel_id=1, source_target_pairs={{0,6},{1,7},{2,4},{3,5},{4,2},{5,3},{6,0},{7,1},{8,14},{9,15},{10,... | collective-permute-start | bytes 331784 | tf_op jit(solution)/shard_map/ppermute | solution.py:169
  71.4 9.6 %collective-permute-start.23 = (f32[216,128]{1,0:T(8,128)S(1)}, f32[216,128]{1,0:T(8,128)S(1)}, u32[]{:S(2)}, u32[]{:S(2)}) collective-permute-start(f32[216,128]{1,0:T(8,128)S(1)} %get-tuple-element.136), channel_id=1, source_target_pairs={{0,4},{1,5},{2,6},{3,7},{4,0},{5,1},{6,2},{7,3},{8,12},{9,13},{10,... | collective-permute-start | bytes 331784 | tf_op jit(solution)/shard_map/ppermute | solution.py:169
  71.4 9.6 %collective-permute-start.24 = (f32[216,128]{1,0:T(8,128)S(1)}, f32[216,128]{1,0:T(8,128)S(1)}, u32[]{:S(2)}, u32[]{:S(2)}) collective-permute-start(f32[216,128]{1,0:T(8,128)S(1)} %get-tuple-element.137), channel_id=1, source_target_pairs={{0,2},{1,3},{2,0},{3,1},{4,6},{5,7},{6,4},{7,5},{8,10},{9,11},{10,... | collective-permute-start | bytes 331784 | tf_op jit(solution)/shard_map/ppermute | solution.py:169
  82.4 14.0 %collective-permute-start.31 = (f32[6,48,384]{2,1,0:T(8,128)S(1)}, f32[6,48,384]{2,1,0:T(8,128)S(1)}, u32[]{:S(2)}, u32[]{:S(2)}) collective-permute-start(f32[6,48,384]{2,1,0:T(8,128)S(1)} %shard_map.154.refs_0_), channel_id=1, source_target_pairs={{0,16},{8,24},{16,0},{24,8},{1,17},{9,25},{17,1},{25,9},{2,18},{10... | collective-permute-start | bytes 1327112 | tf_op jit(solution)/shard_map/ppermute | solution.py:157
  84.5 7.9 %collective-permute-start.28 = (f32[216,128]{1,0:T(8,128)S(1)}, f32[216,128]{1,0:T(8,128)S(1)}, u32[]{:S(2)}, u32[]{:S(2)}) collective-permute-start(f32[216,128]{1,0:T(8,128)S(1)} %get-tuple-element.146), channel_id=1, source_target_pairs={{0,6},{1,7},{2,4},{3,5},{4,2},{5,3},{6,0},{7,1},{8,14},{9,15},{10,... | collective-permute-start | bytes 331784 | tf_op jit(solution)/shard_map/ppermute | solution.py:169
  86.6 9.8 %collective-permute-start.27 = (f32[216,128]{1,0:T(8,128)S(1)}, f32[216,128]{1,0:T(8,128)S(1)}, u32[]{:S(2)}, u32[]{:S(2)}) collective-permute-start(f32[216,128]{1,0:T(8,128)S(1)} %get-tuple-element.144), channel_id=1, source_target_pairs={{0,4},{1,5},{2,6},{3,7},{4,0},{5,1},{6,2},{7,3},{8,12},{9,13},{10,... | collective-permute-start | bytes 331784 | tf_op jit(solution)/shard_map/ppermute | solution.py:169
  86.6 9.8 %collective-permute-start.26 = (f32[216,128]{1,0:T(8,128)S(1)}, f32[216,128]{1,0:T(8,128)S(1)}, u32[]{:S(2)}, u32[]{:S(2)}) collective-permute-start(f32[216,128]{1,0:T(8,128)S(1)} %get-tuple-element.142), channel_id=1, source_target_pairs={{0,2},{1,3},{2,0},{3,1},{4,6},{5,7},{6,4},{7,5},{8,10},{9,11},{10,... | collective-permute-start | bytes 331784 | tf_op jit(solution)/shard_map/ppermute | solution.py:169
  97.8 12.6 %collective-permute-start.29 = (f32[4,216,128]{2,1,0:T(8,128)S(1)}, f32[4,216,128]{2,1,0:T(8,128)S(1)}, u32[]{:S(2)}, u32[]{:S(2)}) collective-permute-start(f32[4,216,128]{2,1,0:T(8,128)S(1)} %get-tuple-element.149), channel_id=1, source_target_pairs={{0,1},{1,0},{2,3},{3,2},{4,5},{5,4},{6,7},{7,6},{8,9},{9,8},{10,11... | collective-permute-start | bytes 1327112 | tf_op jit(solution)/shard_map/ppermute | solution.py:515
  100.7 10.3 %collective-permute-start.35 = (f32[216,128]{1,0:T(8,128)S(1)}, f32[216,128]{1,0:T(8,128)S(1)}, u32[]{:S(2)}, u32[]{:S(2)}) collective-permute-start(f32[216,128]{1,0:T(8,128)S(1)} %get-tuple-element.159), channel_id=1, source_target_pairs={{0,6},{1,7},{2,4},{3,5},{4,2},{5,3},{6,0},{7,1},{8,14},{9,15},{10,... | collective-permute-start | bytes 331784 | tf_op jit(solution)/shard_map/ppermute | solution.py:169
  102.8 9.6 %collective-permute-start.34 = (f32[216,128]{1,0:T(8,128)S(1)}, f32[216,128]{1,0:T(8,128)S(1)}, u32[]{:S(2)}, u32[]{:S(2)}) collective-permute-start(f32[216,128]{1,0:T(8,128)S(1)} %get-tuple-element.157), channel_id=1, source_target_pairs={{0,4},{1,5},{2,6},{3,7},{4,0},{5,1},{6,2},{7,3},{8,12},{9,13},{10,... | collective-permute-start | bytes 331784 | tf_op jit(solution)/shard_map/ppermute | solution.py:169
  102.8 9.6 %collective-permute-start.33 = (f32[216,128]{1,0:T(8,128)S(1)}, f32[216,128]{1,0:T(8,128)S(1)}, u32[]{:S(2)}, u32[]{:S(2)}) collective-permute-start(f32[216,128]{1,0:T(8,128)S(1)} %get-tuple-element.155), channel_id=1, source_target_pairs={{0,2},{1,3},{2,0},{3,1},{4,6},{5,7},{6,4},{7,5},{8,10},{9,11},{10,... | collective-permute-start | bytes 331784 | tf_op jit(solution)/shard_map/ppermute | solution.py:169
  113.8 12.2 %collective-permute-start.36 = (f32[4,216,128]{2,1,0:T(8,128)S(1)}, f32[4,216,128]{2,1,0:T(8,128)S(1)}, u32[]{:S(2)}, u32[]{:S(2)}) collective-permute-start(f32[4,216,128]{2,1,0:T(8,128)S(1)} %get-tuple-element.163), channel_id=1, source_target_pairs={{0,1},{1,0},{2,3},{3,2},{4,5},{5,4},{6,7},{7,6},{8,9},{9,8},{10,11... | collective-permute-start | bytes 1327112 | tf_op jit(solution)/shard_map/ppermute | solution.py:515
  114.7 14.0 %collective-permute-start.39 = (f32[216,128]{1,0:T(8,128)S(1)}, f32[216,128]{1,0:T(8,128)S(1)}, u32[]{:S(2)}, u32[]{:S(2)}) collective-permute-start(f32[216,128]{1,0:T(8,128)S(1)} %get-tuple-element.172), channel_id=1, source_target_pairs={{0,6},{1,7},{2,4},{3,5},{4,2},{5,3},{6,0},{7,1},{8,14},{9,15},{10,... | collective-permute-start | bytes 331784 | tf_op jit(solution)/shard_map/ppermute | solution.py:169
  116.5 15.3 %collective-permute-start.38 = (f32[216,128]{1,0:T(8,128)S(1)}, f32[216,128]{1,0:T(8,128)S(1)}, u32[]{:S(2)}, u32[]{:S(2)}) collective-permute-start(f32[216,128]{1,0:T(8,128)S(1)} %get-tuple-element.169), channel_id=1, source_target_pairs={{0,4},{1,5},{2,6},{3,7},{4,0},{5,1},{6,2},{7,3},{8,12},{9,13},{10,... | collective-permute-start | bytes 331784 | tf_op jit(solution)/shard_map/ppermute | solution.py:169
  116.5 15.3 %collective-permute-start.37 = (f32[216,128]{1,0:T(8,128)S(1)}, f32[216,128]{1,0:T(8,128)S(1)}, u32[]{:S(2)}, u32[]{:S(2)}) collective-permute-start(f32[216,128]{1,0:T(8,128)S(1)} %get-tuple-element.166), channel_id=1, source_target_pairs={{0,2},{1,3},{2,0},{3,1},{4,6},{5,7},{6,4},{7,5},{8,10},{9,11},{10,... | collective-permute-start | bytes 331784 | tf_op jit(solution)/shard_map/ppermute | solution.py:169
  126.6 7.9 %collective-permute-start.42 = (f32[216,128]{1,0:T(8,128)S(1)}, f32[216,128]{1,0:T(8,128)S(1)}, u32[]{:S(2)}, u32[]{:S(2)}) collective-permute-start(f32[216,128]{1,0:T(8,128)S(1)} %get-tuple-element.180), channel_id=1, source_target_pairs={{0,6},{1,7},{2,4},{3,5},{4,2},{5,3},{6,0},{7,1},{8,14},{9,15},{10,... | collective-permute-start | bytes 331784 | tf_op jit(solution)/shard_map/ppermute | solution.py:169
  128.8 8.9 %collective-permute-start.41 = (f32[216,128]{1,0:T(8,128)S(1)}, f32[216,128]{1,0:T(8,128)S(1)}, u32[]{:S(2)}, u32[]{:S(2)}) collective-permute-start(f32[216,128]{1,0:T(8,128)S(1)} %get-tuple-element.178), channel_id=1, source_target_pairs={{0,4},{1,5},{2,6},{3,7},{4,0},{5,1},{6,2},{7,3},{8,12},{9,13},{10,... | collective-permute-start | bytes 331784 | tf_op jit(solution)/shard_map/ppermute | solution.py:169
  128.8 8.9 %collective-permute-start.40 = (f32[216,128]{1,0:T(8,128)S(1)}, f32[216,128]{1,0:T(8,128)S(1)}, u32[]{:S(2)}, u32[]{:S(2)}) collective-permute-start(f32[216,128]{1,0:T(8,128)S(1)} %get-tuple-element.176), channel_id=1, source_target_pairs={{0,2},{1,3},{2,0},{3,1},{4,6},{5,7},{6,4},{7,5},{8,10},{9,11},{10,... | collective-permute-start | bytes 331784 | tf_op jit(solution)/shard_map/ppermute | solution.py:169
  (22 other events, 246.2 us)

commit v8 on v7

--- a/solution.py
+++ b/solution.py
@@ -95,8 +95,12 @@
         return [shape] * self.parts
 
 
+def gray(number):
+    return number ^ (number >> 1)
+
+
 def part_of(me_ref, mask):
-    return (me_ref[1] // 2) ^ mask
+    return (me_ref[1] // 2) ^ gray(mask)
 
 
 def turn(value, shift):
@@ -165,7 +169,7 @@
 def exchange(blocks, axis, count):
     out = [blocks[0]] + [None] * (len(blocks) - 1)
     for mask in range(1, len(blocks)):
-        pairs = [(i, i ^ (2 * mask)) for i in range(count)]
+        pairs = [(i, i ^ (2 * gray(mask))) for i in range(count)]
         out[mask] = lax.ppermute(blocks[mask], axis, pairs)
     return out
 

time: 151 us -> 151 us (level)
  waiting for transfers between devices: 56.1 us -> 58.7 us
  starting transfers between devices: 48.5 us -> 46.2 us
    ppermute x24, waiting for transfers between devices: 30.3 us -> 36.8 us  [exchange(): out[mask] = lax.ppermute(blocks[mask], axis, pairs)]
    ppermute x4, waiting for transfers between devices: 20.9 us -> 17 us  [body(): other.append(lax.ppermute(for_other, 'gy', side_pairs))]
    ppermute x24, starting transfers between devices: 35.5 us -> 33.1 us  [exchange(): out[mask] = lax.ppermute(blocks[mask], axis, pairs)]
  transfers between devices with their start and end apart: 43 -> 43, of which waited for: 17 -> 18; matrix products, arithmetic and copies ran while one was open for 2% -> 2% of each run, Pallas kernels for 14% -> 14%
where the time goes in v8:
time: 151 us
  waiting for transfers between devices  58.7 us (39%)
  starting transfers between devices  46.2 us (31%)
  Pallas kernels  27.4 us (18%)
  blocking collectives  9.99 us (7%)
  local copies, waits for them, and re-layouts  6.78 us (4%)
  between operations  1.58 us (1%)
    ppermute x24, waiting for transfers between devices, exchange(): out[mask] = lax.ppermute(blocks[mask], axis, pairs)  36.8 us
    ppermute x24, starting transfers between devices, exchange(): out[mask] = lax.ppermute(blocks[mask], axis, pairs)  33.1 us
    pallas_call x22, Pallas kernels, call(): pl.pallas_call(kernel, out_shape=out_shape, in_specs=specs, out_specs=[ou...  25.3 us
    ppermute x4, waiting for transfers between devices, body(): other.append(lax.ppermute(for_other, 'gy', side_pairs))  17 us
    all_to_all x1, blocking collectives, body(): lax.all_to_all(outgoing, ('gx', 'gy'), split_axis=0, concat_axis=0, tiled...  9.99 us
    ppermute x10, starting transfers between devices, gather_far(): lax.ppermute(piece, axis, pairs)  7.05 us
    ppermute x10, waiting for transfers between devices, gather_far(): lax.ppermute(piece, axis, pairs)  4.86 us
    unnamed x24, local copies, waits for them, and re-layouts  4.61 us
  transfers between devices with their start and end apart: 43, of which 18 were waited for; matrix products, arithmetic and copies ran while one was open for 2% of the time, Pallas kernels for 14%

profile of v8, /device:TPU:0, one launch (start us, length us, event | category | flops | bytes accessed | tf_op | source)
XLA Modules:
  0.0 150.7 jit_solution(3175707360845463899)
XLA Ops:
  2.2 2.6 %collective-permute-start.4 = (f32[6,48,384]{2,1,0:T(8,128)S(1)}, f32[6,48,384]{2,1,0:T(8,128)}, u32[]{:S(2)}, u32[]{:S(2)}) collective-permute-start(f32[6,48,384]{2,1,0:T(8,128)S(1)} %slice_bitcast_fusion.1.refs_0_), channel_id=1, source_target_pairs={{0,16},{8,24},{16,0},{24,8},{1,17},{9,25},{17,1},{25,9},{2,18},{10... | collective-permute-start | bytes 1327112 | tf_op jit(solution)/shard_map/ppermute | solution.py:161
  6.0 1.7 %copy-done.2 = f32[384,1536]{1,0:T(8,128)S(1)} copy-done((f32[384,1536]{1,0:T(8,128)S(1)}, f32[384,1536]{1,0:T(8,128)}, u32[]{:S(2)}) %copy-start.2) | copy-done | bytes 2359320
  12.8 4.8 %collective-permute-done.1.refs_2_ = f32[96,192]{1,0:T(8,128)S(1)} collective-permute-done((f32[96,192]{1,0:T(8,128)S(1)}, f32[96,192]{1,0:T(8,128)S(1)}, u32[]{:S(2)}, u32[]{:S(2)}) %collective-permute-start.1) | collective-permute-done | bytes 73760 | tf_op jit(solution)/shard_map/ppermute | solution.py:161
  18.2 1.8 %collective-permute-start.11 = (f32[6,48,384]{2,1,0:T(8,128)S(1)}, f32[6,48,384]{2,1,0:T(8,128)S(1)}, u32[]{:S(2)}, u32[]{:S(2)}) collective-permute-start(f32[6,48,384]{2,1,0:T(8,128)S(1)} %slice_bitcast_fusion.refs_0_), channel_id=1, source_target_pairs={{0,16},{8,24},{16,0},{24,8},{1,17},{9,25},{17,1},{25,9},{2,18},{10... | collective-permute-start | bytes 1327112 | tf_op jit(solution)/shard_map/ppermute | solution.py:161
  20.4 2.1 %shard_map.142 = (f32[216,128]{1,0:T(8,128)S(1)}, f32[216,128]{1,0:T(8,128)S(1)}, f32[216,128]{1,0:T(8,128)S(1)}, f32[216,128]{1,0:T(8,128)S(1)}) custom-call(s32[2]{0:T(128)S(1)} %pad_add_fusion.me_ref, bf16[1536,384]{1,0:T(8,128)(2,1)S(1)} %get-tuple-element.96.high_ref, bf16[1536,384]{1,0:T(8,128)(2,1)S(1)} %get-tuple-element.97.low_ref, ...), custom_call_target="tpu_custom_call" | custom-call | flops 1 | bytes 1 | tf_op jit(solution)/shard_map/pallas_call | solution.py:135
  22.6 2.7 %collective-permute-start.8 = (f32[216,128]{1,0:T(8,128)S(1)}, f32[216,128]{1,0:T(8,128)S(1)}, u32[]{:S(2)}, u32[]{:S(2)}) collective-permute-start(f32[216,128]{1,0:T(8,128)S(1)} %get-tuple-element.106), channel_id=1, source_target_pairs={{0,4},{1,5},{2,6},{3,7},{4,0},{5,1},{6,2},{7,3},{8,12},{9,13},{10,... | collective-permute-start | bytes 331784 | tf_op jit(solution)/shard_map/ppermute | solution.py:173
  29.1 5.1 %collective-permute-done.8.refs_3_ = f32[216,128]{1,0:T(8,128)S(1)} collective-permute-done((f32[216,128]{1,0:T(8,128)S(1)}, f32[216,128]{1,0:T(8,128)S(1)}, u32[]{:S(2)}, u32[]{:S(2)}) %collective-permute-start.8) | collective-permute-done | bytes 110624 | tf_op jit(solution)/shard_map/ppermute | solution.py:173
  37.7 1.6 %shard_map.146 = (f32[216,128]{1,0:T(8,128)S(1)}, f32[216,128]{1,0:T(8,128)S(1)}, f32[216,128]{1,0:T(8,128)S(1)}, f32[216,128]{1,0:T(8,128)S(1)}) custom-call(s32[2]{0:T(128)S(1)} %pad_add_fusion.me_ref, bf16[1536,384]{1,0:T(8,128)(2,1)S(1)} %get-tuple-element.96.high_ref, bf16[1536,384]{1,0:T(8,128)(2,1)S(1)} %get-tuple-element.97.low_ref, ...), custom_call_target="tpu_custom_call" | custom-call | flops 1 | bytes 1 | tf_op jit(solution)/shard_map/pallas_call | solution.py:135
  39.4 3.7 %collective-permute-start.15 = (f32[216,128]{1,0:T(8,128)S(1)}, f32[216,128]{1,0:T(8,128)S(1)}, u32[]{:S(2)}, u32[]{:S(2)}) collective-permute-start(f32[216,128]{1,0:T(8,128)S(1)} %get-tuple-element.119), channel_id=1, source_target_pairs={{0,4},{1,5},{2,6},{3,7},{4,0},{5,1},{6,2},{7,3},{8,12},{9,13},{10,... | collective-permute-start | bytes 331784 | tf_op jit(solution)/shard_map/ppermute | solution.py:173
  43.7 5.0 %collective-permute-done.9.other_ref = f32[4,216,128]{2,1,0:T(8,128)S(1)} collective-permute-done((f32[4,216,128]{2,1,0:T(8,128)S(1)}, f32[4,216,128]{2,1,0:T(8,128)S(1)}, u32[]{:S(2)}, u32[]{:S(2)}) %collective-permute-start.9) | collective-permute-done | bytes 442400 | tf_op jit(solution)/shard_map/ppermute | solution.py:519
  49.4 2.2 %collective-permute-done.15.refs_3_ = f32[216,128]{1,0:T(8,128)S(1)} collective-permute-done((f32[216,128]{1,0:T(8,128)S(1)}, f32[216,128]{1,0:T(8,128)S(1)}, u32[]{:S(2)}, u32[]{:S(2)}) %collective-permute-start.15) | collective-permute-done | bytes 110624 | tf_op jit(solution)/shard_map/ppermute | solution.py:173
  54.5 2.7 %collective-permute-start.19 = (f32[216,128]{1,0:T(8,128)S(1)}, f32[216,128]{1,0:T(8,128)S(1)}, u32[]{:S(2)}, u32[]{:S(2)}) collective-permute-start(f32[216,128]{1,0:T(8,128)S(1)} %get-tuple-element.132), channel_id=1, source_target_pairs={{0,4},{1,5},{2,6},{3,7},{4,0},{5,1},{6,2},{7,3},{8,12},{9,13},{10,... | collective-permute-start | bytes 331784 | tf_op jit(solution)/shard_map/ppermute | solution.py:173
  58.5 7.0 %collective-permute-done.19.refs_3_ = f32[216,128]{1,0:T(8,128)S(1)} collective-permute-done((f32[216,128]{1,0:T(8,128)S(1)}, f32[216,128]{1,0:T(8,128)S(1)}, u32[]{:S(2)}, u32[]{:S(2)}) %collective-permute-start.19) | collective-permute-done | bytes 110624 | tf_op jit(solution)/shard_map/ppermute | solution.py:173
  69.1 2.2 %collective-permute-start.22 = (f32[216,128]{1,0:T(8,128)S(1)}, f32[216,128]{1,0:T(8,128)S(1)}, u32[]{:S(2)}, u32[]{:S(2)}) collective-permute-start(f32[216,128]{1,0:T(8,128)S(1)} %get-tuple-element.135), channel_id=1, source_target_pairs={{0,4},{1,5},{2,6},{3,7},{4,0},{5,1},{6,2},{7,3},{8,12},{9,13},{10,... | collective-permute-start | bytes 331784 | tf_op jit(solution)/shard_map/ppermute | solution.py:173
  71.3 1.8 %collective-permute-start.23 = (f32[216,128]{1,0:T(8,128)S(1)}, f32[216,128]{1,0:T(8,128)S(1)}, u32[]{:S(2)}, u32[]{:S(2)}) collective-permute-start(f32[216,128]{1,0:T(8,128)S(1)} %get-tuple-element.136), channel_id=1, source_target_pairs={{0,6},{1,7},{2,4},{3,5},{4,2},{5,3},{6,0},{7,1},{8,14},{9,15},{10,... | collective-permute-start | bytes 331784 | tf_op jit(solution)/shard_map/ppermute | solution.py:173
  74.6 6.1 %collective-permute-done.22.refs_3_ = f32[216,128]{1,0:T(8,128)S(1)} collective-permute-done((f32[216,128]{1,0:T(8,128)S(1)}, f32[216,128]{1,0:T(8,128)S(1)}, u32[]{:S(2)}, u32[]{:S(2)}) %collective-permute-start.22) | collective-permute-done | bytes 110624 | tf_op jit(solution)/shard_map/ppermute | solution.py:173
  83.2 1.6 %shard_map.151 = (f32[216,128]{1,0:T(8,128)S(1)}, f32[216,128]{1,0:T(8,128)S(1)}, f32[216,128]{1,0:T(8,128)S(1)}, f32[216,128]{1,0:T(8,128)S(1)}) custom-call(s32[2]{0:T(128)S(1)} %pad_add_fusion.me_ref, bf16[1536,384]{1,0:T(8,128)(2,1)S(1)} %get-tuple-element.96.high_ref, bf16[1536,384]{1,0:T(8,128)(2,1)S(1)} %get-tuple-element.97.low_ref, ...), custom_call_target="tpu_custom_call" | custom-call | flops 1 | bytes 1 | tf_op jit(solution)/shard_map/pallas_call | solution.py:135
  84.8 2.2 %collective-permute-start.28 = (f32[216,128]{1,0:T(8,128)S(1)}, f32[216,128]{1,0:T(8,128)S(1)}, u32[]{:S(2)}, u32[]{:S(2)}) collective-permute-start(f32[216,128]{1,0:T(8,128)S(1)} %get-tuple-element.146), channel_id=1, source_target_pairs={{0,4},{1,5},{2,6},{3,7},{4,0},{5,1},{6,2},{7,3},{8,12},{9,13},{10,... | collective-permute-start | bytes 331784 | tf_op jit(solution)/shard_map/ppermute | solution.py:173
  87.1 1.8 %collective-permute-start.27 = (f32[216,128]{1,0:T(8,128)S(1)}, f32[216,128]{1,0:T(8,128)S(1)}, u32[]{:S(2)}, u32[]{:S(2)}) collective-permute-start(f32[216,128]{1,0:T(8,128)S(1)} %get-tuple-element.144), channel_id=1, source_target_pairs={{0,6},{1,7},{2,4},{3,5},{4,2},{5,3},{6,0},{7,1},{8,14},{9,15},{10,... | collective-permute-start | bytes 331784 | tf_op jit(solution)/shard_map/ppermute | solution.py:173
  88.8 1.7 %shard_map.155.total_ref = f32[288,384]{1,0:T(8,128)S(1)} custom-call(s32[2]{0:T(128)S(1)} %pad_add_fusion.me_ref, bf16[1536,384]{1,0:T(8,128)(2,1)S(1)} %get-tuple-element.96.high_ref, bf16[1536,384]{1,0:T(8,128)(2,1)S(1)} %get-tuple-element.97.low_ref, f32[6,48,384]{2,1,0:T(8,128)S(1)} %shard_map.154.refs_0_, f32[6,48,384]{2,1,0:T(8,128)S(1)} %collective-permute-done.30.refs_1_), custom_call_target="tpu_custom_call" | custom-call | flops 1 | bytes 1 | tf_op jit(solution)/shard_map/pallas_call | solution.py:135
  90.5 5.9 %collective-permute-done.28.refs_3_ = f32[216,128]{1,0:T(8,128)S(1)} collective-permute-done((f32[216,128]{1,0:T(8,128)S(1)}, f32[216,128]{1,0:T(8,128)S(1)}, u32[]{:S(2)}, u32[]{:S(2)}) %collective-permute-start.28) | collective-permute-done | bytes 110624 | tf_op jit(solution)/shard_map/ppermute | solution.py:173
  101.4 2.2 %collective-permute-start.35 = (f32[216,128]{1,0:T(8,128)S(1)}, f32[216,128]{1,0:T(8,128)S(1)}, u32[]{:S(2)}, u32[]{:S(2)}) collective-permute-start(f32[216,128]{1,0:T(8,128)S(1)} %get-tuple-element.159), channel_id=1, source_target_pairs={{0,4},{1,5},{2,6},{3,7},{4,0},{5,1},{6,2},{7,3},{8,12},{9,13},{10,... | collective-permute-start | bytes 331784 | tf_op jit(solution)/shard_map/ppermute | solution.py:173
  103.7 1.8 %collective-permute-start.34 = (f32[216,128]{1,0:T(8,128)S(1)}, f32[216,128]{1,0:T(8,128)S(1)}, u32[]{:S(2)}, u32[]{:S(2)}) collective-permute-start(f32[216,128]{1,0:T(8,128)S(1)} %get-tuple-element.157), channel_id=1, source_target_pairs={{0,6},{1,7},{2,4},{3,5},{4,2},{5,3},{6,0},{7,1},{8,14},{9,15},{10,... | collective-permute-start | bytes 331784 | tf_op jit(solution)/shard_map/ppermute | solution.py:173
  105.4 5.4 %collective-permute-done.29.other_ref = f32[4,216,128]{2,1,0:T(8,128)S(1)} collective-permute-done((f32[4,216,128]{2,1,0:T(8,128)S(1)}, f32[4,216,128]{2,1,0:T(8,128)S(1)}, u32[]{:S(2)}, u32[]{:S(2)}) %collective-permute-start.29) | collective-permute-done | bytes 442400 | tf_op jit(solution)/shard_map/ppermute | solution.py:519
  115.7 2.2 %collective-permute-start.39 = (f32[216,128]{1,0:T(8,128)S(1)}, f32[216,128]{1,0:T(8,128)S(1)}, u32[]{:S(2)}, u32[]{:S(2)}) collective-permute-start(f32[216,128]{1,0:T(8,128)S(1)} %get-tuple-element.172), channel_id=1, source_target_pairs={{0,4},{1,5},{2,6},{3,7},{4,0},{5,1},{6,2},{7,3},{8,12},{9,13},{10,... | collective-permute-start | bytes 331784 | tf_op jit(solution)/shard_map/ppermute | solution.py:173
  117.8 1.8 %collective-permute-start.38 = (f32[216,128]{1,0:T(8,128)S(1)}, f32[216,128]{1,0:T(8,128)S(1)}, u32[]{:S(2)}, u32[]{:S(2)}) collective-permute-start(f32[216,128]{1,0:T(8,128)S(1)} %get-tuple-element.169), channel_id=1, source_target_pairs={{0,6},{1,7},{2,4},{3,5},{4,2},{5,3},{6,0},{7,1},{8,14},{9,15},{10,... | collective-permute-start | bytes 331784 | tf_op jit(solution)/shard_map/ppermute | solution.py:173
  119.7 6.5 %collective-permute-done.36.other_ref = f32[4,216,128]{2,1,0:T(8,128)S(1)} collective-permute-done((f32[4,216,128]{2,1,0:T(8,128)S(1)}, f32[4,216,128]{2,1,0:T(8,128)S(1)}, u32[]{:S(2)}, u32[]{:S(2)}) %collective-permute-start.36) | collective-permute-done | bytes 442400 | tf_op jit(solution)/shard_map/ppermute | solution.py:519
  126.8 2.7 %collective-permute-start.42 = (f32[216,128]{1,0:T(8,128)S(1)}, f32[216,128]{1,0:T(8,128)S(1)}, u32[]{:S(2)}, u32[]{:S(2)}) collective-permute-start(f32[216,128]{1,0:T(8,128)S(1)} %get-tuple-element.180), channel_id=1, source_target_pairs={{0,4},{1,5},{2,6},{3,7},{4,0},{5,1},{6,2},{7,3},{8,12},{9,13},{10,... | collective-permute-start | bytes 331784 | tf_op jit(solution)/shard_map/ppermute | solution.py:173
  129.5 1.8 %collective-permute-start.41 = (f32[216,128]{1,0:T(8,128)S(1)}, f32[216,128]{1,0:T(8,128)S(1)}, u32[]{:S(2)}, u32[]{:S(2)}) collective-permute-start(f32[216,128]{1,0:T(8,128)S(1)} %get-tuple-element.178), channel_id=1, source_target_pairs={{0,6},{1,7},{2,4},{3,5},{4,2},{5,3},{6,0},{7,1},{8,14},{9,15},{10,... | collective-permute-start | bytes 331784 | tf_op jit(solution)/shard_map/ppermute | solution.py:173
  132.8 4.3 %collective-permute-done.42.refs_4_ = f32[216,128]{1,0:T(8,128)S(1)} collective-permute-done((f32[216,128]{1,0:T(8,128)S(1)}, f32[216,128]{1,0:T(8,128)S(1)}, u32[]{:S(2)}, u32[]{:S(2)}) %collective-permute-start.42) | collective-permute-done | bytes 110624 | tf_op jit(solution)/shard_map/ppermute | solution.py:173
  137.9 2.1 %shard_map.160 = (f32[2,6,48,384]{3,2,1,0:T(8,128)}, f32[48,384]{1,0:T(8,128)}, f32[32,128]{1,0:T(8,128)S(1)}) custom-call(s32[2]{0:T(128)S(1)} %pad_add_fusion.me_ref, f32[2,6]{1,0:T(2,128)S(1)} %copy-done.8, s32[1]{0:T(128)S(6)} %copy.29.count_ref, f32[5,48,384]{2,1,0:T(8,128)S(1)} %copy-done, s32[48,384]{1,0:T(8,128)S(1)} %copy-done.1, ...), custom_call_target="tpu_custom_call" | custom-call | flops 1 | bytes 1 | tf_op jit(solution)/shard_map/pallas_call | solution.py:451
  140.0 10.0 %all_to_all.11 = f32[32,1,128]{2,1,0:T(1,128)S(1)} all-to-all(f32[32,1,128]{2,1,0:T(1,128)S(1)} %bitcast.18), channel_id=1, replica_groups=mesh['gx'=4,'gy'=8] {'gx','gy'}, dimensions={0} | all-to-all | bytes 32768 | tf_op jit(solution)/shard_map/all_to_all | solution.py:546
  (107 shorter events, 42.0 us)
Async XLA Ops:
  1.7 7.8 %collective-permute-start.3 = (f32[6,48,384]{2,1,0:T(8,128)S(1)}, f32[6,48,384]{2,1,0:T(8,128)S(1)}, u32[]{:S(2)}, u32[]{:S(2)}) collective-permute-start(f32[6,48,384]{2,1,0:T(8,128)S(1)} %slice_bitcast_fusion.1.refs_0_), channel_id=1, source_target_pairs={{0,8},{8,0},{16,24},{24,16},{1,9},{9,1},{17,25},{25,17},{2,10},{10... | collective-permute-start | bytes 1327112 | tf_op jit(solution)/shard_map/ppermute | solution.py:152
  2.2 15.5 %collective-permute-start.4 = (f32[6,48,384]{2,1,0:T(8,128)S(1)}, f32[6,48,384]{2,1,0:T(8,128)}, u32[]{:S(2)}, u32[]{:S(2)}) collective-permute-start(f32[6,48,384]{2,1,0:T(8,128)S(1)} %slice_bitcast_fusion.1.refs_0_), channel_id=1, source_target_pairs={{0,16},{8,24},{16,0},{24,8},{1,17},{9,25},{17,1},{25,9},{2,18},{10... | collective-permute-start | bytes 1327112 | tf_op jit(solution)/shard_map/ppermute | solution.py:161
  5.9 11.7 %collective-permute-start.1 = (f32[96,192]{1,0:T(8,128)S(1)}, f32[96,192]{1,0:T(8,128)S(1)}, u32[]{:S(2)}, u32[]{:S(2)}) collective-permute-start(f32[96,192]{1,0:T(8,128)S(1)} %copy.26.refs_0_), channel_id=1, source_target_pairs={{0,16},{8,24},{16,0},{24,8},{1,17},{9,25},{17,1},{25,9},{2,18},{10... | collective-permute-start | bytes 221192 | tf_op jit(solution)/shard_map/ppermute | solution.py:161
  17.7 9.9 %collective-permute-start.10 = (f32[6,48,384]{2,1,0:T(8,128)S(1)}, f32[6,48,384]{2,1,0:T(8,128)S(1)}, u32[]{:S(2)}, u32[]{:S(2)}) collective-permute-start(f32[6,48,384]{2,1,0:T(8,128)S(1)} %slice_bitcast_fusion.refs_0_), channel_id=1, source_target_pairs={{0,8},{8,0},{16,24},{24,16},{1,9},{9,1},{17,25},{25,17},{2,10},{10... | collective-permute-start | bytes 1327112 | tf_op jit(solution)/shard_map/ppermute | solution.py:152
  18.2 16.6 %collective-permute-start.11 = (f32[6,48,384]{2,1,0:T(8,128)S(1)}, f32[6,48,384]{2,1,0:T(8,128)S(1)}, u32[]{:S(2)}, u32[]{:S(2)}) collective-permute-start(f32[6,48,384]{2,1,0:T(8,128)S(1)} %slice_bitcast_fusion.refs_0_), channel_id=1, source_target_pairs={{0,16},{8,24},{16,0},{24,8},{1,17},{9,25},{17,1},{25,9},{2,18},{10... | collective-permute-start | bytes 1327112 | tf_op jit(solution)/shard_map/ppermute | solution.py:161
  22.6 11.7 %collective-permute-start.8 = (f32[216,128]{1,0:T(8,128)S(1)}, f32[216,128]{1,0:T(8,128)S(1)}, u32[]{:S(2)}, u32[]{:S(2)}) collective-permute-start(f32[216,128]{1,0:T(8,128)S(1)} %get-tuple-element.106), channel_id=1, source_target_pairs={{0,4},{1,5},{2,6},{3,7},{4,0},{5,1},{6,2},{7,3},{8,12},{9,13},{10,... | collective-permute-start | bytes 331784 | tf_op jit(solution)/shard_map/ppermute | solution.py:173
  25.3 8.9 %collective-permute-start.7 = (f32[216,128]{1,0:T(8,128)S(1)}, f32[216,128]{1,0:T(8,128)S(1)}, u32[]{:S(2)}, u32[]{:S(2)}) collective-permute-start(f32[216,128]{1,0:T(8,128)S(1)} %get-tuple-element.104), channel_id=1, source_target_pairs={{0,6},{1,7},{2,4},{3,5},{4,2},{5,3},{6,0},{7,1},{8,14},{9,15},{10,... | collective-permute-start | bytes 331784 | tf_op jit(solution)/shard_map/ppermute | solution.py:173
  26.6 8.1 %collective-permute-start.6 = (f32[216,128]{1,0:T(8,128)S(1)}, f32[216,128]{1,0:T(8,128)S(1)}, u32[]{:S(2)}, u32[]{:S(2)}) collective-permute-start(f32[216,128]{1,0:T(8,128)S(1)} %get-tuple-element.102), channel_id=1, source_target_pairs={{0,2},{1,3},{2,0},{3,1},{4,6},{5,7},{6,4},{7,5},{8,10},{9,11},{10,... | collective-permute-start | bytes 331784 | tf_op jit(solution)/shard_map/ppermute | solution.py:173
  36.1 12.6 %collective-permute-start.9 = (f32[4,216,128]{2,1,0:T(8,128)S(1)}, f32[4,216,128]{2,1,0:T(8,128)S(1)}, u32[]{:S(2)}, u32[]{:S(2)}) collective-permute-start(f32[4,216,128]{2,1,0:T(8,128)S(1)} %get-tuple-element.109), channel_id=1, source_target_pairs={{0,1},{1,0},{2,3},{3,2},{4,5},{5,4},{6,7},{7,6},{8,9},{9,8},{10,11... | collective-permute-start | bytes 1327112 | tf_op jit(solution)/shard_map/ppermute | solution.py:519
  39.4 12.2 %collective-permute-start.15 = (f32[216,128]{1,0:T(8,128)S(1)}, f32[216,128]{1,0:T(8,128)S(1)}, u32[]{:S(2)}, u32[]{:S(2)}) collective-permute-start(f32[216,128]{1,0:T(8,128)S(1)} %get-tuple-element.119), channel_id=1, source_target_pairs={{0,4},{1,5},{2,6},{3,7},{4,0},{5,1},{6,2},{7,3},{8,12},{9,13},{10,... | collective-permute-start | bytes 331784 | tf_op jit(solution)/shard_map/ppermute | solution.py:173
  43.1 8.5 %collective-permute-start.14 = (f32[216,128]{1,0:T(8,128)S(1)}, f32[216,128]{1,0:T(8,128)S(1)}, u32[]{:S(2)}, u32[]{:S(2)}) collective-permute-start(f32[216,128]{1,0:T(8,128)S(1)} %get-tuple-element.117), channel_id=1, source_target_pairs={{0,6},{1,7},{2,4},{3,5},{4,2},{5,3},{6,0},{7,1},{8,14},{9,15},{10,... | collective-permute-start | bytes 331784 | tf_op jit(solution)/shard_map/ppermute | solution.py:173
  43.5 9.1 %collective-permute-start.13 = (f32[216,128]{1,0:T(8,128)S(1)}, f32[216,128]{1,0:T(8,128)S(1)}, u32[]{:S(2)}, u32[]{:S(2)}) collective-permute-start(f32[216,128]{1,0:T(8,128)S(1)} %get-tuple-element.115), channel_id=1, source_target_pairs={{0,2},{1,3},{2,0},{3,1},{4,6},{5,7},{6,4},{7,5},{8,10},{9,11},{10,... | collective-permute-start | bytes 331784 | tf_op jit(solution)/shard_map/ppermute | solution.py:173
  53.9 11.6 %collective-permute-start.16 = (f32[4,216,128]{2,1,0:T(8,128)S(1)}, f32[4,216,128]{2,1,0:T(8,128)S(1)}, u32[]{:S(2)}, u32[]{:S(2)}) collective-permute-start(f32[4,216,128]{2,1,0:T(8,128)S(1)} %get-tuple-element.123), channel_id=1, source_target_pairs={{0,1},{1,0},{2,3},{3,2},{4,5},{5,4},{6,7},{7,6},{8,9},{9,8},{10,11... | collective-permute-start | bytes 1327112 | tf_op jit(solution)/shard_map/ppermute | solution.py:519
  54.5 11.0 %collective-permute-start.19 = (f32[216,128]{1,0:T(8,128)S(1)}, f32[216,128]{1,0:T(8,128)S(1)}, u32[]{:S(2)}, u32[]{:S(2)}) collective-permute-start(f32[216,128]{1,0:T(8,128)S(1)} %get-tuple-element.132), channel_id=1, source_target_pairs={{0,4},{1,5},{2,6},{3,7},{4,0},{5,1},{6,2},{7,3},{8,12},{9,13},{10,... | collective-permute-start | bytes 331784 | tf_op jit(solution)/shard_map/ppermute | solution.py:173
  57.2 8.3 %collective-permute-start.18 = (f32[216,128]{1,0:T(8,128)S(1)}, f32[216,128]{1,0:T(8,128)S(1)}, u32[]{:S(2)}, u32[]{:S(2)}) collective-permute-start(f32[216,128]{1,0:T(8,128)S(1)} %get-tuple-element.129), channel_id=1, source_target_pairs={{0,6},{1,7},{2,4},{3,5},{4,2},{5,3},{6,0},{7,1},{8,14},{9,15},{10,... | collective-permute-start | bytes 331784 | tf_op jit(solution)/shard_map/ppermute | solution.py:173
  66.9 14.4 %collective-permute-start.21 = (f32[6,48,384]{2,1,0:T(8,128)S(1)}, f32[6,48,384]{2,1,0:T(8,128)S(1)}, u32[]{:S(2)}, u32[]{:S(2)}) collective-permute-start(f32[6,48,384]{2,1,0:T(8,128)S(1)} %shard_map.148.refs_0_), channel_id=1, source_target_pairs={{0,16},{8,24},{16,0},{24,8},{1,17},{9,25},{17,1},{25,9},{2,18},{10... | collective-permute-start | bytes 1327112 | tf_op jit(solution)/shard_map/ppermute | solution.py:161
  69.1 11.6 %collective-permute-start.22 = (f32[216,128]{1,0:T(8,128)S(1)}, f32[216,128]{1,0:T(8,128)S(1)}, u32[]{:S(2)}, u32[]{:S(2)}) collective-permute-start(f32[216,128]{1,0:T(8,128)S(1)} %get-tuple-element.135), channel_id=1, source_target_pairs={{0,4},{1,5},{2,6},{3,7},{4,0},{5,1},{6,2},{7,3},{8,12},{9,13},{10,... | collective-permute-start | bytes 331784 | tf_op jit(solution)/shard_map/ppermute | solution.py:173
  71.3 9.4 %collective-permute-start.23 = (f32[216,128]{1,0:T(8,128)S(1)}, f32[216,128]{1,0:T(8,128)S(1)}, u32[]{:S(2)}, u32[]{:S(2)}) collective-permute-start(f32[216,128]{1,0:T(8,128)S(1)} %get-tuple-element.136), channel_id=1, source_target_pairs={{0,6},{1,7},{2,4},{3,5},{4,2},{5,3},{6,0},{7,1},{8,14},{9,15},{10,... | collective-permute-start | bytes 331784 | tf_op jit(solution)/shard_map/ppermute | solution.py:173
  73.1 8.2 %collective-permute-start.24 = (f32[216,128]{1,0:T(8,128)S(1)}, f32[216,128]{1,0:T(8,128)S(1)}, u32[]{:S(2)}, u32[]{:S(2)}) collective-permute-start(f32[216,128]{1,0:T(8,128)S(1)} %get-tuple-element.137), channel_id=1, source_target_pairs={{0,2},{1,3},{2,0},{3,1},{4,6},{5,7},{6,4},{7,5},{8,10},{9,11},{10,... | collective-permute-start | bytes 331784 | tf_op jit(solution)/shard_map/ppermute | solution.py:173
  82.7 14.2 %collective-permute-start.31 = (f32[6,48,384]{2,1,0:T(8,128)S(1)}, f32[6,48,384]{2,1,0:T(8,128)S(1)}, u32[]{:S(2)}, u32[]{:S(2)}) collective-permute-start(f32[6,48,384]{2,1,0:T(8,128)S(1)} %shard_map.154.refs_0_), channel_id=1, source_target_pairs={{0,16},{8,24},{16,0},{24,8},{1,17},{9,25},{17,1},{25,9},{2,18},{10... | collective-permute-start | bytes 1327112 | tf_op jit(solution)/shard_map/ppermute | solution.py:161
  84.8 11.6 %collective-permute-start.28 = (f32[216,128]{1,0:T(8,128)S(1)}, f32[216,128]{1,0:T(8,128)S(1)}, u32[]{:S(2)}, u32[]{:S(2)}) collective-permute-start(f32[216,128]{1,0:T(8,128)S(1)} %get-tuple-element.146), channel_id=1, source_target_pairs={{0,4},{1,5},{2,6},{3,7},{4,0},{5,1},{6,2},{7,3},{8,12},{9,13},{10,... | collective-permute-start | bytes 331784 | tf_op jit(solution)/shard_map/ppermute | solution.py:173
  87.1 9.4 %collective-permute-start.27 = (f32[216,128]{1,0:T(8,128)S(1)}, f32[216,128]{1,0:T(8,128)S(1)}, u32[]{:S(2)}, u32[]{:S(2)}) collective-permute-start(f32[216,128]{1,0:T(8,128)S(1)} %get-tuple-element.144), channel_id=1, source_target_pairs={{0,6},{1,7},{2,4},{3,5},{4,2},{5,3},{6,0},{7,1},{8,14},{9,15},{10,... | collective-permute-start | bytes 331784 | tf_op jit(solution)/shard_map/ppermute | solution.py:173
  88.8 8.1 %collective-permute-start.26 = (f32[216,128]{1,0:T(8,128)S(1)}, f32[216,128]{1,0:T(8,128)S(1)}, u32[]{:S(2)}, u32[]{:S(2)}) collective-permute-start(f32[216,128]{1,0:T(8,128)S(1)} %get-tuple-element.142), channel_id=1, source_target_pairs={{0,2},{1,3},{2,0},{3,1},{4,6},{5,7},{6,4},{7,5},{8,10},{9,11},{10,... | collective-permute-start | bytes 331784 | tf_op jit(solution)/shard_map/ppermute | solution.py:173
  98.2 12.6 %collective-permute-start.29 = (f32[4,216,128]{2,1,0:T(8,128)S(1)}, f32[4,216,128]{2,1,0:T(8,128)S(1)}, u32[]{:S(2)}, u32[]{:S(2)}) collective-permute-start(f32[4,216,128]{2,1,0:T(8,128)S(1)} %get-tuple-element.149), channel_id=1, source_target_pairs={{0,1},{1,0},{2,3},{3,2},{4,5},{5,4},{6,7},{7,6},{8,9},{9,8},{10,11... | collective-permute-start | bytes 1327112 | tf_op jit(solution)/shard_map/ppermute | solution.py:519
  101.4 11.6 %collective-permute-start.35 = (f32[216,128]{1,0:T(8,128)S(1)}, f32[216,128]{1,0:T(8,128)S(1)}, u32[]{:S(2)}, u32[]{:S(2)}) collective-permute-start(f32[216,128]{1,0:T(8,128)S(1)} %get-tuple-element.159), channel_id=1, source_target_pairs={{0,4},{1,5},{2,6},{3,7},{4,0},{5,1},{6,2},{7,3},{8,12},{9,13},{10,... | collective-permute-start | bytes 331784 | tf_op jit(solution)/shard_map/ppermute | solution.py:173
  103.7 9.4 %collective-permute-start.34 = (f32[216,128]{1,0:T(8,128)S(1)}, f32[216,128]{1,0:T(8,128)S(1)}, u32[]{:S(2)}, u32[]{:S(2)}) collective-permute-start(f32[216,128]{1,0:T(8,128)S(1)} %get-tuple-element.157), channel_id=1, source_target_pairs={{0,6},{1,7},{2,4},{3,5},{4,2},{5,3},{6,0},{7,1},{8,14},{9,15},{10,... | collective-permute-start | bytes 331784 | tf_op jit(solution)/shard_map/ppermute | solution.py:173
  105.4 8.3 %collective-permute-start.33 = (f32[216,128]{1,0:T(8,128)S(1)}, f32[216,128]{1,0:T(8,128)S(1)}, u32[]{:S(2)}, u32[]{:S(2)}) collective-permute-start(f32[216,128]{1,0:T(8,128)S(1)} %get-tuple-element.155), channel_id=1, source_target_pairs={{0,2},{1,3},{2,0},{3,1},{4,6},{5,7},{6,4},{7,5},{8,10},{9,11},{10,... | collective-permute-start | bytes 331784 | tf_op jit(solution)/shard_map/ppermute | solution.py:173
  115.1 11.1 %collective-permute-start.36 = (f32[4,216,128]{2,1,0:T(8,128)S(1)}, f32[4,216,128]{2,1,0:T(8,128)S(1)}, u32[]{:S(2)}, u32[]{:S(2)}) collective-permute-start(f32[4,216,128]{2,1,0:T(8,128)S(1)} %get-tuple-element.163), channel_id=1, source_target_pairs={{0,1},{1,0},{2,3},{3,2},{4,5},{5,4},{6,7},{7,6},{8,9},{9,8},{10,11... | collective-permute-start | bytes 1327112 | tf_op jit(solution)/shard_map/ppermute | solution.py:519
  115.7 15.6 %collective-permute-start.39 = (f32[216,128]{1,0:T(8,128)S(1)}, f32[216,128]{1,0:T(8,128)S(1)}, u32[]{:S(2)}, u32[]{:S(2)}) collective-permute-start(f32[216,128]{1,0:T(8,128)S(1)} %get-tuple-element.172), channel_id=1, source_target_pairs={{0,4},{1,5},{2,6},{3,7},{4,0},{5,1},{6,2},{7,3},{8,12},{9,13},{10,... | collective-permute-start | bytes 331784 | tf_op jit(solution)/shard_map/ppermute | solution.py:173
  117.8 14.2 %collective-permute-start.38 = (f32[216,128]{1,0:T(8,128)S(1)}, f32[216,128]{1,0:T(8,128)S(1)}, u32[]{:S(2)}, u32[]{:S(2)}) collective-permute-start(f32[216,128]{1,0:T(8,128)S(1)} %get-tuple-element.169), channel_id=1, source_target_pairs={{0,6},{1,7},{2,4},{3,5},{4,2},{5,3},{6,0},{7,1},{8,14},{9,15},{10,... | collective-permute-start | bytes 331784 | tf_op jit(solution)/shard_map/ppermute | solution.py:173
  119.6 12.4 %collective-permute-start.37 = (f32[216,128]{1,0:T(8,128)S(1)}, f32[216,128]{1,0:T(8,128)S(1)}, u32[]{:S(2)}, u32[]{:S(2)}) collective-permute-start(f32[216,128]{1,0:T(8,128)S(1)} %get-tuple-element.166), channel_id=1, source_target_pairs={{0,2},{1,3},{2,0},{3,1},{4,6},{5,7},{6,4},{7,5},{8,10},{9,11},{10,... | collective-permute-start | bytes 331784 | tf_op jit(solution)/shard_map/ppermute | solution.py:173
  126.8 10.4 %collective-permute-start.42 = (f32[216,128]{1,0:T(8,128)S(1)}, f32[216,128]{1,0:T(8,128)S(1)}, u32[]{:S(2)}, u32[]{:S(2)}) collective-permute-start(f32[216,128]{1,0:T(8,128)S(1)} %get-tuple-element.180), channel_id=1, source_target_pairs={{0,4},{1,5},{2,6},{3,7},{4,0},{5,1},{6,2},{7,3},{8,12},{9,13},{10,... | collective-permute-start | bytes 331784 | tf_op jit(solution)/shard_map/ppermute | solution.py:173
  (22 other events, 236.8 us)

commit v9 on v7

--- a/solution.py
+++ b/solution.py
@@ -404,12 +404,8 @@
         weight_x = jnp.where(along == col, 1.0 - frac_x, jnp.where(along == col + 1, frac_x, 0.0))
         across = lax.broadcasted_iota(jnp.int32, (rows, slots), 0)
         weight_y = jnp.where(across == row, 1.0 - frac_y, jnp.where(across == row + 1, frac_y, 0.0))
-        partial = lax.dot_general(
-            profile_ref[...].reshape(records * rows, cols),
-            weight_x,
-            NN,
-            precision=lax.Precision.HIGHEST,
-            preferred_element_type=jnp.float32,
+        partial = dot_split(
+            split(profile_ref[...].reshape(records * rows, cols)), split(weight_x)
         ).reshape(records, rows, slots)
         interp = jnp.sum(partial * weight_y[None], axis=1)
         slot = lax.broadcasted_iota(jnp.int32, (1, slots), 1)

time: 151 us -> 151 us (level)
  no operation moved by 1% of the time
where the time goes in v9:
time: 151 us; the launch traced here: 150 us
  waiting for transfers between devices  56.1 us (37%)
  starting transfers between devices  48.5 us (32%)
  Pallas kernels  27.3 us (18%)
  blocking collectives  10 us (7%)
  local copies, waits for them, and re-layouts  6.78 us (4%)
  between operations  1.62 us (1%)
    ppermute x24, starting transfers between devices, exchange(): out[mask] = lax.ppermute(blocks[mask], axis, pairs)  35.5 us
    ppermute x24, waiting for transfers between devices, exchange(): out[mask] = lax.ppermute(blocks[mask], axis, pairs)  30.3 us
    pallas_call x22, Pallas kernels, call(): pl.pallas_call(kernel, out_shape=out_shape, in_specs=specs, out_specs=[ou...  25.3 us
    ppermute x4, waiting for transfers between devices, body(): other.append(lax.ppermute(for_other, 'gy', side_pairs))  20.9 us
    all_to_all x1, blocking collectives, body(): lax.all_to_all(outgoing, ('gx', 'gy'), split_axis=0, concat_axis=0, tiled...  10 us
    ppermute x10, starting transfers between devices, gather_far(): lax.ppermute(piece, axis, pairs)  7.07 us
    ppermute x10, waiting for transfers between devices, gather_far(): lax.ppermute(piece, axis, pairs)  4.86 us
    unnamed x24, local copies, waits for them, and re-layouts  4.6 us
  transfers between devices with their start and end apart: 43, of which 17 were waited for; matrix products, arithmetic and copies ran while one was open for 2% of the time, Pallas kernels for 14%

profile of v9, /device:TPU:0, one launch (start us, length us, event | category | flops | bytes accessed | tf_op | source)
XLA Modules:
  0.0 150.3 jit_solution(13267264825690714480)
XLA Ops:
  2.2 2.6 %collective-permute-start.4 = (f32[6,48,384]{2,1,0:T(8,128)S(1)}, f32[6,48,384]{2,1,0:T(8,128)}, u32[]{:S(2)}, u32[]{:S(2)}) collective-permute-start(f32[6,48,384]{2,1,0:T(8,128)S(1)} %slice_bitcast_fusion.1.refs_0_), channel_id=1, source_target_pairs={{0,16},{8,24},{16,0},{24,8},{1,17},{9,25},{17,1},{25,9},{2,18},{10... | collective-permute-start | bytes 1327112 | tf_op jit(solution)/shard_map/ppermute | solution.py:157
  12.8 4.8 %collective-permute-done.1.refs_2_ = f32[96,192]{1,0:T(8,128)S(1)} collective-permute-done((f32[96,192]{1,0:T(8,128)S(1)}, f32[96,192]{1,0:T(8,128)S(1)}, u32[]{:S(2)}, u32[]{:S(2)}) %collective-permute-start.1) | collective-permute-done | bytes 73760 | tf_op jit(solution)/shard_map/ppermute | solution.py:157
  20.4 2.1 %shard_map.142 = (f32[216,128]{1,0:T(8,128)S(1)}, f32[216,128]{1,0:T(8,128)S(1)}, f32[216,128]{1,0:T(8,128)S(1)}, f32[216,128]{1,0:T(8,128)S(1)}) custom-call(s32[2]{0:T(128)S(1)} %pad_add_fusion.me_ref, bf16[1536,384]{1,0:T(8,128)(2,1)S(1)} %get-tuple-element.96.high_ref, bf16[1536,384]{1,0:T(8,128)(2,1)S(1)} %get-tuple-element.97.low_ref, ...), custom_call_target="tpu_custom_call" | custom-call | flops 1 | bytes 1 | tf_op jit(solution)/shard_map/pallas_call | solution.py:131
  22.6 3.7 %collective-permute-start.8 = (f32[216,128]{1,0:T(8,128)S(1)}, f32[216,128]{1,0:T(8,128)S(1)}, u32[]{:S(2)}, u32[]{:S(2)}) collective-permute-start(f32[216,128]{1,0:T(8,128)S(1)} %get-tuple-element.106), channel_id=1, source_target_pairs={{0,6},{1,7},{2,4},{3,5},{4,2},{5,3},{6,0},{7,1},{8,14},{9,15},{10,... | collective-permute-start | bytes 331784 | tf_op jit(solution)/shard_map/ppermute | solution.py:169
  30.4 5.5 %collective-permute-done.7.refs_2_ = f32[216,128]{1,0:T(8,128)S(1)} collective-permute-done((f32[216,128]{1,0:T(8,128)S(1)}, f32[216,128]{1,0:T(8,128)S(1)}, u32[]{:S(2)}, u32[]{:S(2)}) %collective-permute-start.7) | collective-permute-done | bytes 110624 | tf_op jit(solution)/shard_map/ppermute | solution.py:169
  40.5 2.5 %collective-permute-start.15 = (f32[216,128]{1,0:T(8,128)S(1)}, f32[216,128]{1,0:T(8,128)S(1)}, u32[]{:S(2)}, u32[]{:S(2)}) collective-permute-start(f32[216,128]{1,0:T(8,128)S(1)} %get-tuple-element.119), channel_id=1, source_target_pairs={{0,6},{1,7},{2,4},{3,5},{4,2},{5,3},{6,0},{7,1},{8,14},{9,15},{10,... | collective-permute-start | bytes 331784 | tf_op jit(solution)/shard_map/ppermute | solution.py:169
  43.0 1.9 %collective-permute-start.13 = (f32[216,128]{1,0:T(8,128)S(1)}, f32[216,128]{1,0:T(8,128)S(1)}, u32[]{:S(2)}, u32[]{:S(2)}) collective-permute-start(f32[216,128]{1,0:T(8,128)S(1)} %get-tuple-element.115), channel_id=1, source_target_pairs={{0,2},{1,3},{2,0},{3,1},{4,6},{5,7},{6,4},{7,5},{8,10},{9,11},{10,... | collective-permute-start | bytes 331784 | tf_op jit(solution)/shard_map/ppermute | solution.py:169
  44.9 5.0 %collective-permute-done.9.other_ref = f32[4,216,128]{2,1,0:T(8,128)S(1)} collective-permute-done((f32[4,216,128]{2,1,0:T(8,128)S(1)}, f32[4,216,128]{2,1,0:T(8,128)S(1)}, u32[]{:S(2)}, u32[]{:S(2)}) %collective-permute-start.9) | collective-permute-done | bytes 442400 | tf_op jit(solution)/shard_map/ppermute | solution.py:511
  50.5 2.0 %collective-permute-done.14.refs_2_ = f32[216,128]{1,0:T(8,128)S(1)} collective-permute-done((f32[216,128]{1,0:T(8,128)S(1)}, f32[216,128]{1,0:T(8,128)S(1)}, u32[]{:S(2)}, u32[]{:S(2)}) %collective-permute-start.14) | collective-permute-done | bytes 110624 | tf_op jit(solution)/shard_map/ppermute | solution.py:169
  54.4 2.2 %collective-permute-start.19 = (f32[216,128]{1,0:T(8,128)S(1)}, f32[216,128]{1,0:T(8,128)S(1)}, u32[]{:S(2)}, u32[]{:S(2)}) collective-permute-start(f32[216,128]{1,0:T(8,128)S(1)} %get-tuple-element.132), channel_id=1, source_target_pairs={{0,6},{1,7},{2,4},{3,5},{4,2},{5,3},{6,0},{7,1},{8,14},{9,15},{10,... | collective-permute-start | bytes 331784 | tf_op jit(solution)/shard_map/ppermute | solution.py:169
  56.7 2.2 %collective-permute-start.17 = (f32[216,128]{1,0:T(8,128)S(1)}, f32[216,128]{1,0:T(8,128)S(1)}, u32[]{:S(2)}, u32[]{:S(2)}) collective-permute-start(f32[216,128]{1,0:T(8,128)S(1)} %get-tuple-element.126), channel_id=1, source_target_pairs={{0,2},{1,3},{2,0},{3,1},{4,6},{5,7},{6,4},{7,5},{8,10},{9,11},{10,... | collective-permute-start | bytes 331784 | tf_op jit(solution)/shard_map/ppermute | solution.py:169
  58.8 3.4 %collective-permute-done.19.refs_3_ = f32[216,128]{1,0:T(8,128)S(1)} collective-permute-done((f32[216,128]{1,0:T(8,128)S(1)}, f32[216,128]{1,0:T(8,128)S(1)}, u32[]{:S(2)}, u32[]{:S(2)}) %collective-permute-start.19) | collective-permute-done | bytes 110624 | tf_op jit(solution)/shard_map/ppermute | solution.py:169
  62.2 3.8 %collective-permute-done.16.other_ref = f32[4,216,128]{2,1,0:T(8,128)S(1)} collective-permute-done((f32[4,216,128]{2,1,0:T(8,128)S(1)}, f32[4,216,128]{2,1,0:T(8,128)S(1)}, u32[]{:S(2)}, u32[]{:S(2)}) %collective-permute-start.16) | collective-permute-done | bytes 442400 | tf_op jit(solution)/shard_map/ppermute | solution.py:511
  69.3 2.1 %collective-permute-start.22 = (f32[216,128]{1,0:T(8,128)S(1)}, f32[216,128]{1,0:T(8,128)S(1)}, u32[]{:S(2)}, u32[]{:S(2)}) collective-permute-start(f32[216,128]{1,0:T(8,128)S(1)} %get-tuple-element.135), channel_id=1, source_target_pairs={{0,6},{1,7},{2,4},{3,5},{4,2},{5,3},{6,0},{7,1},{8,14},{9,15},{10,... | collective-permute-start | bytes 331784 | tf_op jit(solution)/shard_map/ppermute | solution.py:169
  71.4 2.4 %collective-permute-start.24 = (f32[216,128]{1,0:T(8,128)S(1)}, f32[216,128]{1,0:T(8,128)S(1)}, u32[]{:S(2)}, u32[]{:S(2)}) collective-permute-start(f32[216,128]{1,0:T(8,128)S(1)} %get-tuple-element.137), channel_id=1, source_target_pairs={{0,2},{1,3},{2,0},{3,1},{4,6},{5,7},{6,4},{7,5},{8,10},{9,11},{10,... | collective-permute-start | bytes 331784 | tf_op jit(solution)/shard_map/ppermute | solution.py:169
  75.2 1.9 %collective-permute-done.22.refs_3_ = f32[216,128]{1,0:T(8,128)S(1)} collective-permute-done((f32[216,128]{1,0:T(8,128)S(1)}, f32[216,128]{1,0:T(8,128)S(1)}, u32[]{:S(2)}, u32[]{:S(2)}) %collective-permute-start.22) | collective-permute-done | bytes 110624 | tf_op jit(solution)/shard_map/ppermute | solution.py:169
  77.1 3.9 %collective-permute-done.23.refs_2_ = f32[216,128]{1,0:T(8,128)S(1)} collective-permute-done((f32[216,128]{1,0:T(8,128)S(1)}, f32[216,128]{1,0:T(8,128)S(1)}, u32[]{:S(2)}, u32[]{:S(2)}) %collective-permute-start.23) | collective-permute-done | bytes 110624 | tf_op jit(solution)/shard_map/ppermute | solution.py:169
  84.5 2.1 %collective-permute-start.28 = (f32[216,128]{1,0:T(8,128)S(1)}, f32[216,128]{1,0:T(8,128)S(1)}, u32[]{:S(2)}, u32[]{:S(2)}) collective-permute-start(f32[216,128]{1,0:T(8,128)S(1)} %get-tuple-element.146), channel_id=1, source_target_pairs={{0,6},{1,7},{2,4},{3,5},{4,2},{5,3},{6,0},{7,1},{8,14},{9,15},{10,... | collective-permute-start | bytes 331784 | tf_op jit(solution)/shard_map/ppermute | solution.py:169
  86.6 2.4 %collective-permute-start.26 = (f32[216,128]{1,0:T(8,128)S(1)}, f32[216,128]{1,0:T(8,128)S(1)}, u32[]{:S(2)}, u32[]{:S(2)}) collective-permute-start(f32[216,128]{1,0:T(8,128)S(1)} %get-tuple-element.142), channel_id=1, source_target_pairs={{0,2},{1,3},{2,0},{3,1},{4,6},{5,7},{6,4},{7,5},{8,10},{9,11},{10,... | collective-permute-start | bytes 331784 | tf_op jit(solution)/shard_map/ppermute | solution.py:169
  92.4 4.0 %collective-permute-done.27.refs_2_ = f32[216,128]{1,0:T(8,128)S(1)} collective-permute-done((f32[216,128]{1,0:T(8,128)S(1)}, f32[216,128]{1,0:T(8,128)S(1)}, u32[]{:S(2)}, u32[]{:S(2)}) %collective-permute-start.27) | collective-permute-done | bytes 110624 | tf_op jit(solution)/shard_map/ppermute | solution.py:169
  100.7 2.1 %collective-permute-start.35 = (f32[216,128]{1,0:T(8,128)S(1)}, f32[216,128]{1,0:T(8,128)S(1)}, u32[]{:S(2)}, u32[]{:S(2)}) collective-permute-start(f32[216,128]{1,0:T(8,128)S(1)} %get-tuple-element.159), channel_id=1, source_target_pairs={{0,6},{1,7},{2,4},{3,5},{4,2},{5,3},{6,0},{7,1},{8,14},{9,15},{10,... | collective-permute-start | bytes 331784 | tf_op jit(solution)/shard_map/ppermute | solution.py:169
  102.8 2.3 %collective-permute-start.33 = (f32[216,128]{1,0:T(8,128)S(1)}, f32[216,128]{1,0:T(8,128)S(1)}, u32[]{:S(2)}, u32[]{:S(2)}) collective-permute-start(f32[216,128]{1,0:T(8,128)S(1)} %get-tuple-element.155), channel_id=1, source_target_pairs={{0,2},{1,3},{2,0},{3,1},{4,6},{5,7},{6,4},{7,5},{8,10},{9,11},{10,... | collective-permute-start | bytes 331784 | tf_op jit(solution)/shard_map/ppermute | solution.py:169
  105.1 5.3 %collective-permute-done.29.other_ref = f32[4,216,128]{2,1,0:T(8,128)S(1)} collective-permute-done((f32[4,216,128]{2,1,0:T(8,128)S(1)}, f32[4,216,128]{2,1,0:T(8,128)S(1)}, u32[]{:S(2)}, u32[]{:S(2)}) %collective-permute-start.29) | collective-permute-done | bytes 442400 | tf_op jit(solution)/shard_map/ppermute | solution.py:511
  114.7 1.8 %collective-permute-start.39 = (f32[216,128]{1,0:T(8,128)S(1)}, f32[216,128]{1,0:T(8,128)S(1)}, u32[]{:S(2)}, u32[]{:S(2)}) collective-permute-start(f32[216,128]{1,0:T(8,128)S(1)} %get-tuple-element.172), channel_id=1, source_target_pairs={{0,6},{1,7},{2,4},{3,5},{4,2},{5,3},{6,0},{7,1},{8,14},{9,15},{10,... | collective-permute-start | bytes 331784 | tf_op jit(solution)/shard_map/ppermute | solution.py:169
  116.5 2.6 %collective-permute-start.37 = (f32[216,128]{1,0:T(8,128)S(1)}, f32[216,128]{1,0:T(8,128)S(1)}, u32[]{:S(2)}, u32[]{:S(2)}) collective-permute-start(f32[216,128]{1,0:T(8,128)S(1)} %get-tuple-element.166), channel_id=1, source_target_pairs={{0,2},{1,3},{2,0},{3,1},{4,6},{5,7},{6,4},{7,5},{8,10},{9,11},{10,... | collective-permute-start | bytes 331784 | tf_op jit(solution)/shard_map/ppermute | solution.py:169
  119.1 6.9 %collective-permute-done.36.other_ref = f32[4,216,128]{2,1,0:T(8,128)S(1)} collective-permute-done((f32[4,216,128]{2,1,0:T(8,128)S(1)}, f32[4,216,128]{2,1,0:T(8,128)S(1)}, u32[]{:S(2)}, u32[]{:S(2)}) %collective-permute-start.36) | collective-permute-done | bytes 442400 | tf_op jit(solution)/shard_map/ppermute | solution.py:511
  126.6 2.1 %collective-permute-start.42 = (f32[216,128]{1,0:T(8,128)S(1)}, f32[216,128]{1,0:T(8,128)S(1)}, u32[]{:S(2)}, u32[]{:S(2)}) collective-permute-start(f32[216,128]{1,0:T(8,128)S(1)} %get-tuple-element.180), channel_id=1, source_target_pairs={{0,6},{1,7},{2,4},{3,5},{4,2},{5,3},{6,0},{7,1},{8,14},{9,15},{10,... | collective-permute-start | bytes 331784 | tf_op jit(solution)/shard_map/ppermute | solution.py:169
  128.8 2.3 %collective-permute-start.40 = (f32[216,128]{1,0:T(8,128)S(1)}, f32[216,128]{1,0:T(8,128)S(1)}, u32[]{:S(2)}, u32[]{:S(2)}) collective-permute-start(f32[216,128]{1,0:T(8,128)S(1)} %get-tuple-element.176), channel_id=1, source_target_pairs={{0,2},{1,3},{2,0},{3,1},{4,6},{5,7},{6,4},{7,5},{8,10},{9,11},{10,... | collective-permute-start | bytes 331784 | tf_op jit(solution)/shard_map/ppermute | solution.py:169
  132.6 1.9 %collective-permute-done.42.refs_4_ = f32[216,128]{1,0:T(8,128)S(1)} collective-permute-done((f32[216,128]{1,0:T(8,128)S(1)}, f32[216,128]{1,0:T(8,128)S(1)}, u32[]{:S(2)}, u32[]{:S(2)}) %collective-permute-start.42) | collective-permute-done | bytes 110624 | tf_op jit(solution)/shard_map/ppermute | solution.py:169
  134.5 3.2 %collective-permute-done.41.refs_3_ = f32[216,128]{1,0:T(8,128)S(1)} collective-permute-done((f32[216,128]{1,0:T(8,128)S(1)}, f32[216,128]{1,0:T(8,128)S(1)}, u32[]{:S(2)}, u32[]{:S(2)}) %collective-permute-start.41) | collective-permute-done | bytes 110624 | tf_op jit(solution)/shard_map/ppermute | solution.py:169
  137.7 1.9 %shard_map.160 = (f32[2,6,48,384]{3,2,1,0:T(8,128)}, f32[48,384]{1,0:T(8,128)}, f32[32,128]{1,0:T(8,128)S(1)}) custom-call(s32[2]{0:T(128)S(1)} %pad_add_fusion.me_ref, f32[2,6]{1,0:T(2,128)S(1)} %copy-done.8, s32[1]{0:T(128)S(6)} %copy.29.count_ref, f32[5,48,384]{2,1,0:T(8,128)S(1)} %copy-done, s32[48,384]{1,0:T(8,128)S(1)} %copy-done.1, ...), custom_call_target="tpu_custom_call" | custom-call | flops 1 | bytes 1 | tf_op jit(solution)/shard_map/pallas_call | solution.py:443
  139.7 10.0 %all_to_all.11 = f32[32,1,128]{2,1,0:T(1,128)S(1)} all-to-all(f32[32,1,128]{2,1,0:T(1,128)S(1)} %bitcast.18), channel_id=1, replica_groups=mesh['gx'=4,'gy'=8] {'gx','gy'}, dimensions={0} | all-to-all | bytes 32768 | tf_op jit(solution)/shard_map/all_to_all | solution.py:538
  (107 shorter events, 45.9 us)
Async XLA Ops:
  2.2 15.5 %collective-permute-start.4 = (f32[6,48,384]{2,1,0:T(8,128)S(1)}, f32[6,48,384]{2,1,0:T(8,128)}, u32[]{:S(2)}, u32[]{:S(2)}) collective-permute-start(f32[6,48,384]{2,1,0:T(8,128)S(1)} %slice_bitcast_fusion.1.refs_0_), channel_id=1, source_target_pairs={{0,16},{8,24},{16,0},{24,8},{1,17},{9,25},{17,1},{25,9},{2,18},{10... | collective-permute-start | bytes 1327112 | tf_op jit(solution)/shard_map/ppermute | solution.py:157
  5.9 11.7 %collective-permute-start.1 = (f32[96,192]{1,0:T(8,128)S(1)}, f32[96,192]{1,0:T(8,128)S(1)}, u32[]{:S(2)}, u32[]{:S(2)}) collective-permute-start(f32[96,192]{1,0:T(8,128)S(1)} %copy.26.refs_0_), channel_id=1, source_target_pairs={{0,16},{8,24},{16,0},{24,8},{1,17},{9,25},{17,1},{25,9},{2,18},{10... | collective-permute-start | bytes 221192 | tf_op jit(solution)/shard_map/ppermute | solution.py:157
  17.7 10.0 %collective-permute-start.10 = (f32[6,48,384]{2,1,0:T(8,128)S(1)}, f32[6,48,384]{2,1,0:T(8,128)S(1)}, u32[]{:S(2)}, u32[]{:S(2)}) collective-permute-start(f32[6,48,384]{2,1,0:T(8,128)S(1)} %slice_bitcast_fusion.refs_0_), channel_id=1, source_target_pairs={{0,8},{8,0},{16,24},{24,16},{1,9},{9,1},{17,25},{25,17},{2,10},{10... | collective-permute-start | bytes 1327112 | tf_op jit(solution)/shard_map/ppermute | solution.py:148
  18.2 17.7 %collective-permute-start.11 = (f32[6,48,384]{2,1,0:T(8,128)S(1)}, f32[6,48,384]{2,1,0:T(8,128)S(1)}, u32[]{:S(2)}, u32[]{:S(2)}) collective-permute-start(f32[6,48,384]{2,1,0:T(8,128)S(1)} %slice_bitcast_fusion.refs_0_), channel_id=1, source_target_pairs={{0,16},{8,24},{16,0},{24,8},{1,17},{9,25},{17,1},{25,9},{2,18},{10... | collective-permute-start | bytes 1327112 | tf_op jit(solution)/shard_map/ppermute | solution.py:157
  26.3 9.6 %collective-permute-start.7 = (f32[216,128]{1,0:T(8,128)S(1)}, f32[216,128]{1,0:T(8,128)S(1)}, u32[]{:S(2)}, u32[]{:S(2)}) collective-permute-start(f32[216,128]{1,0:T(8,128)S(1)} %get-tuple-element.104), channel_id=1, source_target_pairs={{0,4},{1,5},{2,6},{3,7},{4,0},{5,1},{6,2},{7,3},{8,12},{9,13},{10,... | collective-permute-start | bytes 331784 | tf_op jit(solution)/shard_map/ppermute | solution.py:169
  26.3 9.6 %collective-permute-start.6 = (f32[216,128]{1,0:T(8,128)S(1)}, f32[216,128]{1,0:T(8,128)S(1)}, u32[]{:S(2)}, u32[]{:S(2)}) collective-permute-start(f32[216,128]{1,0:T(8,128)S(1)} %get-tuple-element.102), channel_id=1, source_target_pairs={{0,2},{1,3},{2,0},{3,1},{4,6},{5,7},{6,4},{7,5},{8,10},{9,11},{10,... | collective-permute-start | bytes 331784 | tf_op jit(solution)/shard_map/ppermute | solution.py:169
  37.2 12.6 %collective-permute-start.9 = (f32[4,216,128]{2,1,0:T(8,128)S(1)}, f32[4,216,128]{2,1,0:T(8,128)S(1)}, u32[]{:S(2)}, u32[]{:S(2)}) collective-permute-start(f32[4,216,128]{2,1,0:T(8,128)S(1)} %get-tuple-element.109), channel_id=1, source_target_pairs={{0,1},{1,0},{2,3},{3,2},{4,5},{5,4},{6,7},{7,6},{8,9},{9,8},{10,11... | collective-permute-start | bytes 1327112 | tf_op jit(solution)/shard_map/ppermute | solution.py:511
  40.5 10.0 %collective-permute-start.15 = (f32[216,128]{1,0:T(8,128)S(1)}, f32[216,128]{1,0:T(8,128)S(1)}, u32[]{:S(2)}, u32[]{:S(2)}) collective-permute-start(f32[216,128]{1,0:T(8,128)S(1)} %get-tuple-element.119), channel_id=1, source_target_pairs={{0,6},{1,7},{2,4},{3,5},{4,2},{5,3},{6,0},{7,1},{8,14},{9,15},{10,... | collective-permute-start | bytes 331784 | tf_op jit(solution)/shard_map/ppermute | solution.py:169
  43.0 9.5 %collective-permute-start.14 = (f32[216,128]{1,0:T(8,128)S(1)}, f32[216,128]{1,0:T(8,128)S(1)}, u32[]{:S(2)}, u32[]{:S(2)}) collective-permute-start(f32[216,128]{1,0:T(8,128)S(1)} %get-tuple-element.117), channel_id=1, source_target_pairs={{0,4},{1,5},{2,6},{3,7},{4,0},{5,1},{6,2},{7,3},{8,12},{9,13},{10,... | collective-permute-start | bytes 331784 | tf_op jit(solution)/shard_map/ppermute | solution.py:169
  43.0 9.5 %collective-permute-start.13 = (f32[216,128]{1,0:T(8,128)S(1)}, f32[216,128]{1,0:T(8,128)S(1)}, u32[]{:S(2)}, u32[]{:S(2)}) collective-permute-start(f32[216,128]{1,0:T(8,128)S(1)} %get-tuple-element.115), channel_id=1, source_target_pairs={{0,2},{1,3},{2,0},{3,1},{4,6},{5,7},{6,4},{7,5},{8,10},{9,11},{10,... | collective-permute-start | bytes 331784 | tf_op jit(solution)/shard_map/ppermute | solution.py:169
  53.8 12.2 %collective-permute-start.16 = (f32[4,216,128]{2,1,0:T(8,128)S(1)}, f32[4,216,128]{2,1,0:T(8,128)S(1)}, u32[]{:S(2)}, u32[]{:S(2)}) collective-permute-start(f32[4,216,128]{2,1,0:T(8,128)S(1)} %get-tuple-element.123), channel_id=1, source_target_pairs={{0,1},{1,0},{2,3},{3,2},{4,5},{5,4},{6,7},{7,6},{8,9},{9,8},{10,11... | collective-permute-start | bytes 1327112 | tf_op jit(solution)/shard_map/ppermute | solution.py:511
  56.7 9.5 %collective-permute-start.18 = (f32[216,128]{1,0:T(8,128)S(1)}, f32[216,128]{1,0:T(8,128)S(1)}, u32[]{:S(2)}, u32[]{:S(2)}) collective-permute-start(f32[216,128]{1,0:T(8,128)S(1)} %get-tuple-element.129), channel_id=1, source_target_pairs={{0,4},{1,5},{2,6},{3,7},{4,0},{5,1},{6,2},{7,3},{8,12},{9,13},{10,... | collective-permute-start | bytes 331784 | tf_op jit(solution)/shard_map/ppermute | solution.py:169
  56.7 9.5 %collective-permute-start.17 = (f32[216,128]{1,0:T(8,128)S(1)}, f32[216,128]{1,0:T(8,128)S(1)}, u32[]{:S(2)}, u32[]{:S(2)}) collective-permute-start(f32[216,128]{1,0:T(8,128)S(1)} %get-tuple-element.126), channel_id=1, source_target_pairs={{0,2},{1,3},{2,0},{3,1},{4,6},{5,7},{6,4},{7,5},{8,10},{9,11},{10,... | collective-permute-start | bytes 331784 | tf_op jit(solution)/shard_map/ppermute | solution.py:169
  67.1 13.9 %collective-permute-start.21 = (f32[6,48,384]{2,1,0:T(8,128)S(1)}, f32[6,48,384]{2,1,0:T(8,128)S(1)}, u32[]{:S(2)}, u32[]{:S(2)}) collective-permute-start(f32[6,48,384]{2,1,0:T(8,128)S(1)} %shard_map.148.refs_0_), channel_id=1, source_target_pairs={{0,16},{8,24},{16,0},{24,8},{1,17},{9,25},{17,1},{25,9},{2,18},{10... | collective-permute-start | bytes 1327112 | tf_op jit(solution)/shard_map/ppermute | solution.py:157
  69.3 7.9 %collective-permute-start.22 = (f32[216,128]{1,0:T(8,128)S(1)}, f32[216,128]{1,0:T(8,128)S(1)}, u32[]{:S(2)}, u32[]{:S(2)}) collective-permute-start(f32[216,128]{1,0:T(8,128)S(1)} %get-tuple-element.135), channel_id=1, source_target_pairs={{0,6},{1,7},{2,4},{3,5},{4,2},{5,3},{6,0},{7,1},{8,14},{9,15},{10,... | collective-permute-start | bytes 331784 | tf_op jit(solution)/shard_map/ppermute | solution.py:169
  71.4 9.6 %collective-permute-start.23 = (f32[216,128]{1,0:T(8,128)S(1)}, f32[216,128]{1,0:T(8,128)S(1)}, u32[]{:S(2)}, u32[]{:S(2)}) collective-permute-start(f32[216,128]{1,0:T(8,128)S(1)} %get-tuple-element.136), channel_id=1, source_target_pairs={{0,4},{1,5},{2,6},{3,7},{4,0},{5,1},{6,2},{7,3},{8,12},{9,13},{10,... | collective-permute-start | bytes 331784 | tf_op jit(solution)/shard_map/ppermute | solution.py:169
  71.4 9.6 %collective-permute-start.24 = (f32[216,128]{1,0:T(8,128)S(1)}, f32[216,128]{1,0:T(8,128)S(1)}, u32[]{:S(2)}, u32[]{:S(2)}) collective-permute-start(f32[216,128]{1,0:T(8,128)S(1)} %get-tuple-element.137), channel_id=1, source_target_pairs={{0,2},{1,3},{2,0},{3,1},{4,6},{5,7},{6,4},{7,5},{8,10},{9,11},{10,... | collective-permute-start | bytes 331784 | tf_op jit(solution)/shard_map/ppermute | solution.py:169
  82.4 14.0 %collective-permute-start.31 = (f32[6,48,384]{2,1,0:T(8,128)S(1)}, f32[6,48,384]{2,1,0:T(8,128)S(1)}, u32[]{:S(2)}, u32[]{:S(2)}) collective-permute-start(f32[6,48,384]{2,1,0:T(8,128)S(1)} %shard_map.154.refs_0_), channel_id=1, source_target_pairs={{0,16},{8,24},{16,0},{24,8},{1,17},{9,25},{17,1},{25,9},{2,18},{10... | collective-permute-start | bytes 1327112 | tf_op jit(solution)/shard_map/ppermute | solution.py:157
  84.5 7.9 %collective-permute-start.28 = (f32[216,128]{1,0:T(8,128)S(1)}, f32[216,128]{1,0:T(8,128)S(1)}, u32[]{:S(2)}, u32[]{:S(2)}) collective-permute-start(f32[216,128]{1,0:T(8,128)S(1)} %get-tuple-element.146), channel_id=1, source_target_pairs={{0,6},{1,7},{2,4},{3,5},{4,2},{5,3},{6,0},{7,1},{8,14},{9,15},{10,... | collective-permute-start | bytes 331784 | tf_op jit(solution)/shard_map/ppermute | solution.py:169
  86.6 9.8 %collective-permute-start.27 = (f32[216,128]{1,0:T(8,128)S(1)}, f32[216,128]{1,0:T(8,128)S(1)}, u32[]{:S(2)}, u32[]{:S(2)}) collective-permute-start(f32[216,128]{1,0:T(8,128)S(1)} %get-tuple-element.144), channel_id=1, source_target_pairs={{0,4},{1,5},{2,6},{3,7},{4,0},{5,1},{6,2},{7,3},{8,12},{9,13},{10,... | collective-permute-start | bytes 331784 | tf_op jit(solution)/shard_map/ppermute | solution.py:169
  86.6 9.8 %collective-permute-start.26 = (f32[216,128]{1,0:T(8,128)S(1)}, f32[216,128]{1,0:T(8,128)S(1)}, u32[]{:S(2)}, u32[]{:S(2)}) collective-permute-start(f32[216,128]{1,0:T(8,128)S(1)} %get-tuple-element.142), channel_id=1, source_target_pairs={{0,2},{1,3},{2,0},{3,1},{4,6},{5,7},{6,4},{7,5},{8,10},{9,11},{10,... | collective-permute-start | bytes 331784 | tf_op jit(solution)/shard_map/ppermute | solution.py:169
  97.8 12.6 %collective-permute-start.29 = (f32[4,216,128]{2,1,0:T(8,128)S(1)}, f32[4,216,128]{2,1,0:T(8,128)S(1)}, u32[]{:S(2)}, u32[]{:S(2)}) collective-permute-start(f32[4,216,128]{2,1,0:T(8,128)S(1)} %get-tuple-element.149), channel_id=1, source_target_pairs={{0,1},{1,0},{2,3},{3,2},{4,5},{5,4},{6,7},{7,6},{8,9},{9,8},{10,11... | collective-permute-start | bytes 1327112 | tf_op jit(solution)/shard_map/ppermute | solution.py:511
  100.7 10.3 %collective-permute-start.35 = (f32[216,128]{1,0:T(8,128)S(1)}, f32[216,128]{1,0:T(8,128)S(1)}, u32[]{:S(2)}, u32[]{:S(2)}) collective-permute-start(f32[216,128]{1,0:T(8,128)S(1)} %get-tuple-element.159), channel_id=1, source_target_pairs={{0,6},{1,7},{2,4},{3,5},{4,2},{5,3},{6,0},{7,1},{8,14},{9,15},{10,... | collective-permute-start | bytes 331784 | tf_op jit(solution)/shard_map/ppermute | solution.py:169
  102.8 9.6 %collective-permute-start.34 = (f32[216,128]{1,0:T(8,128)S(1)}, f32[216,128]{1,0:T(8,128)S(1)}, u32[]{:S(2)}, u32[]{:S(2)}) collective-permute-start(f32[216,128]{1,0:T(8,128)S(1)} %get-tuple-element.157), channel_id=1, source_target_pairs={{0,4},{1,5},{2,6},{3,7},{4,0},{5,1},{6,2},{7,3},{8,12},{9,13},{10,... | collective-permute-start | bytes 331784 | tf_op jit(solution)/shard_map/ppermute | solution.py:169
  102.8 9.6 %collective-permute-start.33 = (f32[216,128]{1,0:T(8,128)S(1)}, f32[216,128]{1,0:T(8,128)S(1)}, u32[]{:S(2)}, u32[]{:S(2)}) collective-permute-start(f32[216,128]{1,0:T(8,128)S(1)} %get-tuple-element.155), channel_id=1, source_target_pairs={{0,2},{1,3},{2,0},{3,1},{4,6},{5,7},{6,4},{7,5},{8,10},{9,11},{10,... | collective-permute-start | bytes 331784 | tf_op jit(solution)/shard_map/ppermute | solution.py:169
  113.8 12.2 %collective-permute-start.36 = (f32[4,216,128]{2,1,0:T(8,128)S(1)}, f32[4,216,128]{2,1,0:T(8,128)S(1)}, u32[]{:S(2)}, u32[]{:S(2)}) collective-permute-start(f32[4,216,128]{2,1,0:T(8,128)S(1)} %get-tuple-element.163), channel_id=1, source_target_pairs={{0,1},{1,0},{2,3},{3,2},{4,5},{5,4},{6,7},{7,6},{8,9},{9,8},{10,11... | collective-permute-start | bytes 1327112 | tf_op jit(solution)/shard_map/ppermute | solution.py:511
  114.7 14.0 %collective-permute-start.39 = (f32[216,128]{1,0:T(8,128)S(1)}, f32[216,128]{1,0:T(8,128)S(1)}, u32[]{:S(2)}, u32[]{:S(2)}) collective-permute-start(f32[216,128]{1,0:T(8,128)S(1)} %get-tuple-element.172), channel_id=1, source_target_pairs={{0,6},{1,7},{2,4},{3,5},{4,2},{5,3},{6,0},{7,1},{8,14},{9,15},{10,... | collective-permute-start | bytes 331784 | tf_op jit(solution)/shard_map/ppermute | solution.py:169
  116.5 15.3 %collective-permute-start.38 = (f32[216,128]{1,0:T(8,128)S(1)}, f32[216,128]{1,0:T(8,128)S(1)}, u32[]{:S(2)}, u32[]{:S(2)}) collective-permute-start(f32[216,128]{1,0:T(8,128)S(1)} %get-tuple-element.169), channel_id=1, source_target_pairs={{0,4},{1,5},{2,6},{3,7},{4,0},{5,1},{6,2},{7,3},{8,12},{9,13},{10,... | collective-permute-start | bytes 331784 | tf_op jit(solution)/shard_map/ppermute | solution.py:169
  116.5 15.3 %collective-permute-start.37 = (f32[216,128]{1,0:T(8,128)S(1)}, f32[216,128]{1,0:T(8,128)S(1)}, u32[]{:S(2)}, u32[]{:S(2)}) collective-permute-start(f32[216,128]{1,0:T(8,128)S(1)} %get-tuple-element.166), channel_id=1, source_target_pairs={{0,2},{1,3},{2,0},{3,1},{4,6},{5,7},{6,4},{7,5},{8,10},{9,11},{10,... | collective-permute-start | bytes 331784 | tf_op jit(solution)/shard_map/ppermute | solution.py:169
  126.6 7.9 %collective-permute-start.42 = (f32[216,128]{1,0:T(8,128)S(1)}, f32[216,128]{1,0:T(8,128)S(1)}, u32[]{:S(2)}, u32[]{:S(2)}) collective-permute-start(f32[216,128]{1,0:T(8,128)S(1)} %get-tuple-element.180), channel_id=1, source_target_pairs={{0,6},{1,7},{2,4},{3,5},{4,2},{5,3},{6,0},{7,1},{8,14},{9,15},{10,... | collective-permute-start | bytes 331784 | tf_op jit(solution)/shard_map/ppermute | solution.py:169
  128.8 8.9 %collective-permute-start.41 = (f32[216,128]{1,0:T(8,128)S(1)}, f32[216,128]{1,0:T(8,128)S(1)}, u32[]{:S(2)}, u32[]{:S(2)}) collective-permute-start(f32[216,128]{1,0:T(8,128)S(1)} %get-tuple-element.178), channel_id=1, source_target_pairs={{0,4},{1,5},{2,6},{3,7},{4,0},{5,1},{6,2},{7,3},{8,12},{9,13},{10,... | collective-permute-start | bytes 331784 | tf_op jit(solution)/shard_map/ppermute | solution.py:169
  128.8 8.9 %collective-permute-start.40 = (f32[216,128]{1,0:T(8,128)S(1)}, f32[216,128]{1,0:T(8,128)S(1)}, u32[]{:S(2)}, u32[]{:S(2)}) collective-permute-start(f32[216,128]{1,0:T(8,128)S(1)} %get-tuple-element.176), channel_id=1, source_target_pairs={{0,2},{1,3},{2,0},{3,1},{4,6},{5,7},{6,4},{7,5},{8,10},{9,11},{10,... | collective-permute-start | bytes 331784 | tf_op jit(solution)/shard_map/ppermute | solution.py:169
  (22 other events, 246.2 us)
